TPU v7x, 512 devices: a whole 4x8x8 slice. The times are simulated.
512 devices in a mesh: dp: 32 (over y, x), seq: 16 (over z, core).
Axes of the slice: x: 4, y: 8, z: 8, core: 2. Of those that a mesh axis runs over, the one named last changes fastest.
Arguments:
- qkv_vis: bfloat16 [57344, 9216], P(('dp', 'seq')), may hold values from -8 to 8
- qkv_txt: bfloat16 [8192, 9216], P(('dp', 'seq')), may hold values from -8 to 8
- vis_segments: int32 [57344], P(('dp', 'seq')), may hold values from 0 to 63, as said below
- txt_segments: int32 [8192], P(('dp', 'seq')), may hold values from 0 to 63, as said below
- head_map: int32 [24], replicated, may hold values from 0 to 15, as said below
- w_out: bfloat16 [3072, 1536], P('dp'), may hold values from -0.109375 to 0.109375
Outputs:
- vis_out: bfloat16 [57344, 1536], P(('dp', 'seq'))
- txt_out: bfloat16 [8192, 3072], P(('dp', 'seq'))
- lse_slots: float32 [32, 65536], P('seq', 'dp')
Inputs may be any that keep to these rules, and one draw needn't show every extreme that they name: `vis_segments`: within each group of 1792 rows (group g), a first run of rows carries 2 g and the rest 2 g + 1; each run holds 448 rows or more. `txt_segments`: within each group of 256 rows (group g), a first run of rows carries 2 g and the rest 2 g + 1; each run holds 64 rows or more. `head_map`: each index of seq is named by 2 heads or by one fewer; which indices are named 2 times changes from draw to draw.
All inputs are finite; a program needn't handle non-finite values.
Results may differ from a plain program's by a relative error of at most 0.008.
Values may be sent and summed in bfloat16 or wider, within the bound.
No kernel may reach another device: no remote copies, remote signals or barrier semaphores. Data moves between devices by JAX's collectives and lax.ppermute only.
A program may use at most 64 MiB of HBM per device.

v0:
```python
import math

import jax
import jax.numpy as jnp
from jax import lax
from jax.sharding import PartitionSpec as P

HEADS = 24
HEAD_DIM = 128


neg_large = -1e30


def attend_rows(queries, key_rows, value_rows, seg_queries, seg_keys):
    row_count = queries.shape[0]
    block_rows = math.gcd(row_count, 512)
    scaling = queries.shape[-1] ** (-0.5)

    def one_block(number):
        offset = number * block_rows
        query_block = lax.dynamic_slice_in_dim(queries, offset, block_rows, 0)
        labels = lax.dynamic_slice_in_dim(seg_queries, offset, block_rows, 0)
        scores = (
            jnp.einsum("qd,kd->qk", query_block, key_rows, preferred_element_type=jnp.float32)
            * scaling
        )
        scores = jnp.where(labels[:, None] == seg_keys[None, :], scores, neg_large)
        highest = jnp.max(scores, axis=1, keepdims=True)
        exponent = jnp.exp(scores - highest)
        totals = jnp.sum(exponent, axis=1, keepdims=True)
        weights = (exponent / totals).astype(jnp.bfloat16)
        blended = jnp.dot(weights, value_rows, preferred_element_type=jnp.float32).astype(
            jnp.bfloat16
        )
        return (blended, highest[:, 0] + jnp.log(totals[:, 0]))

    blended, log_totals = lax.map(one_block, jnp.arange(row_count // block_rows, dtype=jnp.int32))
    return (blended.reshape(row_count, value_rows.shape[-1]), log_totals.reshape(row_count))


def slot_table(head_map, seq_count, slot_most):
    devices_all = jnp.arange(seq_count, dtype=jnp.int32)
    same_device = (head_map[None, :] == devices_all[:, None]).astype(jnp.int32)
    head_ranks = jnp.cumsum(same_device, axis=1) - 1
    slot_ids = jnp.arange(slot_most, dtype=jnp.int32)
    picked = same_device[:, None, :] * (head_ranks[:, None, :] == slot_ids[None, :, None]).astype(
        jnp.int32
    )
    head_ids = jnp.arange(head_map.shape[0], dtype=jnp.int32)
    head_of_slot = jnp.sum(picked * head_ids[None, None, :], axis=2)
    slot_valid = jnp.sum(picked, axis=2)
    own_rank = jnp.sum(same_device * head_ranks, axis=0)
    slot_of_head = head_map * slot_most + own_rank
    return (head_of_slot, slot_valid, slot_of_head)


def joint_order(rows_first, seq_count, vis_local):
    trailing = rows_first.shape[1:]
    shaped = rows_first.reshape((seq_count, -1) + trailing)
    vis_part = shaped[:, :vis_local].reshape((-1,) + trailing)
    txt_part = shaped[:, vis_local:].reshape((-1,) + trailing)
    return jnp.concatenate([vis_part, txt_part], axis=0)


def on_device(qkv_vis, qkv_txt, vis_segments, txt_segments, head_map, w_out):
    seq_count = lax.axis_size("seq")
    seq_index = lax.axis_index("seq")
    vis_local = qkv_vis.shape[0]
    txt_local = qkv_txt.shape[0]
    row_local = vis_local + txt_local
    slot_most = (HEADS + seq_count - 1) // seq_count
    local_rows = jnp.concatenate([qkv_vis, qkv_txt], axis=0).reshape(row_local, 3, HEADS, HEAD_DIM)
    vis_labels, txt_labels = (
        lax.all_gather(vis_segments, "seq", axis=0, tiled=True),
        lax.all_gather(txt_segments, "seq", axis=0, tiled=True),
    )
    labels_all = jnp.concatenate(
        [vis_labels.reshape(seq_count, vis_local), txt_labels.reshape(seq_count, txt_local)], axis=1
    ).reshape(-1)
    head_of_slot, slot_valid, slot_of_head = slot_table(head_map, seq_count, slot_most)
    flat_heads = head_of_slot.reshape(-1)
    flat_valid = slot_valid.reshape(-1)
    outgoing = (
        jnp.take(local_rows, flat_heads, axis=2)
        * flat_valid.astype(jnp.bfloat16)[None, None, :, None]
    )
    outgoing = outgoing.reshape(row_local, 3, seq_count, slot_most, HEAD_DIM)
    received = lax.all_to_all(outgoing, "seq", split_axis=2, concat_axis=0, tiled=True)
    blended_list = []
    lse_list = []
    for slot_item in range(received.shape[3]):
        part_rows = received[:, :, 0, slot_item]
        blended, log_totals = attend_rows(
            part_rows[:, 0], part_rows[:, 1], part_rows[:, 2], labels_all, labels_all
        )
        blended_list.append(blended)
        lse_list.append(log_totals)
    slot_blended = jnp.stack(blended_list, axis=1)
    slot_lse = jnp.stack(lse_list, axis=1)
    returned = lax.all_to_all(slot_blended, "seq", split_axis=0, concat_axis=1, tiled=True)
    attention = jnp.take(returned, slot_of_head, axis=1).reshape(row_local, HEADS * HEAD_DIM)
    own_valid = lax.dynamic_index_in_dim(slot_valid, seq_index, 0, keepdims=False)
    ordered = joint_order(slot_lse, seq_count, vis_local)
    lse_slots = jnp.where(own_valid[None, :] > 0, ordered, jnp.zeros_like(ordered)).T
    vis_attention = attention[:vis_local]
    txt_out = attention[vis_local:]
    vis_sum = jnp.dot(
        vis_attention,
        lax.all_gather(w_out, "dp", axis=0, tiled=True),
        preferred_element_type=jnp.float32,
    )
    vis_out = vis_sum.astype(jnp.bfloat16)
    return (vis_out, txt_out, lse_slots)


def solution(mesh):
    in_specs = (
        P(("dp", "seq"), None),
        P(("dp", "seq"), None),
        P(("dp", "seq")),
        P(("dp", "seq")),
        P(),
        P("dp", None),
    )
    out_specs = (P(("dp", "seq"), None), P(("dp", "seq"), None), P("seq", "dp"))
    return jax.shard_map(
        on_device, mesh=mesh, in_specs=in_specs, out_specs=out_specs, check_vma=False
    )
```

profile of v0, /device:TPU:1, one launch (start us, length us, event | category | flops | bytes accessed | tf_op | source)
XLA Modules:
  0.0 247.8 jit_solution(1399461664454287985)
XLA Ops:
  9.7 3.0 %copy.42 = bf16[112,9216]{0,1:T(8,128)(2,1)S(1)} copy(bf16[112,9216]{1,0:T(8,128)(2,1)} %param.10) | data formatting | bytes 4128768 | tf_op args[0]
  12.7 1.9 copy.43
  14.6 3.6 %pad_maximum_fusion = bf16[128,9216]{0,1:T(8,128)(2,1)} fusion(bf16[16,9216]{0,1:T(8,128)(2,1)} %copy.43, bf16[112,9216]{0,1:T(8,128)(2,1)S(1)} %copy.42), kind=kLoop, calls=%fused_computation.26 | loop fusion | flops 4718592 | bytes 4718592 | tf_op jit(solution)/shard_map/concatenate | solution.py:73
  18.2 3.0 %copy.45 = bf16[128,3,24,128]{3,0,2,1:T(8,128)(2,1)S(1)} copy(bf16[128,3,24,128]{0,3,2,1:T(8,128)(2,1)} %bitcast.103) | data formatting | bytes 4718592 | tf_op jit(solution)/shard_map/reshape | solution.py:73
  21.2 2.6 %gather_fusion = bf16[32,128,3,128]{3,1,2,0:T(8,128)(2,1)} fusion(bf16[128,3,24,128]{3,0,2,1:T(8,128)(2,1)S(1)} %copy.45, s32[1024]{0:T(1024)S(1)} %get-tuple-element.160), kind=kCustom, calls=%fused_computation | custom fusion | bytes 6291584 | tf_op jit(solution)/shard_map/jit(_take)/gather | solution.py:85
  23.9 2.1 copy.46
  26.6 1.8 copy.48
  28.5 12.0 %all-to-all-start = ((bf16[128,3,16,2,128]{4,0,3,1,2:T(8,128)(2,1)}), bf16[128,3,16,2,128]{4,0,3,1,2:T(8,128)(2,1)S(1)}, u32[]{:S(2)}, u32[]{:S(2)}) async-start(bf16[128,3,16,2,128]{4,0,3,1,2:T(8,128)(2,1)} %copy.48), calls=%async_computation | async-start | bytes 6291456 | tf_op jit(solution)/shard_map/all_to_all | solution.py:89
  44.3 73.9 %all-reduce.2 = (s32[256]{0:T(256)S(1)}, s32[1792]{0:T(1024)S(1)}) all-reduce(s32[256]{0:T(256)S(1)} %dynamic-update-slice.1, s32[1792]{0:T(1024)S(1)} %dynamic-update-slice), channel_id=1, replica_groups=mesh['dp'=32,'seq'=16] {'seq'}, use_global_device_ids=true, to_apply=%add.1 | all-reduce | flops 2048 | bytes 16384
  120.0 36.4 %while.24 = (s32[]{:T(128)}, bf16[4,512,128]{2,1,0:T(8,128)(2,1)S(1)}, f32[4,512]{1,0:T(4,128)S(1)}, s32[4]{0:T(128)S(1)}, s32[2048]{0:T(1024)S(1)}, /*index=5*/...) while((s32[]{:T(128)}, ...), condition=%wide.region_7.8_spmd, body=%wide.region_4.7_spmd.sunk | while | flops 546373120 | bytes 30705892 | solution.py:38
  123.1 2.1 copy-done
  126.0 3.2 %fusion.42 = bf16[4,512,128]{2,1,0:T(8,128)(2,1)S(1)} fusion(bf16[4,512,128]{2,1,0:T(8,128)(2,1)S(1)} %get-tuple-element.332, s32[]{:T(128)} %get-tuple-element.331, bf16[2048,128]{1,0:T(8,128)(2,1)S(1)} %get-tuple-element.352, f32[512,2048]{1,0:T(8,128)} %copy-done, f32[512]{0:T(512)S(1)} %fusion.41, f32[512]{0:T(512)S(1)} %get-tuple-element.267), kind=kOutput, calls=%fused_computation.9.clone.1 | convolution fusion | flops 271646720 | bytes 4853764 | tf_op jit(solution)/shard_map/while/body/eval_jaxpr/dot_general | solution.py:33
  132.3 2.1 copy-done
  135.1 3.1 %fusion.42 = bf16[4,512,128]{2,1,0:T(8,128)(2,1)S(1)} fusion(bf16[4,512,128]{2,1,0:T(8,128)(2,1)S(1)} %get-tuple-element.332, s32[]{:T(128)} %get-tuple-element.331, bf16[2048,128]{1,0:T(8,128)(2,1)S(1)} %get-tuple-element.352, f32[512,2048]{1,0:T(8,128)} %copy-done, f32[512]{0:T(512)S(1)} %fusion.41, f32[512]{0:T(512)S(1)} %get-tuple-element.267), kind=kOutput, calls=%fused_computation.9.clone.1 | convolution fusion | flops 271646720 | bytes 4853764 | tf_op jit(solution)/shard_map/while/body/eval_jaxpr/dot_general | solution.py:33
  139.6 1.8 fusion.40
  141.4 2.1 copy-done
  144.2 3.1 %fusion.42 = bf16[4,512,128]{2,1,0:T(8,128)(2,1)S(1)} fusion(bf16[4,512,128]{2,1,0:T(8,128)(2,1)S(1)} %get-tuple-element.332, s32[]{:T(128)} %get-tuple-element.331, bf16[2048,128]{1,0:T(8,128)(2,1)S(1)} %get-tuple-element.352, f32[512,2048]{1,0:T(8,128)} %copy-done, f32[512]{0:T(512)S(1)} %fusion.41, f32[512]{0:T(512)S(1)} %get-tuple-element.267), kind=kOutput, calls=%fused_computation.9.clone.1 | convolution fusion | flops 271646720 | bytes 4853764 | tf_op jit(solution)/shard_map/while/body/eval_jaxpr/dot_general | solution.py:33
  150.5 2.1 copy-done
  153.3 3.1 %fusion.42 = bf16[4,512,128]{2,1,0:T(8,128)(2,1)S(1)} fusion(bf16[4,512,128]{2,1,0:T(8,128)(2,1)S(1)} %get-tuple-element.332, s32[]{:T(128)} %get-tuple-element.331, bf16[2048,128]{1,0:T(8,128)(2,1)S(1)} %get-tuple-element.352, f32[512,2048]{1,0:T(8,128)} %copy-done, f32[512]{0:T(512)S(1)} %fusion.41, f32[512]{0:T(512)S(1)} %get-tuple-element.267), kind=kOutput, calls=%fused_computation.9.clone.1 | convolution fusion | flops 271646720 | bytes 4853764 | tf_op jit(solution)/shard_map/while/body/eval_jaxpr/dot_general | solution.py:33
  156.5 32.7 %while.25 = (s32[]{:T(128)}, bf16[4,512,128]{2,1,0:T(8,128)(2,1)S(1)}, f32[4,512]{1,0:T(4,128)S(1)}, s32[4]{0:T(128)S(1)}, s32[2048]{0:T(1024)S(1)}, /*index=5*/...) while((s32[]{:T(128)}, ...), condition=%wide.region_11.12_spmd, body=%wide.region_8.11_spmd.sunk | while | flops 546373120 | bytes 30705892 | solution.py:38
  158.7 2.1 copy-done.1
  161.6 3.1 %fusion.47 = bf16[4,512,128]{2,1,0:T(8,128)(2,1)S(1)} fusion(bf16[4,512,128]{2,1,0:T(8,128)(2,1)S(1)} %get-tuple-element.293, s32[]{:T(128)} %get-tuple-element.292, bf16[2048,128]{1,0:T(8,128)(2,1)S(1)} %get-tuple-element.313, f32[512,2048]{1,0:T(8,128)} %copy-done.1, f32[512]{0:T(512)S(1)} %fusion.46, f32[512]{0:T(512)S(1)} %get-tuple-element.278), kind=kOutput, calls=%fused_computation.20.clone.1 | convolution fusion | flops 271646720 | bytes 4853764 | tf_op jit(solution)/shard_map/while/body/eval_jaxpr/dot_general | solution.py:33
  166.9 2.1 copy-done.1
  169.7 3.1 %fusion.47 = bf16[4,512,128]{2,1,0:T(8,128)(2,1)S(1)} fusion(bf16[4,512,128]{2,1,0:T(8,128)(2,1)S(1)} %get-tuple-element.293, s32[]{:T(128)} %get-tuple-element.292, bf16[2048,128]{1,0:T(8,128)(2,1)S(1)} %get-tuple-element.313, f32[512,2048]{1,0:T(8,128)} %copy-done.1, f32[512]{0:T(512)S(1)} %fusion.46, f32[512]{0:T(512)S(1)} %get-tuple-element.278), kind=kOutput, calls=%fused_computation.20.clone.1 | convolution fusion | flops 271646720 | bytes 4853764 | tf_op jit(solution)/shard_map/while/body/eval_jaxpr/dot_general | solution.py:33
  175.1 2.1 copy-done.1
  177.9 3.1 %fusion.47 = bf16[4,512,128]{2,1,0:T(8,128)(2,1)S(1)} fusion(bf16[4,512,128]{2,1,0:T(8,128)(2,1)S(1)} %get-tuple-element.293, s32[]{:T(128)} %get-tuple-element.292, bf16[2048,128]{1,0:T(8,128)(2,1)S(1)} %get-tuple-element.313, f32[512,2048]{1,0:T(8,128)} %copy-done.1, f32[512]{0:T(512)S(1)} %fusion.46, f32[512]{0:T(512)S(1)} %get-tuple-element.278), kind=kOutput, calls=%fused_computation.20.clone.1 | convolution fusion | flops 271646720 | bytes 4853764 | tf_op jit(solution)/shard_map/while/body/eval_jaxpr/dot_general | solution.py:33
  183.2 2.1 copy-done.1
  186.1 3.1 %fusion.47 = bf16[4,512,128]{2,1,0:T(8,128)(2,1)S(1)} fusion(bf16[4,512,128]{2,1,0:T(8,128)(2,1)S(1)} %get-tuple-element.293, s32[]{:T(128)} %get-tuple-element.292, bf16[2048,128]{1,0:T(8,128)(2,1)S(1)} %get-tuple-element.313, f32[512,2048]{1,0:T(8,128)} %copy-done.1, f32[512]{0:T(512)S(1)} %fusion.46, f32[512]{0:T(512)S(1)} %get-tuple-element.278), kind=kOutput, calls=%fused_computation.20.clone.1 | convolution fusion | flops 271646720 | bytes 4853764 | tf_op jit(solution)/shard_map/while/body/eval_jaxpr/dot_general | solution.py:33
  189.3 9.5 %copy.50 = bf16[2048,2,128]{2,1,0:T(2,128)(2,1)} copy(bf16[2048,2,128]{2,0,1:T(8,128)(2,1)S(1)} %pad_maximum_fusion.1) | data formatting | bytes 2097152 | tf_op jit(solution)/shard_map/stack | solution.py:99
  198.7 6.7 %all-to-all-start.1 = ((bf16[2048,2,128]{2,1,0:T(2,128)(2,1)}), bf16[2048,2,128]{2,1,0:T(2,128)(2,1)S(1)}, u32[]{:S(2)}, u32[]{:S(2)}) async-start(bf16[2048,2,128]{2,1,0:T(2,128)(2,1)} %copy.50), calls=%async_computation.1 | async-start | bytes 2097152 | tf_op jit(solution)/shard_map/all_to_all | solution.py:101
  206.5 26.8 %all-to-all-done.1 = bf16[2048,2,128]{2,1,0:T(2,128)(2,1)S(1)} async-done(((bf16[2048,2,128]{2,1,0:T(2,128)(2,1)}), bf16[2048,2,128]{2,1,0:T(2,128)(2,1)S(1)}, u32[]{:S(2)}, u32[]{:S(2)}) %all-to-all-start.1) | async-done | bytes 1048608 | tf_op jit(solution)/shard_map/all_to_all | solution.py:101
  235.1 5.9 %convolution_convert_fusion = bf16[112,1536]{1,0:T(8,128)(2,1)} fusion(bf16[3072,1536]{1,0:T(8,128)(2,1)} %all-gather.2.cloned.1.call-done, bf16[128,24,128]{2,0,1:T(8,128)(2,1)S(1)} %select_bitcast_fusion), kind=kOutput, calls=%fused_computation.25 | convolution fusion | flops 1057136640 | bytes 10469376 | tf_op jit(solution)/shard_map/dot_general | solution.py:108
  (113 shorter events, 31.0 us)
Async XLA Ops:
  7.2 5.6 %copy-start.2 = (bf16[16,9216]{1,0:T(8,128)(2,1)S(1)}, bf16[16,9216]{1,0:T(8,128)(2,1)}, u32[]{:S(2)}) copy-start(bf16[16,9216]{1,0:T(8,128)(2,1)} %param.11) | copy-start | bytes 884740
  28.4 15.3 %copy-start.3 = (s32[112]{0:T(128)S(1)}, s32[112]{0:T(128)}, u32[]{:S(2)}) copy-start(s32[112]{0:T(128)} %param.12) | copy-start | bytes 1348
  28.5 15.6 %copy-start.4 = (s32[16]{0:T(128)S(1)}, s32[16]{0:T(128)}, u32[]{:S(2)}) copy-start(s32[16]{0:T(128)} %param.13) | copy-start | bytes 196
  28.5 90.0 %all-to-all-start = ((bf16[128,3,16,2,128]{4,0,3,1,2:T(8,128)(2,1)}), bf16[128,3,16,2,128]{4,0,3,1,2:T(8,128)(2,1)S(1)}, u32[]{:S(2)}, u32[]{:S(2)}) async-start(bf16[128,3,16,2,128]{4,0,3,1,2:T(8,128)(2,1)} %copy.48), calls=%async_computation | async-start | bytes 6291456 | tf_op jit(solution)/shard_map/all_to_all | solution.py:89
  40.4 194.7 %all-gather.2.cloned.1.call-start = ((), (), s32[]{:S(2)}) async-start(), calls=%async_computation.2 | async-start | bytes 9732096 | tf_op jit(solution)/shard_map/all_gather | solution.py:110
  123.1 2.1 copy-start
  132.3 2.1 copy-start
  141.4 2.1 copy-start
  150.5 2.1 copy-start
  158.7 2.1 copy-start.1
  166.9 2.1 copy-start.1
  175.1 2.1 copy-start.1
  183.2 2.1 copy-start.1
  198.7 34.6 %all-to-all-start.1 = ((bf16[2048,2,128]{2,1,0:T(2,128)(2,1)}), bf16[2048,2,128]{2,1,0:T(2,128)(2,1)S(1)}, u32[]{:S(2)}, u32[]{:S(2)}) async-start(bf16[2048,2,128]{2,1,0:T(2,128)(2,1)} %copy.50), calls=%async_computation.1 | async-start | bytes 2097152 | tf_op jit(solution)/shard_map/all_to_all | solution.py:101
Sparse Core Ops, SparseCore 0:
  44.4 109.3 all-gather.1
where the time goes:
time: 249 us; the launch traced here: 248 us
  blocking collectives  73.9 us (30%)
  local copies, waits for them, and re-layouts  51.9 us (21%)
  matrix products  41.5 us (17%)
  waiting for transfers between devices  27.5 us (11%)
  starting transfers between devices  18.7 us (8%)
  between operations  15.6 us (6%)
  other arithmetic  13.3 us (5%)
  loops' own time  5.47 us (2%)
    unnamed x1, blocking collectives  73.9 us
    all_to_all x1, waiting for transfers between devices, on_device(): lax.all_to_all(slot_blended, 'seq', split_axis=0, concat_axis=1, tiled=True)  26.8 us
    dot_general x8, matrix products, one_block(): jnp.dot(weights, value_rows, preferred_element_type=jnp.float32)  24.8 us
    while x16, local copies, waits for them, and re-layouts  16.6 us
    all_to_all x1, starting transfers between devices, on_device(): lax.all_to_all(outgoing, 'seq', split_axis=2, concat_axis=0, tiled=True)  12 us
    dot_general x8, matrix products, one_block(): jnp.einsum('qd,kd->qk', query_block, key_rows, preferred_element_type=jnp...  10.8 us
    another operation x1, local copies, waits for them, and re-layouts, on_device(): slot_blended = jnp.stack(blended_list, axis=1)  9.46 us
    all_to_all x1, starting transfers between devices, on_device(): lax.all_to_all(slot_blended, 'seq', split_axis=0, concat_axis=1, tiled=True)  6.66 us
  transfers between devices with their start and end apart: 3, of which 1 were waited for; matrix products, arithmetic and copies ran while one was open for 25% of the time, Pallas kernels for 0%

commit v1 on v0

v1 whole, which is shorter than its diff:
```python
import functools

import jax
import jax.numpy as jnp
from jax import lax
from jax.experimental import pallas as pl
from jax.experimental.pallas import tpu as pltpu
from jax.sharding import PartitionSpec as P

HEADS = 24
HEAD_DIM = 128
N_SEQ = 16
VIS_ROWS = 112
TXT_ROWS = 16
ROWS = VIS_ROWS + TXT_ROWS
HALF = ROWS // 2
TRIO = 3 * HEAD_DIM
CHIPS = 8
A_ROWS = 3 * ROWS
SEND_ROWS = A_ROWS + 3 * HALF
CUT_ROWS = 16
PAYLOAD = SEND_ROWS + CUT_ROWS
RET_ROWS = ROWS + HALF
VIS_SEQ = VIS_ROWS * N_SEQ
TXT_SEQ = TXT_ROWS * N_SEQ
SLOTS = 2
LOG2E = 1.4426950408889634
LN2 = 0.6931471805599453
BIG = -1e30


def pack_kernel(seg_vis, seg_txt, vq, vk, vv, tq, tk, tv, out):
    for part, (vis, txt) in enumerate(((vq, tq), (vk, tk), (vv, tv))):
        row = part * ROWS
        for core, column in ((0, 0), (1, 2 * HEAD_DIM)):
            out[core, row : row + VIS_ROWS, :] = vis[:, column : column + HEAD_DIM]
            out[core, row + VIS_ROWS : row + ROWS, :] = txt[:, column : column + HEAD_DIM]
        row = A_ROWS + part * HALF
        middle = slice(HEAD_DIM, 2 * HEAD_DIM)
        out[0, row : row + HALF, :] = vis[:HALF, middle]
        out[1, row : row + VIS_ROWS - HALF, :] = vis[HALF:, middle]
        out[1, row + VIS_ROWS - HALF : row + HALF, :] = txt[:, middle]

    def even(ref):
        parity = (ref[...] & 1).astype(jnp.float32)
        count = jnp.sum(1.0 - parity, axis=1, keepdims=True)
        return jnp.broadcast_to(count, (CUT_ROWS // 2, HEAD_DIM))

    cuts = jnp.concatenate([even(seg_vis), even(seg_txt)], axis=0).astype(jnp.bfloat16)
    out[0, SEND_ROWS:PAYLOAD, :] = cuts
    out[1, SEND_ROWS:PAYLOAD, :] = cuts


def pack(qkv_vis, qkv_txt, vis_segments, txt_segments):
    def spec(rows, part):
        return pl.BlockSpec((rows, TRIO), lambda i: (0, part * CHIPS + i))

    return pl.pallas_call(
        pack_kernel,
        grid=(CHIPS,),
        in_specs=[
            pl.BlockSpec((1, VIS_ROWS), lambda i: (0, 0)),
            pl.BlockSpec((1, TXT_ROWS), lambda i: (0, 0)),
            *[spec(VIS_ROWS, part) for part in range(3)],
            *[spec(TXT_ROWS, part) for part in range(3)],
        ],
        out_specs=pl.BlockSpec((2, PAYLOAD, HEAD_DIM), lambda i: (i, 0, 0)),
        out_shape=jax.ShapeDtypeStruct((N_SEQ, PAYLOAD, HEAD_DIM), jnp.bfloat16),
        name="pack",
    )(
        vis_segments.reshape(1, VIS_ROWS),
        txt_segments.reshape(1, TXT_ROWS),
        *[qkv_vis] * 3,
        *[qkv_txt] * 3,
    )


def second_clip(cut_ref, source, row):
    cuts = jnp.sum(cut_ref[...].astype(jnp.float32), axis=0)
    vis_cut, txt_cut = cuts[0:1, 0:1], cuts[CUT_ROWS // 2 : CUT_ROWS // 2 + 1, 0:1]
    vis_place = (source * VIS_ROWS + row).astype(jnp.float32)
    txt_place = (source * TXT_ROWS + row - VIS_ROWS).astype(jnp.float32)
    is_second = jnp.where(row < VIS_ROWS, vis_place - vis_cut, txt_place - txt_cut) >= 0.0
    return jnp.where(is_second, 1.0, 0.0)


def clip_columns(second, first_value, second_value):
    lane = lax.broadcasted_iota(jnp.int32, second.shape, 1)
    feature = jnp.where(lane == 0, first_value(second), second_value(second))
    return jnp.where(lane < 2, feature, 0.0).astype(jnp.bfloat16)


def attend_block(q, q_clip, k_wide, v_turned, keys):
    q_wide = jnp.concatenate([q, q_clip], axis=1)
    scores = lax.dot_general(
        k_wide, q_wide, (((1,), (1,)), ((), ())), preferred_element_type=jnp.float32
    )
    factor = HEAD_DIM**-0.5 * LOG2E
    highest = jnp.max(scores, axis=0, keepdims=True)
    exponent = jnp.exp2((scores - highest) * factor)
    total = jnp.sum(exponent, axis=0, keepdims=True)
    blended = jnp.dot(v_turned, exponent.astype(jnp.bfloat16), preferred_element_type=jnp.float32)
    out = jnp.swapaxes(blended * (1.0 / total), 0, 1).astype(jnp.bfloat16)
    return out, highest * HEAD_DIM**-0.5 + jnp.log2(total) * LN2


def attention_kernel(q_rows, half, *refs):
    if half is None:
        cut, q, k, v, out, lse, k_wide, v_turned = refs
        pairs = ((k, v, 0),)
    else:
        core, cut, q, own_kv, far_kv, _, out, lse, k_wide, v_turned = refs
        pairs = ((own_kv, None, 0), (far_kv, None, 1))
    step = pl.program_id(0)
    rows = ROWS if half is None else HALF

    def token(shape, first_source, offset):
        index = lax.broadcasted_iota(jnp.int32, shape, 0)
        return first_source + index // rows, index % rows + offset

    @pl.when(step == 0)
    def _():
        for k_ref, v_ref, place in pairs:
            keys = N_SEQ * rows
            offset = 0
            if half is not None:
                offset = HALF * (core[0] if place == 0 else 1 - core[0])
                kv = k_ref[...]
                k_now, v_now = kv[:, :HALF], kv[:, HALF:]
            else:
                k_now, v_now = k_ref[...], v_ref[...]
            source, row = token((keys, HEAD_DIM), 0, offset)
            second = second_clip(cut, source, row)
            at = slice(place * keys, (place + 1) * keys)
            k_wide[at, :HEAD_DIM] = k_now.reshape(keys, HEAD_DIM)
            k_wide[at, HEAD_DIM:] = clip_columns(second, lambda s: BIG * s, lambda s: BIG * (1.0 - s))
            v_turned[:, at] = jnp.swapaxes(v_now.reshape(keys, HEAD_DIM), 0, 1)

    offset = 0 if half is None else HALF * core[0]
    source, row = token((q_rows, HEAD_DIM), step * (q_rows // rows), offset)
    q_clip = clip_columns(second_clip(cut, source, row), lambda s: 1.0 - s, lambda s: s)
    result, log_total = attend_block(
        q[...].reshape(q_rows, HEAD_DIM), q_clip, k_wide[...], v_turned[...], None
    )
    out[...] = result.reshape(out.shape)
    lse[...] = log_total.reshape(lse.shape)


Q_ROWS = 256
VMEM = 48 * 2**20


def attention_cost(queries, keys):
    return pl.CostEstimate(
        flops=queries * keys * HEAD_DIM * 8,
        bytes_accessed=4 * keys * HEAD_DIM * 2,
        transcendentals=queries * keys,
    )


def attend_whole(received):
    sources = Q_ROWS // ROWS
    steps = N_SEQ // sources
    keys = N_SEQ * ROWS
    return pl.pallas_call(
        functools.partial(attention_kernel, Q_ROWS, None),
        grid=(steps,),
        in_specs=[
            pl.BlockSpec((N_SEQ, CUT_ROWS, HEAD_DIM), lambda i: (0, SEND_ROWS // CUT_ROWS, 0)),
            pl.BlockSpec((sources, ROWS, HEAD_DIM), lambda i: (i, 0, 0)),
            pl.BlockSpec((N_SEQ, ROWS, HEAD_DIM), lambda i: (0, 1, 0)),
            pl.BlockSpec((N_SEQ, ROWS, HEAD_DIM), lambda i: (0, 2, 0)),
        ],
        out_specs=[
            pl.BlockSpec((sources, ROWS, HEAD_DIM), lambda i: (i, 0, 0)),
            pl.BlockSpec((1, 1, Q_ROWS), lambda i: (i, 0, 0)),
        ],
        out_shape=[
            jax.ShapeDtypeStruct((N_SEQ, RET_ROWS, HEAD_DIM), jnp.bfloat16),
            jax.ShapeDtypeStruct((steps, 1, Q_ROWS), jnp.float32),
        ],
        scratch_shapes=[
            pltpu.VMEM((keys, 2 * HEAD_DIM), jnp.bfloat16),
            pltpu.VMEM((HEAD_DIM, keys), jnp.bfloat16),
        ],
        compiler_params=pltpu.CompilerParams(vmem_limit_bytes=VMEM),
        cost_estimate=attention_cost(keys, keys),
        name="attend_whole",
    )(*[received] * 4)


def attend_shared(core, received, far_kv, returning):
    sources = Q_ROWS // HALF
    steps = N_SEQ // sources
    keys = N_SEQ * ROWS
    return pl.pallas_call(
        functools.partial(attention_kernel, Q_ROWS, True),
        grid_spec=pltpu.PrefetchScalarGridSpec(
            num_scalar_prefetch=1,
            grid=(steps,),
            in_specs=[
                pl.BlockSpec((N_SEQ, CUT_ROWS, HEAD_DIM), lambda i, c: (0, SEND_ROWS // CUT_ROWS, 0)),
                pl.BlockSpec((sources, HALF, HEAD_DIM), lambda i, c: (i, A_ROWS // HALF, 0)),
                pl.BlockSpec((N_SEQ, 2 * HALF, HEAD_DIM), lambda i, c: (0, 0, 0)),
                pl.BlockSpec((N_SEQ, 2 * HALF, HEAD_DIM), lambda i, c: (0, 0, 0)),
                pl.BlockSpec(memory_space=pl.ANY),
            ],
            out_specs=[
                pl.BlockSpec((sources, HALF, HEAD_DIM), lambda i, c: (i, ROWS // HALF, 0)),
                pl.BlockSpec((1, 1, Q_ROWS), lambda i, c: (i, 0, 0)),
            ],
            scratch_shapes=[
                pltpu.VMEM((keys, 2 * HEAD_DIM), jnp.bfloat16),
                pltpu.VMEM((HEAD_DIM, keys), jnp.bfloat16),
            ],
        ),
        out_shape=[
            jax.ShapeDtypeStruct((N_SEQ, RET_ROWS, HEAD_DIM), jnp.bfloat16),
            jax.ShapeDtypeStruct((steps, 1, Q_ROWS), jnp.float32),
        ],
        input_output_aliases={5: 0},
        compiler_params=pltpu.CompilerParams(vmem_limit_bytes=VMEM),
        cost_estimate=attention_cost(keys // 2, keys),
        name="attend_shared",
    )(core, received, received, *far_kv, returning)


def project_kernel(core, ret, own, far, vis_out, txt_out, total):
    step = pl.program_id(0)
    columns = own.shape[1]
    pieces = []
    for chip in range(2):
        low, high = ret[2 * chip], ret[2 * chip + 1]
        shared = jnp.concatenate([low[ROWS:], high[ROWS:]], axis=0)
        pieces += [low[:ROWS], shared, high[:ROWS]]
    attention = jnp.concatenate(pieces, axis=1)
    txt_out[...] = attention[VIS_ROWS:]

    @pl.when(step == 0)
    def _():
        total[...] = jnp.zeros_like(total)

    for index, weights in ((0, own), (1, far)):
        total[index] += jnp.dot(attention, weights[...], preferred_element_type=jnp.float32)

    @pl.when(step == pl.num_programs(0) - 1)
    def _():
        for index in range(2):
            at = index + core[0] - 2 * index * core[0]
            start = pl.multiple_of(at * columns, columns)
            vis_out[:, pl.ds(start, columns)] = total[index, :VIS_ROWS].astype(jnp.bfloat16)


def project(core, returned, own, far):
    columns = own.shape[1]
    depth = 2 * TRIO
    steps = CHIPS // 2
    return pl.pallas_call(
        project_kernel,
        grid_spec=pltpu.PrefetchScalarGridSpec(
            num_scalar_prefetch=1,
            grid=(steps,),
            in_specs=[
                pl.BlockSpec((4, RET_ROWS, HEAD_DIM), lambda i, c: (i, 0, 0)),
                pl.BlockSpec((depth, columns), lambda i, c: (i, 0)),
                pl.BlockSpec((depth, columns), lambda i, c: (i, 0)),
            ],
            out_specs=[
                pl.BlockSpec((VIS_ROWS, 2 * columns), lambda i, c: (0, 0)),
                pl.BlockSpec((TXT_ROWS, depth), lambda i, c: (0, i)),
            ],
            scratch_shapes=[pltpu.VMEM((2, ROWS, columns), jnp.float32)],
        ),
        out_shape=[
            jax.ShapeDtypeStruct((VIS_ROWS, 2 * columns), jnp.bfloat16),
            jax.ShapeDtypeStruct((TXT_ROWS, HEADS * HEAD_DIM), jnp.bfloat16),
        ],
        compiler_params=pltpu.CompilerParams(vmem_limit_bytes=VMEM),
        name="project",
    )(core, returned, own, far)


def slot_rows(gathered, head_map, seq_index):
    whole = gathered[:, :N_SEQ].reshape(CHIPS, 2, N_SEQ, ROWS)
    shared = gathered[:, N_SEQ:].reshape(CHIPS, 2, N_SEQ, HALF)
    shared = jnp.concatenate([shared[:, 0], shared[:, 1]], axis=2)
    table = jnp.stack([whole[:, 0], shared, whole[:, 1]], axis=1).reshape(HEADS, N_SEQ, ROWS)
    mine = (head_map == seq_index).astype(jnp.int32)
    rank = jnp.cumsum(mine) - 1
    rows = []
    for slot in range(SLOTS):
        picked = (mine * (rank == slot)) > 0
        rows.append(jnp.sum(jnp.where(picked[:, None, None], table, 0.0), axis=0))
    rows = jnp.stack(rows)
    vis = rows[:, :, :VIS_ROWS].reshape(SLOTS, VIS_SEQ)
    txt = rows[:, :, VIS_ROWS:].reshape(SLOTS, TXT_SEQ)
    return jnp.concatenate([vis, txt], axis=1)


def on_device(qkv_vis, qkv_txt, vis_segments, txt_segments, head_map, w_out):
    seq_index = lax.axis_index("seq")
    core = seq_index % 2
    core_scalar = core.reshape(1).astype(jnp.int32)
    swap = [(i, i ^ 1) for i in range(N_SEQ)]
    columns = w_out.shape[1] // 2

    half = lax.dynamic_slice_in_dim(w_out, core * columns, columns, 1)
    own_w = lax.all_gather(half, "dp", axis=0, tiled=True)
    far_w = lax.ppermute(own_w, "seq", swap)

    sending = pack(qkv_vis, qkv_txt, vis_segments, txt_segments)
    received = lax.all_to_all(sending, "seq", split_axis=0, concat_axis=0, tiled=True)
    own_kv = received[:, A_ROWS + HALF : SEND_ROWS]
    far_kv = lax.ppermute(own_kv, "seq", swap)
    returning, lse_whole = attend_whole(received)
    returning, lse_shared = attend_shared(core_scalar, received, (own_kv, far_kv), returning)
    returned = lax.all_to_all(returning, "seq", split_axis=0, concat_axis=0, tiled=True)
    lse = jnp.concatenate([lse_whole.reshape(-1, HEAD_DIM), lse_shared.reshape(-1, HEAD_DIM)], axis=0)
    lse_slots = slot_rows(lax.all_gather(lse, "seq", axis=0), head_map, seq_index)
    vis_out, txt_out = project(core_scalar, returned, own_w, far_w)
    return vis_out, txt_out, lse_slots


def solution(mesh):
    in_specs = (
        P(("dp", "seq"), None),
        P(("dp", "seq"), None),
        P(("dp", "seq")),
        P(("dp", "seq")),
        P(),
        P("dp", None),
    )
    out_specs = (P(("dp", "seq"), None), P(("dp", "seq"), None), P("seq", "dp"))
    return jax.shard_map(
        on_device, mesh=mesh, in_specs=in_specs, out_specs=out_specs, check_vma=False
    )
```

time: 249 us -> 189 us (0.76)
  waiting for transfers between devices: 27.5 us -> 76.5 us
  local copies, waits for them, and re-layouts: 51.9 us -> 4.7 us
  blocking collectives: 73.9 us -> 31.4 us
  matrix products: 41.5 us -> 0 us
  Pallas kernels: 0 us -> 33.7 us
  other arithmetic: 13.3 us -> 1.07 us
  starting transfers between devices: 18.7 us -> 26.8 us
  loops' own time: 5.47 us -> 0 us
    all_gather x1, waiting for transfers between devices: 0.01 us -> 76.5 us  [on_device(): own_w = lax.all_gather(half, 'dp', axis=0, tiled=True)]
    unnamed x1 -> x0, blocking collectives: 73.9 us -> none
    dot_general x17 -> x0, matrix products: 41.5 us -> none  [the longest x8 24.8 us: one_block(): jnp.dot(weights, value_rows, preferred_element_type=jnp.float32)]
    pallas_call x0 -> x4, Pallas kernels: none -> 33.7 us  [the longest x1 13.5 us: attend_whole(): pl.pallas_call(functools.partial(attention_kernel, Q_ROWS, None), grid=(s...]
    all_gather x0 -> x1, blocking collectives: none -> 31.4 us  [on_device(): lax.all_gather(lse, 'seq', axis=0)]
    all_to_all x2, waiting for transfers between devices: 26.8 us -> 0.01 us  [the longest x1 0.01 us: on_device(): lax.all_to_all(returning, 'seq', split_axis=0, concat_axis=0, tiled=True)]
    while x16 -> x0, local copies, waits for them, and re-layouts: 16.6 us -> none
    another operation x8 -> x1, local copies, waits for them, and re-layouts: 9.62 us -> 0.09 us  [the longest x1 9.46 us: on_device(): slot_blended = jnp.stack(blended_list, axis=1)]
  transfers between devices with their start and end apart: 3 -> 5, of which waited for: 1 -> 1; matrix products, arithmetic and copies ran while one was open for 25% -> 1% of each run, Pallas kernels for 0% -> 15%
where the time goes in v1:
time: 189 us; the launch traced here: 188 us
  waiting for transfers between devices  76.5 us (40%)
  Pallas kernels  33.7 us (18%)
  blocking collectives  31.4 us (17%)
  starting transfers between devices  26.8 us (14%)
  between operations  14.2 us (8%)
  local copies, waits for them, and re-layouts  4.7 us (2%)
    all_gather x1, waiting for transfers between devices, on_device(): own_w = lax.all_gather(half, 'dp', axis=0, tiled=True)  76.5 us
    all_gather x1, blocking collectives, on_device(): lax.all_gather(lse, 'seq', axis=0)  31.4 us
    pallas_call x1, Pallas kernels, attend_whole(): pl.pallas_call(functools.partial(attention_kernel, Q_ROWS, None), grid=(s...  13.5 us
    all_to_all x1, starting transfers between devices, on_device(): lax.all_to_all(sending, 'seq', split_axis=0, concat_axis=0, tiled=True)  12 us
    pallas_call x1, Pallas kernels, attend_shared(): pl.pallas_call(functools.partial(attention_kernel, Q_ROWS, True), grid_sp...  8.95 us
    all_to_all x1, starting transfers between devices, on_device(): lax.all_to_all(returning, 'seq', split_axis=0, concat_axis=0, tiled=True)  8.03 us
    pallas_call x1, Pallas kernels, pack(): pl.pallas_call(pack_kernel, grid=(CHIPS,), in_specs=[pl.BlockSpec((1, VIS...  6.14 us
    pallas_call x1, Pallas kernels, project(): pl.pallas_call(project_kernel, grid_spec=pltpu.PrefetchScalarGridSpec(num...  5.03 us
  transfers between devices with their start and end apart: 5, of which 1 were waited for; matrix products, arithmetic and copies ran while one was open for 1% of the time, Pallas kernels for 15%

profile of v1, /device:TPU:1, one launch (start us, length us, event | category | flops | bytes accessed | tf_op | source)
XLA Modules:
  0.0 188.3 jit_solution(3135059684371321240)
XLA Ops:
  7.2 0.0 copy-start
  7.2 0.0 all-gather.3.cloned.1.call-start
  7.2 0.9 copy-done
  8.1 0.7 constant_dynamic-slice_fusion
  8.8 0.0 all-gather.3.cloned.1.call-update
  8.8 6.1 %pack.1 = bf16[16,592,128]{2,1,0:T(8,128)(2,1)} custom-call(s32[1,112]{1,0:T(1,128)} %bitcast.32, s32[1,16]{1,0:T(1,128)} %bitcast.33, bf16[112,9216]{1,0:T(8,128)(2,1)} %vv.1, bf16[112,9216]{1,0:T(8,128)(2,1)} %vv.1, bf16[112,9216]{1,0:T(8,128)(2,1)} %vv.1, bf16[16,9216]{1,0:T(8,128)(2,1)} %tv.1, bf16[16,9216]{1,0:T(8,128)(2,1)} %tv.1, bf16[16,9216]{1,0:T(8,128)(2,1)} %tv.1), custom_call_target="tpu_custom_call" | custom-call | tf_op jit(solution)/shard_map/pack/pallas_call | solution.py:58
  15.0 12.0 %all-to-all-start = ((bf16[16,592,128]{2,1,0:T(8,128)(2,1)}), bf16[16,592,128]{2,1,0:T(8,128)(2,1)S(1)}, u32[]{:S(2)}, u32[]{:S(2)}) async-start(bf16[16,592,128]{2,1,0:T(8,128)(2,1)} %pack.1), calls=%async_computation | async-start | bytes 4849664 | tf_op jit(solution)/shard_map/all_to_all | solution.py:312
  26.9 76.5 %all-gather.3.cloned.1.call-done.own = bf16[3072,768]{1,0:T(8,128)(2,1)} async-done(((bf16[96,768]{1,0:T(8,128)(2,1)}), bf16[3072,768]{1,0:T(8,128)(2,1)}) %all-gather.3.cloned.1.call-update) | async-done | bytes 4718608 | tf_op jit(solution)/shard_map/all_gather | solution.py:308
  103.4 4.9 %collective-permute-start.1 = (bf16[3072,768]{1,0:T(8,128)(2,1)}, bf16[3072,768]{1,0:T(8,128)(2,1)}, u32[]{:S(2)}, u32[]{:S(2)}) collective-permute-start(bf16[3072,768]{1,0:T(8,128)(2,1)} %all-gather.3.cloned.1.call-done.own), channel_id=1, source_target_pairs={{0,1},{1,0},{2,3},{3,2},{4,5},{5,4},{6,7},{7,6},{8,9},{9,8},{10,11... | collective-permute-start | bytes 14155784 | tf_op jit(solution)/shard_map/ppermute | solution.py:309
  108.3 0.0 all-to-all-done.refs_0_.refs_1_.refs_2_.refs_3_
  108.4 1.9 %collective-permute-start = (bf16[16,128,128]{2,1,0:T(8,128)(2,1)S(1)}, bf16[16,128,128]{2,1,0:T(8,128)(2,1)}, u32[]{:S(2)}, u32[]{:S(2)}) collective-permute-start(bf16[16,128,128]{2,1,0:T(8,128)(2,1)S(1)} %slice.36.refs_3_), channel_id=1, source_target_pairs={{0,1},{1,0},{2,3},{3,2},{4,5},{5,4},{6,7},{7,6},{8,9},{9,8},{10,11... | collective-permute-start | bytes 1572872 | tf_op jit(solution)/shard_map/ppermute | solution.py:314
  110.3 0.1 copy.16
  110.5 0.1 compare_reduce_fusion.1
  110.6 13.5 %attend_whole.1 = (bf16[16,192,128]{2,1,0:T(8,128)(2,1)}, f32[8,1,256]{2,1,0:T(1,128)S(1)}) custom-call(bf16[16,592,128]{2,1,0:T(8,128)(2,1)S(1)} %all-to-all-done.refs_0_.refs_1_.refs_2_.refs_3_, bf16[16,592,128]{2,1,0:T(8,128)(2,1)S(1)} %all-to-all-done.refs_0_.refs_1_.refs_2_.refs_3_, ...), custom_call_target="tpu_custom_call" | custom-call | flops 4294967296 | bytes 2097152 | tf_op jit(solution)/shard_map/attend_whole/pallas_call | solution.py:165
  124.1 9.0 %attend_shared.1 = (bf16[16,192,128]{2,1,0:T(8,128)(2,1)}, f32[4,1,256]{2,1,0:T(1,128)S(1)}) custom-call(s32[1]{0:T(128)} %bitcast.refs_0_.core, bf16[16,592,128]{2,1,0:T(8,128)(2,1)S(1)} %all-to-all-done.refs_0_.refs_1_.refs_2_.refs_3_, bf16[16,592,128]{2,1,0:T(8,128)(2,1)S(1)} %all-to-all-done.refs_0_.refs_1_.refs_2_.refs_3_, ...), custom_call_target="tpu_custom_call", output_to_operand_aliasing={{0}: (5, {})} | custom-call | flops 2147483648 | bytes 2097152 | tf_op jit(solution)/shard_map/attend_shared/pallas_call | solution.py:196
  133.1 8.0 %all-to-all-start.1 = ((bf16[16,192,128]{2,1,0:T(8,128)(2,1)}), bf16[16,192,128]{2,1,0:T(8,128)(2,1)S(1)}, u32[]{:S(2)}, u32[]{:S(2)}) async-start(bf16[16,192,128]{2,1,0:T(8,128)(2,1)} %get-tuple-element.10), calls=%async_computation.1 | async-start | bytes 1572864 | tf_op jit(solution)/shard_map/all_to_all | solution.py:317
  141.1 0.1 broadcast_in_dim.24
  141.2 0.1 copy.17
  141.3 0.1 broadcast_in_dim.27
  141.4 0.1 copy.21
  141.5 31.4 %all-gather = f32[384,128]{1,0:T(8,128)S(1)} all-gather(f32[24,128]{1,0:T(8,128)S(1)} %pad_maximum_fusion.3), channel_id=2, replica_groups=mesh['dp'=32,'seq'=16] {'seq'}, dimensions={0}, use_global_device_ids=true | all-gather | bytes 208896 | tf_op jit(solution)/shard_map/all_gather | solution.py:319
  172.9 0.1 reshape.77
  173.0 0.1 maximum_bitcast_fusion
  173.1 0.1 select_reduce_fusion.1
  173.2 0.1 pad_maximum_fusion.1
  173.3 0.1 reshape.79
  173.4 0.1 reshape.78
  173.5 0.6 pad_maximum_fusion.2
  174.1 0.0 all-to-all-done.1.ret
  174.1 0.0 collective-permute-done.1.far
  174.1 2.3 %copy-done.1 = bf16[3072,768]{1,0:T(8,128)(2,1)S(1)} copy-done((bf16[3072,768]{1,0:T(8,128)(2,1)S(1)}, bf16[3072,768]{1,0:T(8,128)(2,1)}, u32[]{:S(2)}) %copy-start.1) | copy-done | bytes 4718616
  176.4 5.0 %project.1 = (bf16[112,1536]{1,0:T(8,128)(2,1)}, bf16[16,3072]{1,0:T(8,128)(2,1)}) custom-call(s32[1]{0:T(128)} %bitcast.refs_0_.core, bf16[16,192,128]{2,1,0:T(8,128)(2,1)S(1)} %all-to-all-done.1.ret, bf16[3072,768]{1,0:T(8,128)(2,1)S(1)} %copy-done.1, bf16[3072,768]{1,0:T(8,128)(2,1)} %collective-permute-done.1.far), custom_call_target="tpu_custom_call" | custom-call | tf_op jit(solution)/shard_map/project/pallas_call | solution.py:258
  (14 shorter events, 0.2 us)
Async XLA Ops:
  7.2 1.0 copy-start
  7.2 96.2 %all-gather.3.cloned.1.call-start = ((), (), s32[]{:S(2)}) async-start(), calls=%async_computation.2 | async-start | bytes 4866048 | tf_op jit(solution)/shard_map/all_gather | solution.py:308
  15.0 95.4 %copy-start.2 = (s32[24]{0:T(128)S(1)}, s32[24]{0:T(128)}, u32[]{:S(2)}) copy-start(s32[24]{0:T(128)} %param.10) | copy-start | bytes 292
  15.0 93.4 %all-to-all-start = ((bf16[16,592,128]{2,1,0:T(8,128)(2,1)}), bf16[16,592,128]{2,1,0:T(8,128)(2,1)S(1)}, u32[]{:S(2)}, u32[]{:S(2)}) async-start(bf16[16,592,128]{2,1,0:T(8,128)(2,1)} %pack.1), calls=%async_computation | async-start | bytes 4849664 | tf_op jit(solution)/shard_map/all_to_all | solution.py:312
  103.4 70.7 %collective-permute-start.1 = (bf16[3072,768]{1,0:T(8,128)(2,1)}, bf16[3072,768]{1,0:T(8,128)(2,1)}, u32[]{:S(2)}, u32[]{:S(2)}) collective-permute-start(bf16[3072,768]{1,0:T(8,128)(2,1)} %all-gather.3.cloned.1.call-done.own), channel_id=1, source_target_pairs={{0,1},{1,0},{2,3},{3,2},{4,5},{5,4},{6,7},{7,6},{8,9},{9,8},{10,11... | collective-permute-start | bytes 14155784 | tf_op jit(solution)/shard_map/ppermute | solution.py:309
  108.4 15.7 %collective-permute-start = (bf16[16,128,128]{2,1,0:T(8,128)(2,1)S(1)}, bf16[16,128,128]{2,1,0:T(8,128)(2,1)}, u32[]{:S(2)}, u32[]{:S(2)}) collective-permute-start(bf16[16,128,128]{2,1,0:T(8,128)(2,1)S(1)} %slice.36.refs_3_), channel_id=1, source_target_pairs={{0,1},{1,0},{2,3},{3,2},{4,5},{5,4},{6,7},{7,6},{8,9},{9,8},{10,11... | collective-permute-start | bytes 1572872 | tf_op jit(solution)/shard_map/ppermute | solution.py:314
  133.1 41.0 %all-to-all-start.1 = ((bf16[16,192,128]{2,1,0:T(8,128)(2,1)}), bf16[16,192,128]{2,1,0:T(8,128)(2,1)S(1)}, u32[]{:S(2)}, u32[]{:S(2)}) async-start(bf16[16,192,128]{2,1,0:T(8,128)(2,1)} %get-tuple-element.10), calls=%async_computation.1 | async-start | bytes 1572864 | tf_op jit(solution)/shard_map/all_to_all | solution.py:317
  174.1 2.3 %copy-start.1 = (bf16[3072,768]{1,0:T(8,128)(2,1)S(1)}, bf16[3072,768]{1,0:T(8,128)(2,1)}, u32[]{:S(2)}) copy-start(bf16[3072,768]{1,0:T(8,128)(2,1)} %all-gather.3.cloned.1.call-done.own) | copy-start | bytes 14155780
Sparse Core Ops, SparseCore 0:
  11.7 91.6 all-gather.2

commit v2 on v1

v2 whole, which is shorter than its diff:
```python
import functools

import jax
import jax.numpy as jnp
from jax import lax
from jax.experimental import pallas as pl
from jax.experimental.pallas import tpu as pltpu
from jax.sharding import PartitionSpec as P

HEADS = 24
HEAD_DIM = 128
N_SEQ = 16
VIS_ROWS = 112
TXT_ROWS = 16
ROWS = VIS_ROWS + TXT_ROWS
HALF = ROWS // 2
TRIO = 3 * HEAD_DIM
CHIPS = 8
A_ROWS = 3 * ROWS
SEND_ROWS = A_ROWS + 3 * HALF
CUT_ROWS = 16
PAYLOAD = SEND_ROWS + CUT_ROWS
RET_ROWS = ROWS + HALF
WHOLE_LSE = RET_ROWS
SHARED_LSE = WHOLE_LSE + N_SEQ
RETURN = SHARED_LSE + N_SEQ
PACK_CHIPS = 4
VIS_SEQ = VIS_ROWS * N_SEQ
TXT_SEQ = TXT_ROWS * N_SEQ
SLOTS = 2
LOG2E = 1.4426950408889634
LN2 = 0.6931471805599453
BIG = -1e30


def pack_kernel(seg_vis, seg_txt, vq, vk, vv, tq, tk, tv, out):
    def even(ref):
        parity = (ref[...] & 1).astype(jnp.float32)
        count = jnp.sum(1.0 - parity, axis=1, keepdims=True)
        return jnp.broadcast_to(count, (CUT_ROWS // 2, HEAD_DIM))

    cuts = jnp.concatenate([even(seg_vis), even(seg_txt)], axis=0).astype(jnp.bfloat16)
    for chip in range(PACK_CHIPS):
        low, high = 2 * chip, 2 * chip + 1
        for part, (vis, txt) in enumerate(((vq, tq), (vk, tk), (vv, tv))):
            row = part * ROWS
            for device, column in ((low, chip * TRIO), (high, chip * TRIO + 2 * HEAD_DIM)):
                columns = slice(column, column + HEAD_DIM)
                out[device, row : row + VIS_ROWS, :] = vis[:, columns]
                out[device, row + VIS_ROWS : row + ROWS, :] = txt[:, columns]
            row = A_ROWS + part * HALF
            columns = slice(chip * TRIO + HEAD_DIM, chip * TRIO + 2 * HEAD_DIM)
            out[low, row : row + HALF, :] = vis[:HALF, columns]
            out[high, row : row + VIS_ROWS - HALF, :] = vis[HALF:, columns]
            out[high, row + VIS_ROWS - HALF : row + HALF, :] = txt[:, columns]
        out[low, SEND_ROWS:PAYLOAD, :] = cuts
        out[high, SEND_ROWS:PAYLOAD, :] = cuts


def pack(qkv_vis, qkv_txt, vis_segments, txt_segments):
    steps = CHIPS // PACK_CHIPS

    def spec(rows, part):
        return pl.BlockSpec((rows, PACK_CHIPS * TRIO), lambda i: (0, part * steps + i))

    return pl.pallas_call(
        pack_kernel,
        grid=(steps,),
        in_specs=[
            pl.BlockSpec((1, VIS_ROWS), lambda i: (0, 0)),
            pl.BlockSpec((1, TXT_ROWS), lambda i: (0, 0)),
            *[spec(VIS_ROWS, part) for part in range(3)],
            *[spec(TXT_ROWS, part) for part in range(3)],
        ],
        out_specs=pl.BlockSpec((2 * PACK_CHIPS, PAYLOAD, HEAD_DIM), lambda i: (i, 0, 0)),
        out_shape=jax.ShapeDtypeStruct((N_SEQ, PAYLOAD, HEAD_DIM), jnp.bfloat16),
        name="pack",
    )(
        vis_segments.reshape(1, VIS_ROWS),
        txt_segments.reshape(1, TXT_ROWS),
        *[qkv_vis] * 3,
        *[qkv_txt] * 3,
    )


def second_clip(cut_ref, source, row):
    cuts = jnp.sum(cut_ref[...].astype(jnp.float32), axis=0)
    vis_cut, txt_cut = cuts[0:1, 0:1], cuts[CUT_ROWS // 2 : CUT_ROWS // 2 + 1, 0:1]
    vis_place = (source * VIS_ROWS + row).astype(jnp.float32)
    txt_place = (source * TXT_ROWS + row - VIS_ROWS).astype(jnp.float32)
    is_second = jnp.where(row < VIS_ROWS, vis_place - vis_cut, txt_place - txt_cut) >= 0.0
    return jnp.where(is_second, 1.0, 0.0)


def clip_columns(second, first_value, second_value):
    lane = lax.broadcasted_iota(jnp.int32, second.shape, 1)
    feature = jnp.where(lane == 0, first_value(second), second_value(second))
    return jnp.where(lane < 2, feature, 0.0).astype(jnp.bfloat16)


def attend(queries, k_wide, v_turned, write):
    factor = HEAD_DIM**-0.5 * LOG2E

    def score(block):
        return lax.dot_general(
            k_wide[...], queries(block), (((1,), (1,)), ((), ())), preferred_element_type=jnp.float32
        )

    blocks = STEP_ROWS // Q_ROWS
    scores = score(0)
    for block in range(blocks):
        upcoming = score(block + 1) if block + 1 < blocks else None
        highest = jnp.max(scores, axis=0, keepdims=True)
        exponent = jnp.exp2((scores - highest) * factor)
        total = jnp.sum(exponent, axis=0, keepdims=True)
        blended = jnp.dot(
            v_turned[...], exponent.astype(jnp.bfloat16), preferred_element_type=jnp.float32
        )
        result = jnp.swapaxes(blended * (1.0 / total), 0, 1).astype(jnp.bfloat16)
        write(block, result, highest * HEAD_DIM**-0.5 + jnp.log2(total) * LN2)
        scores = upcoming


def place_of(shape, rows, first_source, offset):
    index = lax.broadcasted_iota(jnp.int32, shape, 0)
    return first_source + index // rows, index % rows + offset


def key_features(cut, keys, rows, offset):
    second = second_clip(cut, *place_of((keys, HEAD_DIM), rows, 0, offset))
    return clip_columns(second, lambda s: BIG * s, lambda s: BIG * (1.0 - s))


def query_features(cut, count, rows, first_source, offset):
    second = second_clip(cut, *place_of((count, HEAD_DIM), rows, first_source, offset))
    return clip_columns(second, lambda s: 1.0 - s, lambda s: s)


def whole_kernel(cut, q, k, v, out, lse, k_wide, v_turned, q_wide):
    step = pl.program_id(0)
    keys = N_SEQ * ROWS
    sources = STEP_ROWS // ROWS

    @pl.when(step == 0)
    def _():
        k_wide[:, :HEAD_DIM] = k[...].reshape(keys, HEAD_DIM)
        k_wide[:, HEAD_DIM:] = key_features(cut, keys, ROWS, 0)
        v_turned[...] = jnp.swapaxes(v[...].reshape(keys, HEAD_DIM), 0, 1)

    q_wide[:, :HEAD_DIM] = q[...].reshape(STEP_ROWS, HEAD_DIM)
    q_wide[:, HEAD_DIM:] = query_features(cut, STEP_ROWS, ROWS, step * sources, 0)

    def write(block, result, log_total):
        count = Q_ROWS // ROWS
        out[block * count : (block + 1) * count] = result.reshape(count, ROWS, HEAD_DIM)
        for row in range(count):
            lse[block * count + row : block * count + row + 1, :] = log_total[
                :, row * HEAD_DIM : (row + 1) * HEAD_DIM
            ]

    attend(lambda block: q_wide[block * Q_ROWS : (block + 1) * Q_ROWS, :], k_wide, v_turned, write)


def shared_kernel(where, cut, q, own_kv, far_kv, whole, whole_lse, out, k_wide, v_turned, q_wide):
    core = where[2]
    keys = N_SEQ * HALF
    for place, (kv, offset) in enumerate(((own_kv, HALF * core), (far_kv, HALF * (1 - core)))):
        at = slice(place * keys, (place + 1) * keys)
        k_wide[at, :HEAD_DIM] = kv[:, :HALF].reshape(keys, HEAD_DIM)
        k_wide[at, HEAD_DIM:] = key_features(cut, keys, HALF, offset)
        v_turned[:, at] = jnp.swapaxes(kv[:, HALF:].reshape(keys, HEAD_DIM), 0, 1)
    q_wide[:, :HEAD_DIM] = q[...].reshape(STEP_ROWS, HEAD_DIM)
    q_wide[:, HEAD_DIM:] = query_features(cut, STEP_ROWS, HALF, 0, HALF * core)
    log_totals = []

    def write(block, result, log_total):
        count = Q_ROWS // HALF
        out[block * count : (block + 1) * count, ROWS:RET_ROWS, :] = result.reshape(count, HALF, HEAD_DIM)
        for row in range(Q_ROWS // HEAD_DIM):
            log_totals.append(log_total[:, row * HEAD_DIM : (row + 1) * HEAD_DIM])

    attend(lambda block: q_wide[block * Q_ROWS : (block + 1) * Q_ROWS, :], k_wide, v_turned, write)
    out[:, :ROWS, :] = whole[...]
    log_totals.append(jnp.zeros((RETURN - SHARED_LSE - len(log_totals), HEAD_DIM), jnp.float32))
    rows = jnp.concatenate([whole_lse[...], *log_totals], axis=0).astype(jnp.bfloat16)
    for device in range(N_SEQ):
        out[device, WHOLE_LSE:, :] = rows


Q_ROWS = 512
STEP_ROWS = 1024
VMEM = 40 * 2**20


def attention_scratch():
    keys = N_SEQ * ROWS
    return [
        pltpu.VMEM((keys, 2 * HEAD_DIM), jnp.bfloat16),
        pltpu.VMEM((HEAD_DIM, keys), jnp.bfloat16),
        pltpu.VMEM((STEP_ROWS, 2 * HEAD_DIM), jnp.bfloat16),
    ]


def attention_cost(queries, keys):
    return pl.CostEstimate(
        flops=queries * keys * HEAD_DIM * 8,
        bytes_accessed=4 * keys * HEAD_DIM * 2,
        transcendentals=queries * keys,
    )


def attend_whole(received):
    keys = N_SEQ * ROWS
    steps = keys // STEP_ROWS
    sources = STEP_ROWS // ROWS
    return pl.pallas_call(
        whole_kernel,
        grid=(steps,),
        in_specs=[
            pl.BlockSpec((N_SEQ, CUT_ROWS, HEAD_DIM), lambda i: (0, SEND_ROWS // CUT_ROWS, 0)),
            pl.BlockSpec((sources, ROWS, HEAD_DIM), lambda i: (i, 0, 0)),
            pl.BlockSpec((N_SEQ, ROWS, HEAD_DIM), lambda i: (0, 1, 0)),
            pl.BlockSpec((N_SEQ, ROWS, HEAD_DIM), lambda i: (0, 2, 0)),
        ],
        out_specs=[
            pl.BlockSpec((sources, ROWS, HEAD_DIM), lambda i: (i, 0, 0)),
            pl.BlockSpec((sources, ROWS), lambda i: (i, 0)),
        ],
        out_shape=[
            jax.ShapeDtypeStruct((N_SEQ, ROWS, HEAD_DIM), jnp.bfloat16),
            jax.ShapeDtypeStruct((N_SEQ, ROWS), jnp.float32),
        ],
        scratch_shapes=attention_scratch(),
        compiler_params=pltpu.CompilerParams(vmem_limit_bytes=VMEM),
        cost_estimate=attention_cost(keys, keys),
        name="attend_whole",
    )(*[received] * 4)


def attend_shared(where, received, own_kv, far_kv, whole, whole_lse):
    keys = N_SEQ * ROWS
    full = lambda *shape: pl.BlockSpec(shape, lambda i, c: (0,) * len(shape))
    return pl.pallas_call(
        shared_kernel,
        grid_spec=pltpu.PrefetchScalarGridSpec(
            num_scalar_prefetch=1,
            grid=(1,),
            in_specs=[
                pl.BlockSpec((N_SEQ, CUT_ROWS, HEAD_DIM), lambda i, c: (0, SEND_ROWS // CUT_ROWS, 0)),
                pl.BlockSpec((N_SEQ, HALF, HEAD_DIM), lambda i, c: (0, A_ROWS // HALF, 0)),
                full(N_SEQ, 2 * HALF, HEAD_DIM),
                full(N_SEQ, 2 * HALF, HEAD_DIM),
                full(N_SEQ, ROWS, HEAD_DIM),
                full(N_SEQ, ROWS),
            ],
            out_specs=full(N_SEQ, RETURN, HEAD_DIM),
            scratch_shapes=attention_scratch(),
        ),
        out_shape=jax.ShapeDtypeStruct((N_SEQ, RETURN, HEAD_DIM), jnp.bfloat16),
        compiler_params=pltpu.CompilerParams(vmem_limit_bytes=VMEM),
        cost_estimate=attention_cost(keys // 2, keys),
        name="attend_shared",
    )(where, received, received, own_kv, far_kv, whole, whole_lse)


def place_kernel(where, mine, near, near_far, part, part_far, out):
    x, core = where[1], where[2]
    sign = 1 - 2 * core
    out[x] = mine[...]
    out[(x - sign + 4) % 4] = near[...]
    out[(x + sign + 4) % 4] = near_far[...]
    columns = part.shape[1]
    low, high = pl.multiple_of(core * columns, columns), pl.multiple_of((1 - core) * columns, columns)
    opposite = (x + 2) % 4
    out[opposite, :, pl.ds(low, columns)] = part[...]
    out[opposite, :, pl.ds(high, columns)] = part_far[...]


def place(where, mine, near, near_far, part, part_far):
    rows, columns = mine.shape
    return pl.pallas_call(
        place_kernel,
        grid_spec=pltpu.PrefetchScalarGridSpec(
            num_scalar_prefetch=1,
            grid=(),
            in_specs=[pl.BlockSpec(memory_space=pltpu.VMEM)] * 5,
            out_specs=pl.BlockSpec(memory_space=pltpu.VMEM),
        ),
        out_shape=jax.ShapeDtypeStruct((4, rows, columns), jnp.bfloat16),
        name="place",
    )(where, mine, near, near_far, part, part_far)


def slot_of(ret, head):
    chip, member = head // 3, head % 3
    low, high = ret.at[2 * chip], ret.at[2 * chip + 1]
    lane = lax.broadcasted_iota(jnp.int32, (1, HEAD_DIM), 1)
    rows = []
    for source in range(N_SEQ):
        whole = [ref[WHOLE_LSE : WHOLE_LSE + N_SEQ, :].astype(jnp.float32) for ref in (low, high)]
        shared = [ref[SHARED_LSE : SHARED_LSE + N_SEQ, :].astype(jnp.float32) for ref in (low, high)]
        left, right = (item[source // 2 : source // 2 + 1] for item in shared)
        if source % 2 == 0:
            right = pltpu.roll(right, HALF, 1)
        else:
            left = pltpu.roll(left, HALF, 1)
        both = jnp.where(lane < HALF, left, right)
        first, last = (item[source : source + 1] for item in whole)
        rows.append(jnp.where(member == 0, first, jnp.where(member == 1, both, last)))
    return rows


def project_kernel(where, ret, *refs):
    weights, (vis_out, txt_out, slots, held, sems) = refs[:9], refs[9:]
    y, core = where[0], where[2]
    sign = 1 - 2 * core
    columns = held.shape[2] // 2
    copies = []
    for index in range(7):
        copies.append(pltpu.make_async_copy(weights[index], held.at[index], sems.at[index]))
    for index in range(2):
        at = core if index == 0 else 1 - core
        start = pl.multiple_of(at * columns, columns)
        copies.append(
            pltpu.make_async_copy(
                weights[7 + index], held.at[7, :, pl.ds(start, columns)], sems.at[7 + index]
            )
        )
    for copy in copies:
        copy.start()
    for slot in range(SLOTS):
        valid = where[5 + slot] > 0
        for source, row in enumerate(slot_of(ret, where[3 + slot])):
            row = jnp.where(valid, row, 0.0)
            at = source * VIS_ROWS
            slots[slot : slot + 1, at : at + VIS_ROWS] = row[:, :VIS_ROWS]
            at = VIS_SEQ + source * TXT_ROWS
            slots[slot : slot + 1, at : at + TXT_ROWS] = row[:, VIS_ROWS:]
    total = jnp.zeros((ROWS, 2 * columns), jnp.float32)
    for index, hops in enumerate((0, 1, 2, 3, -1, -2, -3, 4)):
        chip = (y - hops * sign + 8) % 8
        low, high = ret[2 * chip], ret[2 * chip + 1]
        shared = jnp.concatenate([low[ROWS:RET_ROWS], high[ROWS:RET_ROWS]], axis=0)
        attention = jnp.concatenate([low[:ROWS], shared, high[:ROWS]], axis=1)
        txt_out[:, pl.ds(pl.multiple_of(chip * TRIO, TRIO), TRIO)] = attention[VIS_ROWS:]
        copies[index].wait()
        if index == 7:
            copies[8].wait()
        total += jnp.dot(attention, held[index], preferred_element_type=jnp.float32)
    vis_out[...] = total[:VIS_ROWS].astype(jnp.bfloat16)


def project(where, returned, chunks, far_chunks):
    columns = chunks[0].shape[1]
    return pl.pallas_call(
        project_kernel,
        grid_spec=pltpu.PrefetchScalarGridSpec(
            num_scalar_prefetch=1,
            grid=(),
            in_specs=[pl.BlockSpec(memory_space=pltpu.VMEM)] + [pl.BlockSpec(memory_space=pl.ANY)] * 9,
            out_specs=[pl.BlockSpec(memory_space=pltpu.VMEM)] * 3,
            scratch_shapes=[
                pltpu.VMEM((8, TRIO, columns), jnp.bfloat16),
                pltpu.SemaphoreType.DMA((9,)),
            ],
        ),
        out_shape=[
            jax.ShapeDtypeStruct((VIS_ROWS, columns), jnp.bfloat16),
            jax.ShapeDtypeStruct((TXT_ROWS, HEADS * HEAD_DIM), jnp.bfloat16),
            jax.ShapeDtypeStruct((SLOTS, VIS_SEQ + TXT_SEQ), jnp.float32),
        ],
        compiler_params=pltpu.CompilerParams(vmem_limit_bytes=VMEM),
        name="project",
    )(where, returned, *chunks[:4], *far_chunks[:3], chunks[4], far_chunks[3])


AXES = ("dp", "seq")
X_SIZE = 4
Y_SIZE = 8


def permute(operand, target):
    pairs = []
    for y in range(Y_SIZE):
        for x in range(X_SIZE):
            for s in range(N_SEQ):
                ty, tx, ts = target(y, x, s)
                there = (ty % Y_SIZE) * X_SIZE + tx % X_SIZE
                pairs.append(((y * X_SIZE + x) * N_SEQ + s, there * N_SEQ + ts))
    return lax.ppermute(operand, AXES, pairs)


def swap(operand):
    return permute(operand, lambda y, x, s: (y, x, s ^ 1))


def shift_x(operand, hops):
    return permute(operand, lambda y, x, s: (y, x + hops * (1 - 2 * (s % 2)), s))


def shift_y(operand):
    return permute(operand, lambda y, x, s: (y + 1 - 2 * (s % 2), x, s))


def heads_of_slots(head_map, seq_index):
    mine = (head_map == seq_index).astype(jnp.int32)
    rank = jnp.cumsum(mine) - 1
    ids = jnp.arange(HEADS, dtype=jnp.int32)
    picked = mine[None] * (rank[None] == jnp.arange(SLOTS, dtype=jnp.int32)[:, None])
    return jnp.concatenate([jnp.sum(picked * ids[None], axis=1), jnp.sum(picked, axis=1)])


def on_device(qkv_vis, qkv_txt, vis_segments, txt_segments, head_map, w_out):
    seq_index = lax.axis_index("seq")
    dp_index = lax.axis_index("dp")
    core = seq_index % 2
    half = w_out.shape[1] // 2
    place_here = jnp.stack([dp_index // X_SIZE, dp_index % X_SIZE, core]).astype(jnp.int32)
    where = jnp.concatenate([place_here, heads_of_slots(head_map, seq_index)])

    near = shift_x(w_out, 1)
    part = shift_x(lax.dynamic_slice_in_dim(w_out, core * half, half, 1), 2)
    sending = pack(qkv_vis, qkv_txt, vis_segments, txt_segments)
    sending, near, part = lax.optimization_barrier((sending, near, part))
    received = lax.all_to_all(sending, "seq", split_axis=0, concat_axis=0, tiled=True)
    chunks = [place(where, w_out, near, swap(near), part, swap(part)).reshape(-1, 2 * half)]
    chunks.append(shift_y(chunks[0]))
    chunks.append(shift_y(chunks[1]))
    received, chunks[2] = lax.optimization_barrier((received, chunks[2]))
    chunks.append(shift_y(chunks[2]))
    own_kv = received[:, A_ROWS + HALF : SEND_ROWS]
    far_kv = swap(own_kv)
    whole, whole_lse = attend_whole(received)
    returning = attend_shared(where, received, own_kv, far_kv, whole, whole_lse)
    returning, chunks[1], chunks[2], chunks[3] = lax.optimization_barrier((returning, *chunks[1:]))
    returned = lax.all_to_all(returning, "seq", split_axis=0, concat_axis=0, tiled=True)
    chunks.append(shift_y(lax.dynamic_slice_in_dim(chunks[3], core * half, half, 1)))
    far_chunks = [swap(chunk) for chunk in chunks[1:]]
    vis_out, txt_out, lse_slots = project(where, returned, chunks, far_chunks)
    return vis_out, txt_out, lse_slots


def solution(mesh):
    in_specs = (
        P(("dp", "seq"), None),
        P(("dp", "seq"), None),
        P(("dp", "seq")),
        P(("dp", "seq")),
        P(),
        P("dp", None),
    )
    out_specs = (P(("dp", "seq"), None), P(("dp", "seq"), None), P("seq", "dp"))
    return jax.shard_map(
        on_device, mesh=mesh, in_specs=in_specs, out_specs=out_specs, check_vma=False
    )
```

time: 189 us -> 146 us (0.77)
  starting transfers between devices: 26.8 us -> 61.2 us
  waiting for transfers between devices: 76.5 us -> 43.1 us
  blocking collectives: 31.4 us -> 0 us
  between operations: 14.2 us -> 0.91 us
  local copies, waits for them, and re-layouts: 4.7 us -> 16 us
  Pallas kernels: 33.7 us -> 23.6 us
    all_gather x1 -> x0, waiting for transfers between devices: 76.5 us -> none  [on_device(): own_w = lax.all_gather(half, 'dp', axis=0, tiled=True)]
    ppermute x2 -> x13, starting transfers between devices: 6.81 us -> 43 us  [permute(): return lax.ppermute(operand, AXES, pairs)]
    all_gather x1 -> x0, blocking collectives: 31.4 us -> none  [on_device(): lax.all_gather(lse, 'seq', axis=0)]
    ppermute x2 -> x13, waiting for transfers between devices: 0.01 us -> 30.7 us  [permute(): return lax.ppermute(operand, AXES, pairs)]
    pallas_call x3 -> x4, Pallas kernels: 28.6 us -> 17.9 us  [the longest x1 7.63 us: attend_whole(): pl.pallas_call(whole_kernel, grid=(steps,), in_specs=[pl.BlockSpec((N_SEQ...]
    unnamed x7 -> x40, local copies, waits for them, and re-layouts: 3.25 us -> 13.1 us
    all_to_all x1, waiting for transfers between devices: 0.01 us -> 8.79 us  [on_device(): lax.all_to_all(sending, 'seq', split_axis=0, concat_axis=0, tiled=True)]
    all_to_all x1, waiting for transfers between devices: 0.01 us -> 3.54 us  [on_device(): lax.all_to_all(returning, 'seq', split_axis=0, concat_axis=0, tiled=True)]
  transfers between devices with their start and end apart: 5 -> 15, of which waited for: 1 -> 8; matrix products, arithmetic and copies ran while one was open for 1% -> 2% of each run, Pallas kernels for 15% -> 12%
where the time goes in v2:
time: 146 us; the launch traced here: 145 us
  starting transfers between devices  61.2 us (42%)
  waiting for transfers between devices  43.1 us (30%)
  Pallas kernels  23.6 us (16%)
  local copies, waits for them, and re-layouts  16 us (11%)
    ppermute x13, starting transfers between devices, permute(): return lax.ppermute(operand, AXES, pairs)  43 us
    ppermute x13, waiting for transfers between devices, permute(): return lax.ppermute(operand, AXES, pairs)  30.7 us
    unnamed x40, local copies, waits for them, and re-layouts  13.1 us
    all_to_all x1, starting transfers between devices, on_device(): lax.all_to_all(sending, 'seq', split_axis=0, concat_axis=0, tiled=True)  12.5 us
    all_to_all x1, waiting for transfers between devices, on_device(): lax.all_to_all(sending, 'seq', split_axis=0, concat_axis=0, tiled=True)  8.79 us
    pallas_call x1, Pallas kernels, attend_whole(): pl.pallas_call(whole_kernel, grid=(steps,), in_specs=[pl.BlockSpec((N_SEQ...  7.63 us
    pallas_call x1, Pallas kernels, project(): pl.pallas_call(project_kernel, grid_spec=pltpu.PrefetchScalarGridSpec(num...  5.78 us
    all_to_all x1, starting transfers between devices, on_device(): lax.all_to_all(returning, 'seq', split_axis=0, concat_axis=0, tiled=True)  5.63 us
  transfers between devices with their start and end apart: 15, of which 8 were waited for; matrix products, arithmetic and copies ran while one was open for 2% of the time, Pallas kernels for 12%

profile of v2, /device:TPU:1, one launch (start us, length us, event | category | flops | bytes accessed | tf_op | source)
XLA Modules:
  0.0 145.0 jit_solution(13876388397489469645)
XLA Ops:
  0.6 5.2 %collective-permute-start = (bf16[96,1536]{1,0:T(8,128)(2,1)}, bf16[96,1536]{1,0:T(8,128)(2,1)S(1)}, u32[]{:S(2)}, u32[]{:S(2)}) collective-permute-start(bf16[96,1536]{1,0:T(8,128)(2,1)} %mine.1), channel_id=1, source_target_pairs={{0,16},{1,49},{2,18},{3,51},{4,20},{5,53},{6,22},{7,55},{8,24},{9,... | collective-permute-start | bytes 884744 | tf_op jit(solution)/shard_map/ppermute | solution.py:390
  6.8 2.4 %collective-permute-start.1 = (bf16[96,768]{1,0:T(8,128)(2,1)S(1)}, bf16[96,768]{1,0:T(8,128)(2,1)S(1)}, u32[]{:S(2)}, u32[]{:S(2)}) collective-permute-start(bf16[96,768]{1,0:T(8,128)(2,1)S(1)} %constant_dynamic-slice_fusion.1), channel_id=1, source_target_pairs={{0,32},{1,33},{2,34},{3,35},{4,36},{5,37},{6,38},{7,39},{8,40},{9,... | collective-permute-start | bytes 442376 | tf_op jit(solution)/shard_map/ppermute | solution.py:390
  9.3 3.0 %pack.1 = bf16[16,592,128]{2,1,0:T(8,128)(2,1)} custom-call(s32[1,112]{1,0:T(1,128)} %bitcast.10, s32[1,16]{1,0:T(1,128)} %bitcast.11, bf16[112,9216]{1,0:T(8,128)(2,1)} %vv.1, bf16[112,9216]{1,0:T(8,128)(2,1)} %vv.1, bf16[112,9216]{1,0:T(8,128)(2,1)} %vv.1, bf16[16,9216]{1,0:T(8,128)(2,1)} %tv.1, bf16[16,9216]{1,0:T(8,128)(2,1)} %tv.1, bf16[16,9216]{1,0:T(8,128)(2,1)} %tv.1), custom_call_target="tpu_custom_call" | custom-call | tf_op jit(solution)/shard_map/pack/pallas_call | solution.py:66
  12.2 2.1 %collective-permute-done.1.part = bf16[96,768]{1,0:T(8,128)(2,1)S(1)} collective-permute-done((bf16[96,768]{1,0:T(8,128)(2,1)S(1)}, bf16[96,768]{1,0:T(8,128)(2,1)S(1)}, u32[]{:S(2)}, u32[]{:S(2)}) %collective-permute-start.1) | collective-permute-done | bytes 147488 | tf_op jit(solution)/shard_map/ppermute | solution.py:390
  14.3 12.5 %all-to-all-start = ((bf16[16,592,128]{2,1,0:T(8,128)(2,1)}), bf16[16,592,128]{2,1,0:T(8,128)(2,1)S(1)}, u32[]{:S(2)}, u32[]{:S(2)}) async-start(bf16[16,592,128]{2,1,0:T(8,128)(2,1)} %pack.1), calls=%async_computation | async-start | bytes 4849664 | tf_op jit(solution)/shard_map/all_to_all | solution.py:425
  26.9 2.0 %collective-permute-start.2 = (bf16[96,1536]{1,0:T(8,128)(2,1)S(1)}, bf16[96,1536]{1,0:T(8,128)(2,1)S(1)}, u32[]{:S(2)}, u32[]{:S(2)}) collective-permute-start(bf16[96,1536]{1,0:T(8,128)(2,1)S(1)} %collective-permute-done.near), channel_id=1, source_target_pairs={{0,1},{1,0},{2,3},{3,2},{4,5},{5,4},{6,7},{7,6},{8,9},{9,8},{10,11... | collective-permute-start | bytes 884744 | tf_op jit(solution)/shard_map/ppermute | solution.py:390
  29.0 2.3 %collective-permute-start.3 = (bf16[96,768]{1,0:T(8,128)(2,1)S(1)}, bf16[96,768]{1,0:T(8,128)(2,1)S(1)}, u32[]{:S(2)}, u32[]{:S(2)}) collective-permute-start(bf16[96,768]{1,0:T(8,128)(2,1)S(1)} %collective-permute-done.1.part), channel_id=1, source_target_pairs={{0,1},{1,0},{2,3},{3,2},{4,5},{5,4},{6,7},{7,6},{8,9},{9,8},{10,11... | collective-permute-start | bytes 442376 | tf_op jit(solution)/shard_map/ppermute | solution.py:390
  33.7 3.0 %place.1 = bf16[4,96,1536]{2,1,0:T(8,128)(2,1)} custom-call(s32[7]{0:T(128)} %concatenate.3.where, bf16[96,1536]{1,0:T(8,128)(2,1)} %mine.1, bf16[96,1536]{1,0:T(8,128)(2,1)} %copy-done.15, bf16[96,1536]{1,0:T(8,128)(2,1)} %copy-done.16, bf16[96,768]{1,0:T(8,128)(2,1)} %copy-done.17, bf16[96,768]{1,0:T(8,128)(2,1)} %copy-done.18), custom_call_target="tpu_custom_call" | custom-call | tf_op jit(solution)/shard_map/place/pallas_call | solution.py:281
  36.7 5.1 %collective-permute-start.4 = (bf16[384,1536]{1,0:T(8,128)(2,1)}, bf16[384,1536]{1,0:T(8,128)(2,1)S(1)}, u32[]{:S(2)}, u32[]{:S(2)}) collective-permute-start(bf16[384,1536]{1,0:T(8,128)(2,1)} %bitcast.8), channel_id=1, source_target_pairs={{0,64},{1,449},{2,66},{3,451},{4,68},{5,453},{6,70},{7,455},{8,72}... | collective-permute-start | bytes 3538952 | tf_op jit(solution)/shard_map/ppermute | solution.py:390
  41.8 13.4 %collective-permute-done.4.refs_1_ = bf16[384,1536]{1,0:T(8,128)(2,1)S(1)} collective-permute-done((bf16[384,1536]{1,0:T(8,128)(2,1)}, bf16[384,1536]{1,0:T(8,128)(2,1)S(1)}, u32[]{:S(2)}, u32[]{:S(2)}) %collective-permute-start.4) | collective-permute-done | bytes 1179680 | tf_op jit(solution)/shard_map/ppermute | solution.py:390
  55.3 5.2 %collective-permute-start.5 = (bf16[384,1536]{1,0:T(8,128)(2,1)S(1)}, bf16[384,1536]{1,0:T(8,128)(2,1)}, u32[]{:S(2)}, u32[]{:S(2)}) collective-permute-start(bf16[384,1536]{1,0:T(8,128)(2,1)S(1)} %collective-permute-done.4.refs_1_), channel_id=1, source_target_pairs={{0,64},{1,449},{2,66},{3,451},{4,68},{5,453},{6,70},{7,455},{8,72}... | collective-permute-start | bytes 3538952 | tf_op jit(solution)/shard_map/ppermute | solution.py:390
  60.5 13.1 %collective-permute-done.5.refs_2_ = bf16[384,1536]{1,0:T(8,128)(2,1)} collective-permute-done((bf16[384,1536]{1,0:T(8,128)(2,1)S(1)}, bf16[384,1536]{1,0:T(8,128)(2,1)}, u32[]{:S(2)}, u32[]{:S(2)}) %collective-permute-start.5) | collective-permute-done | bytes 1179680 | tf_op jit(solution)/shard_map/ppermute | solution.py:390
  73.6 8.8 %all-to-all-done.cut.q.k.v = bf16[16,592,128]{2,1,0:T(8,128)(2,1)S(1)} async-done(((bf16[16,592,128]{2,1,0:T(8,128)(2,1)}), bf16[16,592,128]{2,1,0:T(8,128)(2,1)S(1)}, u32[]{:S(2)}, u32[]{:S(2)}) %all-to-all-start) | async-done | bytes 2424864 | tf_op jit(solution)/shard_map/all_to_all | solution.py:425
  82.4 5.1 %collective-permute-start.7 = (bf16[384,1536]{1,0:T(8,128)(2,1)}, bf16[384,1536]{1,0:T(8,128)(2,1)}, u32[]{:S(2)}, u32[]{:S(2)}) collective-permute-start(bf16[384,1536]{1,0:T(8,128)(2,1)} %collective-permute-done.5.refs_2_), channel_id=1, source_target_pairs={{0,64},{1,449},{2,66},{3,451},{4,68},{5,453},{6,70},{7,455},{8,72}... | collective-permute-start | bytes 3538952 | tf_op jit(solution)/shard_map/ppermute | solution.py:390
  87.6 1.9 %collective-permute-start.6 = (bf16[16,128,128]{2,1,0:T(8,128)(2,1)S(1)}, bf16[16,128,128]{2,1,0:T(8,128)(2,1)S(1)}, u32[]{:S(2)}, u32[]{:S(2)}) collective-permute-start(bf16[16,128,128]{2,1,0:T(8,128)(2,1)S(1)} %slice.3.own_kv), channel_id=1, source_target_pairs={{0,1},{1,0},{2,3},{3,2},{4,5},{5,4},{6,7},{7,6},{8,9},{9,8},{10,11... | collective-permute-start | bytes 1572872 | tf_op jit(solution)/shard_map/ppermute | solution.py:390
  89.5 7.6 %attend_whole.1 = (bf16[16,128,128]{2,1,0:T(8,128)(2,1)S(1)}, f32[16,128]{1,0:T(8,128)S(1)}) custom-call(bf16[16,592,128]{2,1,0:T(8,128)(2,1)S(1)} %all-to-all-done.cut.q.k.v, bf16[16,592,128]{2,1,0:T(8,128)(2,1)S(1)} %all-to-all-done.cut.q.k.v, bf16[16,592,128]{2,1,0:T(8,128)(2,1)S(1)} %all-to-all-done.cut.q.k.v, ...), custom_call_target="tpu_custom_call" | custom-call | flops 4294967296 | bytes 2097152 | tf_op jit(solution)/shard_map/attend_whole/pallas_call | solution.py:216
  97.1 4.3 %attend_shared.1 = bf16[16,224,128]{2,1,0:T(8,128)(2,1)S(1)} custom-call(s32[7]{0:T(128)S(1)} %copy-done.14, bf16[16,592,128]{2,1,0:T(8,128)(2,1)S(1)} %all-to-all-done.cut.q.k.v, bf16[16,592,128]{2,1,0:T(8,128)(2,1)S(1)} %all-to-all-done.cut.q.k.v, bf16[16,128,128]{2,1,0:T(8,128)(2,1)S(1)} %slice.3.own_kv, ...), custom_call_target="tpu_custom_call" | custom-call | flops 2147483648 | bytes 2097152 | tf_op jit(solution)/shard_map/attend_shared/pallas_call | solution.py:243
  102.4 5.6 %all-to-all-start.1 = ((bf16[16,224,128]{2,1,0:T(8,128)(2,1)}), bf16[16,224,128]{2,1,0:T(8,128)(2,1)S(1)}, u32[]{:S(2)}, u32[]{:S(2)}) async-start(bf16[16,224,128]{2,1,0:T(8,128)(2,1)} %copy-done.9), calls=%async_computation.1 | async-start | bytes 1835008 | tf_op jit(solution)/shard_map/all_to_all | solution.py:436
  108.0 1.1 constant_dynamic-slice_fusion
  109.1 3.4 %collective-permute-start.11 = (bf16[384,768]{1,0:T(8,128)(2,1)S(1)}, bf16[384,768]{1,0:T(8,128)(2,1)S(1)}, u32[]{:S(2)}, u32[]{:S(2)}) collective-permute-start(bf16[384,768]{1,0:T(8,128)(2,1)S(1)} %constant_dynamic-slice_fusion), channel_id=1, source_target_pairs={{0,64},{1,449},{2,66},{3,451},{4,68},{5,453},{6,70},{7,455},{8,72}... | collective-permute-start | bytes 1769480 | tf_op jit(solution)/shard_map/ppermute | solution.py:390
  112.5 1.9 %collective-permute-start.8 = (bf16[384,1536]{1,0:T(8,128)(2,1)S(1)}, bf16[384,1536]{1,0:T(8,128)(2,1)S(1)}, u32[]{:S(2)}, u32[]{:S(2)}) collective-permute-start(bf16[384,1536]{1,0:T(8,128)(2,1)S(1)} %copy-done.2), channel_id=1, source_target_pairs={{0,1},{1,0},{2,3},{3,2},{4,5},{5,4},{6,7},{7,6},{8,9},{9,8},{10,11... | collective-permute-start | bytes 3538952 | tf_op jit(solution)/shard_map/ppermute | solution.py:390
  114.5 2.4 %collective-permute-start.9 = (bf16[384,1536]{1,0:T(8,128)(2,1)}, bf16[384,1536]{1,0:T(8,128)(2,1)S(1)}, u32[]{:S(2)}, u32[]{:S(2)}) collective-permute-start(bf16[384,1536]{1,0:T(8,128)(2,1)} %collective-permute-done.5.refs_2_), channel_id=1, source_target_pairs={{0,1},{1,0},{2,3},{3,2},{4,5},{5,4},{6,7},{7,6},{8,9},{9,8},{10,11... | collective-permute-start | bytes 3538952 | tf_op jit(solution)/shard_map/ppermute | solution.py:390
  116.9 1.9 %collective-permute-start.10 = (bf16[384,1536]{1,0:T(8,128)(2,1)}, bf16[384,1536]{1,0:T(8,128)(2,1)S(1)}, u32[]{:S(2)}, u32[]{:S(2)}) collective-permute-start(bf16[384,1536]{1,0:T(8,128)(2,1)} %collective-permute-done.7.refs_3_), channel_id=1, source_target_pairs={{0,1},{1,0},{2,3},{3,2},{4,5},{5,4},{6,7},{7,6},{8,9},{9,8},{10,11... | collective-permute-start | bytes 3538952 | tf_op jit(solution)/shard_map/ppermute | solution.py:390
  118.8 1.2 collective-permute-done.11.refs_7_
  120.0 4.1 %collective-permute-start.12 = (bf16[384,768]{1,0:T(8,128)(2,1)S(1)}, bf16[384,768]{1,0:T(8,128)(2,1)S(1)}, u32[]{:S(2)}, u32[]{:S(2)}) collective-permute-start(bf16[384,768]{1,0:T(8,128)(2,1)S(1)} %collective-permute-done.11.refs_7_), channel_id=1, source_target_pairs={{0,1},{1,0},{2,3},{3,2},{4,5},{5,4},{6,7},{7,6},{8,9},{9,8},{10,11... | collective-permute-start | bytes 1769480 | tf_op jit(solution)/shard_map/ppermute | solution.py:390
  128.7 1.1 copy-done.7
  129.8 3.5 %all-to-all-done.1.ret = bf16[16,224,128]{2,1,0:T(8,128)(2,1)S(1)} async-done(((bf16[16,224,128]{2,1,0:T(8,128)(2,1)}), bf16[16,224,128]{2,1,0:T(8,128)(2,1)S(1)}, u32[]{:S(2)}, u32[]{:S(2)}) %all-to-all-start.1) | async-done | bytes 917536 | tf_op jit(solution)/shard_map/all_to_all | solution.py:436
  133.3 1.3 copy-done.4
  134.6 1.3 copy-done.6
  135.9 1.3 copy-done.8
  137.1 1.1 copy-done.11
  139.3 5.8 %project.1 = (bf16[112,1536]{1,0:T(8,128)(2,1)}, bf16[16,3072]{1,0:T(8,128)(2,1)}, f32[2,2048]{1,0:T(2,128)}) custom-call(s32[7]{0:T(128)S(1)} %copy-done.14, bf16[16,224,128]{2,1,0:T(8,128)(2,1)S(1)} %all-to-all-done.1.ret, bf16[384,1536]{1,0:T(8,128)(2,1)S(1)} %bitcast.9, bf16[384,1536]{1,0:T(8,128)(2,1)S(1)} %copy-done.2, ...), custom_call_target="tpu_custom_call" | custom-call | tf_op jit(solution)/shard_map/project/pallas_call | solution.py:355
  (53 shorter events, 10.1 us)
Async XLA Ops:
  0.6 13.7 %collective-permute-start = (bf16[96,1536]{1,0:T(8,128)(2,1)}, bf16[96,1536]{1,0:T(8,128)(2,1)S(1)}, u32[]{:S(2)}, u32[]{:S(2)}) collective-permute-start(bf16[96,1536]{1,0:T(8,128)(2,1)} %mine.1), channel_id=1, source_target_pairs={{0,16},{1,49},{2,18},{3,51},{4,20},{5,53},{6,22},{7,55},{8,24},{9,... | collective-permute-start | bytes 884744 | tf_op jit(solution)/shard_map/ppermute | solution.py:390
  6.8 7.4 %collective-permute-start.1 = (bf16[96,768]{1,0:T(8,128)(2,1)S(1)}, bf16[96,768]{1,0:T(8,128)(2,1)S(1)}, u32[]{:S(2)}, u32[]{:S(2)}) collective-permute-start(bf16[96,768]{1,0:T(8,128)(2,1)S(1)} %constant_dynamic-slice_fusion.1), channel_id=1, source_target_pairs={{0,32},{1,33},{2,34},{3,35},{4,36},{5,37},{6,38},{7,39},{8,40},{9,... | collective-permute-start | bytes 442376 | tf_op jit(solution)/shard_map/ppermute | solution.py:390
  12.2 14.6 %copy-start.19 = (s32[24]{0:T(128)S(1)}, s32[24]{0:T(128)}, u32[]{:S(2)}) copy-start(s32[24]{0:T(128)} %param.10) | copy-start | bytes 292
  14.3 14.8 %copy-start.17 = (bf16[96,768]{1,0:T(8,128)(2,1)}, bf16[96,768]{1,0:T(8,128)(2,1)S(1)}, u32[]{:S(2)}) copy-start(bf16[96,768]{1,0:T(8,128)(2,1)S(1)} %collective-permute-done.1.part) | copy-start | bytes 442372
  14.3 12.6 %copy-start.15 = (bf16[96,1536]{1,0:T(8,128)(2,1)}, bf16[96,1536]{1,0:T(8,128)(2,1)S(1)}, u32[]{:S(2)}) copy-start(bf16[96,1536]{1,0:T(8,128)(2,1)S(1)} %collective-permute-done.near) | copy-start | bytes 884740
  14.3 68.1 %all-to-all-start = ((bf16[16,592,128]{2,1,0:T(8,128)(2,1)}), bf16[16,592,128]{2,1,0:T(8,128)(2,1)S(1)}, u32[]{:S(2)}, u32[]{:S(2)}) async-start(bf16[16,592,128]{2,1,0:T(8,128)(2,1)} %pack.1), calls=%async_computation | async-start | bytes 4849664 | tf_op jit(solution)/shard_map/all_to_all | solution.py:425
  26.9 5.5 %collective-permute-start.2 = (bf16[96,1536]{1,0:T(8,128)(2,1)S(1)}, bf16[96,1536]{1,0:T(8,128)(2,1)S(1)}, u32[]{:S(2)}, u32[]{:S(2)}) collective-permute-start(bf16[96,1536]{1,0:T(8,128)(2,1)S(1)} %collective-permute-done.near), channel_id=1, source_target_pairs={{0,1},{1,0},{2,3},{3,2},{4,5},{5,4},{6,7},{7,6},{8,9},{9,8},{10,11... | collective-permute-start | bytes 884744 | tf_op jit(solution)/shard_map/ppermute | solution.py:390
  29.0 3.3 %collective-permute-start.3 = (bf16[96,768]{1,0:T(8,128)(2,1)S(1)}, bf16[96,768]{1,0:T(8,128)(2,1)S(1)}, u32[]{:S(2)}, u32[]{:S(2)}) collective-permute-start(bf16[96,768]{1,0:T(8,128)(2,1)S(1)} %collective-permute-done.1.part), channel_id=1, source_target_pairs={{0,1},{1,0},{2,3},{3,2},{4,5},{5,4},{6,7},{7,6},{8,9},{9,8},{10,11... | collective-permute-start | bytes 442376 | tf_op jit(solution)/shard_map/ppermute | solution.py:390
  36.7 18.5 %collective-permute-start.4 = (bf16[384,1536]{1,0:T(8,128)(2,1)}, bf16[384,1536]{1,0:T(8,128)(2,1)S(1)}, u32[]{:S(2)}, u32[]{:S(2)}) collective-permute-start(bf16[384,1536]{1,0:T(8,128)(2,1)} %bitcast.8), channel_id=1, source_target_pairs={{0,64},{1,449},{2,66},{3,451},{4,68},{5,453},{6,70},{7,455},{8,72}... | collective-permute-start | bytes 3538952 | tf_op jit(solution)/shard_map/ppermute | solution.py:390
  55.3 5.2 %copy-start.1 = (bf16[384,1536]{1,0:T(8,128)(2,1)}, bf16[384,1536]{1,0:T(8,128)(2,1)S(1)}, u32[]{:S(2)}) copy-start(bf16[384,1536]{1,0:T(8,128)(2,1)S(1)} %collective-permute-done.4.refs_1_) | copy-start | bytes 3538948
  55.3 18.3 %collective-permute-start.5 = (bf16[384,1536]{1,0:T(8,128)(2,1)S(1)}, bf16[384,1536]{1,0:T(8,128)(2,1)}, u32[]{:S(2)}, u32[]{:S(2)}) collective-permute-start(bf16[384,1536]{1,0:T(8,128)(2,1)S(1)} %collective-permute-done.4.refs_1_), channel_id=1, source_target_pairs={{0,64},{1,449},{2,66},{3,451},{4,68},{5,453},{6,70},{7,455},{8,72}... | collective-permute-start | bytes 3538952 | tf_op jit(solution)/shard_map/ppermute | solution.py:390
  82.4 20.0 %collective-permute-start.7 = (bf16[384,1536]{1,0:T(8,128)(2,1)}, bf16[384,1536]{1,0:T(8,128)(2,1)}, u32[]{:S(2)}, u32[]{:S(2)}) collective-permute-start(bf16[384,1536]{1,0:T(8,128)(2,1)} %collective-permute-done.5.refs_2_), channel_id=1, source_target_pairs={{0,64},{1,449},{2,66},{3,451},{4,68},{5,453},{6,70},{7,455},{8,72}... | collective-permute-start | bytes 3538952 | tf_op jit(solution)/shard_map/ppermute | solution.py:390
  87.5 9.6 %copy-start.14 = (s32[7]{0:T(128)S(1)}, s32[7]{0:T(128)}, u32[]{:S(2)}) copy-start(s32[7]{0:T(128)} %concatenate.3.where) | copy-start | bytes 88
  87.6 9.6 %collective-permute-start.6 = (bf16[16,128,128]{2,1,0:T(8,128)(2,1)S(1)}, bf16[16,128,128]{2,1,0:T(8,128)(2,1)S(1)}, u32[]{:S(2)}, u32[]{:S(2)}) collective-permute-start(bf16[16,128,128]{2,1,0:T(8,128)(2,1)S(1)} %slice.3.own_kv), channel_id=1, source_target_pairs={{0,1},{1,0},{2,3},{3,2},{4,5},{5,4},{6,7},{7,6},{8,9},{9,8},{10,11... | collective-permute-start | bytes 1572872 | tf_op jit(solution)/shard_map/ppermute | solution.py:390
  101.4 1.0 copy-start.9
  102.4 10.1 %copy-start.2 = (bf16[384,1536]{1,0:T(8,128)(2,1)S(1)}, bf16[384,1536]{1,0:T(8,128)(2,1)}, u32[]{:S(2)}) copy-start(bf16[384,1536]{1,0:T(8,128)(2,1)} %copy-done.1) | copy-start | bytes 3538948
  102.4 30.9 %copy-start = (bf16[4,96,1536]{2,1,0:T(8,128)(2,1)S(1)}, bf16[4,96,1536]{2,1,0:T(8,128)(2,1)}, u32[]{:S(2)}) copy-start(bf16[4,96,1536]{2,1,0:T(8,128)(2,1)} %place.1) | copy-start | bytes 3538948
  102.4 30.9 %all-to-all-start.1 = ((bf16[16,224,128]{2,1,0:T(8,128)(2,1)}), bf16[16,224,128]{2,1,0:T(8,128)(2,1)S(1)}, u32[]{:S(2)}, u32[]{:S(2)}) async-start(bf16[16,224,128]{2,1,0:T(8,128)(2,1)} %copy-done.9), calls=%async_computation.1 | async-start | bytes 1835008 | tf_op jit(solution)/shard_map/all_to_all | solution.py:436
  109.1 10.9 %collective-permute-start.11 = (bf16[384,768]{1,0:T(8,128)(2,1)S(1)}, bf16[384,768]{1,0:T(8,128)(2,1)S(1)}, u32[]{:S(2)}, u32[]{:S(2)}) collective-permute-start(bf16[384,768]{1,0:T(8,128)(2,1)S(1)} %constant_dynamic-slice_fusion), channel_id=1, source_target_pairs={{0,64},{1,449},{2,66},{3,451},{4,68},{5,453},{6,70},{7,455},{8,72}... | collective-permute-start | bytes 1769480 | tf_op jit(solution)/shard_map/ppermute | solution.py:390
  112.5 14.0 %collective-permute-start.8 = (bf16[384,1536]{1,0:T(8,128)(2,1)S(1)}, bf16[384,1536]{1,0:T(8,128)(2,1)S(1)}, u32[]{:S(2)}, u32[]{:S(2)}) collective-permute-start(bf16[384,1536]{1,0:T(8,128)(2,1)S(1)} %copy-done.2), channel_id=1, source_target_pairs={{0,1},{1,0},{2,3},{3,2},{4,5},{5,4},{6,7},{7,6},{8,9},{9,8},{10,11... | collective-permute-start | bytes 3538952 | tf_op jit(solution)/shard_map/ppermute | solution.py:390
  114.5 13.2 %collective-permute-start.9 = (bf16[384,1536]{1,0:T(8,128)(2,1)}, bf16[384,1536]{1,0:T(8,128)(2,1)S(1)}, u32[]{:S(2)}, u32[]{:S(2)}) collective-permute-start(bf16[384,1536]{1,0:T(8,128)(2,1)} %collective-permute-done.5.refs_2_), channel_id=1, source_target_pairs={{0,1},{1,0},{2,3},{3,2},{4,5},{5,4},{6,7},{7,6},{8,9},{9,8},{10,11... | collective-permute-start | bytes 3538952 | tf_op jit(solution)/shard_map/ppermute | solution.py:390
  116.9 11.8 %collective-permute-start.10 = (bf16[384,1536]{1,0:T(8,128)(2,1)}, bf16[384,1536]{1,0:T(8,128)(2,1)S(1)}, u32[]{:S(2)}, u32[]{:S(2)}) collective-permute-start(bf16[384,1536]{1,0:T(8,128)(2,1)} %collective-permute-done.7.refs_3_), channel_id=1, source_target_pairs={{0,1},{1,0},{2,3},{3,2},{4,5},{5,4},{6,7},{7,6},{8,9},{9,8},{10,11... | collective-permute-start | bytes 3538952 | tf_op jit(solution)/shard_map/ppermute | solution.py:390
  120.0 5.7 %collective-permute-start.12 = (bf16[384,768]{1,0:T(8,128)(2,1)S(1)}, bf16[384,768]{1,0:T(8,128)(2,1)S(1)}, u32[]{:S(2)}, u32[]{:S(2)}) collective-permute-start(bf16[384,768]{1,0:T(8,128)(2,1)S(1)} %collective-permute-done.11.refs_7_), channel_id=1, source_target_pairs={{0,1},{1,0},{2,3},{3,2},{4,5},{5,4},{6,7},{7,6},{8,9},{9,8},{10,11... | collective-permute-start | bytes 1769480 | tf_op jit(solution)/shard_map/ppermute | solution.py:390
  125.7 0.8 copy-start.12
  126.6 1.1 copy-start.3
  127.6 1.0 copy-start.5
  128.7 1.1 copy-start.7
  133.3 1.3 copy-start.4
  134.6 1.3 copy-start.6
  135.9 1.3 copy-start.8
  137.1 1.1 copy-start.11
  138.2 1.1 copy-start.13
  (3 other events, 2.2 us)

commit v3 on v2

--- a/solution.py
+++ b/solution.py
@@ -189,7 +189,8 @@
 
 Q_ROWS = 512
 STEP_ROWS = 1024
-VMEM = 40 * 2**20
+VMEM = 32 * 2**20
+PROJECT_VMEM = 50 * 2**20
 
 
 def attention_scratch():
@@ -203,9 +204,9 @@
 
 def attention_cost(queries, keys):
     return pl.CostEstimate(
-        flops=queries * keys * HEAD_DIM * 8,
+        flops=queries * keys * HEAD_DIM // 4,
         bytes_accessed=4 * keys * HEAD_DIM * 2,
-        transcendentals=queries * keys,
+        transcendentals=0,
     )
 
 
@@ -263,17 +264,27 @@
     )(where, received, received, own_kv, far_kv, whole, whole_lse)
 
 
-def place_kernel(where, mine, near, near_far, part, part_far, out):
+def place_kernel(where, mine, near, near_far, part, part_far, out, sems):
     x, core = where[1], where[2]
     sign = 1 - 2 * core
-    out[x] = mine[...]
-    out[(x - sign + 4) % 4] = near[...]
-    out[(x + sign + 4) % 4] = near_far[...]
-    columns = part.shape[1]
-    low, high = pl.multiple_of(core * columns, columns), pl.multiple_of((1 - core) * columns, columns)
-    opposite = (x + 2) % 4
-    out[opposite, :, pl.ds(low, columns)] = part[...]
-    out[opposite, :, pl.ds(high, columns)] = part_far[...]
+
+    def copy(source, to, index):
+        return pltpu.make_async_copy(source, out.at[(to + 4) % 4], sems.at[index])
+
+    copies = [copy(mine, x, 0), copy(near, x - sign, 1), copy(near_far, x + sign, 2)]
+    for item in copies:
+        item.start()
+
+    @pl.when(core == 0)
+    def _():
+        copy(part, x + 2, 3).start()
+
+    @pl.when(core == 1)
+    def _():
+        copy(part_far, x + 2, 3).start()
+
+    for item in copies + [copy(part, x + 2, 3)]:
+        item.wait()
 
 
 def place(where, mine, near, near_far, part, part_far):
@@ -283,8 +294,9 @@
         grid_spec=pltpu.PrefetchScalarGridSpec(
             num_scalar_prefetch=1,
             grid=(),
-            in_specs=[pl.BlockSpec(memory_space=pltpu.VMEM)] * 5,
-            out_specs=pl.BlockSpec(memory_space=pltpu.VMEM),
+            in_specs=[pl.BlockSpec(memory_space=pl.ANY)] * 5,
+            out_specs=pl.BlockSpec(memory_space=pl.ANY),
+            scratch_shapes=[pltpu.SemaphoreType.DMA((4,))],
         ),
         out_shape=jax.ShapeDtypeStruct((4, rows, columns), jnp.bfloat16),
         name="place",
@@ -310,24 +322,67 @@
     return rows
 
 
-def project_kernel(where, ret, *refs):
-    weights, (vis_out, txt_out, slots, held, sems) = refs[:9], refs[9:]
-    y, core = where[0], where[2]
-    sign = 1 - 2 * core
-    columns = held.shape[2] // 2
+def stage_kernel(where, *refs):
+    weights, out, sems = refs[:9], refs[9], refs[10]
+    core = where[2]
+    columns = out.shape[2] // 2
     copies = []
     for index in range(7):
-        copies.append(pltpu.make_async_copy(weights[index], held.at[index], sems.at[index]))
+        to = out.at[index // 2, pl.ds(index % 2 * TRIO, TRIO)]
+        copies.append(pltpu.make_async_copy(weights[index], to, sems.at[index]))
     for index in range(2):
         at = core if index == 0 else 1 - core
         start = pl.multiple_of(at * columns, columns)
-        copies.append(
-            pltpu.make_async_copy(
-                weights[7 + index], held.at[7, :, pl.ds(start, columns)], sems.at[7 + index]
-            )
-        )
+        to = out.at[3, pl.ds(TRIO, TRIO), pl.ds(start, columns)]
+        copies.append(pltpu.make_async_copy(weights[7 + index], to, sems.at[7 + index]))
     for copy in copies:
         copy.start()
+    for copy in copies:
+        copy.wait()
+
+
+def stage(where, chunks, far_chunks):
+    columns = chunks[0].shape[1]
+    return pl.pallas_call(
+        stage_kernel,
+        grid_spec=pltpu.PrefetchScalarGridSpec(
+            num_scalar_prefetch=1,
+            grid=(),
+            in_specs=[pl.BlockSpec(memory_space=pl.ANY)] * 9,
+            out_specs=pl.BlockSpec(memory_space=pl.ANY),
+            scratch_shapes=[pltpu.SemaphoreType.DMA((9,))],
+        ),
+        out_shape=jax.ShapeDtypeStruct((4, 2 * TRIO, columns), jnp.bfloat16),
+        name="stage",
+    )(where, *chunks[:4], *far_chunks[:3], chunks[4], far_chunks[3])
+
+
+HOPS = (0, 1, 2, 3, -1, -2, -3, 4)
+
+
+def project_kernel(where, ret, weights, vis_out, txt_out, slots, held, sems):
+    y, core = where[0], where[2]
+    sign = 1 - 2 * core
+    copies = [
+        pltpu.make_async_copy(weights.at[block], held.at[block], sems.at[block])
+        for block in range(weights.shape[0])
+    ]
+    for copy in copies:
+        copy.start()
+    total = jnp.zeros((ROWS, weights.shape[2]), jnp.float32)
+    pieces = []
+    for index, hops in enumerate(HOPS):
+        chip = (y - hops * sign + 8) % 8
+        low, high = ret[2 * chip], ret[2 * chip + 1]
+        shared = jnp.concatenate([low[ROWS:RET_ROWS], high[ROWS:RET_ROWS]], axis=0)
+        attention = jnp.concatenate([low[:ROWS], shared, high[:ROWS]], axis=1)
+        txt_out[:, pl.ds(pl.multiple_of(chip * TRIO, TRIO), TRIO)] = attention[VIS_ROWS:]
+        pieces.append(attention)
+        if index % 2 == 1:
+            both = jnp.concatenate(pieces[-2:], axis=1)
+            copies[index // 2].wait()
+            total += jnp.dot(both, held[index // 2], preferred_element_type=jnp.float32)
+    vis_out[...] = total[:VIS_ROWS].astype(jnp.bfloat16)
     for slot in range(SLOTS):
         valid = where[5 + slot] > 0
         for source, row in enumerate(slot_of(ret, where[3 + slot])):
@@ -336,32 +391,20 @@
             slots[slot : slot + 1, at : at + VIS_ROWS] = row[:, :VIS_ROWS]
             at = VIS_SEQ + source * TXT_ROWS
             slots[slot : slot + 1, at : at + TXT_ROWS] = row[:, VIS_ROWS:]
-    total = jnp.zeros((ROWS, 2 * columns), jnp.float32)
-    for index, hops in enumerate((0, 1, 2, 3, -1, -2, -3, 4)):
-        chip = (y - hops * sign + 8) % 8
-        low, high = ret[2 * chip], ret[2 * chip + 1]
-        shared = jnp.concatenate([low[ROWS:RET_ROWS], high[ROWS:RET_ROWS]], axis=0)
-        attention = jnp.concatenate([low[:ROWS], shared, high[:ROWS]], axis=1)
-        txt_out[:, pl.ds(pl.multiple_of(chip * TRIO, TRIO), TRIO)] = attention[VIS_ROWS:]
-        copies[index].wait()
-        if index == 7:
-            copies[8].wait()
-        total += jnp.dot(attention, held[index], preferred_element_type=jnp.float32)
-    vis_out[...] = total[:VIS_ROWS].astype(jnp.bfloat16)
-
-
-def project(where, returned, chunks, far_chunks):
-    columns = chunks[0].shape[1]
+
+
+def project(where, returned, weights):
+    columns = weights.shape[2]
     return pl.pallas_call(
         project_kernel,
         grid_spec=pltpu.PrefetchScalarGridSpec(
             num_scalar_prefetch=1,
             grid=(),
-            in_specs=[pl.BlockSpec(memory_space=pltpu.VMEM)] + [pl.BlockSpec(memory_space=pl.ANY)] * 9,
+            in_specs=[pl.BlockSpec(memory_space=pltpu.VMEM), pl.BlockSpec(memory_space=pl.ANY)],
             out_specs=[pl.BlockSpec(memory_space=pltpu.VMEM)] * 3,
             scratch_shapes=[
-                pltpu.VMEM((8, TRIO, columns), jnp.bfloat16),
-                pltpu.SemaphoreType.DMA((9,)),
+                pltpu.VMEM(weights.shape, jnp.bfloat16),
+                pltpu.SemaphoreType.DMA((weights.shape[0],)),
             ],
         ),
         out_shape=[
@@ -369,9 +412,9 @@
             jax.ShapeDtypeStruct((TXT_ROWS, HEADS * HEAD_DIM), jnp.bfloat16),
             jax.ShapeDtypeStruct((SLOTS, VIS_SEQ + TXT_SEQ), jnp.float32),
         ],
-        compiler_params=pltpu.CompilerParams(vmem_limit_bytes=VMEM),
+        compiler_params=pltpu.CompilerParams(vmem_limit_bytes=PROJECT_VMEM),
         name="project",
-    )(where, returned, *chunks[:4], *far_chunks[:3], chunks[4], far_chunks[3])
+    )(where, returned, weights)
 
 
 AXES = ("dp", "seq")
@@ -379,23 +422,24 @@
 Y_SIZE = 8
 
 
-def permute(operand, target):
+def permute(operand, target, cores=(0, 1)):
     pairs = []
     for y in range(Y_SIZE):
         for x in range(X_SIZE):
             for s in range(N_SEQ):
                 ty, tx, ts = target(y, x, s)
                 there = (ty % Y_SIZE) * X_SIZE + tx % X_SIZE
-                pairs.append(((y * X_SIZE + x) * N_SEQ + s, there * N_SEQ + ts))
+                if s % 2 in cores:
+                    pairs.append(((y * X_SIZE + x) * N_SEQ + s, there * N_SEQ + ts))
     return lax.ppermute(operand, AXES, pairs)
 
 
-def swap(operand):
-    return permute(operand, lambda y, x, s: (y, x, s ^ 1))
-
-
-def shift_x(operand, hops):
-    return permute(operand, lambda y, x, s: (y, x + hops * (1 - 2 * (s % 2)), s))
+def swap(operand, cores=(0, 1)):
+    return permute(operand, lambda y, x, s: (y, x, s ^ 1), cores)
+
+
+def shift_x(operand, hops, cores=(0, 1)):
+    return permute(operand, lambda y, x, s: (y, x + hops * (1 - 2 * (s % 2)), s), cores)
 
 
 def shift_y(operand):
@@ -419,14 +463,12 @@
     where = jnp.concatenate([place_here, heads_of_slots(head_map, seq_index)])
 
     near = shift_x(w_out, 1)
-    part = shift_x(lax.dynamic_slice_in_dim(w_out, core * half, half, 1), 2)
+    part = shift_x(w_out, 2, cores=(0,))
     sending = pack(qkv_vis, qkv_txt, vis_segments, txt_segments)
-    sending, near, part = lax.optimization_barrier((sending, near, part))
     received = lax.all_to_all(sending, "seq", split_axis=0, concat_axis=0, tiled=True)
-    chunks = [place(where, w_out, near, swap(near), part, swap(part)).reshape(-1, 2 * half)]
+    chunks = [place(where, w_out, near, swap(near), part, swap(part, cores=(0,))).reshape(-1, 2 * half)]
     chunks.append(shift_y(chunks[0]))
     chunks.append(shift_y(chunks[1]))
-    received, chunks[2] = lax.optimization_barrier((received, chunks[2]))
     chunks.append(shift_y(chunks[2]))
     own_kv = received[:, A_ROWS + HALF : SEND_ROWS]
     far_kv = swap(own_kv)
@@ -436,7 +478,7 @@
     returned = lax.all_to_all(returning, "seq", split_axis=0, concat_axis=0, tiled=True)
     chunks.append(shift_y(lax.dynamic_slice_in_dim(chunks[3], core * half, half, 1)))
     far_chunks = [swap(chunk) for chunk in chunks[1:]]
-    vis_out, txt_out, lse_slots = project(where, returned, chunks, far_chunks)
+    vis_out, txt_out, lse_slots = project(where, returned, stage(where, chunks, far_chunks))
     return vis_out, txt_out, lse_slots
 
 

time: 146 us -> 450 us (3.08)
  Pallas kernels: 23.6 us -> 347 us
  local copies, waits for them, and re-layouts: 16 us -> 4.89 us
  waiting for transfers between devices: 43.1 us -> 35.6 us
    pallas_call x0 -> x1, Pallas kernels: none -> 288 us  [stage(): pl.pallas_call(stage_kernel, grid_spec=pltpu.PrefetchScalarGridSpec(num_s...]
    pallas_call x1, Pallas kernels: 3.01 us -> 37.5 us  [place(): pl.pallas_call(place_kernel, grid_spec=pltpu.PrefetchScalarGridSpec(num_s...]
    unnamed x40 -> x26, local copies, waits for them, and re-layouts: 13.1 us -> 2.97 us
    all_to_all x1, waiting for transfers between devices: 8.79 us -> 0.01 us  [on_device(): lax.all_to_all(sending, 'seq', split_axis=0, concat_axis=0, tiled=True)]
    ppermute x13, waiting for transfers between devices: 30.7 us -> 35.6 us  [permute(): return lax.ppermute(operand, AXES, pairs)]
  transfers between devices with their start and end apart: 15 -> 15, of which waited for: 8 -> 6; matrix products, arithmetic and copies ran while one was open for 2% -> 0% of each run, Pallas kernels for 12% -> 75%
where the time goes in v3:
time: 450 us
  Pallas kernels  347 us (77%)
  starting transfers between devices  61.2 us (14%)
  waiting for transfers between devices  35.6 us (8%)
  local copies, waits for them, and re-layouts  4.89 us (1%)
    pallas_call x1, Pallas kernels, stage(): pl.pallas_call(stage_kernel, grid_spec=pltpu.PrefetchScalarGridSpec(num_s...  288 us
    ppermute x13, starting transfers between devices, permute(): return lax.ppermute(operand, AXES, pairs)  39.8 us
    pallas_call x1, Pallas kernels, place(): pl.pallas_call(place_kernel, grid_spec=pltpu.PrefetchScalarGridSpec(num_s...  37.5 us
    ppermute x13, waiting for transfers between devices, permute(): return lax.ppermute(operand, AXES, pairs)  35.6 us
    all_to_all x1, starting transfers between devices, on_device(): lax.all_to_all(sending, 'seq', split_axis=0, concat_axis=0, tiled=True)  12 us
    all_to_all x1, starting transfers between devices, on_device(): lax.all_to_all(returning, 'seq', split_axis=0, concat_axis=0, tiled=True)  9.43 us
  transfers between devices with their start and end apart: 15, of which 6 were waited for; matrix products, arithmetic and copies ran while one was open for 0% of the time, Pallas kernels for 75%

profile of v3, /device:TPU:1, one launch (start us, length us, event | category | flops | bytes accessed | tf_op | source)
XLA Modules:
  0.0 449.6 jit_solution(7443795609398150285)
XLA Ops:
  0.6 3.0 pack.1
  3.6 12.0 %all-to-all-start = ((bf16[16,592,128]{2,1,0:T(8,128)(2,1)}), bf16[16,592,128]{2,1,0:T(8,128)(2,1)S(1)}, u32[]{:S(2)}, u32[]{:S(2)}) async-start(bf16[16,592,128]{2,1,0:T(8,128)(2,1)} %pack.1), calls=%async_computation | async-start | bytes 4849664 | tf_op jit(solution)/shard_map/all_to_all | solution.py:468
  15.6 4.4 collective-permute-start.1
  20.0 0.7 collective-permute-start.3
  21.0 2.7 collective-permute-done.1.near
  23.7 3.8 collective-permute-start.2
  27.5 1.3 collective-permute-start.4
  28.9 0.7 concatenate.3.where
  29.6 2.4 collective-permute-done.4.part_far
  32.0 0.7 copy-done.11
  32.8 37.5 %place.1 = bf16[4,96,1536]{2,1,0:T(8,128)(2,1)} custom-call(s32[7]{0:T(128)} %concatenate.3.where, bf16[96,1536]{1,0:T(8,128)(2,1)} %mine.1, bf16[96,1536]{1,0:T(8,128)(2,1)} %copy-done.9, bf16[96,1536]{1,0:T(8,128)(2,1)} %collective-permute-done.2.near_far, bf16[96,1536]{1,0:T(8,128)(2,1)} %copy-done.10, bf16[96,1536]{1,0:T(8,128)(2,1)} %copy-done.11), custom_call_target="tpu_custom_call" | custom-call | tf_op jit(solution)/shard_map/place/pallas_call | solution.py:292
  70.3 5.1 %collective-permute-start.5 = (bf16[384,1536]{1,0:T(8,128)(2,1)}, bf16[384,1536]{1,0:T(8,128)(2,1)S(1)}, u32[]{:S(2)}, u32[]{:S(2)}) collective-permute-start(bf16[384,1536]{1,0:T(8,128)(2,1)} %bitcast.8), channel_id=1, source_target_pairs={{0,64},{1,449},{2,66},{3,451},{4,68},{5,453},{6,70},{7,455},{8,72}... | collective-permute-start | bytes 3538952 | tf_op jit(solution)/shard_map/ppermute | solution.py:434
  75.4 13.4 %collective-permute-done.5.refs_1_ = bf16[384,1536]{1,0:T(8,128)(2,1)S(1)} collective-permute-done((bf16[384,1536]{1,0:T(8,128)(2,1)}, bf16[384,1536]{1,0:T(8,128)(2,1)S(1)}, u32[]{:S(2)}, u32[]{:S(2)}) %collective-permute-start.5) | collective-permute-done | bytes 1179680 | tf_op jit(solution)/shard_map/ppermute | solution.py:434
  88.9 4.9 %collective-permute-start.6 = (bf16[384,1536]{1,0:T(8,128)(2,1)S(1)}, bf16[384,1536]{1,0:T(8,128)(2,1)}, u32[]{:S(2)}, u32[]{:S(2)}) collective-permute-start(bf16[384,1536]{1,0:T(8,128)(2,1)S(1)} %collective-permute-done.5.refs_1_), channel_id=1, source_target_pairs={{0,64},{1,449},{2,66},{3,451},{4,68},{5,453},{6,70},{7,455},{8,72}... | collective-permute-start | bytes 3538952 | tf_op jit(solution)/shard_map/ppermute | solution.py:434
  93.8 13.1 %collective-permute-done.6.refs_2_ = bf16[384,1536]{1,0:T(8,128)(2,1)} collective-permute-done((bf16[384,1536]{1,0:T(8,128)(2,1)S(1)}, bf16[384,1536]{1,0:T(8,128)(2,1)}, u32[]{:S(2)}, u32[]{:S(2)}) %collective-permute-start.6) | collective-permute-done | bytes 1179680 | tf_op jit(solution)/shard_map/ppermute | solution.py:434
  106.9 5.1 %collective-permute-start.7 = (bf16[384,1536]{1,0:T(8,128)(2,1)}, bf16[384,1536]{1,0:T(8,128)(2,1)}, u32[]{:S(2)}, u32[]{:S(2)}) collective-permute-start(bf16[384,1536]{1,0:T(8,128)(2,1)} %collective-permute-done.6.refs_2_), channel_id=1, source_target_pairs={{0,64},{1,449},{2,66},{3,451},{4,68},{5,453},{6,70},{7,455},{8,72}... | collective-permute-start | bytes 3538952 | tf_op jit(solution)/shard_map/ppermute | solution.py:434
  112.1 1.9 collective-permute-start
  114.0 7.6 %attend_whole.1 = (bf16[16,128,128]{2,1,0:T(8,128)(2,1)S(1)}, f32[16,128]{1,0:T(8,128)S(1)}) custom-call(bf16[16,592,128]{2,1,0:T(8,128)(2,1)S(1)} %all-to-all-done.cut.q.k.v, bf16[16,592,128]{2,1,0:T(8,128)(2,1)S(1)} %all-to-all-done.cut.q.k.v, bf16[16,592,128]{2,1,0:T(8,128)(2,1)S(1)} %all-to-all-done.cut.q.k.v, ...), custom_call_target="tpu_custom_call" | custom-call | flops 134217728 | bytes 2097152 | tf_op jit(solution)/shard_map/attend_whole/pallas_call | solution.py:217
  121.7 5.2 %attend_shared.1 = bf16[16,224,128]{2,1,0:T(8,128)(2,1)} custom-call(s32[7]{0:T(128)S(1)} %copy-done, bf16[16,592,128]{2,1,0:T(8,128)(2,1)S(1)} %all-to-all-done.cut.q.k.v, bf16[16,592,128]{2,1,0:T(8,128)(2,1)S(1)} %all-to-all-done.cut.q.k.v, bf16[16,128,128]{2,1,0:T(8,128)(2,1)S(1)} %slice.4.own_kv, bf16[16,128,128]{2,1,0:T(8,128)(2,1)S(1)} %collective-permute-done.far_kv, ...), custom_call_target="tpu_custom_call" | custom-call | flops 67108864 | bytes 2097152 | tf_op jit(solution)/shard_map/attend_shared/pallas_call | solution.py:244
  126.9 9.4 %all-to-all-start.1 = ((bf16[16,224,128]{2,1,0:T(8,128)(2,1)}), bf16[16,224,128]{2,1,0:T(8,128)(2,1)S(1)}, u32[]{:S(2)}, u32[]{:S(2)}) async-start(bf16[16,224,128]{2,1,0:T(8,128)(2,1)} %attend_shared.1), calls=%async_computation.1 | async-start | bytes 1835008 | tf_op jit(solution)/shard_map/all_to_all | solution.py:478
  136.3 1.1 constant_dynamic-slice_fusion
  137.5 2.3 collective-permute-start.11
  139.8 1.9 collective-permute-start.8
  141.7 2.4 collective-permute-start.9
  144.1 1.9 collective-permute-start.10
  146.0 2.3 collective-permute-done.11.refs_7_
  148.4 4.1 collective-permute-start.12
  152.5 1.6 collective-permute-done.12.refs_8_
  154.1 1.0 copy-done.4
  155.3 1.0 copy-done.5
  156.3 287.7 %stage.1.weights = bf16[4,768,1536]{2,1,0:T(8,128)(2,1)} custom-call(s32[7]{0:T(128)} %concatenate.3.where, bf16[384,1536]{1,0:T(8,128)(2,1)} %bitcast.9, bf16[384,1536]{1,0:T(8,128)(2,1)} %copy-done.2, bf16[384,1536]{1,0:T(8,128)(2,1)} %collective-permute-done.6.refs_2_, bf16[384,1536]{1,0:T(8,128)(2,1)} %collective-permute-done.7.refs_3_, ...), custom_call_target="tpu_custom_call" | custom-call | tf_op jit(solution)/shard_map/stage/pallas_call | solution.py:346
  444.1 5.6 %project.1 = (bf16[112,1536]{1,0:T(8,128)(2,1)}, bf16[16,3072]{1,0:T(8,128)(2,1)}, f32[2,2048]{1,0:T(2,128)}) custom-call(s32[7]{0:T(128)S(1)} %copy-done.1, bf16[16,224,128]{2,1,0:T(8,128)(2,1)S(1)} %all-to-all-done.1.ret, bf16[4,768,1536]{2,1,0:T(8,128)(2,1)} %stage.1.weights), custom_call_target="tpu_custom_call" | custom-call | tf_op jit(solution)/shard_map/project/pallas_call | solution.py:398
  (39 shorter events, 0.7 us)
Async XLA Ops:
  3.6 12.0 %copy-start.8 = (bf16[96,1536]{1,0:T(8,128)(2,1)S(1)}, bf16[96,1536]{1,0:T(8,128)(2,1)}, u32[]{:S(2)}) copy-start(bf16[96,1536]{1,0:T(8,128)(2,1)} %mine.1) | copy-start | bytes 884740
  3.6 17.1 %copy-start.12 = (s32[24]{0:T(128)S(1)}, s32[24]{0:T(128)}, u32[]{:S(2)}) copy-start(s32[24]{0:T(128)} %param.10) | copy-start | bytes 292
  3.6 108.4 %all-to-all-start = ((bf16[16,592,128]{2,1,0:T(8,128)(2,1)}), bf16[16,592,128]{2,1,0:T(8,128)(2,1)S(1)}, u32[]{:S(2)}, u32[]{:S(2)}) async-start(bf16[16,592,128]{2,1,0:T(8,128)(2,1)} %pack.1), calls=%async_computation | async-start | bytes 4849664 | tf_op jit(solution)/shard_map/all_to_all | solution.py:468
  15.6 8.0 %collective-permute-start.1 = (bf16[96,1536]{1,0:T(8,128)(2,1)S(1)}, bf16[96,1536]{1,0:T(8,128)(2,1)S(1)}, u32[]{:S(2)}, u32[]{:S(2)}) collective-permute-start(bf16[96,1536]{1,0:T(8,128)(2,1)S(1)} %copy-done.8), channel_id=1, source_target_pairs={{0,16},{1,49},{2,18},{3,51},{4,20},{5,53},{6,22},{7,55},{8,24},{9,... | collective-permute-start | bytes 884744 | tf_op jit(solution)/shard_map/ppermute | solution.py:434
  20.0 7.4 %collective-permute-start.3 = (bf16[96,1536]{1,0:T(8,128)(2,1)S(1)}, bf16[96,1536]{1,0:T(8,128)(2,1)S(1)}, u32[]{:S(2)}, u32[]{:S(2)}) collective-permute-start(bf16[96,1536]{1,0:T(8,128)(2,1)S(1)} %copy-done.8), channel_id=1, source_target_pairs={{0,32},{2,34},{4,36},{6,38},{8,40},{10,42},{12,44},{14,46},{16,48}... | collective-permute-start | bytes 884744 | tf_op jit(solution)/shard_map/ppermute | solution.py:434
  23.7 8.4 %copy-start.9 = (bf16[96,1536]{1,0:T(8,128)(2,1)}, bf16[96,1536]{1,0:T(8,128)(2,1)S(1)}, u32[]{:S(2)}) copy-start(bf16[96,1536]{1,0:T(8,128)(2,1)S(1)} %collective-permute-done.1.near) | copy-start | bytes 884740
  23.7 6.0 %collective-permute-start.2 = (bf16[96,1536]{1,0:T(8,128)(2,1)S(1)}, bf16[96,1536]{1,0:T(8,128)(2,1)}, u32[]{:S(2)}, u32[]{:S(2)}) collective-permute-start(bf16[96,1536]{1,0:T(8,128)(2,1)S(1)} %collective-permute-done.1.near), channel_id=1, source_target_pairs={{0,1},{1,0},{2,3},{3,2},{4,5},{5,4},{6,7},{7,6},{8,9},{9,8},{10,11... | collective-permute-start | bytes 884744 | tf_op jit(solution)/shard_map/ppermute | solution.py:434
  27.5 4.6 %copy-start.10 = (bf16[96,1536]{1,0:T(8,128)(2,1)}, bf16[96,1536]{1,0:T(8,128)(2,1)S(1)}, u32[]{:S(2)}) copy-start(bf16[96,1536]{1,0:T(8,128)(2,1)S(1)} %collective-permute-done.3.part) | copy-start | bytes 884740
  27.5 4.6 %collective-permute-start.4 = (bf16[96,1536]{1,0:T(8,128)(2,1)S(1)}, bf16[96,1536]{1,0:T(8,128)(2,1)S(1)}, u32[]{:S(2)}, u32[]{:S(2)}) collective-permute-start(bf16[96,1536]{1,0:T(8,128)(2,1)S(1)} %collective-permute-done.3.part), channel_id=1, source_target_pairs={{0,1},{2,3},{4,5},{6,7},{8,9},{10,11},{12,13},{14,15},{16,17},{18,... | collective-permute-start | bytes 884744 | tf_op jit(solution)/shard_map/ppermute | solution.py:434
  32.0 0.7 copy-start.11
  70.3 18.5 %collective-permute-start.5 = (bf16[384,1536]{1,0:T(8,128)(2,1)}, bf16[384,1536]{1,0:T(8,128)(2,1)S(1)}, u32[]{:S(2)}, u32[]{:S(2)}) collective-permute-start(bf16[384,1536]{1,0:T(8,128)(2,1)} %bitcast.8), channel_id=1, source_target_pairs={{0,64},{1,449},{2,66},{3,451},{4,68},{5,453},{6,70},{7,455},{8,72}... | collective-permute-start | bytes 3538952 | tf_op jit(solution)/shard_map/ppermute | solution.py:434
  88.8 18.0 %copy-start.2 = (bf16[384,1536]{1,0:T(8,128)(2,1)}, bf16[384,1536]{1,0:T(8,128)(2,1)S(1)}, u32[]{:S(2)}) copy-start(bf16[384,1536]{1,0:T(8,128)(2,1)S(1)} %collective-permute-done.5.refs_1_) | copy-start | bytes 3538948
  88.9 18.0 %collective-permute-start.6 = (bf16[384,1536]{1,0:T(8,128)(2,1)S(1)}, bf16[384,1536]{1,0:T(8,128)(2,1)}, u32[]{:S(2)}, u32[]{:S(2)}) collective-permute-start(bf16[384,1536]{1,0:T(8,128)(2,1)S(1)} %collective-permute-done.5.refs_1_), channel_id=1, source_target_pairs={{0,64},{1,449},{2,66},{3,451},{4,68},{5,453},{6,70},{7,455},{8,72}... | collective-permute-start | bytes 3538952 | tf_op jit(solution)/shard_map/ppermute | solution.py:434
  106.9 20.0 %collective-permute-start.7 = (bf16[384,1536]{1,0:T(8,128)(2,1)}, bf16[384,1536]{1,0:T(8,128)(2,1)}, u32[]{:S(2)}, u32[]{:S(2)}) collective-permute-start(bf16[384,1536]{1,0:T(8,128)(2,1)} %collective-permute-done.6.refs_2_), channel_id=1, source_target_pairs={{0,64},{1,449},{2,66},{3,451},{4,68},{5,453},{6,70},{7,455},{8,72}... | collective-permute-start | bytes 3538952 | tf_op jit(solution)/shard_map/ppermute | solution.py:434
  112.1 9.6 %copy-start = (s32[7]{0:T(128)S(1)}, s32[7]{0:T(128)}, u32[]{:S(2)}) copy-start(s32[7]{0:T(128)} %concatenate.3.where) | copy-start | bytes 88
  112.1 9.6 %collective-permute-start = (bf16[16,128,128]{2,1,0:T(8,128)(2,1)S(1)}, bf16[16,128,128]{2,1,0:T(8,128)(2,1)S(1)}, u32[]{:S(2)}, u32[]{:S(2)}) collective-permute-start(bf16[16,128,128]{2,1,0:T(8,128)(2,1)S(1)} %slice.4.own_kv), channel_id=1, source_target_pairs={{0,1},{1,0},{2,3},{3,2},{4,5},{5,4},{6,7},{7,6},{8,9},{9,8},{10,11... | collective-permute-start | bytes 1572872 | tf_op jit(solution)/shard_map/ppermute | solution.py:434
  126.9 12.8 %copy-start.3 = (bf16[384,1536]{1,0:T(8,128)(2,1)S(1)}, bf16[384,1536]{1,0:T(8,128)(2,1)}, u32[]{:S(2)}) copy-start(bf16[384,1536]{1,0:T(8,128)(2,1)} %copy-done.2) | copy-start | bytes 3538948
  126.9 317.1 %all-to-all-start.1 = ((bf16[16,224,128]{2,1,0:T(8,128)(2,1)}), bf16[16,224,128]{2,1,0:T(8,128)(2,1)S(1)}, u32[]{:S(2)}, u32[]{:S(2)}) async-start(bf16[16,224,128]{2,1,0:T(8,128)(2,1)} %attend_shared.1), calls=%async_computation.1 | async-start | bytes 1835008 | tf_op jit(solution)/shard_map/all_to_all | solution.py:478
  137.4 306.6 %copy-start.1 = (s32[7]{0:T(128)S(1)}, s32[7]{0:T(128)}, u32[]{:S(2)}) copy-start(s32[7]{0:T(128)} %concatenate.3.where) | copy-start | bytes 88
  137.5 10.9 %collective-permute-start.11 = (bf16[384,768]{1,0:T(8,128)(2,1)S(1)}, bf16[384,768]{1,0:T(8,128)(2,1)S(1)}, u32[]{:S(2)}, u32[]{:S(2)}) collective-permute-start(bf16[384,768]{1,0:T(8,128)(2,1)S(1)} %constant_dynamic-slice_fusion), channel_id=1, source_target_pairs={{0,64},{1,449},{2,66},{3,451},{4,68},{5,453},{6,70},{7,455},{8,72}... | collective-permute-start | bytes 1769480 | tf_op jit(solution)/shard_map/ppermute | solution.py:434
  139.8 14.3 %collective-permute-start.8 = (bf16[384,1536]{1,0:T(8,128)(2,1)S(1)}, bf16[384,1536]{1,0:T(8,128)(2,1)S(1)}, u32[]{:S(2)}, u32[]{:S(2)}) collective-permute-start(bf16[384,1536]{1,0:T(8,128)(2,1)S(1)} %copy-done.3), channel_id=1, source_target_pairs={{0,1},{1,0},{2,3},{3,2},{4,5},{5,4},{6,7},{7,6},{8,9},{9,8},{10,11... | collective-permute-start | bytes 3538952 | tf_op jit(solution)/shard_map/ppermute | solution.py:434
  141.7 13.4 %collective-permute-start.9 = (bf16[384,1536]{1,0:T(8,128)(2,1)}, bf16[384,1536]{1,0:T(8,128)(2,1)S(1)}, u32[]{:S(2)}, u32[]{:S(2)}) collective-permute-start(bf16[384,1536]{1,0:T(8,128)(2,1)} %collective-permute-done.6.refs_2_), channel_id=1, source_target_pairs={{0,1},{1,0},{2,3},{3,2},{4,5},{5,4},{6,7},{7,6},{8,9},{9,8},{10,11... | collective-permute-start | bytes 3538952 | tf_op jit(solution)/shard_map/ppermute | solution.py:434
  144.1 12.2 %collective-permute-start.10 = (bf16[384,1536]{1,0:T(8,128)(2,1)}, bf16[384,1536]{1,0:T(8,128)(2,1)}, u32[]{:S(2)}, u32[]{:S(2)}) collective-permute-start(bf16[384,1536]{1,0:T(8,128)(2,1)} %collective-permute-done.7.refs_3_), channel_id=1, source_target_pairs={{0,1},{1,0},{2,3},{3,2},{4,5},{5,4},{6,7},{7,6},{8,9},{9,8},{10,11... | collective-permute-start | bytes 3538952 | tf_op jit(solution)/shard_map/ppermute | solution.py:434
  148.4 7.9 %copy-start.6 = (bf16[384,768]{1,0:T(8,128)(2,1)}, bf16[384,768]{1,0:T(8,128)(2,1)S(1)}, u32[]{:S(2)}) copy-start(bf16[384,768]{1,0:T(8,128)(2,1)S(1)} %collective-permute-done.11.refs_7_) | copy-start | bytes 1769476
  148.4 5.7 %collective-permute-start.12 = (bf16[384,768]{1,0:T(8,128)(2,1)S(1)}, bf16[384,768]{1,0:T(8,128)(2,1)S(1)}, u32[]{:S(2)}, u32[]{:S(2)}) collective-permute-start(bf16[384,768]{1,0:T(8,128)(2,1)S(1)} %collective-permute-done.11.refs_7_), channel_id=1, source_target_pairs={{0,1},{1,0},{2,3},{3,2},{4,5},{5,4},{6,7},{7,6},{8,9},{9,8},{10,11... | collective-permute-start | bytes 1769480 | tf_op jit(solution)/shard_map/ppermute | solution.py:434
  154.1 1.2 copy-start.7
  154.1 1.0 copy-start.4
  155.3 1.0 copy-start.5

commit v4 on v2

--- a/solution.py
+++ b/solution.py
@@ -189,7 +189,9 @@
 
 Q_ROWS = 512
 STEP_ROWS = 1024
-VMEM = 40 * 2**20
+VMEM = 32 * 2**20
+PLACE_VMEM = 8 * 2**20
+PROJECT_VMEM = 50 * 2**20
 
 
 def attention_scratch():
@@ -203,9 +205,9 @@
 
 def attention_cost(queries, keys):
     return pl.CostEstimate(
-        flops=queries * keys * HEAD_DIM * 8,
+        flops=queries * keys * HEAD_DIM // 4,
         bytes_accessed=4 * keys * HEAD_DIM * 2,
-        transcendentals=queries * keys,
+        transcendentals=0,
     )
 
 
@@ -269,11 +271,14 @@
     out[x] = mine[...]
     out[(x - sign + 4) % 4] = near[...]
     out[(x + sign + 4) % 4] = near_far[...]
-    columns = part.shape[1]
-    low, high = pl.multiple_of(core * columns, columns), pl.multiple_of((1 - core) * columns, columns)
-    opposite = (x + 2) % 4
-    out[opposite, :, pl.ds(low, columns)] = part[...]
-    out[opposite, :, pl.ds(high, columns)] = part_far[...]
+
+    @pl.when(core == 0)
+    def _():
+        out[(x + 2) % 4] = part[...]
+
+    @pl.when(core == 1)
+    def _():
+        out[(x + 2) % 4] = part_far[...]
 
 
 def place(where, mine, near, near_far, part, part_far):
@@ -287,6 +292,7 @@
             out_specs=pl.BlockSpec(memory_space=pltpu.VMEM),
         ),
         out_shape=jax.ShapeDtypeStruct((4, rows, columns), jnp.bfloat16),
+        compiler_params=pltpu.CompilerParams(vmem_limit_bytes=PLACE_VMEM),
         name="place",
     )(where, mine, near, near_far, part, part_far)
 
@@ -317,15 +323,13 @@
     columns = held.shape[2] // 2
     copies = []
     for index in range(7):
-        copies.append(pltpu.make_async_copy(weights[index], held.at[index], sems.at[index]))
+        to = held.at[index // 2, pl.ds(index % 2 * TRIO, TRIO)]
+        copies.append(pltpu.make_async_copy(weights[index], to, sems.at[index]))
     for index in range(2):
         at = core if index == 0 else 1 - core
         start = pl.multiple_of(at * columns, columns)
-        copies.append(
-            pltpu.make_async_copy(
-                weights[7 + index], held.at[7, :, pl.ds(start, columns)], sems.at[7 + index]
-            )
-        )
+        to = held.at[3, pl.ds(TRIO, TRIO), pl.ds(start, columns)]
+        copies.append(pltpu.make_async_copy(weights[7 + index], to, sems.at[7 + index]))
     for copy in copies:
         copy.start()
     for slot in range(SLOTS):
@@ -337,16 +341,20 @@
             at = VIS_SEQ + source * TXT_ROWS
             slots[slot : slot + 1, at : at + TXT_ROWS] = row[:, VIS_ROWS:]
     total = jnp.zeros((ROWS, 2 * columns), jnp.float32)
+    pieces = []
     for index, hops in enumerate((0, 1, 2, 3, -1, -2, -3, 4)):
         chip = (y - hops * sign + 8) % 8
         low, high = ret[2 * chip], ret[2 * chip + 1]
         shared = jnp.concatenate([low[ROWS:RET_ROWS], high[ROWS:RET_ROWS]], axis=0)
         attention = jnp.concatenate([low[:ROWS], shared, high[:ROWS]], axis=1)
         txt_out[:, pl.ds(pl.multiple_of(chip * TRIO, TRIO), TRIO)] = attention[VIS_ROWS:]
+        pieces.append(attention)
         copies[index].wait()
-        if index == 7:
-            copies[8].wait()
-        total += jnp.dot(attention, held[index], preferred_element_type=jnp.float32)
+        if index % 2 == 1:
+            if index == 7:
+                copies[8].wait()
+            both = jnp.concatenate(pieces[-2:], axis=1)
+            total += jnp.dot(both, held[index // 2], preferred_element_type=jnp.float32)
     vis_out[...] = total[:VIS_ROWS].astype(jnp.bfloat16)
 
 
@@ -357,10 +365,10 @@
         grid_spec=pltpu.PrefetchScalarGridSpec(
             num_scalar_prefetch=1,
             grid=(),
-            in_specs=[pl.BlockSpec(memory_space=pltpu.VMEM)] + [pl.BlockSpec(memory_space=pl.ANY)] * 9,
+            in_specs=[pl.BlockSpec(memory_space=pltpu.VMEM)] + [pl.BlockSpec(memory_space=pltpu.HBM)] * 9,
             out_specs=[pl.BlockSpec(memory_space=pltpu.VMEM)] * 3,
             scratch_shapes=[
-                pltpu.VMEM((8, TRIO, columns), jnp.bfloat16),
+                pltpu.VMEM((4, 2 * TRIO, columns), jnp.bfloat16),
                 pltpu.SemaphoreType.DMA((9,)),
             ],
         ),
@@ -369,7 +377,7 @@
             jax.ShapeDtypeStruct((TXT_ROWS, HEADS * HEAD_DIM), jnp.bfloat16),
             jax.ShapeDtypeStruct((SLOTS, VIS_SEQ + TXT_SEQ), jnp.float32),
         ],
-        compiler_params=pltpu.CompilerParams(vmem_limit_bytes=VMEM),
+        compiler_params=pltpu.CompilerParams(vmem_limit_bytes=PROJECT_VMEM),
         name="project",
     )(where, returned, *chunks[:4], *far_chunks[:3], chunks[4], far_chunks[3])
 
@@ -379,23 +387,24 @@
 Y_SIZE = 8
 
 
-def permute(operand, target):
+def permute(operand, target, cores=(0, 1)):
     pairs = []
     for y in range(Y_SIZE):
         for x in range(X_SIZE):
             for s in range(N_SEQ):
                 ty, tx, ts = target(y, x, s)
                 there = (ty % Y_SIZE) * X_SIZE + tx % X_SIZE
-                pairs.append(((y * X_SIZE + x) * N_SEQ + s, there * N_SEQ + ts))
+                if s % 2 in cores:
+                    pairs.append(((y * X_SIZE + x) * N_SEQ + s, there * N_SEQ + ts))
     return lax.ppermute(operand, AXES, pairs)
 
 
-def swap(operand):
-    return permute(operand, lambda y, x, s: (y, x, s ^ 1))
-
-
-def shift_x(operand, hops):
-    return permute(operand, lambda y, x, s: (y, x + hops * (1 - 2 * (s % 2)), s))
+def swap(operand, cores=(0, 1)):
+    return permute(operand, lambda y, x, s: (y, x, s ^ 1), cores)
+
+
+def shift_x(operand, hops, cores=(0, 1)):
+    return permute(operand, lambda y, x, s: (y, x + hops * (1 - 2 * (s % 2)), s), cores)
 
 
 def shift_y(operand):
@@ -419,14 +428,12 @@
     where = jnp.concatenate([place_here, heads_of_slots(head_map, seq_index)])
 
     near = shift_x(w_out, 1)
-    part = shift_x(lax.dynamic_slice_in_dim(w_out, core * half, half, 1), 2)
+    part = shift_x(w_out, 2, cores=(0,))
     sending = pack(qkv_vis, qkv_txt, vis_segments, txt_segments)
-    sending, near, part = lax.optimization_barrier((sending, near, part))
     received = lax.all_to_all(sending, "seq", split_axis=0, concat_axis=0, tiled=True)
-    chunks = [place(where, w_out, near, swap(near), part, swap(part)).reshape(-1, 2 * half)]
+    chunks = [place(where, w_out, near, swap(near), part, swap(part, cores=(0,))).reshape(-1, 2 * half)]
     chunks.append(shift_y(chunks[0]))
     chunks.append(shift_y(chunks[1]))
-    received, chunks[2] = lax.optimization_barrier((received, chunks[2]))
     chunks.append(shift_y(chunks[2]))
     own_kv = received[:, A_ROWS + HALF : SEND_ROWS]
     far_kv = swap(own_kv)

time: 146 us -> 131 us (0.90)
  local copies, waits for them, and re-layouts: 16 us -> 4.46 us
  waiting for transfers between devices: 43.1 us -> 40.4 us
    unnamed x40 -> x14, local copies, waits for them, and re-layouts: 13.1 us -> 3.15 us
    all_to_all x1, waiting for transfers between devices: 8.79 us -> 0.01 us  [on_device(): lax.all_to_all(sending, 'seq', split_axis=0, concat_axis=0, tiled=True)]
    ppermute x13, waiting for transfers between devices: 30.7 us -> 35 us  [permute(): return lax.ppermute(operand, AXES, pairs)]
    all_to_all x1, starting transfers between devices: 5.63 us -> 8.91 us  [on_device(): lax.all_to_all(returning, 'seq', split_axis=0, concat_axis=0, tiled=True)]
    ppermute x13, starting transfers between devices: 43 us -> 40.4 us  [permute(): return lax.ppermute(operand, AXES, pairs)]
    all_to_all x1, waiting for transfers between devices: 3.54 us -> 5.46 us  [on_device(): lax.all_to_all(returning, 'seq', split_axis=0, concat_axis=0, tiled=True)]
  transfers between devices with their start and end apart: 15 -> 15, of which waited for: 8 -> 7; matrix products, arithmetic and copies ran while one was open for 2% -> 1% of each run, Pallas kernels for 12% -> 11%
where the time goes in v4:
time: 131 us; the launch traced here: 130 us
  starting transfers between devices  61.3 us (47%)
  waiting for transfers between devices  40.4 us (31%)
  Pallas kernels  22.9 us (17%)
  local copies, waits for them, and re-layouts  4.46 us (3%)
    ppermute x13, starting transfers between devices, permute(): return lax.ppermute(operand, AXES, pairs)  40.4 us
    ppermute x13, waiting for transfers between devices, permute(): return lax.ppermute(operand, AXES, pairs)  35 us
    all_to_all x1, starting transfers between devices, on_device(): lax.all_to_all(sending, 'seq', split_axis=0, concat_axis=0, tiled=True)  12 us
    all_to_all x1, starting transfers between devices, on_device(): lax.all_to_all(returning, 'seq', split_axis=0, concat_axis=0, tiled=True)  8.91 us
    pallas_call x1, Pallas kernels, attend_whole(): pl.pallas_call(whole_kernel, grid=(steps,), in_specs=[pl.BlockSpec((N_SEQ...  7.64 us
    all_to_all x1, waiting for transfers between devices, on_device(): lax.all_to_all(returning, 'seq', split_axis=0, concat_axis=0, tiled=True)  5.46 us
    pallas_call x1, Pallas kernels, project(): pl.pallas_call(project_kernel, grid_spec=pltpu.PrefetchScalarGridSpec(num...  5.33 us
    pallas_call x1, Pallas kernels, attend_shared(): pl.pallas_call(shared_kernel, grid_spec=pltpu.PrefetchScalarGridSpec(num_...  5.27 us
  transfers between devices with their start and end apart: 15, of which 7 were waited for; matrix products, arithmetic and copies ran while one was open for 1% of the time, Pallas kernels for 11%

profile of v4, /device:TPU:1, one launch (start us, length us, event | category | flops | bytes accessed | tf_op | source)
XLA Modules:
  0.0 130.3 jit_solution(3616648538700810756)
XLA Ops:
  0.6 2.9 %pack.1 = bf16[16,592,128]{2,1,0:T(8,128)(2,1)} custom-call(s32[1,112]{1,0:T(1,128)} %bitcast.10, s32[1,16]{1,0:T(1,128)} %bitcast.11, bf16[112,9216]{1,0:T(8,128)(2,1)} %vv.1, bf16[112,9216]{1,0:T(8,128)(2,1)} %vv.1, bf16[112,9216]{1,0:T(8,128)(2,1)} %vv.1, bf16[16,9216]{1,0:T(8,128)(2,1)} %tv.1, bf16[16,9216]{1,0:T(8,128)(2,1)} %tv.1, bf16[16,9216]{1,0:T(8,128)(2,1)} %tv.1), custom_call_target="tpu_custom_call" | custom-call | tf_op jit(solution)/shard_map/pack/pallas_call | solution.py:66
  3.6 12.0 %all-to-all-start = ((bf16[16,592,128]{2,1,0:T(8,128)(2,1)}), bf16[16,592,128]{2,1,0:T(8,128)(2,1)S(1)}, u32[]{:S(2)}, u32[]{:S(2)}) async-start(bf16[16,592,128]{2,1,0:T(8,128)(2,1)} %pack.1), calls=%async_computation | async-start | bytes 4849664 | tf_op jit(solution)/shard_map/all_to_all | solution.py:433
  15.6 4.4 %collective-permute-start.1 = (bf16[96,1536]{1,0:T(8,128)(2,1)S(1)}, bf16[96,1536]{1,0:T(8,128)(2,1)S(1)}, u32[]{:S(2)}, u32[]{:S(2)}) collective-permute-start(bf16[96,1536]{1,0:T(8,128)(2,1)S(1)} %copy-done.2), channel_id=1, source_target_pairs={{0,16},{1,49},{2,18},{3,51},{4,20},{5,53},{6,22},{7,55},{8,24},{9,... | collective-permute-start | bytes 884744 | tf_op jit(solution)/shard_map/ppermute | solution.py:399
  20.0 0.7 collective-permute-start.3
  20.9 2.7 %collective-permute-done.1.near = bf16[96,1536]{1,0:T(8,128)(2,1)S(1)} collective-permute-done((bf16[96,1536]{1,0:T(8,128)(2,1)S(1)}, bf16[96,1536]{1,0:T(8,128)(2,1)S(1)}, u32[]{:S(2)}, u32[]{:S(2)}) %collective-permute-start.1) | collective-permute-done | bytes 294944 | tf_op jit(solution)/shard_map/ppermute | solution.py:399
  23.6 3.8 %collective-permute-start.2 = (bf16[96,1536]{1,0:T(8,128)(2,1)S(1)}, bf16[96,1536]{1,0:T(8,128)(2,1)}, u32[]{:S(2)}, u32[]{:S(2)}) collective-permute-start(bf16[96,1536]{1,0:T(8,128)(2,1)S(1)} %collective-permute-done.1.near), channel_id=1, source_target_pairs={{0,1},{1,0},{2,3},{3,2},{4,5},{5,4},{6,7},{7,6},{8,9},{9,8},{10,11... | collective-permute-start | bytes 884744 | tf_op jit(solution)/shard_map/ppermute | solution.py:399
  27.4 1.3 collective-permute-start.4
  28.7 0.1 fusion
  29.0 3.2 %collective-permute-done.4.part_far = bf16[96,1536]{1,0:T(8,128)(2,1)} collective-permute-done((bf16[96,1536]{1,0:T(8,128)(2,1)S(1)}, bf16[96,1536]{1,0:T(8,128)(2,1)}, u32[]{:S(2)}, u32[]{:S(2)}) %collective-permute-start.4) | collective-permute-done | bytes 294944 | tf_op jit(solution)/shard_map/ppermute | solution.py:399
  32.1 1.7 %place.1 = bf16[4,96,1536]{2,1,0:T(8,128)(2,1)S(1)} custom-call(s32[7]{0:T(128)S(1)} %concatenate.3.where, bf16[96,1536]{1,0:T(8,128)(2,1)S(1)} %copy-done.2, bf16[96,1536]{1,0:T(8,128)(2,1)S(1)} %collective-permute-done.1.near, bf16[96,1536]{1,0:T(8,128)(2,1)} %collective-permute-done.2.near_far, bf16[96,1536]{1,0:T(8,128)(2,1)S(1)} %collective-permute-done.3.part, ...), custom_call_target="tpu_custom_call" | custom-call | tf_op jit(solution)/shard_map/place/pallas_call | solution.py:286
  33.8 5.1 %collective-permute-start.5 = (bf16[384,1536]{1,0:T(8,128)(2,1)S(1)}, bf16[384,1536]{1,0:T(8,128)(2,1)S(1)}, u32[]{:S(2)}, u32[]{:S(2)}) collective-permute-start(bf16[384,1536]{1,0:T(8,128)(2,1)S(1)} %bitcast.8), channel_id=1, source_target_pairs={{0,64},{1,449},{2,66},{3,451},{4,68},{5,453},{6,70},{7,455},{8,72}... | collective-permute-start | bytes 3538952 | tf_op jit(solution)/shard_map/ppermute | solution.py:399
  38.9 1.0 copy-done
  39.9 12.1 %collective-permute-done.5.refs_1_ = bf16[384,1536]{1,0:T(8,128)(2,1)S(1)} collective-permute-done((bf16[384,1536]{1,0:T(8,128)(2,1)S(1)}, bf16[384,1536]{1,0:T(8,128)(2,1)S(1)}, u32[]{:S(2)}, u32[]{:S(2)}) %collective-permute-start.5) | collective-permute-done | bytes 1179680 | tf_op jit(solution)/shard_map/ppermute | solution.py:399
  52.0 5.3 %collective-permute-start.6 = (bf16[384,1536]{1,0:T(8,128)(2,1)S(1)}, bf16[384,1536]{1,0:T(8,128)(2,1)}, u32[]{:S(2)}, u32[]{:S(2)}) collective-permute-start(bf16[384,1536]{1,0:T(8,128)(2,1)S(1)} %collective-permute-done.5.refs_1_), channel_id=1, source_target_pairs={{0,64},{1,449},{2,66},{3,451},{4,68},{5,453},{6,70},{7,455},{8,72}... | collective-permute-start | bytes 3538952 | tf_op jit(solution)/shard_map/ppermute | solution.py:399
  57.3 13.1 %collective-permute-done.6.refs_2_ = bf16[384,1536]{1,0:T(8,128)(2,1)} collective-permute-done((bf16[384,1536]{1,0:T(8,128)(2,1)S(1)}, bf16[384,1536]{1,0:T(8,128)(2,1)}, u32[]{:S(2)}, u32[]{:S(2)}) %collective-permute-start.6) | collective-permute-done | bytes 1179680 | tf_op jit(solution)/shard_map/ppermute | solution.py:399
  70.5 5.3 %collective-permute-start.7 = (bf16[384,1536]{1,0:T(8,128)(2,1)}, bf16[384,1536]{1,0:T(8,128)(2,1)}, u32[]{:S(2)}, u32[]{:S(2)}) collective-permute-start(bf16[384,1536]{1,0:T(8,128)(2,1)} %collective-permute-done.6.refs_2_), channel_id=1, source_target_pairs={{0,64},{1,449},{2,66},{3,451},{4,68},{5,453},{6,70},{7,455},{8,72}... | collective-permute-start | bytes 3538952 | tf_op jit(solution)/shard_map/ppermute | solution.py:399
  75.9 1.9 %collective-permute-start = (bf16[16,128,128]{2,1,0:T(8,128)(2,1)S(1)}, bf16[16,128,128]{2,1,0:T(8,128)(2,1)S(1)}, u32[]{:S(2)}, u32[]{:S(2)}) collective-permute-start(bf16[16,128,128]{2,1,0:T(8,128)(2,1)S(1)} %slice.4.own_kv), channel_id=1, source_target_pairs={{0,1},{1,0},{2,3},{3,2},{4,5},{5,4},{6,7},{7,6},{8,9},{9,8},{10,11... | collective-permute-start | bytes 1572872 | tf_op jit(solution)/shard_map/ppermute | solution.py:399
  77.8 7.6 %attend_whole.1 = (bf16[16,128,128]{2,1,0:T(8,128)(2,1)S(1)}, f32[16,128]{1,0:T(8,128)S(1)}) custom-call(bf16[16,592,128]{2,1,0:T(8,128)(2,1)S(1)} %all-to-all-done.cut.q.k.v, bf16[16,592,128]{2,1,0:T(8,128)(2,1)S(1)} %all-to-all-done.cut.q.k.v, bf16[16,592,128]{2,1,0:T(8,128)(2,1)S(1)} %all-to-all-done.cut.q.k.v, ...), custom_call_target="tpu_custom_call" | custom-call | flops 134217728 | bytes 2097152 | tf_op jit(solution)/shard_map/attend_whole/pallas_call | solution.py:218
  85.4 5.3 %attend_shared.1 = bf16[16,224,128]{2,1,0:T(8,128)(2,1)} custom-call(s32[7]{0:T(128)S(1)} %concatenate.3.where, bf16[16,592,128]{2,1,0:T(8,128)(2,1)S(1)} %all-to-all-done.cut.q.k.v, bf16[16,592,128]{2,1,0:T(8,128)(2,1)S(1)} %all-to-all-done.cut.q.k.v, bf16[16,128,128]{2,1,0:T(8,128)(2,1)S(1)} %slice.4.own_kv, ...), custom_call_target="tpu_custom_call" | custom-call | flops 67108864 | bytes 2097152 | tf_op jit(solution)/shard_map/attend_shared/pallas_call | solution.py:245
  90.7 8.9 %all-to-all-start.1 = ((bf16[16,224,128]{2,1,0:T(8,128)(2,1)}), bf16[16,224,128]{2,1,0:T(8,128)(2,1)S(1)}, u32[]{:S(2)}, u32[]{:S(2)}) async-start(bf16[16,224,128]{2,1,0:T(8,128)(2,1)} %attend_shared.1), calls=%async_computation.1 | async-start | bytes 1835008 | tf_op jit(solution)/shard_map/all_to_all | solution.py:443
  99.6 1.1 constant_dynamic-slice_fusion
  100.7 2.3 %collective-permute-start.11 = (bf16[384,768]{1,0:T(8,128)(2,1)S(1)}, bf16[384,768]{1,0:T(8,128)(2,1)S(1)}, u32[]{:S(2)}, u32[]{:S(2)}) collective-permute-start(bf16[384,768]{1,0:T(8,128)(2,1)S(1)} %constant_dynamic-slice_fusion), channel_id=1, source_target_pairs={{0,64},{1,449},{2,66},{3,451},{4,68},{5,453},{6,70},{7,455},{8,72}... | collective-permute-start | bytes 1769480 | tf_op jit(solution)/shard_map/ppermute | solution.py:399
  103.1 1.9 %collective-permute-start.8 = (bf16[384,1536]{1,0:T(8,128)(2,1)}, bf16[384,1536]{1,0:T(8,128)(2,1)S(1)}, u32[]{:S(2)}, u32[]{:S(2)}) collective-permute-start(bf16[384,1536]{1,0:T(8,128)(2,1)} %copy-done.3), channel_id=1, source_target_pairs={{0,1},{1,0},{2,3},{3,2},{4,5},{5,4},{6,7},{7,6},{8,9},{9,8},{10,11... | collective-permute-start | bytes 3538952 | tf_op jit(solution)/shard_map/ppermute | solution.py:399
  105.0 2.4 %collective-permute-start.9 = (bf16[384,1536]{1,0:T(8,128)(2,1)}, bf16[384,1536]{1,0:T(8,128)(2,1)S(1)}, u32[]{:S(2)}, u32[]{:S(2)}) collective-permute-start(bf16[384,1536]{1,0:T(8,128)(2,1)} %collective-permute-done.6.refs_2_), channel_id=1, source_target_pairs={{0,1},{1,0},{2,3},{3,2},{4,5},{5,4},{6,7},{7,6},{8,9},{9,8},{10,11... | collective-permute-start | bytes 3538952 | tf_op jit(solution)/shard_map/ppermute | solution.py:399
  107.4 1.9 %collective-permute-start.10 = (bf16[384,1536]{1,0:T(8,128)(2,1)}, bf16[384,1536]{1,0:T(8,128)(2,1)}, u32[]{:S(2)}, u32[]{:S(2)}) collective-permute-start(bf16[384,1536]{1,0:T(8,128)(2,1)} %collective-permute-done.7.refs_3_), channel_id=1, source_target_pairs={{0,1},{1,0},{2,3},{3,2},{4,5},{5,4},{6,7},{7,6},{8,9},{9,8},{10,11... | collective-permute-start | bytes 3538952 | tf_op jit(solution)/shard_map/ppermute | solution.py:399
  109.3 2.3 %collective-permute-done.11.refs_7_ = bf16[384,768]{1,0:T(8,128)(2,1)S(1)} collective-permute-done((bf16[384,768]{1,0:T(8,128)(2,1)S(1)}, bf16[384,768]{1,0:T(8,128)(2,1)S(1)}, u32[]{:S(2)}, u32[]{:S(2)}) %collective-permute-start.11) | collective-permute-done | bytes 589856 | tf_op jit(solution)/shard_map/ppermute | solution.py:399
  111.7 4.1 %collective-permute-start.12 = (bf16[384,768]{1,0:T(8,128)(2,1)S(1)}, bf16[384,768]{1,0:T(8,128)(2,1)S(1)}, u32[]{:S(2)}, u32[]{:S(2)}) collective-permute-start(bf16[384,768]{1,0:T(8,128)(2,1)S(1)} %collective-permute-done.11.refs_7_), channel_id=1, source_target_pairs={{0,1},{1,0},{2,3},{3,2},{4,5},{5,4},{6,7},{7,6},{8,9},{9,8},{10,11... | collective-permute-start | bytes 1769480 | tf_op jit(solution)/shard_map/ppermute | solution.py:399
  115.7 1.6 %collective-permute-done.12.refs_8_ = bf16[384,768]{1,0:T(8,128)(2,1)S(1)} collective-permute-done((bf16[384,768]{1,0:T(8,128)(2,1)S(1)}, bf16[384,768]{1,0:T(8,128)(2,1)S(1)}, u32[]{:S(2)}, u32[]{:S(2)}) %collective-permute-start.12) | collective-permute-done | bytes 589856 | tf_op jit(solution)/shard_map/ppermute | solution.py:399
  117.4 1.0 copy-done.4
  118.4 1.1 copy-done.5
  119.5 5.5 %all-to-all-done.1.ret = bf16[16,224,128]{2,1,0:T(8,128)(2,1)S(1)} async-done(((bf16[16,224,128]{2,1,0:T(8,128)(2,1)}), bf16[16,224,128]{2,1,0:T(8,128)(2,1)S(1)}, u32[]{:S(2)}, u32[]{:S(2)}) %all-to-all-start.1) | async-done | bytes 917536 | tf_op jit(solution)/shard_map/all_to_all | solution.py:443
  124.9 5.3 %project.1 = (bf16[112,1536]{1,0:T(8,128)(2,1)}, bf16[16,3072]{1,0:T(8,128)(2,1)}, f32[2,2048]{1,0:T(2,128)}) custom-call(s32[7]{0:T(128)S(1)} %concatenate.3.where, bf16[16,224,128]{2,1,0:T(8,128)(2,1)S(1)} %all-to-all-done.1.ret, bf16[384,1536]{1,0:T(8,128)(2,1)S(1)} %bitcast.9, bf16[384,1536]{1,0:T(8,128)(2,1)} %copy-done.3, ...), custom_call_target="tpu_custom_call" | custom-call | tf_op jit(solution)/shard_map/project/pallas_call | solution.py:363
  (26 shorter events, 0.4 us)
Async XLA Ops:
  3.6 12.0 %copy-start.2 = (bf16[96,1536]{1,0:T(8,128)(2,1)S(1)}, bf16[96,1536]{1,0:T(8,128)(2,1)}, u32[]{:S(2)}) copy-start(bf16[96,1536]{1,0:T(8,128)(2,1)} %mine.1) | copy-start | bytes 884740
  3.6 17.1 %copy-start.6 = (s32[24]{0:T(128)S(1)}, s32[24]{0:T(128)}, u32[]{:S(2)}) copy-start(s32[24]{0:T(128)} %param.10) | copy-start | bytes 292
  3.6 72.2 %all-to-all-start = ((bf16[16,592,128]{2,1,0:T(8,128)(2,1)}), bf16[16,592,128]{2,1,0:T(8,128)(2,1)S(1)}, u32[]{:S(2)}, u32[]{:S(2)}) async-start(bf16[16,592,128]{2,1,0:T(8,128)(2,1)} %pack.1), calls=%async_computation | async-start | bytes 4849664 | tf_op jit(solution)/shard_map/all_to_all | solution.py:433
  15.6 8.0 %collective-permute-start.1 = (bf16[96,1536]{1,0:T(8,128)(2,1)S(1)}, bf16[96,1536]{1,0:T(8,128)(2,1)S(1)}, u32[]{:S(2)}, u32[]{:S(2)}) collective-permute-start(bf16[96,1536]{1,0:T(8,128)(2,1)S(1)} %copy-done.2), channel_id=1, source_target_pairs={{0,16},{1,49},{2,18},{3,51},{4,20},{5,53},{6,22},{7,55},{8,24},{9,... | collective-permute-start | bytes 884744 | tf_op jit(solution)/shard_map/ppermute | solution.py:399
  20.0 7.4 %collective-permute-start.3 = (bf16[96,1536]{1,0:T(8,128)(2,1)S(1)}, bf16[96,1536]{1,0:T(8,128)(2,1)S(1)}, u32[]{:S(2)}, u32[]{:S(2)}) collective-permute-start(bf16[96,1536]{1,0:T(8,128)(2,1)S(1)} %copy-done.2), channel_id=1, source_target_pairs={{0,32},{2,34},{4,36},{6,38},{8,40},{10,42},{12,44},{14,46},{16,48}... | collective-permute-start | bytes 884744 | tf_op jit(solution)/shard_map/ppermute | solution.py:399
  23.6 5.3 %collective-permute-start.2 = (bf16[96,1536]{1,0:T(8,128)(2,1)S(1)}, bf16[96,1536]{1,0:T(8,128)(2,1)}, u32[]{:S(2)}, u32[]{:S(2)}) collective-permute-start(bf16[96,1536]{1,0:T(8,128)(2,1)S(1)} %collective-permute-done.1.near), channel_id=1, source_target_pairs={{0,1},{1,0},{2,3},{3,2},{4,5},{5,4},{6,7},{7,6},{8,9},{9,8},{10,11... | collective-permute-start | bytes 884744 | tf_op jit(solution)/shard_map/ppermute | solution.py:399
  27.4 4.7 %collective-permute-start.4 = (bf16[96,1536]{1,0:T(8,128)(2,1)S(1)}, bf16[96,1536]{1,0:T(8,128)(2,1)}, u32[]{:S(2)}, u32[]{:S(2)}) collective-permute-start(bf16[96,1536]{1,0:T(8,128)(2,1)S(1)} %collective-permute-done.3.part), channel_id=1, source_target_pairs={{0,1},{2,3},{4,5},{6,7},{8,9},{10,11},{12,13},{14,15},{16,17},{18,... | collective-permute-start | bytes 884744 | tf_op jit(solution)/shard_map/ppermute | solution.py:399
  33.8 18.2 %collective-permute-start.5 = (bf16[384,1536]{1,0:T(8,128)(2,1)S(1)}, bf16[384,1536]{1,0:T(8,128)(2,1)S(1)}, u32[]{:S(2)}, u32[]{:S(2)}) collective-permute-start(bf16[384,1536]{1,0:T(8,128)(2,1)S(1)} %bitcast.8), channel_id=1, source_target_pairs={{0,64},{1,449},{2,66},{3,451},{4,68},{5,453},{6,70},{7,455},{8,72}... | collective-permute-start | bytes 3538952 | tf_op jit(solution)/shard_map/ppermute | solution.py:399
  38.9 1.0 copy-start
  52.0 18.4 %copy-start.3 = (bf16[384,1536]{1,0:T(8,128)(2,1)}, bf16[384,1536]{1,0:T(8,128)(2,1)S(1)}, u32[]{:S(2)}) copy-start(bf16[384,1536]{1,0:T(8,128)(2,1)S(1)} %collective-permute-done.5.refs_1_) | copy-start | bytes 3538948
  52.0 18.4 %collective-permute-start.6 = (bf16[384,1536]{1,0:T(8,128)(2,1)S(1)}, bf16[384,1536]{1,0:T(8,128)(2,1)}, u32[]{:S(2)}, u32[]{:S(2)}) collective-permute-start(bf16[384,1536]{1,0:T(8,128)(2,1)S(1)} %collective-permute-done.5.refs_1_), channel_id=1, source_target_pairs={{0,64},{1,449},{2,66},{3,451},{4,68},{5,453},{6,70},{7,455},{8,72}... | collective-permute-start | bytes 3538952 | tf_op jit(solution)/shard_map/ppermute | solution.py:399
  70.5 20.2 %collective-permute-start.7 = (bf16[384,1536]{1,0:T(8,128)(2,1)}, bf16[384,1536]{1,0:T(8,128)(2,1)}, u32[]{:S(2)}, u32[]{:S(2)}) collective-permute-start(bf16[384,1536]{1,0:T(8,128)(2,1)} %collective-permute-done.6.refs_2_), channel_id=1, source_target_pairs={{0,64},{1,449},{2,66},{3,451},{4,68},{5,453},{6,70},{7,455},{8,72}... | collective-permute-start | bytes 3538952 | tf_op jit(solution)/shard_map/ppermute | solution.py:399
  75.9 9.6 %collective-permute-start = (bf16[16,128,128]{2,1,0:T(8,128)(2,1)S(1)}, bf16[16,128,128]{2,1,0:T(8,128)(2,1)S(1)}, u32[]{:S(2)}, u32[]{:S(2)}) collective-permute-start(bf16[16,128,128]{2,1,0:T(8,128)(2,1)S(1)} %slice.4.own_kv), channel_id=1, source_target_pairs={{0,1},{1,0},{2,3},{3,2},{4,5},{5,4},{6,7},{7,6},{8,9},{9,8},{10,11... | collective-permute-start | bytes 1572872 | tf_op jit(solution)/shard_map/ppermute | solution.py:399
  90.7 34.2 %copy-start.1 = (bf16[4,96,1536]{2,1,0:T(8,128)(2,1)S(1)}, bf16[4,96,1536]{2,1,0:T(8,128)(2,1)}, u32[]{:S(2)}) copy-start(bf16[4,96,1536]{2,1,0:T(8,128)(2,1)} %copy-done) | copy-start | bytes 3538948
  90.7 34.2 %all-to-all-start.1 = ((bf16[16,224,128]{2,1,0:T(8,128)(2,1)}), bf16[16,224,128]{2,1,0:T(8,128)(2,1)S(1)}, u32[]{:S(2)}, u32[]{:S(2)}) async-start(bf16[16,224,128]{2,1,0:T(8,128)(2,1)} %attend_shared.1), calls=%async_computation.1 | async-start | bytes 1835008 | tf_op jit(solution)/shard_map/all_to_all | solution.py:443
  100.7 10.9 %collective-permute-start.11 = (bf16[384,768]{1,0:T(8,128)(2,1)S(1)}, bf16[384,768]{1,0:T(8,128)(2,1)S(1)}, u32[]{:S(2)}, u32[]{:S(2)}) collective-permute-start(bf16[384,768]{1,0:T(8,128)(2,1)S(1)} %constant_dynamic-slice_fusion), channel_id=1, source_target_pairs={{0,64},{1,449},{2,66},{3,451},{4,68},{5,453},{6,70},{7,455},{8,72}... | collective-permute-start | bytes 1769480 | tf_op jit(solution)/shard_map/ppermute | solution.py:399
  103.1 14.3 %collective-permute-start.8 = (bf16[384,1536]{1,0:T(8,128)(2,1)}, bf16[384,1536]{1,0:T(8,128)(2,1)S(1)}, u32[]{:S(2)}, u32[]{:S(2)}) collective-permute-start(bf16[384,1536]{1,0:T(8,128)(2,1)} %copy-done.3), channel_id=1, source_target_pairs={{0,1},{1,0},{2,3},{3,2},{4,5},{5,4},{6,7},{7,6},{8,9},{9,8},{10,11... | collective-permute-start | bytes 3538952 | tf_op jit(solution)/shard_map/ppermute | solution.py:399
  105.0 12.4 %collective-permute-start.9 = (bf16[384,1536]{1,0:T(8,128)(2,1)}, bf16[384,1536]{1,0:T(8,128)(2,1)S(1)}, u32[]{:S(2)}, u32[]{:S(2)}) collective-permute-start(bf16[384,1536]{1,0:T(8,128)(2,1)} %collective-permute-done.6.refs_2_), channel_id=1, source_target_pairs={{0,1},{1,0},{2,3},{3,2},{4,5},{5,4},{6,7},{7,6},{8,9},{9,8},{10,11... | collective-permute-start | bytes 3538952 | tf_op jit(solution)/shard_map/ppermute | solution.py:399
  107.4 12.1 %collective-permute-start.10 = (bf16[384,1536]{1,0:T(8,128)(2,1)}, bf16[384,1536]{1,0:T(8,128)(2,1)}, u32[]{:S(2)}, u32[]{:S(2)}) collective-permute-start(bf16[384,1536]{1,0:T(8,128)(2,1)} %collective-permute-done.7.refs_3_), channel_id=1, source_target_pairs={{0,1},{1,0},{2,3},{3,2},{4,5},{5,4},{6,7},{7,6},{8,9},{9,8},{10,11... | collective-permute-start | bytes 3538952 | tf_op jit(solution)/shard_map/ppermute | solution.py:399
  111.7 5.7 %collective-permute-start.12 = (bf16[384,768]{1,0:T(8,128)(2,1)S(1)}, bf16[384,768]{1,0:T(8,128)(2,1)S(1)}, u32[]{:S(2)}, u32[]{:S(2)}) collective-permute-start(bf16[384,768]{1,0:T(8,128)(2,1)S(1)} %collective-permute-done.11.refs_7_), channel_id=1, source_target_pairs={{0,1},{1,0},{2,3},{3,2},{4,5},{5,4},{6,7},{7,6},{8,9},{9,8},{10,11... | collective-permute-start | bytes 1769480 | tf_op jit(solution)/shard_map/ppermute | solution.py:399
  117.4 1.0 copy-start.4
  118.4 1.1 copy-start.5

commit v5 on v4

--- a/solution.py
+++ b/solution.py
@@ -190,7 +190,7 @@
 Q_ROWS = 512
 STEP_ROWS = 1024
 VMEM = 32 * 2**20
-PLACE_VMEM = 8 * 2**20
+PLACE_VMEM = 12 * 2**20
 PROJECT_VMEM = 50 * 2**20
 
 
@@ -265,36 +265,48 @@
     )(where, received, received, own_kv, far_kv, whole, whole_lse)
 
 
-def place_kernel(where, mine, near, near_far, part, part_far, out):
-    x, core = where[1], where[2]
+def place_kernel(where, mine, *refs):
+    ring, far_ring, opposite, opposite_far, halves = refs[:3], refs[3:6], refs[6], refs[7], refs[8:]
+    y, core = where[0], where[2]
     sign = 1 - 2 * core
-    out[x] = mine[...]
-    out[(x - sign + 4) % 4] = near[...]
-    out[(x + sign + 4) % 4] = near_far[...]
+
+    def put(to, shard):
+        to = (to + Y_SIZE) % Y_SIZE
+        for half, out in enumerate(halves):
+
+            @pl.when(to // Y_HALF == half)
+            def _():
+                out[to % Y_HALF] = shard[...]
+
+    put(y, mine)
+    for index in range(3):
+        hops = (index + 1) * sign
+        put(y - hops, ring[index])
+        put(y + hops, far_ring[index])
 
     @pl.when(core == 0)
     def _():
-        out[(x + 2) % 4] = part[...]
+        put(y + 4, opposite)
 
     @pl.when(core == 1)
     def _():
-        out[(x + 2) % 4] = part_far[...]
-
-
-def place(where, mine, near, near_far, part, part_far):
-    rows, columns = mine.shape
+        put(y + 4, opposite_far)
+
+
+def place(where, shards):
+    rows, columns = shards[0].shape
     return pl.pallas_call(
         place_kernel,
         grid_spec=pltpu.PrefetchScalarGridSpec(
             num_scalar_prefetch=1,
             grid=(),
-            in_specs=[pl.BlockSpec(memory_space=pltpu.VMEM)] * 5,
-            out_specs=pl.BlockSpec(memory_space=pltpu.VMEM),
+            in_specs=[pl.BlockSpec(memory_space=pltpu.VMEM)] * len(shards),
+            out_specs=[pl.BlockSpec(memory_space=pltpu.VMEM)] * 2,
         ),
-        out_shape=jax.ShapeDtypeStruct((4, rows, columns), jnp.bfloat16),
+        out_shape=[jax.ShapeDtypeStruct((Y_HALF, rows, columns), jnp.bfloat16)] * 2,
         compiler_params=pltpu.CompilerParams(vmem_limit_bytes=PLACE_VMEM),
         name="place",
-    )(where, mine, near, near_far, part, part_far)
+    )(where, *shards)
 
 
 def slot_of(ret, head):
@@ -317,20 +329,30 @@
 
 
 def project_kernel(where, ret, *refs):
-    weights, (vis_out, txt_out, slots, held, sems) = refs[:9], refs[9:]
-    y, core = where[0], where[2]
+    weights, (vis_out, txt_out, slots, held, sems) = refs[:10], refs[10:]
+    x, core = where[1], where[2]
     sign = 1 - 2 * core
-    columns = held.shape[2] // 2
-    copies = []
-    for index in range(7):
-        to = held.at[index // 2, pl.ds(index % 2 * TRIO, TRIO)]
-        copies.append(pltpu.make_async_copy(weights[index], to, sems.at[index]))
-    for index in range(2):
-        at = core if index == 0 else 1 - core
-        start = pl.multiple_of(at * columns, columns)
-        to = held.at[3, pl.ds(TRIO, TRIO), pl.ds(start, columns)]
-        copies.append(pltpu.make_async_copy(weights[7 + index], to, sems.at[7 + index]))
-    for copy in copies:
+    shard = weights[0].shape[1]
+
+    def copies_of(index, to_x, first_y, count):
+        column = (to_x + X_SIZE) % X_SIZE
+        pieces = []
+        for item in range(count):
+            start = ((first_y + item) * X_SIZE + column) * shard
+            to = held.at[pl.ds(pl.multiple_of(start, 32), shard)]
+            pieces.append(pltpu.make_async_copy(weights[index].at[item], to, sems.at[index, item]))
+        return pieces
+
+    rounds = [[], []]
+    for pair, to_x in enumerate((x, x - sign, x + sign)):
+        for half in range(2):
+            pieces = copies_of(2 * pair + half, to_x, half * Y_HALF, Y_HALF)
+            for item in range(Y_HALF):
+                rounds[item // 2].append(pieces[item])
+    for pair, half in enumerate((core, 1 - core)):
+        for item in range(2):
+            rounds[item] += copies_of(6 + 2 * pair + item, x + 2, half * Y_HALF + 2 * item, 2)
+    for copy in rounds[0] + rounds[1]:
         copy.start()
     for slot in range(SLOTS):
         valid = where[5 + slot] > 0
@@ -340,36 +362,37 @@
             slots[slot : slot + 1, at : at + VIS_ROWS] = row[:, :VIS_ROWS]
             at = VIS_SEQ + source * TXT_ROWS
             slots[slot : slot + 1, at : at + TXT_ROWS] = row[:, VIS_ROWS:]
-    total = jnp.zeros((ROWS, 2 * columns), jnp.float32)
-    pieces = []
-    for index, hops in enumerate((0, 1, 2, 3, -1, -2, -3, 4)):
-        chip = (y - hops * sign + 8) % 8
-        low, high = ret[2 * chip], ret[2 * chip + 1]
-        shared = jnp.concatenate([low[ROWS:RET_ROWS], high[ROWS:RET_ROWS]], axis=0)
-        attention = jnp.concatenate([low[:ROWS], shared, high[:ROWS]], axis=1)
-        txt_out[:, pl.ds(pl.multiple_of(chip * TRIO, TRIO), TRIO)] = attention[VIS_ROWS:]
-        pieces.append(attention)
-        copies[index].wait()
-        if index % 2 == 1:
-            if index == 7:
-                copies[8].wait()
-            both = jnp.concatenate(pieces[-2:], axis=1)
-            total += jnp.dot(both, held[index // 2], preferred_element_type=jnp.float32)
+    total = jnp.zeros((ROWS, held.shape[1]), jnp.float32)
+    depth = 2 * TRIO
+    for item in range(2):
+        for copy in rounds[item]:
+            copy.wait()
+        for first in (2 * item, 2 * item + Y_HALF):
+            pieces = []
+            for chip in (first, first + 1):
+                low, high = ret[2 * chip], ret[2 * chip + 1]
+                shared = jnp.concatenate([low[ROWS:RET_ROWS], high[ROWS:RET_ROWS]], axis=0)
+                pieces += [low[:ROWS], shared, high[:ROWS]]
+            attention = jnp.concatenate(pieces, axis=1)
+            txt_out[:, first * TRIO : first * TRIO + depth] = attention[VIS_ROWS:]
+            total += jnp.dot(
+                attention, held[first * TRIO : first * TRIO + depth, :], preferred_element_type=jnp.float32
+            )
     vis_out[...] = total[:VIS_ROWS].astype(jnp.bfloat16)
 
 
-def project(where, returned, chunks, far_chunks):
-    columns = chunks[0].shape[1]
+def project(where, returned, weights):
+    columns = weights[0].shape[2]
     return pl.pallas_call(
         project_kernel,
         grid_spec=pltpu.PrefetchScalarGridSpec(
             num_scalar_prefetch=1,
             grid=(),
-            in_specs=[pl.BlockSpec(memory_space=pltpu.VMEM)] + [pl.BlockSpec(memory_space=pltpu.HBM)] * 9,
+            in_specs=[pl.BlockSpec(memory_space=pltpu.VMEM)] + [pl.BlockSpec(memory_space=pl.ANY)] * 10,
             out_specs=[pl.BlockSpec(memory_space=pltpu.VMEM)] * 3,
             scratch_shapes=[
-                pltpu.VMEM((4, 2 * TRIO, columns), jnp.bfloat16),
-                pltpu.SemaphoreType.DMA((9,)),
+                pltpu.VMEM((HEADS * HEAD_DIM, columns), jnp.bfloat16),
+                pltpu.SemaphoreType.DMA((10, Y_HALF)),
             ],
         ),
         out_shape=[
@@ -379,12 +402,13 @@
         ],
         compiler_params=pltpu.CompilerParams(vmem_limit_bytes=PROJECT_VMEM),
         name="project",
-    )(where, returned, *chunks[:4], *far_chunks[:3], chunks[4], far_chunks[3])
+    )(where, returned, *weights)
 
 
 AXES = ("dp", "seq")
 X_SIZE = 4
 Y_SIZE = 8
+Y_HALF = Y_SIZE // 2
 
 
 def permute(operand, target, cores=(0, 1)):
@@ -403,12 +427,21 @@
     return permute(operand, lambda y, x, s: (y, x, s ^ 1), cores)
 
 
-def shift_x(operand, hops, cores=(0, 1)):
-    return permute(operand, lambda y, x, s: (y, x + hops * (1 - 2 * (s % 2)), s), cores)
-
-
-def shift_y(operand):
-    return permute(operand, lambda y, x, s: (y + 1 - 2 * (s % 2), x, s))
+def shift_x(operand):
+    return permute(operand, lambda y, x, s: (y, x + 1 - 2 * (s % 2), s))
+
+
+def shift_y(operand, hops=1, cores=(0, 1)):
+    return permute(operand, lambda y, x, s: (y + hops * (1 - 2 * (s % 2)), x, s), cores)
+
+
+def gather_along_y(where, w_out):
+    ring = [shift_y(w_out)]
+    opposite = shift_y(w_out, Y_SIZE // 2, cores=(0,))
+    for _ in range(2):
+        ring.append(shift_y(ring[-1]))
+    far_ring = [swap(shard) for shard in ring]
+    return place(where, [w_out, *ring, *far_ring, opposite, swap(opposite, cores=(0,))])
 
 
 def heads_of_slots(head_map, seq_index):
@@ -423,27 +456,25 @@
     seq_index = lax.axis_index("seq")
     dp_index = lax.axis_index("dp")
     core = seq_index % 2
-    half = w_out.shape[1] // 2
     place_here = jnp.stack([dp_index // X_SIZE, dp_index % X_SIZE, core]).astype(jnp.int32)
     where = jnp.concatenate([place_here, heads_of_slots(head_map, seq_index)])
 
-    near = shift_x(w_out, 1)
-    part = shift_x(w_out, 2, cores=(0,))
     sending = pack(qkv_vis, qkv_txt, vis_segments, txt_segments)
     received = lax.all_to_all(sending, "seq", split_axis=0, concat_axis=0, tiled=True)
-    chunks = [place(where, w_out, near, swap(near), part, swap(part, cores=(0,))).reshape(-1, 2 * half)]
-    chunks.append(shift_y(chunks[0]))
-    chunks.append(shift_y(chunks[1]))
-    chunks.append(shift_y(chunks[2]))
+    own_x = gather_along_y(where, w_out)
+    near = [shift_x(shards) for shards in own_x]
     own_kv = received[:, A_ROWS + HALF : SEND_ROWS]
     far_kv = swap(own_kv)
     whole, whole_lse = attend_whole(received)
     returning = attend_shared(where, received, own_kv, far_kv, whole, whole_lse)
-    returning, chunks[1], chunks[2], chunks[3] = lax.optimization_barrier((returning, *chunks[1:]))
+    returning, near = lax.optimization_barrier((returning, near))
     returned = lax.all_to_all(returning, "seq", split_axis=0, concat_axis=0, tiled=True)
-    chunks.append(shift_y(lax.dynamic_slice_in_dim(chunks[3], core * half, half, 1)))
-    far_chunks = [swap(chunk) for chunk in chunks[1:]]
-    vis_out, txt_out, lse_slots = project(where, returned, chunks, far_chunks)
+    opposite = [
+        shift_x(jnp.where(core == 0, near[0][2 * part : 2 * part + 2], near[1][2 * part : 2 * part + 2]))
+        for part in range(2)
+    ]
+    weights = [*own_x, *near, *map(swap, near), *opposite, *map(swap, opposite)]
+    vis_out, txt_out, lse_slots = project(where, returned, weights)
     return vis_out, txt_out, lse_slots
 
 

time: 131 us -> 131 us (level)
  the two profiles are of different devices: /device:TPU:1 before, /device:TPU:25 now
where the time goes in v5:
time: 131 us; the launch traced here: 130 us
  starting transfers between devices  74.4 us (57%)
  waiting for transfers between devices  26.9 us (21%)
  Pallas kernels  24.9 us (19%)
  other arithmetic  2.03 us (2%)
    ppermute x17, starting transfers between devices, permute(): return lax.ppermute(operand, AXES, pairs)  54.2 us
    ppermute x17, waiting for transfers between devices, permute(): return lax.ppermute(operand, AXES, pairs)  23.2 us
    all_to_all x1, starting transfers between devices, on_device(): lax.all_to_all(sending, 'seq', split_axis=0, concat_axis=0, tiled=True)  11.1 us
    all_to_all x1, starting transfers between devices, on_device(): lax.all_to_all(returning, 'seq', split_axis=0, concat_axis=0, tiled=True)  9.04 us
    pallas_call x1, Pallas kernels, attend_whole(): pl.pallas_call(whole_kernel, grid=(steps,), in_specs=[pl.BlockSpec((N_SEQ...  7.63 us
    pallas_call x1, Pallas kernels, project(): pl.pallas_call(project_kernel, grid_spec=pltpu.PrefetchScalarGridSpec(num...  5.49 us
    pallas_call x1, Pallas kernels, attend_shared(): pl.pallas_call(shared_kernel, grid_spec=pltpu.PrefetchScalarGridSpec(num_...  5.22 us
    all_to_all x1, waiting for transfers between devices, on_device(): lax.all_to_all(sending, 'seq', split_axis=0, concat_axis=0, tiled=True)  3.71 us
  transfers between devices with their start and end apart: 19, of which 8 were waited for; matrix products, arithmetic and copies ran while one was open for 2% of the time, Pallas kernels for 13%

profile of v5, /device:TPU:25, one launch (start us, length us, event | category | flops | bytes accessed | tf_op | source)
XLA Modules:
  0.0 130.4 jit_solution(12552440104720217101)
XLA Ops:
  0.6 2.9 %pack.1 = bf16[16,592,128]{2,1,0:T(8,128)(2,1)} custom-call(s32[1,112]{1,0:T(1,128)} %bitcast.7, s32[1,16]{1,0:T(1,128)} %bitcast.8, bf16[112,9216]{1,0:T(8,128)(2,1)} %vv.1, bf16[112,9216]{1,0:T(8,128)(2,1)} %vv.1, bf16[112,9216]{1,0:T(8,128)(2,1)} %vv.1, bf16[16,9216]{1,0:T(8,128)(2,1)} %tv.1, bf16[16,9216]{1,0:T(8,128)(2,1)} %tv.1, bf16[16,9216]{1,0:T(8,128)(2,1)} %tv.1), custom_call_target="tpu_custom_call" | custom-call | tf_op jit(solution)/shard_map/pack/pallas_call | solution.py:66
  3.5 11.1 %all-to-all-start = ((bf16[16,592,128]{2,1,0:T(8,128)(2,1)}), bf16[16,592,128]{2,1,0:T(8,128)(2,1)S(1)}, u32[]{:S(2)}, u32[]{:S(2)}) async-start(bf16[16,592,128]{2,1,0:T(8,128)(2,1)} %pack.1), calls=%async_computation | async-start | bytes 4849664 | tf_op jit(solution)/shard_map/all_to_all | solution.py:463
  14.7 2.1 %collective-permute-start.1 = (bf16[96,1536]{1,0:T(8,128)(2,1)S(1)}, bf16[96,1536]{1,0:T(8,128)(2,1)S(1)}, u32[]{:S(2)}, u32[]{:S(2)}) collective-permute-start(bf16[96,1536]{1,0:T(8,128)(2,1)S(1)} %copy-done), channel_id=1, source_target_pairs={{0,64},{1,449},{2,66},{3,451},{4,68},{5,453},{6,70},{7,455},{8,72}... | collective-permute-start | bytes 884744 | tf_op jit(solution)/shard_map/ppermute | solution.py:423
  16.8 6.9 %collective-permute-done.1.refs_0_ = bf16[96,1536]{1,0:T(8,128)(2,1)S(1)} collective-permute-done((bf16[96,1536]{1,0:T(8,128)(2,1)S(1)}, bf16[96,1536]{1,0:T(8,128)(2,1)S(1)}, u32[]{:S(2)}, u32[]{:S(2)}) %collective-permute-start.1) | collective-permute-done | bytes 294944 | tf_op jit(solution)/shard_map/ppermute | solution.py:423
  23.7 1.9 %collective-permute-start.2 = (bf16[96,1536]{1,0:T(8,128)(2,1)S(1)}, bf16[96,1536]{1,0:T(8,128)(2,1)S(1)}, u32[]{:S(2)}, u32[]{:S(2)}) collective-permute-start(bf16[96,1536]{1,0:T(8,128)(2,1)S(1)} %collective-permute-done.1.refs_0_), channel_id=1, source_target_pairs={{0,64},{1,449},{2,66},{3,451},{4,68},{5,453},{6,70},{7,455},{8,72}... | collective-permute-start | bytes 884744 | tf_op jit(solution)/shard_map/ppermute | solution.py:423
  25.6 1.4 %collective-permute-start.7 = (bf16[96,1536]{1,0:T(8,128)(2,1)S(1)}, bf16[96,1536]{1,0:T(8,128)(2,1)}, u32[]{:S(2)}, u32[]{:S(2)}) collective-permute-start(bf16[96,1536]{1,0:T(8,128)(2,1)S(1)} %copy-done), channel_id=1, source_target_pairs={{0,256},{2,258},{4,260},{6,262},{8,264},{10,266},{12,268},{14,270}... | collective-permute-start | bytes 884744 | tf_op jit(solution)/shard_map/ppermute | solution.py:423
  27.0 5.6 %collective-permute-done.2.refs_1_ = bf16[96,1536]{1,0:T(8,128)(2,1)S(1)} collective-permute-done((bf16[96,1536]{1,0:T(8,128)(2,1)S(1)}, bf16[96,1536]{1,0:T(8,128)(2,1)S(1)}, u32[]{:S(2)}, u32[]{:S(2)}) %collective-permute-start.2) | collective-permute-done | bytes 294944 | tf_op jit(solution)/shard_map/ppermute | solution.py:423
  32.6 1.9 %collective-permute-start.3 = (bf16[96,1536]{1,0:T(8,128)(2,1)S(1)}, bf16[96,1536]{1,0:T(8,128)(2,1)}, u32[]{:S(2)}, u32[]{:S(2)}) collective-permute-start(bf16[96,1536]{1,0:T(8,128)(2,1)S(1)} %collective-permute-done.2.refs_1_), channel_id=1, source_target_pairs={{0,64},{1,449},{2,66},{3,451},{4,68},{5,453},{6,70},{7,455},{8,72}... | collective-permute-start | bytes 884744 | tf_op jit(solution)/shard_map/ppermute | solution.py:423
  34.8 12.3 %collective-permute-start.4 = (bf16[96,1536]{1,0:T(8,128)(2,1)S(1)}, bf16[96,1536]{1,0:T(8,128)(2,1)}, u32[]{:S(2)}, u32[]{:S(2)}) collective-permute-start(bf16[96,1536]{1,0:T(8,128)(2,1)S(1)} %collective-permute-done.1.refs_0_), channel_id=1, source_target_pairs={{0,1},{1,0},{2,3},{3,2},{4,5},{5,4},{6,7},{7,6},{8,9},{9,8},{10,11... | collective-permute-start | bytes 884744 | tf_op jit(solution)/shard_map/ppermute | solution.py:423
  47.1 1.3 collective-permute-start.8
  48.4 3.7 %collective-permute-start.5 = (bf16[96,1536]{1,0:T(8,128)(2,1)S(1)}, bf16[96,1536]{1,0:T(8,128)(2,1)}, u32[]{:S(2)}, u32[]{:S(2)}) collective-permute-start(bf16[96,1536]{1,0:T(8,128)(2,1)S(1)} %collective-permute-done.2.refs_1_), channel_id=1, source_target_pairs={{0,1},{1,0},{2,3},{3,2},{4,5},{5,4},{6,7},{7,6},{8,9},{9,8},{10,11... | collective-permute-start | bytes 884744 | tf_op jit(solution)/shard_map/ppermute | solution.py:423
  52.2 1.9 %collective-permute-start.6 = (bf16[96,1536]{1,0:T(8,128)(2,1)}, bf16[96,1536]{1,0:T(8,128)(2,1)}, u32[]{:S(2)}, u32[]{:S(2)}) collective-permute-start(bf16[96,1536]{1,0:T(8,128)(2,1)} %collective-permute-done.3.refs_2_), channel_id=1, source_target_pairs={{0,1},{1,0},{2,3},{3,2},{4,5},{5,4},{6,7},{7,6},{8,9},{9,8},{10,11... | collective-permute-start | bytes 884744 | tf_op jit(solution)/shard_map/ppermute | solution.py:423
  54.4 1.6 %collective-permute-done.6.refs_5_ = bf16[96,1536]{1,0:T(8,128)(2,1)} collective-permute-done((bf16[96,1536]{1,0:T(8,128)(2,1)}, bf16[96,1536]{1,0:T(8,128)(2,1)}, u32[]{:S(2)}, u32[]{:S(2)}) %collective-permute-start.6) | collective-permute-done | bytes 294944 | tf_op jit(solution)/shard_map/ppermute | solution.py:423
  56.0 3.7 %place.1 = (bf16[4,96,1536]{2,1,0:T(8,128)(2,1)}, bf16[4,96,1536]{2,1,0:T(8,128)(2,1)}) custom-call(s32[7]{0:T(128)S(1)} %concatenate.3.where, bf16[96,1536]{1,0:T(8,128)(2,1)S(1)} %copy-done, bf16[96,1536]{1,0:T(8,128)(2,1)S(1)} %collective-permute-done.1.refs_0_, bf16[96,1536]{1,0:T(8,128)(2,1)S(1)} %collective-permute-done.2.refs_1_, ...), custom_call_target="tpu_custom_call" | custom-call | tf_op jit(solution)/shard_map/place/pallas_call | solution.py:298
  59.7 4.4 %collective-permute-start.9 = (bf16[4,96,1536]{2,1,0:T(8,128)(2,1)}, bf16[4,96,1536]{2,1,0:T(8,128)(2,1)}, u32[]{:S(2)}, u32[]{:S(2)}) collective-permute-start(bf16[4,96,1536]{2,1,0:T(8,128)(2,1)} %get-tuple-element.12.refs_0_), channel_id=1, source_target_pairs={{0,16},{1,49},{2,18},{3,51},{4,20},{5,53},{6,22},{7,55},{8,24},{9,... | collective-permute-start | bytes 3538952 | tf_op jit(solution)/shard_map/ppermute | solution.py:423
  64.1 2.5 %collective-permute-start.10 = (bf16[4,96,1536]{2,1,0:T(8,128)(2,1)}, bf16[4,96,1536]{2,1,0:T(8,128)(2,1)}, u32[]{:S(2)}, u32[]{:S(2)}) collective-permute-start(bf16[4,96,1536]{2,1,0:T(8,128)(2,1)} %get-tuple-element.13.refs_1_), channel_id=1, source_target_pairs={{0,16},{1,49},{2,18},{3,51},{4,20},{5,53},{6,22},{7,55},{8,24},{9,... | collective-permute-start | bytes 3538952 | tf_op jit(solution)/shard_map/ppermute | solution.py:423
  66.6 3.7 %all-to-all-done.cut.q.k.v = bf16[16,592,128]{2,1,0:T(8,128)(2,1)S(1)} async-done(((bf16[16,592,128]{2,1,0:T(8,128)(2,1)}), bf16[16,592,128]{2,1,0:T(8,128)(2,1)S(1)}, u32[]{:S(2)}, u32[]{:S(2)}) %all-to-all-start) | async-done | bytes 2424864 | tf_op jit(solution)/shard_map/all_to_all | solution.py:463
  70.3 2.8 %collective-permute-start = (bf16[16,128,128]{2,1,0:T(8,128)(2,1)S(1)}, bf16[16,128,128]{2,1,0:T(8,128)(2,1)S(1)}, u32[]{:S(2)}, u32[]{:S(2)}) collective-permute-start(bf16[16,128,128]{2,1,0:T(8,128)(2,1)S(1)} %slice.20.own_kv), channel_id=1, source_target_pairs={{0,1},{1,0},{2,3},{3,2},{4,5},{5,4},{6,7},{7,6},{8,9},{9,8},{10,11... | collective-permute-start | bytes 1572872 | tf_op jit(solution)/shard_map/ppermute | solution.py:423
  73.1 7.6 %attend_whole.1 = (bf16[16,128,128]{2,1,0:T(8,128)(2,1)S(1)}, f32[16,128]{1,0:T(8,128)S(1)}) custom-call(bf16[16,592,128]{2,1,0:T(8,128)(2,1)S(1)} %all-to-all-done.cut.q.k.v, bf16[16,592,128]{2,1,0:T(8,128)(2,1)S(1)} %all-to-all-done.cut.q.k.v, bf16[16,592,128]{2,1,0:T(8,128)(2,1)S(1)} %all-to-all-done.cut.q.k.v, ...), custom_call_target="tpu_custom_call" | custom-call | flops 134217728 | bytes 2097152 | tf_op jit(solution)/shard_map/attend_whole/pallas_call | solution.py:218
  80.7 5.2 %attend_shared.1 = bf16[16,224,128]{2,1,0:T(8,128)(2,1)} custom-call(s32[7]{0:T(128)S(1)} %concatenate.3.where, bf16[16,592,128]{2,1,0:T(8,128)(2,1)S(1)} %all-to-all-done.cut.q.k.v, bf16[16,592,128]{2,1,0:T(8,128)(2,1)S(1)} %all-to-all-done.cut.q.k.v, bf16[16,128,128]{2,1,0:T(8,128)(2,1)S(1)} %slice.20.own_kv, ...), custom_call_target="tpu_custom_call" | custom-call | flops 67108864 | bytes 2097152 | tf_op jit(solution)/shard_map/attend_shared/pallas_call | solution.py:245
  86.0 4.2 %collective-permute-done.10.refs_3_ = bf16[4,96,1536]{2,1,0:T(8,128)(2,1)} collective-permute-done((bf16[4,96,1536]{2,1,0:T(8,128)(2,1)}, bf16[4,96,1536]{2,1,0:T(8,128)(2,1)}, u32[]{:S(2)}, u32[]{:S(2)}) %collective-permute-start.10) | collective-permute-done | bytes 1179680 | tf_op jit(solution)/shard_map/ppermute | solution.py:423
  90.2 9.0 %all-to-all-start.1 = ((bf16[16,224,128]{2,1,0:T(8,128)(2,1)}), bf16[16,224,128]{2,1,0:T(8,128)(2,1)S(1)}, u32[]{:S(2)}, u32[]{:S(2)}) async-start(bf16[16,224,128]{2,1,0:T(8,128)(2,1)} %attend_shared.1), calls=%async_computation.1 | async-start | bytes 1835008 | tf_op jit(solution)/shard_map/all_to_all | solution.py:471
  99.2 1.7 %slice_select_fusion = (bf16[2,96,1536]{2,1,0:T(8,128)(2,1)S(1)}, bf16[2,96,1536]{2,1,0:T(8,128)(2,1)S(1)}) fusion(bf16[4,96,1536]{2,1,0:T(8,128)(2,1)} %collective-permute-done.10.refs_3_, bf16[4,96,1536]{2,1,0:T(8,128)(2,1)} %collective-permute-done.9.refs_2_, pred[]{:T(512)S(6)} %eq.31), kind=kLoop, calls=%fused_computation | loop fusion | flops 589824 | bytes 3538945 | tf_op jit(solution)/shard_map/jit(_where)/select_n | solution.py:473
  100.9 3.2 %collective-permute-start.14 = (bf16[2,96,1536]{2,1,0:T(8,128)(2,1)S(1)}, bf16[2,96,1536]{2,1,0:T(8,128)(2,1)S(1)}, u32[]{:S(2)}, u32[]{:S(2)}) collective-permute-start(bf16[2,96,1536]{2,1,0:T(8,128)(2,1)S(1)} %get-tuple-element.19), channel_id=1, source_target_pairs={{0,16},{1,49},{2,18},{3,51},{4,20},{5,53},{6,22},{7,55},{8,24},{9,... | collective-permute-start | bytes 1769480 | tf_op jit(solution)/shard_map/ppermute | solution.py:423
  104.2 2.4 %collective-permute-start.13 = (bf16[2,96,1536]{2,1,0:T(8,128)(2,1)S(1)}, bf16[2,96,1536]{2,1,0:T(8,128)(2,1)S(1)}, u32[]{:S(2)}, u32[]{:S(2)}) collective-permute-start(bf16[2,96,1536]{2,1,0:T(8,128)(2,1)S(1)} %get-tuple-element.20), channel_id=1, source_target_pairs={{0,16},{1,49},{2,18},{3,51},{4,20},{5,53},{6,22},{7,55},{8,24},{9,... | collective-permute-start | bytes 1769480 | tf_op jit(solution)/shard_map/ppermute | solution.py:423
  106.6 2.0 %collective-permute-start.11 = (bf16[4,96,1536]{2,1,0:T(8,128)(2,1)}, bf16[4,96,1536]{2,1,0:T(8,128)(2,1)S(1)}, u32[]{:S(2)}, u32[]{:S(2)}) collective-permute-start(bf16[4,96,1536]{2,1,0:T(8,128)(2,1)} %collective-permute-done.9.refs_2_), channel_id=1, source_target_pairs={{0,1},{1,0},{2,3},{3,2},{4,5},{5,4},{6,7},{7,6},{8,9},{9,8},{10,11... | collective-permute-start | bytes 3538952 | tf_op jit(solution)/shard_map/ppermute | solution.py:423
  108.6 2.4 %collective-permute-start.12 = (bf16[4,96,1536]{2,1,0:T(8,128)(2,1)}, bf16[4,96,1536]{2,1,0:T(8,128)(2,1)}, u32[]{:S(2)}, u32[]{:S(2)}) collective-permute-start(bf16[4,96,1536]{2,1,0:T(8,128)(2,1)} %collective-permute-done.10.refs_3_), channel_id=1, source_target_pairs={{0,1},{1,0},{2,3},{3,2},{4,5},{5,4},{6,7},{7,6},{8,9},{9,8},{10,11... | collective-permute-start | bytes 3538952 | tf_op jit(solution)/shard_map/ppermute | solution.py:423
  111.9 4.1 %collective-permute-start.16 = (bf16[2,96,1536]{2,1,0:T(8,128)(2,1)S(1)}, bf16[2,96,1536]{2,1,0:T(8,128)(2,1)S(1)}, u32[]{:S(2)}, u32[]{:S(2)}) collective-permute-start(bf16[2,96,1536]{2,1,0:T(8,128)(2,1)S(1)} %collective-permute-done.14.refs_7_), channel_id=1, source_target_pairs={{0,1},{1,0},{2,3},{3,2},{4,5},{5,4},{6,7},{7,6},{8,9},{9,8},{10,11... | collective-permute-start | bytes 1769480 | tf_op jit(solution)/shard_map/ppermute | solution.py:423
  115.9 2.2 %collective-permute-done.13.refs_6_ = bf16[2,96,1536]{2,1,0:T(8,128)(2,1)S(1)} collective-permute-done((bf16[2,96,1536]{2,1,0:T(8,128)(2,1)S(1)}, bf16[2,96,1536]{2,1,0:T(8,128)(2,1)S(1)}, u32[]{:S(2)}, u32[]{:S(2)}) %collective-permute-start.13) | collective-permute-done | bytes 589856 | tf_op jit(solution)/shard_map/ppermute | solution.py:423
  118.2 4.1 %collective-permute-start.15 = (bf16[2,96,1536]{2,1,0:T(8,128)(2,1)S(1)}, bf16[2,96,1536]{2,1,0:T(8,128)(2,1)S(1)}, u32[]{:S(2)}, u32[]{:S(2)}) collective-permute-start(bf16[2,96,1536]{2,1,0:T(8,128)(2,1)S(1)} %collective-permute-done.13.refs_6_), channel_id=1, source_target_pairs={{0,1},{1,0},{2,3},{3,2},{4,5},{5,4},{6,7},{7,6},{8,9},{9,8},{10,11... | collective-permute-start | bytes 1769480 | tf_op jit(solution)/shard_map/ppermute | solution.py:423
  122.3 1.6 %collective-permute-done.15.refs_8_ = bf16[2,96,1536]{2,1,0:T(8,128)(2,1)S(1)} collective-permute-done((bf16[2,96,1536]{2,1,0:T(8,128)(2,1)S(1)}, bf16[2,96,1536]{2,1,0:T(8,128)(2,1)S(1)}, u32[]{:S(2)}, u32[]{:S(2)}) %collective-permute-start.15) | collective-permute-done | bytes 589856 | tf_op jit(solution)/shard_map/ppermute | solution.py:423
  124.9 5.5 %project.1 = (bf16[112,1536]{1,0:T(8,128)(2,1)}, bf16[16,3072]{1,0:T(8,128)(2,1)}, f32[2,2048]{1,0:T(2,128)}) custom-call(s32[7]{0:T(128)S(1)} %concatenate.3.where, bf16[16,224,128]{2,1,0:T(8,128)(2,1)S(1)} %all-to-all-done.1.ret, bf16[4,96,1536]{2,1,0:T(8,128)(2,1)} %get-tuple-element.12.refs_0_, bf16[4,96,1536]{2,1,0:T(8,128)(2,1)} %get-tuple-element.13.refs_1_, ...), custom_call_target="tpu_custom_call" | custom-call | tf_op jit(solution)/shard_map/project/pallas_call | solution.py:386
  (26 shorter events, 2.5 us)
Async XLA Ops:
  3.5 11.2 %copy-start = (bf16[96,1536]{1,0:T(8,128)(2,1)S(1)}, bf16[96,1536]{1,0:T(8,128)(2,1)}, u32[]{:S(2)}) copy-start(bf16[96,1536]{1,0:T(8,128)(2,1)} %mine.1) | copy-start | bytes 884740
  3.5 31.0 %copy-start.2 = (s32[24]{0:T(128)S(1)}, s32[24]{0:T(128)}, u32[]{:S(2)}) copy-start(s32[24]{0:T(128)} %param.10) | copy-start | bytes 292
  3.5 66.7 %all-to-all-start = ((bf16[16,592,128]{2,1,0:T(8,128)(2,1)}), bf16[16,592,128]{2,1,0:T(8,128)(2,1)S(1)}, u32[]{:S(2)}, u32[]{:S(2)}) async-start(bf16[16,592,128]{2,1,0:T(8,128)(2,1)} %pack.1), calls=%async_computation | async-start | bytes 4849664 | tf_op jit(solution)/shard_map/all_to_all | solution.py:463
  14.7 9.0 %collective-permute-start.1 = (bf16[96,1536]{1,0:T(8,128)(2,1)S(1)}, bf16[96,1536]{1,0:T(8,128)(2,1)S(1)}, u32[]{:S(2)}, u32[]{:S(2)}) collective-permute-start(bf16[96,1536]{1,0:T(8,128)(2,1)S(1)} %copy-done), channel_id=1, source_target_pairs={{0,64},{1,449},{2,66},{3,451},{4,68},{5,453},{6,70},{7,455},{8,72}... | collective-permute-start | bytes 884744 | tf_op jit(solution)/shard_map/ppermute | solution.py:423
  23.7 9.0 %collective-permute-start.2 = (bf16[96,1536]{1,0:T(8,128)(2,1)S(1)}, bf16[96,1536]{1,0:T(8,128)(2,1)S(1)}, u32[]{:S(2)}, u32[]{:S(2)}) collective-permute-start(bf16[96,1536]{1,0:T(8,128)(2,1)S(1)} %collective-permute-done.1.refs_0_), channel_id=1, source_target_pairs={{0,64},{1,449},{2,66},{3,451},{4,68},{5,453},{6,70},{7,455},{8,72}... | collective-permute-start | bytes 884744 | tf_op jit(solution)/shard_map/ppermute | solution.py:423
  25.6 21.5 %collective-permute-start.7 = (bf16[96,1536]{1,0:T(8,128)(2,1)S(1)}, bf16[96,1536]{1,0:T(8,128)(2,1)}, u32[]{:S(2)}, u32[]{:S(2)}) collective-permute-start(bf16[96,1536]{1,0:T(8,128)(2,1)S(1)} %copy-done), channel_id=1, source_target_pairs={{0,256},{2,258},{4,260},{6,262},{8,264},{10,266},{12,268},{14,270}... | collective-permute-start | bytes 884744 | tf_op jit(solution)/shard_map/ppermute | solution.py:423
  32.6 19.6 %collective-permute-start.3 = (bf16[96,1536]{1,0:T(8,128)(2,1)S(1)}, bf16[96,1536]{1,0:T(8,128)(2,1)}, u32[]{:S(2)}, u32[]{:S(2)}) collective-permute-start(bf16[96,1536]{1,0:T(8,128)(2,1)S(1)} %collective-permute-done.2.refs_1_), channel_id=1, source_target_pairs={{0,64},{1,449},{2,66},{3,451},{4,68},{5,453},{6,70},{7,455},{8,72}... | collective-permute-start | bytes 884744 | tf_op jit(solution)/shard_map/ppermute | solution.py:423
  34.8 19.5 %collective-permute-start.4 = (bf16[96,1536]{1,0:T(8,128)(2,1)S(1)}, bf16[96,1536]{1,0:T(8,128)(2,1)}, u32[]{:S(2)}, u32[]{:S(2)}) collective-permute-start(bf16[96,1536]{1,0:T(8,128)(2,1)S(1)} %collective-permute-done.1.refs_0_), channel_id=1, source_target_pairs={{0,1},{1,0},{2,3},{3,2},{4,5},{5,4},{6,7},{7,6},{8,9},{9,8},{10,11... | collective-permute-start | bytes 884744 | tf_op jit(solution)/shard_map/ppermute | solution.py:423
  47.1 7.2 %collective-permute-start.8 = (bf16[96,1536]{1,0:T(8,128)(2,1)}, bf16[96,1536]{1,0:T(8,128)(2,1)}, u32[]{:S(2)}, u32[]{:S(2)}) collective-permute-start(bf16[96,1536]{1,0:T(8,128)(2,1)} %collective-permute-done.7.refs_6_), channel_id=1, source_target_pairs={{0,1},{2,3},{4,5},{6,7},{8,9},{10,11},{12,13},{14,15},{16,17},{18,... | collective-permute-start | bytes 884744 | tf_op jit(solution)/shard_map/ppermute | solution.py:423
  48.4 5.9 %collective-permute-start.5 = (bf16[96,1536]{1,0:T(8,128)(2,1)S(1)}, bf16[96,1536]{1,0:T(8,128)(2,1)}, u32[]{:S(2)}, u32[]{:S(2)}) collective-permute-start(bf16[96,1536]{1,0:T(8,128)(2,1)S(1)} %collective-permute-done.2.refs_1_), channel_id=1, source_target_pairs={{0,1},{1,0},{2,3},{3,2},{4,5},{5,4},{6,7},{7,6},{8,9},{9,8},{10,11... | collective-permute-start | bytes 884744 | tf_op jit(solution)/shard_map/ppermute | solution.py:423
  52.2 3.8 %collective-permute-start.6 = (bf16[96,1536]{1,0:T(8,128)(2,1)}, bf16[96,1536]{1,0:T(8,128)(2,1)}, u32[]{:S(2)}, u32[]{:S(2)}) collective-permute-start(bf16[96,1536]{1,0:T(8,128)(2,1)} %collective-permute-done.3.refs_2_), channel_id=1, source_target_pairs={{0,1},{1,0},{2,3},{3,2},{4,5},{5,4},{6,7},{7,6},{8,9},{9,8},{10,11... | collective-permute-start | bytes 884744 | tf_op jit(solution)/shard_map/ppermute | solution.py:423
  59.7 26.3 %collective-permute-start.9 = (bf16[4,96,1536]{2,1,0:T(8,128)(2,1)}, bf16[4,96,1536]{2,1,0:T(8,128)(2,1)}, u32[]{:S(2)}, u32[]{:S(2)}) collective-permute-start(bf16[4,96,1536]{2,1,0:T(8,128)(2,1)} %get-tuple-element.12.refs_0_), channel_id=1, source_target_pairs={{0,16},{1,49},{2,18},{3,51},{4,20},{5,53},{6,22},{7,55},{8,24},{9,... | collective-permute-start | bytes 3538952 | tf_op jit(solution)/shard_map/ppermute | solution.py:423
  64.1 26.1 %collective-permute-start.10 = (bf16[4,96,1536]{2,1,0:T(8,128)(2,1)}, bf16[4,96,1536]{2,1,0:T(8,128)(2,1)}, u32[]{:S(2)}, u32[]{:S(2)}) collective-permute-start(bf16[4,96,1536]{2,1,0:T(8,128)(2,1)} %get-tuple-element.13.refs_1_), channel_id=1, source_target_pairs={{0,16},{1,49},{2,18},{3,51},{4,20},{5,53},{6,22},{7,55},{8,24},{9,... | collective-permute-start | bytes 3538952 | tf_op jit(solution)/shard_map/ppermute | solution.py:423
  70.3 10.4 %collective-permute-start = (bf16[16,128,128]{2,1,0:T(8,128)(2,1)S(1)}, bf16[16,128,128]{2,1,0:T(8,128)(2,1)S(1)}, u32[]{:S(2)}, u32[]{:S(2)}) collective-permute-start(bf16[16,128,128]{2,1,0:T(8,128)(2,1)S(1)} %slice.20.own_kv), channel_id=1, source_target_pairs={{0,1},{1,0},{2,3},{3,2},{4,5},{5,4},{6,7},{7,6},{8,9},{9,8},{10,11... | collective-permute-start | bytes 1572872 | tf_op jit(solution)/shard_map/ppermute | solution.py:423
  90.2 34.7 %all-to-all-start.1 = ((bf16[16,224,128]{2,1,0:T(8,128)(2,1)}), bf16[16,224,128]{2,1,0:T(8,128)(2,1)S(1)}, u32[]{:S(2)}, u32[]{:S(2)}) async-start(bf16[16,224,128]{2,1,0:T(8,128)(2,1)} %attend_shared.1), calls=%async_computation.1 | async-start | bytes 1835008 | tf_op jit(solution)/shard_map/all_to_all | solution.py:471
  100.9 10.9 %collective-permute-start.14 = (bf16[2,96,1536]{2,1,0:T(8,128)(2,1)S(1)}, bf16[2,96,1536]{2,1,0:T(8,128)(2,1)S(1)}, u32[]{:S(2)}, u32[]{:S(2)}) collective-permute-start(bf16[2,96,1536]{2,1,0:T(8,128)(2,1)S(1)} %get-tuple-element.19), channel_id=1, source_target_pairs={{0,16},{1,49},{2,18},{3,51},{4,20},{5,53},{6,22},{7,55},{8,24},{9,... | collective-permute-start | bytes 1769480 | tf_op jit(solution)/shard_map/ppermute | solution.py:423
  104.2 14.0 %collective-permute-start.13 = (bf16[2,96,1536]{2,1,0:T(8,128)(2,1)S(1)}, bf16[2,96,1536]{2,1,0:T(8,128)(2,1)S(1)}, u32[]{:S(2)}, u32[]{:S(2)}) collective-permute-start(bf16[2,96,1536]{2,1,0:T(8,128)(2,1)S(1)} %get-tuple-element.20), channel_id=1, source_target_pairs={{0,16},{1,49},{2,18},{3,51},{4,20},{5,53},{6,22},{7,55},{8,24},{9,... | collective-permute-start | bytes 1769480 | tf_op jit(solution)/shard_map/ppermute | solution.py:423
  106.6 17.3 %collective-permute-start.11 = (bf16[4,96,1536]{2,1,0:T(8,128)(2,1)}, bf16[4,96,1536]{2,1,0:T(8,128)(2,1)S(1)}, u32[]{:S(2)}, u32[]{:S(2)}) collective-permute-start(bf16[4,96,1536]{2,1,0:T(8,128)(2,1)} %collective-permute-done.9.refs_2_), channel_id=1, source_target_pairs={{0,1},{1,0},{2,3},{3,2},{4,5},{5,4},{6,7},{7,6},{8,9},{9,8},{10,11... | collective-permute-start | bytes 3538952 | tf_op jit(solution)/shard_map/ppermute | solution.py:423
  108.6 16.3 %collective-permute-start.12 = (bf16[4,96,1536]{2,1,0:T(8,128)(2,1)}, bf16[4,96,1536]{2,1,0:T(8,128)(2,1)}, u32[]{:S(2)}, u32[]{:S(2)}) collective-permute-start(bf16[4,96,1536]{2,1,0:T(8,128)(2,1)} %collective-permute-done.10.refs_3_), channel_id=1, source_target_pairs={{0,1},{1,0},{2,3},{3,2},{4,5},{5,4},{6,7},{7,6},{8,9},{9,8},{10,11... | collective-permute-start | bytes 3538952 | tf_op jit(solution)/shard_map/ppermute | solution.py:423
  111.9 10.4 %collective-permute-start.16 = (bf16[2,96,1536]{2,1,0:T(8,128)(2,1)S(1)}, bf16[2,96,1536]{2,1,0:T(8,128)(2,1)S(1)}, u32[]{:S(2)}, u32[]{:S(2)}) collective-permute-start(bf16[2,96,1536]{2,1,0:T(8,128)(2,1)S(1)} %collective-permute-done.14.refs_7_), channel_id=1, source_target_pairs={{0,1},{1,0},{2,3},{3,2},{4,5},{5,4},{6,7},{7,6},{8,9},{9,8},{10,11... | collective-permute-start | bytes 1769480 | tf_op jit(solution)/shard_map/ppermute | solution.py:423
  118.2 5.7 %collective-permute-start.15 = (bf16[2,96,1536]{2,1,0:T(8,128)(2,1)S(1)}, bf16[2,96,1536]{2,1,0:T(8,128)(2,1)S(1)}, u32[]{:S(2)}, u32[]{:S(2)}) collective-permute-start(bf16[2,96,1536]{2,1,0:T(8,128)(2,1)S(1)} %collective-permute-done.13.refs_6_), channel_id=1, source_target_pairs={{0,1},{1,0},{2,3},{3,2},{4,5},{5,4},{6,7},{7,6},{8,9},{9,8},{10,11... | collective-permute-start | bytes 1769480 | tf_op jit(solution)/shard_map/ppermute | solution.py:423
  123.9 1.0 copy-start.1

commit v6 on v4

--- a/solution.py
+++ b/solution.py
@@ -434,15 +434,18 @@
     chunks = [place(where, w_out, near, swap(near), part, swap(part, cores=(0,))).reshape(-1, 2 * half)]
     chunks.append(shift_y(chunks[0]))
     chunks.append(shift_y(chunks[1]))
-    chunks.append(shift_y(chunks[2]))
+    far_chunks = [swap(chunks[1])]
+    received, far_chunks[0] = lax.optimization_barrier((received, far_chunks[0]))
     own_kv = received[:, A_ROWS + HALF : SEND_ROWS]
     far_kv = swap(own_kv)
     whole, whole_lse = attend_whole(received)
+    whole, far_kv, chunks[2] = lax.optimization_barrier((whole, far_kv, chunks[2]))
+    chunks.append(shift_y(chunks[2]))
     returning = attend_shared(where, received, own_kv, far_kv, whole, whole_lse)
-    returning, chunks[1], chunks[2], chunks[3] = lax.optimization_barrier((returning, *chunks[1:]))
+    returning, chunks[2] = lax.optimization_barrier((returning, chunks[2]))
     returned = lax.all_to_all(returning, "seq", split_axis=0, concat_axis=0, tiled=True)
     chunks.append(shift_y(lax.dynamic_slice_in_dim(chunks[3], core * half, half, 1)))
-    far_chunks = [swap(chunk) for chunk in chunks[1:]]
+    far_chunks += [swap(chunk) for chunk in chunks[2:]]
     vis_out, txt_out, lse_slots = project(where, returned, chunks, far_chunks)
     return vis_out, txt_out, lse_slots
 

time: 131 us -> 128 us (0.977)
  local copies, waits for them, and re-layouts: 4.46 us -> 2.37 us
    all_to_all x1, waiting for transfers between devices: 0.01 us -> 11.8 us  [on_device(): lax.all_to_all(sending, 'seq', split_axis=0, concat_axis=0, tiled=True)]
    ppermute x13, waiting for transfers between devices: 35 us -> 24.1 us  [permute(): return lax.ppermute(operand, AXES, pairs)]
    all_to_all x1, starting transfers between devices: 8.91 us -> 4.78 us  [on_device(): lax.all_to_all(returning, 'seq', split_axis=0, concat_axis=0, tiled=True)]
    ppermute x13, starting transfers between devices: 40.4 us -> 43.7 us  [permute(): return lax.ppermute(operand, AXES, pairs)]
    unnamed x14 -> x8, local copies, waits for them, and re-layouts: 3.15 us -> 1.06 us
where the time goes in v6:
time: 128 us; the launch traced here: 127 us
  starting transfers between devices  60.5 us (47%)
  waiting for transfers between devices  40.6 us (32%)
  Pallas kernels  22.9 us (18%)
  local copies, waits for them, and re-layouts  2.37 us (2%)
    ppermute x13, starting transfers between devices, permute(): return lax.ppermute(operand, AXES, pairs)  43.7 us
    ppermute x13, waiting for transfers between devices, permute(): return lax.ppermute(operand, AXES, pairs)  24.1 us
    all_to_all x1, starting transfers between devices, on_device(): lax.all_to_all(sending, 'seq', split_axis=0, concat_axis=0, tiled=True)  12 us
    all_to_all x1, waiting for transfers between devices, on_device(): lax.all_to_all(sending, 'seq', split_axis=0, concat_axis=0, tiled=True)  11.8 us
    pallas_call x1, Pallas kernels, attend_whole(): pl.pallas_call(whole_kernel, grid=(steps,), in_specs=[pl.BlockSpec((N_SEQ...  7.63 us
    pallas_call x1, Pallas kernels, project(): pl.pallas_call(project_kernel, grid_spec=pltpu.PrefetchScalarGridSpec(num...  5.35 us
    pallas_call x1, Pallas kernels, attend_shared(): pl.pallas_call(shared_kernel, grid_spec=pltpu.PrefetchScalarGridSpec(num_...  5.28 us
    all_to_all x1, starting transfers between devices, on_device(): lax.all_to_all(returning, 'seq', split_axis=0, concat_axis=0, tiled=True)  4.78 us
  transfers between devices with their start and end apart: 15, of which 7 were waited for; matrix products, arithmetic and copies ran while one was open for 1% of the time, Pallas kernels for 11%

profile of v6, /device:TPU:1, one launch (start us, length us, event | category | flops | bytes accessed | tf_op | source)
XLA Modules:
  0.0 127.4 jit_solution(11689833424496199161)
XLA Ops:
  0.6 2.9 %pack.1 = bf16[16,592,128]{2,1,0:T(8,128)(2,1)} custom-call(s32[1,112]{1,0:T(1,128)} %bitcast.10, s32[1,16]{1,0:T(1,128)} %bitcast.11, bf16[112,9216]{1,0:T(8,128)(2,1)} %vv.1, bf16[112,9216]{1,0:T(8,128)(2,1)} %vv.1, bf16[112,9216]{1,0:T(8,128)(2,1)} %vv.1, bf16[16,9216]{1,0:T(8,128)(2,1)} %tv.1, bf16[16,9216]{1,0:T(8,128)(2,1)} %tv.1, bf16[16,9216]{1,0:T(8,128)(2,1)} %tv.1), custom_call_target="tpu_custom_call" | custom-call | tf_op jit(solution)/shard_map/pack/pallas_call | solution.py:66
  3.6 12.0 %all-to-all-start = ((bf16[16,592,128]{2,1,0:T(8,128)(2,1)}), bf16[16,592,128]{2,1,0:T(8,128)(2,1)S(1)}, u32[]{:S(2)}, u32[]{:S(2)}) async-start(bf16[16,592,128]{2,1,0:T(8,128)(2,1)} %pack.1), calls=%async_computation | async-start | bytes 4849664 | tf_op jit(solution)/shard_map/all_to_all | solution.py:433
  15.5 4.4 %collective-permute-start = (bf16[96,1536]{1,0:T(8,128)(2,1)S(1)}, bf16[96,1536]{1,0:T(8,128)(2,1)S(1)}, u32[]{:S(2)}, u32[]{:S(2)}) collective-permute-start(bf16[96,1536]{1,0:T(8,128)(2,1)S(1)} %copy-done.2), channel_id=1, source_target_pairs={{0,16},{1,49},{2,18},{3,51},{4,20},{5,53},{6,22},{7,55},{8,24},{9,... | collective-permute-start | bytes 884744 | tf_op jit(solution)/shard_map/ppermute | solution.py:399
  19.9 0.7 collective-permute-start.2
  20.7 0.1 copy.11
  20.8 0.1 add_reduce_fusion
  20.9 2.7 %collective-permute-done.near = bf16[96,1536]{1,0:T(8,128)(2,1)S(1)} collective-permute-done((bf16[96,1536]{1,0:T(8,128)(2,1)S(1)}, bf16[96,1536]{1,0:T(8,128)(2,1)S(1)}, u32[]{:S(2)}, u32[]{:S(2)}) %collective-permute-start) | collective-permute-done | bytes 294944 | tf_op jit(solution)/shard_map/ppermute | solution.py:399
  23.6 3.8 %collective-permute-start.1 = (bf16[96,1536]{1,0:T(8,128)(2,1)S(1)}, bf16[96,1536]{1,0:T(8,128)(2,1)}, u32[]{:S(2)}, u32[]{:S(2)}) collective-permute-start(bf16[96,1536]{1,0:T(8,128)(2,1)S(1)} %collective-permute-done.near), channel_id=1, source_target_pairs={{0,1},{1,0},{2,3},{3,2},{4,5},{5,4},{6,7},{7,6},{8,9},{9,8},{10,11... | collective-permute-start | bytes 884744 | tf_op jit(solution)/shard_map/ppermute | solution.py:399
  27.4 1.3 %collective-permute-start.3 = (bf16[96,1536]{1,0:T(8,128)(2,1)S(1)}, bf16[96,1536]{1,0:T(8,128)(2,1)}, u32[]{:S(2)}, u32[]{:S(2)}) collective-permute-start(bf16[96,1536]{1,0:T(8,128)(2,1)S(1)} %collective-permute-done.2.part), channel_id=1, source_target_pairs={{0,1},{2,3},{4,5},{6,7},{8,9},{10,11},{12,13},{14,15},{16,17},{18,... | collective-permute-start | bytes 884744 | tf_op jit(solution)/shard_map/ppermute | solution.py:399
  28.7 0.1 fusion
  28.9 3.2 %collective-permute-done.3.part_far = bf16[96,1536]{1,0:T(8,128)(2,1)} collective-permute-done((bf16[96,1536]{1,0:T(8,128)(2,1)S(1)}, bf16[96,1536]{1,0:T(8,128)(2,1)}, u32[]{:S(2)}, u32[]{:S(2)}) %collective-permute-start.3) | collective-permute-done | bytes 294944 | tf_op jit(solution)/shard_map/ppermute | solution.py:399
  32.1 1.7 %place.1 = bf16[4,96,1536]{2,1,0:T(8,128)(2,1)S(1)} custom-call(s32[7]{0:T(128)S(1)} %concatenate.3.where, bf16[96,1536]{1,0:T(8,128)(2,1)S(1)} %copy-done.2, bf16[96,1536]{1,0:T(8,128)(2,1)S(1)} %collective-permute-done.near, bf16[96,1536]{1,0:T(8,128)(2,1)} %collective-permute-done.1.near_far, bf16[96,1536]{1,0:T(8,128)(2,1)S(1)} %collective-permute-done.2.part, ...), custom_call_target="tpu_custom_call" | custom-call | tf_op jit(solution)/shard_map/place/pallas_call | solution.py:286
  33.8 5.1 %collective-permute-start.4 = (bf16[384,1536]{1,0:T(8,128)(2,1)S(1)}, bf16[384,1536]{1,0:T(8,128)(2,1)}, u32[]{:S(2)}, u32[]{:S(2)}) collective-permute-start(bf16[384,1536]{1,0:T(8,128)(2,1)S(1)} %bitcast.8), channel_id=1, source_target_pairs={{0,64},{1,449},{2,66},{3,451},{4,68},{5,453},{6,70},{7,455},{8,72}... | collective-permute-start | bytes 3538952 | tf_op jit(solution)/shard_map/ppermute | solution.py:399
  38.9 1.0 copy-done
  39.9 12.1 %collective-permute-done.4.refs_1_ = bf16[384,1536]{1,0:T(8,128)(2,1)} collective-permute-done((bf16[384,1536]{1,0:T(8,128)(2,1)S(1)}, bf16[384,1536]{1,0:T(8,128)(2,1)}, u32[]{:S(2)}, u32[]{:S(2)}) %collective-permute-start.4) | collective-permute-done | bytes 1179680 | tf_op jit(solution)/shard_map/ppermute | solution.py:399
  52.0 3.5 %collective-permute-start.5 = (bf16[384,1536]{1,0:T(8,128)(2,1)}, bf16[384,1536]{1,0:T(8,128)(2,1)}, u32[]{:S(2)}, u32[]{:S(2)}) collective-permute-start(bf16[384,1536]{1,0:T(8,128)(2,1)} %collective-permute-done.4.refs_1_), channel_id=1, source_target_pairs={{0,1},{1,0},{2,3},{3,2},{4,5},{5,4},{6,7},{7,6},{8,9},{9,8},{10,11... | collective-permute-start | bytes 3538952 | tf_op jit(solution)/shard_map/ppermute | solution.py:399
  55.5 3.8 %collective-permute-start.7 = (bf16[384,1536]{1,0:T(8,128)(2,1)}, bf16[384,1536]{1,0:T(8,128)(2,1)}, u32[]{:S(2)}, u32[]{:S(2)}) collective-permute-start(bf16[384,1536]{1,0:T(8,128)(2,1)} %collective-permute-done.4.refs_1_), channel_id=1, source_target_pairs={{0,64},{1,449},{2,66},{3,451},{4,68},{5,453},{6,70},{7,455},{8,72}... | collective-permute-start | bytes 3538952 | tf_op jit(solution)/shard_map/ppermute | solution.py:399
  59.3 11.8 %all-to-all-done.cut.q.k.v = bf16[16,592,128]{2,1,0:T(8,128)(2,1)S(1)} async-done(((bf16[16,592,128]{2,1,0:T(8,128)(2,1)}), bf16[16,592,128]{2,1,0:T(8,128)(2,1)S(1)}, u32[]{:S(2)}, u32[]{:S(2)}) %all-to-all-start) | async-done | bytes 2424864 | tf_op jit(solution)/shard_map/all_to_all | solution.py:433
  71.2 2.8 %collective-permute-start.6 = (bf16[16,128,128]{2,1,0:T(8,128)(2,1)S(1)}, bf16[16,128,128]{2,1,0:T(8,128)(2,1)S(1)}, u32[]{:S(2)}, u32[]{:S(2)}) collective-permute-start(bf16[16,128,128]{2,1,0:T(8,128)(2,1)S(1)} %slice.3.own_kv), channel_id=1, source_target_pairs={{0,1},{1,0},{2,3},{3,2},{4,5},{5,4},{6,7},{7,6},{8,9},{9,8},{10,11... | collective-permute-start | bytes 1572872 | tf_op jit(solution)/shard_map/ppermute | solution.py:399
  74.0 7.6 %attend_whole.1 = (bf16[16,128,128]{2,1,0:T(8,128)(2,1)S(1)}, f32[16,128]{1,0:T(8,128)S(1)}) custom-call(bf16[16,592,128]{2,1,0:T(8,128)(2,1)S(1)} %all-to-all-done.cut.q.k.v, bf16[16,592,128]{2,1,0:T(8,128)(2,1)S(1)} %all-to-all-done.cut.q.k.v, bf16[16,592,128]{2,1,0:T(8,128)(2,1)S(1)} %all-to-all-done.cut.q.k.v, ...), custom_call_target="tpu_custom_call" | custom-call | flops 134217728 | bytes 2097152 | tf_op jit(solution)/shard_map/attend_whole/pallas_call | solution.py:218
  81.6 5.1 %collective-permute-start.8 = (bf16[384,1536]{1,0:T(8,128)(2,1)}, bf16[384,1536]{1,0:T(8,128)(2,1)}, u32[]{:S(2)}, u32[]{:S(2)}) collective-permute-start(bf16[384,1536]{1,0:T(8,128)(2,1)} %collective-permute-done.7.refs_2_), channel_id=1, source_target_pairs={{0,64},{1,449},{2,66},{3,451},{4,68},{5,453},{6,70},{7,455},{8,72}... | collective-permute-start | bytes 3538952 | tf_op jit(solution)/shard_map/ppermute | solution.py:399
  86.7 5.3 %attend_shared.1 = bf16[16,224,128]{2,1,0:T(8,128)(2,1)} custom-call(s32[7]{0:T(128)S(1)} %concatenate.3.where, bf16[16,592,128]{2,1,0:T(8,128)(2,1)S(1)} %all-to-all-done.cut.q.k.v, bf16[16,592,128]{2,1,0:T(8,128)(2,1)S(1)} %all-to-all-done.cut.q.k.v, bf16[16,128,128]{2,1,0:T(8,128)(2,1)S(1)} %slice.3.own_kv, ...), custom_call_target="tpu_custom_call" | custom-call | flops 67108864 | bytes 2097152 | tf_op jit(solution)/shard_map/attend_shared/pallas_call | solution.py:245
  92.0 4.8 %all-to-all-start.1 = ((bf16[16,224,128]{2,1,0:T(8,128)(2,1)}), bf16[16,224,128]{2,1,0:T(8,128)(2,1)S(1)}, u32[]{:S(2)}, u32[]{:S(2)}) async-start(bf16[16,224,128]{2,1,0:T(8,128)(2,1)} %attend_shared.1), calls=%async_computation.1 | async-start | bytes 1835008 | tf_op jit(solution)/shard_map/all_to_all | solution.py:446
  96.8 2.0 %collective-permute-start.9 = (bf16[384,1536]{1,0:T(8,128)(2,1)}, bf16[384,1536]{1,0:T(8,128)(2,1)}, u32[]{:S(2)}, u32[]{:S(2)}) collective-permute-start(bf16[384,1536]{1,0:T(8,128)(2,1)} %collective-permute-done.7.refs_2_), channel_id=1, source_target_pairs={{0,1},{1,0},{2,3},{3,2},{4,5},{5,4},{6,7},{7,6},{8,9},{9,8},{10,11... | collective-permute-start | bytes 3538952 | tf_op jit(solution)/shard_map/ppermute | solution.py:399
  98.8 1.4 %collective-permute-done.8.refs_3_ = bf16[384,1536]{1,0:T(8,128)(2,1)} collective-permute-done((bf16[384,1536]{1,0:T(8,128)(2,1)}, bf16[384,1536]{1,0:T(8,128)(2,1)}, u32[]{:S(2)}, u32[]{:S(2)}) %collective-permute-start.8) | collective-permute-done | bytes 1179680 | tf_op jit(solution)/shard_map/ppermute | solution.py:399
  100.2 1.1 constant_dynamic-slice_fusion
  101.3 5.2 %collective-permute-start.11 = (bf16[384,768]{1,0:T(8,128)(2,1)S(1)}, bf16[384,768]{1,0:T(8,128)(2,1)S(1)}, u32[]{:S(2)}, u32[]{:S(2)}) collective-permute-start(bf16[384,768]{1,0:T(8,128)(2,1)S(1)} %constant_dynamic-slice_fusion), channel_id=1, source_target_pairs={{0,64},{1,449},{2,66},{3,451},{4,68},{5,453},{6,70},{7,455},{8,72}... | collective-permute-start | bytes 1769480 | tf_op jit(solution)/shard_map/ppermute | solution.py:399
  106.5 1.9 %collective-permute-start.10 = (bf16[384,1536]{1,0:T(8,128)(2,1)}, bf16[384,1536]{1,0:T(8,128)(2,1)}, u32[]{:S(2)}, u32[]{:S(2)}) collective-permute-start(bf16[384,1536]{1,0:T(8,128)(2,1)} %collective-permute-done.8.refs_3_), channel_id=1, source_target_pairs={{0,1},{1,0},{2,3},{3,2},{4,5},{5,4},{6,7},{7,6},{8,9},{9,8},{10,11... | collective-permute-start | bytes 3538952 | tf_op jit(solution)/shard_map/ppermute | solution.py:399
  108.4 4.9 %collective-permute-done.11.refs_7_ = bf16[384,768]{1,0:T(8,128)(2,1)S(1)} collective-permute-done((bf16[384,768]{1,0:T(8,128)(2,1)S(1)}, bf16[384,768]{1,0:T(8,128)(2,1)S(1)}, u32[]{:S(2)}, u32[]{:S(2)}) %collective-permute-start.11) | collective-permute-done | bytes 589856 | tf_op jit(solution)/shard_map/ppermute | solution.py:399
  113.3 4.2 %collective-permute-start.12 = (bf16[384,768]{1,0:T(8,128)(2,1)S(1)}, bf16[384,768]{1,0:T(8,128)(2,1)S(1)}, u32[]{:S(2)}, u32[]{:S(2)}) collective-permute-start(bf16[384,768]{1,0:T(8,128)(2,1)S(1)} %collective-permute-done.11.refs_7_), channel_id=1, source_target_pairs={{0,1},{1,0},{2,3},{3,2},{4,5},{5,4},{6,7},{7,6},{8,9},{9,8},{10,11... | collective-permute-start | bytes 1769480 | tf_op jit(solution)/shard_map/ppermute | solution.py:399
  117.5 4.6 %all-to-all-done.1.ret = bf16[16,224,128]{2,1,0:T(8,128)(2,1)S(1)} async-done(((bf16[16,224,128]{2,1,0:T(8,128)(2,1)}), bf16[16,224,128]{2,1,0:T(8,128)(2,1)S(1)}, u32[]{:S(2)}, u32[]{:S(2)}) %all-to-all-start.1) | async-done | bytes 917536 | tf_op jit(solution)/shard_map/all_to_all | solution.py:446
  122.1 5.4 %project.1 = (bf16[112,1536]{1,0:T(8,128)(2,1)}, bf16[16,3072]{1,0:T(8,128)(2,1)}, f32[2,2048]{1,0:T(2,128)}) custom-call(s32[7]{0:T(128)S(1)} %concatenate.3.where, bf16[16,224,128]{2,1,0:T(8,128)(2,1)S(1)} %all-to-all-done.1.ret, bf16[384,1536]{1,0:T(8,128)(2,1)S(1)} %bitcast.9, bf16[384,1536]{1,0:T(8,128)(2,1)} %collective-permute-done.4.refs_1_, ...), custom_call_target="tpu_custom_call" | custom-call | tf_op jit(solution)/shard_map/project/pallas_call | solution.py:363
  (20 shorter events, 0.2 us)
Async XLA Ops:
  3.6 12.0 %copy-start.2 = (bf16[96,1536]{1,0:T(8,128)(2,1)S(1)}, bf16[96,1536]{1,0:T(8,128)(2,1)}, u32[]{:S(2)}) copy-start(bf16[96,1536]{1,0:T(8,128)(2,1)} %mine.1) | copy-start | bytes 884740
  3.6 17.1 %copy-start.3 = (s32[24]{0:T(128)S(1)}, s32[24]{0:T(128)}, u32[]{:S(2)}) copy-start(s32[24]{0:T(128)} %param.10) | copy-start | bytes 292
  3.6 67.6 %all-to-all-start = ((bf16[16,592,128]{2,1,0:T(8,128)(2,1)}), bf16[16,592,128]{2,1,0:T(8,128)(2,1)S(1)}, u32[]{:S(2)}, u32[]{:S(2)}) async-start(bf16[16,592,128]{2,1,0:T(8,128)(2,1)} %pack.1), calls=%async_computation | async-start | bytes 4849664 | tf_op jit(solution)/shard_map/all_to_all | solution.py:433
  15.5 8.0 %collective-permute-start = (bf16[96,1536]{1,0:T(8,128)(2,1)S(1)}, bf16[96,1536]{1,0:T(8,128)(2,1)S(1)}, u32[]{:S(2)}, u32[]{:S(2)}) collective-permute-start(bf16[96,1536]{1,0:T(8,128)(2,1)S(1)} %copy-done.2), channel_id=1, source_target_pairs={{0,16},{1,49},{2,18},{3,51},{4,20},{5,53},{6,22},{7,55},{8,24},{9,... | collective-permute-start | bytes 884744 | tf_op jit(solution)/shard_map/ppermute | solution.py:399
  19.9 7.4 %collective-permute-start.2 = (bf16[96,1536]{1,0:T(8,128)(2,1)S(1)}, bf16[96,1536]{1,0:T(8,128)(2,1)S(1)}, u32[]{:S(2)}, u32[]{:S(2)}) collective-permute-start(bf16[96,1536]{1,0:T(8,128)(2,1)S(1)} %copy-done.2), channel_id=1, source_target_pairs={{0,32},{2,34},{4,36},{6,38},{8,40},{10,42},{12,44},{14,46},{16,48}... | collective-permute-start | bytes 884744 | tf_op jit(solution)/shard_map/ppermute | solution.py:399
  23.6 5.3 %collective-permute-start.1 = (bf16[96,1536]{1,0:T(8,128)(2,1)S(1)}, bf16[96,1536]{1,0:T(8,128)(2,1)}, u32[]{:S(2)}, u32[]{:S(2)}) collective-permute-start(bf16[96,1536]{1,0:T(8,128)(2,1)S(1)} %collective-permute-done.near), channel_id=1, source_target_pairs={{0,1},{1,0},{2,3},{3,2},{4,5},{5,4},{6,7},{7,6},{8,9},{9,8},{10,11... | collective-permute-start | bytes 884744 | tf_op jit(solution)/shard_map/ppermute | solution.py:399
  27.4 4.7 %collective-permute-start.3 = (bf16[96,1536]{1,0:T(8,128)(2,1)S(1)}, bf16[96,1536]{1,0:T(8,128)(2,1)}, u32[]{:S(2)}, u32[]{:S(2)}) collective-permute-start(bf16[96,1536]{1,0:T(8,128)(2,1)S(1)} %collective-permute-done.2.part), channel_id=1, source_target_pairs={{0,1},{2,3},{4,5},{6,7},{8,9},{10,11},{12,13},{14,15},{16,17},{18,... | collective-permute-start | bytes 884744 | tf_op jit(solution)/shard_map/ppermute | solution.py:399
  33.8 18.2 %collective-permute-start.4 = (bf16[384,1536]{1,0:T(8,128)(2,1)S(1)}, bf16[384,1536]{1,0:T(8,128)(2,1)}, u32[]{:S(2)}, u32[]{:S(2)}) collective-permute-start(bf16[384,1536]{1,0:T(8,128)(2,1)S(1)} %bitcast.8), channel_id=1, source_target_pairs={{0,64},{1,449},{2,66},{3,451},{4,68},{5,453},{6,70},{7,455},{8,72}... | collective-permute-start | bytes 3538952 | tf_op jit(solution)/shard_map/ppermute | solution.py:399
  38.9 1.1 copy-start
  52.0 7.2 %collective-permute-start.5 = (bf16[384,1536]{1,0:T(8,128)(2,1)}, bf16[384,1536]{1,0:T(8,128)(2,1)}, u32[]{:S(2)}, u32[]{:S(2)}) collective-permute-start(bf16[384,1536]{1,0:T(8,128)(2,1)} %collective-permute-done.4.refs_1_), channel_id=1, source_target_pairs={{0,1},{1,0},{2,3},{3,2},{4,5},{5,4},{6,7},{7,6},{8,9},{9,8},{10,11... | collective-permute-start | bytes 3538952 | tf_op jit(solution)/shard_map/ppermute | solution.py:399
  55.5 26.1 %collective-permute-start.7 = (bf16[384,1536]{1,0:T(8,128)(2,1)}, bf16[384,1536]{1,0:T(8,128)(2,1)}, u32[]{:S(2)}, u32[]{:S(2)}) collective-permute-start(bf16[384,1536]{1,0:T(8,128)(2,1)} %collective-permute-done.4.refs_1_), channel_id=1, source_target_pairs={{0,64},{1,449},{2,66},{3,451},{4,68},{5,453},{6,70},{7,455},{8,72}... | collective-permute-start | bytes 3538952 | tf_op jit(solution)/shard_map/ppermute | solution.py:399
  71.2 10.4 %collective-permute-start.6 = (bf16[16,128,128]{2,1,0:T(8,128)(2,1)S(1)}, bf16[16,128,128]{2,1,0:T(8,128)(2,1)S(1)}, u32[]{:S(2)}, u32[]{:S(2)}) collective-permute-start(bf16[16,128,128]{2,1,0:T(8,128)(2,1)S(1)} %slice.3.own_kv), channel_id=1, source_target_pairs={{0,1},{1,0},{2,3},{3,2},{4,5},{5,4},{6,7},{7,6},{8,9},{9,8},{10,11... | collective-permute-start | bytes 1572872 | tf_op jit(solution)/shard_map/ppermute | solution.py:399
  81.6 18.5 %collective-permute-start.8 = (bf16[384,1536]{1,0:T(8,128)(2,1)}, bf16[384,1536]{1,0:T(8,128)(2,1)}, u32[]{:S(2)}, u32[]{:S(2)}) collective-permute-start(bf16[384,1536]{1,0:T(8,128)(2,1)} %collective-permute-done.7.refs_2_), channel_id=1, source_target_pairs={{0,64},{1,449},{2,66},{3,451},{4,68},{5,453},{6,70},{7,455},{8,72}... | collective-permute-start | bytes 3538952 | tf_op jit(solution)/shard_map/ppermute | solution.py:399
  92.0 30.1 %copy-start.1 = (bf16[4,96,1536]{2,1,0:T(8,128)(2,1)S(1)}, bf16[4,96,1536]{2,1,0:T(8,128)(2,1)}, u32[]{:S(2)}) copy-start(bf16[4,96,1536]{2,1,0:T(8,128)(2,1)} %copy-done) | copy-start | bytes 3538948
  92.0 30.1 %all-to-all-start.1 = ((bf16[16,224,128]{2,1,0:T(8,128)(2,1)}), bf16[16,224,128]{2,1,0:T(8,128)(2,1)S(1)}, u32[]{:S(2)}, u32[]{:S(2)}) async-start(bf16[16,224,128]{2,1,0:T(8,128)(2,1)} %attend_shared.1), calls=%async_computation.1 | async-start | bytes 1835008 | tf_op jit(solution)/shard_map/all_to_all | solution.py:446
  96.8 20.7 %collective-permute-start.9 = (bf16[384,1536]{1,0:T(8,128)(2,1)}, bf16[384,1536]{1,0:T(8,128)(2,1)}, u32[]{:S(2)}, u32[]{:S(2)}) collective-permute-start(bf16[384,1536]{1,0:T(8,128)(2,1)} %collective-permute-done.7.refs_2_), channel_id=1, source_target_pairs={{0,1},{1,0},{2,3},{3,2},{4,5},{5,4},{6,7},{7,6},{8,9},{9,8},{10,11... | collective-permute-start | bytes 3538952 | tf_op jit(solution)/shard_map/ppermute | solution.py:399
  101.3 12.0 %collective-permute-start.11 = (bf16[384,768]{1,0:T(8,128)(2,1)S(1)}, bf16[384,768]{1,0:T(8,128)(2,1)S(1)}, u32[]{:S(2)}, u32[]{:S(2)}) collective-permute-start(bf16[384,768]{1,0:T(8,128)(2,1)S(1)} %constant_dynamic-slice_fusion), channel_id=1, source_target_pairs={{0,64},{1,449},{2,66},{3,451},{4,68},{5,453},{6,70},{7,455},{8,72}... | collective-permute-start | bytes 1769480 | tf_op jit(solution)/shard_map/ppermute | solution.py:399
  106.5 15.6 %collective-permute-start.10 = (bf16[384,1536]{1,0:T(8,128)(2,1)}, bf16[384,1536]{1,0:T(8,128)(2,1)}, u32[]{:S(2)}, u32[]{:S(2)}) collective-permute-start(bf16[384,1536]{1,0:T(8,128)(2,1)} %collective-permute-done.8.refs_3_), channel_id=1, source_target_pairs={{0,1},{1,0},{2,3},{3,2},{4,5},{5,4},{6,7},{7,6},{8,9},{9,8},{10,11... | collective-permute-start | bytes 3538952 | tf_op jit(solution)/shard_map/ppermute | solution.py:399
  113.3 8.8 %collective-permute-start.12 = (bf16[384,768]{1,0:T(8,128)(2,1)S(1)}, bf16[384,768]{1,0:T(8,128)(2,1)S(1)}, u32[]{:S(2)}, u32[]{:S(2)}) collective-permute-start(bf16[384,768]{1,0:T(8,128)(2,1)S(1)} %collective-permute-done.11.refs_7_), channel_id=1, source_target_pairs={{0,1},{1,0},{2,3},{3,2},{4,5},{5,4},{6,7},{7,6},{8,9},{9,8},{10,11... | collective-permute-start | bytes 1769480 | tf_op jit(solution)/shard_map/ppermute | solution.py:399

commit v7 on v6

--- a/solution.py
+++ b/solution.py
@@ -18,7 +18,7 @@
 CHIPS = 8
 A_ROWS = 3 * ROWS
 SEND_ROWS = A_ROWS + 3 * HALF
-CUT_ROWS = 16
+CUT_ROWS = 8
 PAYLOAD = SEND_ROWS + CUT_ROWS
 RET_ROWS = ROWS + HALF
 WHOLE_LSE = RET_ROWS
@@ -83,19 +83,22 @@
     )
 
 
-def second_clip(cut_ref, source, row):
-    cuts = jnp.sum(cut_ref[...].astype(jnp.float32), axis=0)
-    vis_cut, txt_cut = cuts[0:1, 0:1], cuts[CUT_ROWS // 2 : CUT_ROWS // 2 + 1, 0:1]
-    vis_place = (source * VIS_ROWS + row).astype(jnp.float32)
-    txt_place = (source * TXT_ROWS + row - VIS_ROWS).astype(jnp.float32)
-    is_second = jnp.where(row < VIS_ROWS, vis_place - vis_cut, txt_place - txt_cut) >= 0.0
-    return jnp.where(is_second, 1.0, 0.0)
-
-
-def clip_columns(second, first_value, second_value):
-    lane = lax.broadcasted_iota(jnp.int32, second.shape, 1)
-    feature = jnp.where(lane == 0, first_value(second), second_value(second))
-    return jnp.where(lane < 2, feature, 0.0).astype(jnp.bfloat16)
+def clip_features(cut, first_source, count, rows, offset, value, second_lane):
+    cuts = jnp.sum(cut[...].astype(jnp.float32), axis=0)
+    vis_cut, txt_cut = cuts[0:1], cuts[CUT_ROWS // 2 : CUT_ROWS // 2 + 1]
+    row = lax.broadcasted_iota(jnp.int32, (rows, HEAD_DIM), 0) + offset
+    is_vis, row = row < VIS_ROWS, row.astype(jnp.float32)
+    behind = jnp.where(is_vis, row - vis_cut, row - VIS_ROWS - txt_cut)
+    stride = jnp.where(is_vis, float(VIS_ROWS), float(TXT_ROWS))
+    lane = lax.broadcasted_iota(jnp.int32, (1, HEAD_DIM), 1)
+    second = jnp.where(lane == second_lane, value, 0.0)
+    first = jnp.where(lane == 1 - second_lane, value, 0.0)
+    behind = behind + stride * first_source
+    pieces = []
+    for _ in range(count):
+        pieces.append(jnp.where(behind >= 0.0, second, first).astype(jnp.bfloat16))
+        behind = behind + stride
+    return jnp.concatenate(pieces, axis=0)
 
 
 def attend(queries, k_wide, v_turned, write):
@@ -121,19 +124,12 @@
         scores = upcoming
 
 
-def place_of(shape, rows, first_source, offset):
-    index = lax.broadcasted_iota(jnp.int32, shape, 0)
-    return first_source + index // rows, index % rows + offset
-
-
-def key_features(cut, keys, rows, offset):
-    second = second_clip(cut, *place_of((keys, HEAD_DIM), rows, 0, offset))
-    return clip_columns(second, lambda s: BIG * s, lambda s: BIG * (1.0 - s))
-
-
-def query_features(cut, count, rows, first_source, offset):
-    second = second_clip(cut, *place_of((count, HEAD_DIM), rows, first_source, offset))
-    return clip_columns(second, lambda s: 1.0 - s, lambda s: s)
+def key_features(cut, rows, offset):
+    return clip_features(cut, 0.0, N_SEQ, rows, offset, BIG, 0)
+
+
+def query_features(cut, first_source, rows, offset):
+    return clip_features(cut, first_source, STEP_ROWS // rows, rows, offset, 1.0, 1)
 
 
 def whole_kernel(cut, q, k, v, out, lse, k_wide, v_turned, q_wide):
@@ -144,11 +140,11 @@
     @pl.when(step == 0)
     def _():
         k_wide[:, :HEAD_DIM] = k[...].reshape(keys, HEAD_DIM)
-        k_wide[:, HEAD_DIM:] = key_features(cut, keys, ROWS, 0)
+        k_wide[:, HEAD_DIM:] = key_features(cut, ROWS, 0)
         v_turned[...] = jnp.swapaxes(v[...].reshape(keys, HEAD_DIM), 0, 1)
 
     q_wide[:, :HEAD_DIM] = q[...].reshape(STEP_ROWS, HEAD_DIM)
-    q_wide[:, HEAD_DIM:] = query_features(cut, STEP_ROWS, ROWS, step * sources, 0)
+    q_wide[:, HEAD_DIM:] = query_features(cut, (step * sources).astype(jnp.float32), ROWS, 0)
 
     def write(block, result, log_total):
         count = Q_ROWS // ROWS
@@ -167,10 +163,10 @@
     for place, (kv, offset) in enumerate(((own_kv, HALF * core), (far_kv, HALF * (1 - core)))):
         at = slice(place * keys, (place + 1) * keys)
         k_wide[at, :HEAD_DIM] = kv[:, :HALF].reshape(keys, HEAD_DIM)
-        k_wide[at, HEAD_DIM:] = key_features(cut, keys, HALF, offset)
+        k_wide[at, HEAD_DIM:] = key_features(cut, HALF, offset)
         v_turned[:, at] = jnp.swapaxes(kv[:, HALF:].reshape(keys, HEAD_DIM), 0, 1)
     q_wide[:, :HEAD_DIM] = q[...].reshape(STEP_ROWS, HEAD_DIM)
-    q_wide[:, HEAD_DIM:] = query_features(cut, STEP_ROWS, HALF, 0, HALF * core)
+    q_wide[:, HEAD_DIM:] = query_features(cut, 0.0, HALF, HALF * core)
     log_totals = []
 
     def write(block, result, log_total):

time: 128 us -> 126 us (0.984)
  Pallas kernels: 22.9 us -> 21.5 us
where the time goes in v7:
time: 126 us; the launch traced here: 125 us
  starting transfers between devices  60.4 us (48%)
  waiting for transfers between devices  40 us (32%)
  Pallas kernels  21.5 us (17%)
  local copies, waits for them, and re-layouts  2.37 us (2%)
    ppermute x13, starting transfers between devices, permute(): return lax.ppermute(operand, AXES, pairs)  43.6 us
    ppermute x13, waiting for transfers between devices, permute(): return lax.ppermute(operand, AXES, pairs)  24.6 us
    all_to_all x1, starting transfers between devices, on_device(): lax.all_to_all(sending, 'seq', split_axis=0, concat_axis=0, tiled=True)  12 us
    all_to_all x1, waiting for transfers between devices, on_device(): lax.all_to_all(sending, 'seq', split_axis=0, concat_axis=0, tiled=True)  11.2 us
    pallas_call x1, Pallas kernels, attend_whole(): pl.pallas_call(whole_kernel, grid=(steps,), in_specs=[pl.BlockSpec((N_SEQ...  6.82 us
    pallas_call x1, Pallas kernels, project(): pl.pallas_call(project_kernel, grid_spec=pltpu.PrefetchScalarGridSpec(num...  5.34 us
    all_to_all x1, starting transfers between devices, on_device(): lax.all_to_all(returning, 'seq', split_axis=0, concat_axis=0, tiled=True)  4.79 us
    pallas_call x1, Pallas kernels, attend_shared(): pl.pallas_call(shared_kernel, grid_spec=pltpu.PrefetchScalarGridSpec(num_...  4.78 us
  transfers between devices with their start and end apart: 15, of which 7 were waited for; matrix products, arithmetic and copies ran while one was open for 1% of the time, Pallas kernels for 11%

profile of v7, /device:TPU:1, one launch (start us, length us, event | category | flops | bytes accessed | tf_op | source)
XLA Modules:
  0.0 125.4 jit_solution(14132902509255247792)
XLA Ops:
  0.6 2.9 %pack.1 = bf16[16,584,128]{2,1,0:T(8,128)(2,1)} custom-call(s32[1,112]{1,0:T(1,128)} %bitcast.10, s32[1,16]{1,0:T(1,128)} %bitcast.11, bf16[112,9216]{1,0:T(8,128)(2,1)} %vv.1, bf16[112,9216]{1,0:T(8,128)(2,1)} %vv.1, bf16[112,9216]{1,0:T(8,128)(2,1)} %vv.1, bf16[16,9216]{1,0:T(8,128)(2,1)} %tv.1, bf16[16,9216]{1,0:T(8,128)(2,1)} %tv.1, bf16[16,9216]{1,0:T(8,128)(2,1)} %tv.1), custom_call_target="tpu_custom_call" | custom-call | tf_op jit(solution)/shard_map/pack/pallas_call | solution.py:66
  3.5 12.0 %all-to-all-start = ((bf16[16,584,128]{2,1,0:T(8,128)(2,1)}), bf16[16,584,128]{2,1,0:T(8,128)(2,1)S(1)}, u32[]{:S(2)}, u32[]{:S(2)}) async-start(bf16[16,584,128]{2,1,0:T(8,128)(2,1)} %pack.1), calls=%async_computation | async-start | bytes 4784128 | tf_op jit(solution)/shard_map/all_to_all | solution.py:429
  15.5 4.4 %collective-permute-start = (bf16[96,1536]{1,0:T(8,128)(2,1)S(1)}, bf16[96,1536]{1,0:T(8,128)(2,1)S(1)}, u32[]{:S(2)}, u32[]{:S(2)}) collective-permute-start(bf16[96,1536]{1,0:T(8,128)(2,1)S(1)} %copy-done.2), channel_id=1, source_target_pairs={{0,16},{1,49},{2,18},{3,51},{4,20},{5,53},{6,22},{7,55},{8,24},{9,... | collective-permute-start | bytes 884744 | tf_op jit(solution)/shard_map/ppermute | solution.py:395
  19.9 0.7 collective-permute-start.2
  20.7 0.1 copy.11
  20.8 0.1 add_reduce_fusion
  20.9 2.7 %collective-permute-done.near = bf16[96,1536]{1,0:T(8,128)(2,1)S(1)} collective-permute-done((bf16[96,1536]{1,0:T(8,128)(2,1)S(1)}, bf16[96,1536]{1,0:T(8,128)(2,1)S(1)}, u32[]{:S(2)}, u32[]{:S(2)}) %collective-permute-start) | collective-permute-done | bytes 294944 | tf_op jit(solution)/shard_map/ppermute | solution.py:395
  23.6 3.8 %collective-permute-start.1 = (bf16[96,1536]{1,0:T(8,128)(2,1)S(1)}, bf16[96,1536]{1,0:T(8,128)(2,1)}, u32[]{:S(2)}, u32[]{:S(2)}) collective-permute-start(bf16[96,1536]{1,0:T(8,128)(2,1)S(1)} %collective-permute-done.near), channel_id=1, source_target_pairs={{0,1},{1,0},{2,3},{3,2},{4,5},{5,4},{6,7},{7,6},{8,9},{9,8},{10,11... | collective-permute-start | bytes 884744 | tf_op jit(solution)/shard_map/ppermute | solution.py:395
  27.4 1.3 %collective-permute-start.3 = (bf16[96,1536]{1,0:T(8,128)(2,1)S(1)}, bf16[96,1536]{1,0:T(8,128)(2,1)}, u32[]{:S(2)}, u32[]{:S(2)}) collective-permute-start(bf16[96,1536]{1,0:T(8,128)(2,1)S(1)} %collective-permute-done.2.part), channel_id=1, source_target_pairs={{0,1},{2,3},{4,5},{6,7},{8,9},{10,11},{12,13},{14,15},{16,17},{18,... | collective-permute-start | bytes 884744 | tf_op jit(solution)/shard_map/ppermute | solution.py:395
  28.7 0.1 fusion
  28.9 3.2 %collective-permute-done.3.part_far = bf16[96,1536]{1,0:T(8,128)(2,1)} collective-permute-done((bf16[96,1536]{1,0:T(8,128)(2,1)S(1)}, bf16[96,1536]{1,0:T(8,128)(2,1)}, u32[]{:S(2)}, u32[]{:S(2)}) %collective-permute-start.3) | collective-permute-done | bytes 294944 | tf_op jit(solution)/shard_map/ppermute | solution.py:395
  32.1 1.7 %place.1 = bf16[4,96,1536]{2,1,0:T(8,128)(2,1)S(1)} custom-call(s32[7]{0:T(128)S(1)} %concatenate.3.where, bf16[96,1536]{1,0:T(8,128)(2,1)S(1)} %copy-done.2, bf16[96,1536]{1,0:T(8,128)(2,1)S(1)} %collective-permute-done.near, bf16[96,1536]{1,0:T(8,128)(2,1)} %collective-permute-done.1.near_far, bf16[96,1536]{1,0:T(8,128)(2,1)S(1)} %collective-permute-done.2.part, ...), custom_call_target="tpu_custom_call" | custom-call | tf_op jit(solution)/shard_map/place/pallas_call | solution.py:282
  33.8 5.1 %collective-permute-start.4 = (bf16[384,1536]{1,0:T(8,128)(2,1)S(1)}, bf16[384,1536]{1,0:T(8,128)(2,1)}, u32[]{:S(2)}, u32[]{:S(2)}) collective-permute-start(bf16[384,1536]{1,0:T(8,128)(2,1)S(1)} %bitcast.8), channel_id=1, source_target_pairs={{0,64},{1,449},{2,66},{3,451},{4,68},{5,453},{6,70},{7,455},{8,72}... | collective-permute-start | bytes 3538952 | tf_op jit(solution)/shard_map/ppermute | solution.py:395
  38.9 1.0 copy-done
  39.9 12.1 %collective-permute-done.4.refs_1_ = bf16[384,1536]{1,0:T(8,128)(2,1)} collective-permute-done((bf16[384,1536]{1,0:T(8,128)(2,1)S(1)}, bf16[384,1536]{1,0:T(8,128)(2,1)}, u32[]{:S(2)}, u32[]{:S(2)}) %collective-permute-start.4) | collective-permute-done | bytes 1179680 | tf_op jit(solution)/shard_map/ppermute | solution.py:395
  52.0 3.5 %collective-permute-start.5 = (bf16[384,1536]{1,0:T(8,128)(2,1)}, bf16[384,1536]{1,0:T(8,128)(2,1)}, u32[]{:S(2)}, u32[]{:S(2)}) collective-permute-start(bf16[384,1536]{1,0:T(8,128)(2,1)} %collective-permute-done.4.refs_1_), channel_id=1, source_target_pairs={{0,1},{1,0},{2,3},{3,2},{4,5},{5,4},{6,7},{7,6},{8,9},{9,8},{10,11... | collective-permute-start | bytes 3538952 | tf_op jit(solution)/shard_map/ppermute | solution.py:395
  55.5 3.8 %collective-permute-start.7 = (bf16[384,1536]{1,0:T(8,128)(2,1)}, bf16[384,1536]{1,0:T(8,128)(2,1)}, u32[]{:S(2)}, u32[]{:S(2)}) collective-permute-start(bf16[384,1536]{1,0:T(8,128)(2,1)} %collective-permute-done.4.refs_1_), channel_id=1, source_target_pairs={{0,64},{1,449},{2,66},{3,451},{4,68},{5,453},{6,70},{7,455},{8,72}... | collective-permute-start | bytes 3538952 | tf_op jit(solution)/shard_map/ppermute | solution.py:395
  59.3 11.2 %all-to-all-done.cut.q.k.v = bf16[16,584,128]{2,1,0:T(8,128)(2,1)S(1)} async-done(((bf16[16,584,128]{2,1,0:T(8,128)(2,1)}), bf16[16,584,128]{2,1,0:T(8,128)(2,1)S(1)}, u32[]{:S(2)}, u32[]{:S(2)}) %all-to-all-start) | async-done | bytes 2392096 | tf_op jit(solution)/shard_map/all_to_all | solution.py:429
  70.6 2.7 %collective-permute-start.6 = (bf16[16,128,128]{2,1,0:T(8,128)(2,1)S(1)}, bf16[16,128,128]{2,1,0:T(8,128)(2,1)S(1)}, u32[]{:S(2)}, u32[]{:S(2)}) collective-permute-start(bf16[16,128,128]{2,1,0:T(8,128)(2,1)S(1)} %slice.3.own_kv), channel_id=1, source_target_pairs={{0,1},{1,0},{2,3},{3,2},{4,5},{5,4},{6,7},{7,6},{8,9},{9,8},{10,11... | collective-permute-start | bytes 1572872 | tf_op jit(solution)/shard_map/ppermute | solution.py:395
  73.2 6.8 %attend_whole.1 = (bf16[16,128,128]{2,1,0:T(8,128)(2,1)S(1)}, f32[16,128]{1,0:T(8,128)S(1)}) custom-call(bf16[16,584,128]{2,1,0:T(8,128)(2,1)S(1)} %all-to-all-done.cut.q.k.v, bf16[16,584,128]{2,1,0:T(8,128)(2,1)S(1)} %all-to-all-done.cut.q.k.v, bf16[16,584,128]{2,1,0:T(8,128)(2,1)S(1)} %all-to-all-done.cut.q.k.v, ...), custom_call_target="tpu_custom_call" | custom-call | flops 134217728 | bytes 2097152 | tf_op jit(solution)/shard_map/attend_whole/pallas_call | solution.py:214
  80.1 5.1 %collective-permute-start.8 = (bf16[384,1536]{1,0:T(8,128)(2,1)}, bf16[384,1536]{1,0:T(8,128)(2,1)}, u32[]{:S(2)}, u32[]{:S(2)}) collective-permute-start(bf16[384,1536]{1,0:T(8,128)(2,1)} %collective-permute-done.7.refs_2_), channel_id=1, source_target_pairs={{0,64},{1,449},{2,66},{3,451},{4,68},{5,453},{6,70},{7,455},{8,72}... | collective-permute-start | bytes 3538952 | tf_op jit(solution)/shard_map/ppermute | solution.py:395
  85.2 4.8 %attend_shared.1 = bf16[16,224,128]{2,1,0:T(8,128)(2,1)} custom-call(s32[7]{0:T(128)S(1)} %concatenate.3.where, bf16[16,584,128]{2,1,0:T(8,128)(2,1)S(1)} %all-to-all-done.cut.q.k.v, bf16[16,584,128]{2,1,0:T(8,128)(2,1)S(1)} %all-to-all-done.cut.q.k.v, bf16[16,128,128]{2,1,0:T(8,128)(2,1)S(1)} %slice.3.own_kv, ...), custom_call_target="tpu_custom_call" | custom-call | flops 67108864 | bytes 2097152 | tf_op jit(solution)/shard_map/attend_shared/pallas_call | solution.py:241
  90.0 4.8 %all-to-all-start.1 = ((bf16[16,224,128]{2,1,0:T(8,128)(2,1)}), bf16[16,224,128]{2,1,0:T(8,128)(2,1)S(1)}, u32[]{:S(2)}, u32[]{:S(2)}) async-start(bf16[16,224,128]{2,1,0:T(8,128)(2,1)} %attend_shared.1), calls=%async_computation.1 | async-start | bytes 1835008 | tf_op jit(solution)/shard_map/all_to_all | solution.py:442
  94.8 2.0 %collective-permute-start.9 = (bf16[384,1536]{1,0:T(8,128)(2,1)}, bf16[384,1536]{1,0:T(8,128)(2,1)}, u32[]{:S(2)}, u32[]{:S(2)}) collective-permute-start(bf16[384,1536]{1,0:T(8,128)(2,1)} %collective-permute-done.7.refs_2_), channel_id=1, source_target_pairs={{0,1},{1,0},{2,3},{3,2},{4,5},{5,4},{6,7},{7,6},{8,9},{9,8},{10,11... | collective-permute-start | bytes 3538952 | tf_op jit(solution)/shard_map/ppermute | solution.py:395
  96.8 1.8 %collective-permute-done.8.refs_3_ = bf16[384,1536]{1,0:T(8,128)(2,1)} collective-permute-done((bf16[384,1536]{1,0:T(8,128)(2,1)}, bf16[384,1536]{1,0:T(8,128)(2,1)}, u32[]{:S(2)}, u32[]{:S(2)}) %collective-permute-start.8) | collective-permute-done | bytes 1179680 | tf_op jit(solution)/shard_map/ppermute | solution.py:395
  98.6 1.1 constant_dynamic-slice_fusion
  99.7 5.2 %collective-permute-start.11 = (bf16[384,768]{1,0:T(8,128)(2,1)S(1)}, bf16[384,768]{1,0:T(8,128)(2,1)S(1)}, u32[]{:S(2)}, u32[]{:S(2)}) collective-permute-start(bf16[384,768]{1,0:T(8,128)(2,1)S(1)} %constant_dynamic-slice_fusion), channel_id=1, source_target_pairs={{0,64},{1,449},{2,66},{3,451},{4,68},{5,453},{6,70},{7,455},{8,72}... | collective-permute-start | bytes 1769480 | tf_op jit(solution)/shard_map/ppermute | solution.py:395
  105.0 1.9 %collective-permute-start.10 = (bf16[384,1536]{1,0:T(8,128)(2,1)}, bf16[384,1536]{1,0:T(8,128)(2,1)}, u32[]{:S(2)}, u32[]{:S(2)}) collective-permute-start(bf16[384,1536]{1,0:T(8,128)(2,1)} %collective-permute-done.8.refs_3_), channel_id=1, source_target_pairs={{0,1},{1,0},{2,3},{3,2},{4,5},{5,4},{6,7},{7,6},{8,9},{9,8},{10,11... | collective-permute-start | bytes 3538952 | tf_op jit(solution)/shard_map/ppermute | solution.py:395
  106.9 4.9 %collective-permute-done.11.refs_7_ = bf16[384,768]{1,0:T(8,128)(2,1)S(1)} collective-permute-done((bf16[384,768]{1,0:T(8,128)(2,1)S(1)}, bf16[384,768]{1,0:T(8,128)(2,1)S(1)}, u32[]{:S(2)}, u32[]{:S(2)}) %collective-permute-start.11) | collective-permute-done | bytes 589856 | tf_op jit(solution)/shard_map/ppermute | solution.py:395
  111.8 4.2 %collective-permute-start.12 = (bf16[384,768]{1,0:T(8,128)(2,1)S(1)}, bf16[384,768]{1,0:T(8,128)(2,1)S(1)}, u32[]{:S(2)}, u32[]{:S(2)}) collective-permute-start(bf16[384,768]{1,0:T(8,128)(2,1)S(1)} %collective-permute-done.11.refs_7_), channel_id=1, source_target_pairs={{0,1},{1,0},{2,3},{3,2},{4,5},{5,4},{6,7},{7,6},{8,9},{9,8},{10,11... | collective-permute-start | bytes 1769480 | tf_op jit(solution)/shard_map/ppermute | solution.py:395
  116.0 4.1 %all-to-all-done.1.ret = bf16[16,224,128]{2,1,0:T(8,128)(2,1)S(1)} async-done(((bf16[16,224,128]{2,1,0:T(8,128)(2,1)}), bf16[16,224,128]{2,1,0:T(8,128)(2,1)S(1)}, u32[]{:S(2)}, u32[]{:S(2)}) %all-to-all-start.1) | async-done | bytes 917536 | tf_op jit(solution)/shard_map/all_to_all | solution.py:442
  120.1 5.3 %project.1 = (bf16[112,1536]{1,0:T(8,128)(2,1)}, bf16[16,3072]{1,0:T(8,128)(2,1)}, f32[2,2048]{1,0:T(2,128)}) custom-call(s32[7]{0:T(128)S(1)} %concatenate.3.where, bf16[16,224,128]{2,1,0:T(8,128)(2,1)S(1)} %all-to-all-done.1.ret, bf16[384,1536]{1,0:T(8,128)(2,1)S(1)} %bitcast.9, bf16[384,1536]{1,0:T(8,128)(2,1)} %collective-permute-done.4.refs_1_, ...), custom_call_target="tpu_custom_call" | custom-call | tf_op jit(solution)/shard_map/project/pallas_call | solution.py:359
  (20 shorter events, 0.2 us)
Async XLA Ops:
  3.5 12.0 %copy-start.2 = (bf16[96,1536]{1,0:T(8,128)(2,1)S(1)}, bf16[96,1536]{1,0:T(8,128)(2,1)}, u32[]{:S(2)}) copy-start(bf16[96,1536]{1,0:T(8,128)(2,1)} %mine.1) | copy-start | bytes 884740
  3.5 17.1 %copy-start.3 = (s32[24]{0:T(128)S(1)}, s32[24]{0:T(128)}, u32[]{:S(2)}) copy-start(s32[24]{0:T(128)} %param.10) | copy-start | bytes 292
  3.5 67.0 %all-to-all-start = ((bf16[16,584,128]{2,1,0:T(8,128)(2,1)}), bf16[16,584,128]{2,1,0:T(8,128)(2,1)S(1)}, u32[]{:S(2)}, u32[]{:S(2)}) async-start(bf16[16,584,128]{2,1,0:T(8,128)(2,1)} %pack.1), calls=%async_computation | async-start | bytes 4784128 | tf_op jit(solution)/shard_map/all_to_all | solution.py:429
  15.5 8.0 %collective-permute-start = (bf16[96,1536]{1,0:T(8,128)(2,1)S(1)}, bf16[96,1536]{1,0:T(8,128)(2,1)S(1)}, u32[]{:S(2)}, u32[]{:S(2)}) collective-permute-start(bf16[96,1536]{1,0:T(8,128)(2,1)S(1)} %copy-done.2), channel_id=1, source_target_pairs={{0,16},{1,49},{2,18},{3,51},{4,20},{5,53},{6,22},{7,55},{8,24},{9,... | collective-permute-start | bytes 884744 | tf_op jit(solution)/shard_map/ppermute | solution.py:395
  19.9 7.4 %collective-permute-start.2 = (bf16[96,1536]{1,0:T(8,128)(2,1)S(1)}, bf16[96,1536]{1,0:T(8,128)(2,1)S(1)}, u32[]{:S(2)}, u32[]{:S(2)}) collective-permute-start(bf16[96,1536]{1,0:T(8,128)(2,1)S(1)} %copy-done.2), channel_id=1, source_target_pairs={{0,32},{2,34},{4,36},{6,38},{8,40},{10,42},{12,44},{14,46},{16,48}... | collective-permute-start | bytes 884744 | tf_op jit(solution)/shard_map/ppermute | solution.py:395
  23.6 5.3 %collective-permute-start.1 = (bf16[96,1536]{1,0:T(8,128)(2,1)S(1)}, bf16[96,1536]{1,0:T(8,128)(2,1)}, u32[]{:S(2)}, u32[]{:S(2)}) collective-permute-start(bf16[96,1536]{1,0:T(8,128)(2,1)S(1)} %collective-permute-done.near), channel_id=1, source_target_pairs={{0,1},{1,0},{2,3},{3,2},{4,5},{5,4},{6,7},{7,6},{8,9},{9,8},{10,11... | collective-permute-start | bytes 884744 | tf_op jit(solution)/shard_map/ppermute | solution.py:395
  27.4 4.7 %collective-permute-start.3 = (bf16[96,1536]{1,0:T(8,128)(2,1)S(1)}, bf16[96,1536]{1,0:T(8,128)(2,1)}, u32[]{:S(2)}, u32[]{:S(2)}) collective-permute-start(bf16[96,1536]{1,0:T(8,128)(2,1)S(1)} %collective-permute-done.2.part), channel_id=1, source_target_pairs={{0,1},{2,3},{4,5},{6,7},{8,9},{10,11},{12,13},{14,15},{16,17},{18,... | collective-permute-start | bytes 884744 | tf_op jit(solution)/shard_map/ppermute | solution.py:395
  33.8 18.2 %collective-permute-start.4 = (bf16[384,1536]{1,0:T(8,128)(2,1)S(1)}, bf16[384,1536]{1,0:T(8,128)(2,1)}, u32[]{:S(2)}, u32[]{:S(2)}) collective-permute-start(bf16[384,1536]{1,0:T(8,128)(2,1)S(1)} %bitcast.8), channel_id=1, source_target_pairs={{0,64},{1,449},{2,66},{3,451},{4,68},{5,453},{6,70},{7,455},{8,72}... | collective-permute-start | bytes 3538952 | tf_op jit(solution)/shard_map/ppermute | solution.py:395
  38.9 1.1 copy-start
  52.0 7.2 %collective-permute-start.5 = (bf16[384,1536]{1,0:T(8,128)(2,1)}, bf16[384,1536]{1,0:T(8,128)(2,1)}, u32[]{:S(2)}, u32[]{:S(2)}) collective-permute-start(bf16[384,1536]{1,0:T(8,128)(2,1)} %collective-permute-done.4.refs_1_), channel_id=1, source_target_pairs={{0,1},{1,0},{2,3},{3,2},{4,5},{5,4},{6,7},{7,6},{8,9},{9,8},{10,11... | collective-permute-start | bytes 3538952 | tf_op jit(solution)/shard_map/ppermute | solution.py:395
  55.5 24.6 %collective-permute-start.7 = (bf16[384,1536]{1,0:T(8,128)(2,1)}, bf16[384,1536]{1,0:T(8,128)(2,1)}, u32[]{:S(2)}, u32[]{:S(2)}) collective-permute-start(bf16[384,1536]{1,0:T(8,128)(2,1)} %collective-permute-done.4.refs_1_), channel_id=1, source_target_pairs={{0,64},{1,449},{2,66},{3,451},{4,68},{5,453},{6,70},{7,455},{8,72}... | collective-permute-start | bytes 3538952 | tf_op jit(solution)/shard_map/ppermute | solution.py:395
  70.6 9.5 %collective-permute-start.6 = (bf16[16,128,128]{2,1,0:T(8,128)(2,1)S(1)}, bf16[16,128,128]{2,1,0:T(8,128)(2,1)S(1)}, u32[]{:S(2)}, u32[]{:S(2)}) collective-permute-start(bf16[16,128,128]{2,1,0:T(8,128)(2,1)S(1)} %slice.3.own_kv), channel_id=1, source_target_pairs={{0,1},{1,0},{2,3},{3,2},{4,5},{5,4},{6,7},{7,6},{8,9},{9,8},{10,11... | collective-permute-start | bytes 1572872 | tf_op jit(solution)/shard_map/ppermute | solution.py:395
  80.1 18.6 %collective-permute-start.8 = (bf16[384,1536]{1,0:T(8,128)(2,1)}, bf16[384,1536]{1,0:T(8,128)(2,1)}, u32[]{:S(2)}, u32[]{:S(2)}) collective-permute-start(bf16[384,1536]{1,0:T(8,128)(2,1)} %collective-permute-done.7.refs_2_), channel_id=1, source_target_pairs={{0,64},{1,449},{2,66},{3,451},{4,68},{5,453},{6,70},{7,455},{8,72}... | collective-permute-start | bytes 3538952 | tf_op jit(solution)/shard_map/ppermute | solution.py:395
  90.0 30.1 %copy-start.1 = (bf16[4,96,1536]{2,1,0:T(8,128)(2,1)S(1)}, bf16[4,96,1536]{2,1,0:T(8,128)(2,1)}, u32[]{:S(2)}) copy-start(bf16[4,96,1536]{2,1,0:T(8,128)(2,1)} %copy-done) | copy-start | bytes 3538948
  90.0 30.1 %all-to-all-start.1 = ((bf16[16,224,128]{2,1,0:T(8,128)(2,1)}), bf16[16,224,128]{2,1,0:T(8,128)(2,1)S(1)}, u32[]{:S(2)}, u32[]{:S(2)}) async-start(bf16[16,224,128]{2,1,0:T(8,128)(2,1)} %attend_shared.1), calls=%async_computation.1 | async-start | bytes 1835008 | tf_op jit(solution)/shard_map/all_to_all | solution.py:442
  94.8 21.2 %collective-permute-start.9 = (bf16[384,1536]{1,0:T(8,128)(2,1)}, bf16[384,1536]{1,0:T(8,128)(2,1)}, u32[]{:S(2)}, u32[]{:S(2)}) collective-permute-start(bf16[384,1536]{1,0:T(8,128)(2,1)} %collective-permute-done.7.refs_2_), channel_id=1, source_target_pairs={{0,1},{1,0},{2,3},{3,2},{4,5},{5,4},{6,7},{7,6},{8,9},{9,8},{10,11... | collective-permute-start | bytes 3538952 | tf_op jit(solution)/shard_map/ppermute | solution.py:395
  99.7 12.0 %collective-permute-start.11 = (bf16[384,768]{1,0:T(8,128)(2,1)S(1)}, bf16[384,768]{1,0:T(8,128)(2,1)S(1)}, u32[]{:S(2)}, u32[]{:S(2)}) collective-permute-start(bf16[384,768]{1,0:T(8,128)(2,1)S(1)} %constant_dynamic-slice_fusion), channel_id=1, source_target_pairs={{0,64},{1,449},{2,66},{3,451},{4,68},{5,453},{6,70},{7,455},{8,72}... | collective-permute-start | bytes 1769480 | tf_op jit(solution)/shard_map/ppermute | solution.py:395
  105.0 15.1 %collective-permute-start.10 = (bf16[384,1536]{1,0:T(8,128)(2,1)}, bf16[384,1536]{1,0:T(8,128)(2,1)}, u32[]{:S(2)}, u32[]{:S(2)}) collective-permute-start(bf16[384,1536]{1,0:T(8,128)(2,1)} %collective-permute-done.8.refs_3_), channel_id=1, source_target_pairs={{0,1},{1,0},{2,3},{3,2},{4,5},{5,4},{6,7},{7,6},{8,9},{9,8},{10,11... | collective-permute-start | bytes 3538952 | tf_op jit(solution)/shard_map/ppermute | solution.py:395
  111.8 8.3 %collective-permute-start.12 = (bf16[384,768]{1,0:T(8,128)(2,1)S(1)}, bf16[384,768]{1,0:T(8,128)(2,1)S(1)}, u32[]{:S(2)}, u32[]{:S(2)}) collective-permute-start(bf16[384,768]{1,0:T(8,128)(2,1)S(1)} %collective-permute-done.11.refs_7_), channel_id=1, source_target_pairs={{0,1},{1,0},{2,3},{3,2},{4,5},{5,4},{6,7},{7,6},{8,9},{9,8},{10,11... | collective-permute-start | bytes 1769480 | tf_op jit(solution)/shard_map/ppermute | solution.py:395

commit v8 on v7

--- a/solution.py
+++ b/solution.py
@@ -261,20 +261,29 @@
     )(where, received, received, own_kv, far_kv, whole, whole_lse)
 
 
-def place_kernel(where, mine, near, near_far, part, part_far, out):
+def place_kernel(where, mine, near, near_far, part, part_far, *halves):
     x, core = where[1], where[2]
     sign = 1 - 2 * core
-    out[x] = mine[...]
-    out[(x - sign + 4) % 4] = near[...]
-    out[(x + sign + 4) % 4] = near_far[...]
+
+    def put(to, shard):
+        to = (to + X_SIZE) % X_SIZE
+        for half, out in enumerate(halves):
+
+            @pl.when(to // 2 == half)
+            def _():
+                out[to % 2] = shard[...]
+
+    put(x, mine)
+    put(x - sign, near)
+    put(x + sign, near_far)
 
     @pl.when(core == 0)
     def _():
-        out[(x + 2) % 4] = part[...]
+        put(x + 2, part)
 
     @pl.when(core == 1)
     def _():
-        out[(x + 2) % 4] = part_far[...]
+        put(x + 2, part_far)
 
 
 def place(where, mine, near, near_far, part, part_far):
@@ -285,9 +294,9 @@
             num_scalar_prefetch=1,
             grid=(),
             in_specs=[pl.BlockSpec(memory_space=pltpu.VMEM)] * 5,
-            out_specs=pl.BlockSpec(memory_space=pltpu.VMEM),
+            out_specs=[pl.BlockSpec(memory_space=pltpu.VMEM)] * 2,
         ),
-        out_shape=jax.ShapeDtypeStruct((4, rows, columns), jnp.bfloat16),
+        out_shape=[jax.ShapeDtypeStruct((2, rows, columns), jnp.bfloat16)] * 2,
         compiler_params=pltpu.CompilerParams(vmem_limit_bytes=PLACE_VMEM),
         name="place",
     )(where, mine, near, near_far, part, part_far)
@@ -312,20 +321,23 @@
     return rows
 
 
+HOPS = (0, 1, 2, 3, -1, -2, -3)
+PIECES = 2 * len(HOPS) + 2
+
+
 def project_kernel(where, ret, *refs):
-    weights, (vis_out, txt_out, slots, held, sems) = refs[:9], refs[9:]
+    weights, (vis_out, txt_out, slots, held, sems) = refs[:PIECES], refs[PIECES:]
     y, core = where[0], where[2]
     sign = 1 - 2 * core
-    columns = held.shape[2] // 2
+    half_rows = TRIO // 2
     copies = []
-    for index in range(7):
-        to = held.at[index // 2, pl.ds(index % 2 * TRIO, TRIO)]
+    for index in range(PIECES):
+        chunk, half = index // 2, index % 2
+        if chunk == len(HOPS):
+            half = core if half == 0 else 1 - core
+        start = chunk % 2 * TRIO + half * half_rows
+        to = held.at[chunk // 2, pl.ds(pl.multiple_of(start, 64), half_rows)]
         copies.append(pltpu.make_async_copy(weights[index], to, sems.at[index]))
-    for index in range(2):
-        at = core if index == 0 else 1 - core
-        start = pl.multiple_of(at * columns, columns)
-        to = held.at[3, pl.ds(TRIO, TRIO), pl.ds(start, columns)]
-        copies.append(pltpu.make_async_copy(weights[7 + index], to, sems.at[7 + index]))
     for copy in copies:
         copy.start()
     for slot in range(SLOTS):
@@ -336,36 +348,35 @@
             slots[slot : slot + 1, at : at + VIS_ROWS] = row[:, :VIS_ROWS]
             at = VIS_SEQ + source * TXT_ROWS
             slots[slot : slot + 1, at : at + TXT_ROWS] = row[:, VIS_ROWS:]
-    total = jnp.zeros((ROWS, 2 * columns), jnp.float32)
+    total = jnp.zeros((ROWS, held.shape[2]), jnp.float32)
     pieces = []
-    for index, hops in enumerate((0, 1, 2, 3, -1, -2, -3, 4)):
-        chip = (y - hops * sign + 8) % 8
+    for index, hops in enumerate((*HOPS, 4)):
+        chip = (y - hops * sign + Y_SIZE) % Y_SIZE
         low, high = ret[2 * chip], ret[2 * chip + 1]
         shared = jnp.concatenate([low[ROWS:RET_ROWS], high[ROWS:RET_ROWS]], axis=0)
         attention = jnp.concatenate([low[:ROWS], shared, high[:ROWS]], axis=1)
         txt_out[:, pl.ds(pl.multiple_of(chip * TRIO, TRIO), TRIO)] = attention[VIS_ROWS:]
         pieces.append(attention)
-        copies[index].wait()
+        copies[2 * index].wait()
+        copies[2 * index + 1].wait()
         if index % 2 == 1:
-            if index == 7:
-                copies[8].wait()
             both = jnp.concatenate(pieces[-2:], axis=1)
             total += jnp.dot(both, held[index // 2], preferred_element_type=jnp.float32)
     vis_out[...] = total[:VIS_ROWS].astype(jnp.bfloat16)
 
 
-def project(where, returned, chunks, far_chunks):
-    columns = chunks[0].shape[1]
+def project(where, returned, weights):
+    columns = weights[0].shape[1]
     return pl.pallas_call(
         project_kernel,
         grid_spec=pltpu.PrefetchScalarGridSpec(
             num_scalar_prefetch=1,
             grid=(),
-            in_specs=[pl.BlockSpec(memory_space=pltpu.VMEM)] + [pl.BlockSpec(memory_space=pltpu.HBM)] * 9,
+            in_specs=[pl.BlockSpec(memory_space=pltpu.VMEM)] + [pl.BlockSpec(memory_space=pltpu.HBM)] * PIECES,
             out_specs=[pl.BlockSpec(memory_space=pltpu.VMEM)] * 3,
             scratch_shapes=[
-                pltpu.VMEM((4, 2 * TRIO, columns), jnp.bfloat16),
-                pltpu.SemaphoreType.DMA((9,)),
+                pltpu.VMEM((Y_SIZE // 2, 2 * TRIO, columns), jnp.bfloat16),
+                pltpu.SemaphoreType.DMA((PIECES,)),
             ],
         ),
         out_shape=[
@@ -375,7 +386,7 @@
         ],
         compiler_params=pltpu.CompilerParams(vmem_limit_bytes=PROJECT_VMEM),
         name="project",
-    )(where, returned, *chunks[:4], *far_chunks[:3], chunks[4], far_chunks[3])
+    )(where, returned, *weights)
 
 
 AXES = ("dp", "seq")
@@ -419,7 +430,6 @@
     seq_index = lax.axis_index("seq")
     dp_index = lax.axis_index("dp")
     core = seq_index % 2
-    half = w_out.shape[1] // 2
     place_here = jnp.stack([dp_index // X_SIZE, dp_index % X_SIZE, core]).astype(jnp.int32)
     where = jnp.concatenate([place_here, heads_of_slots(head_map, seq_index)])
 
@@ -427,22 +437,20 @@
     part = shift_x(w_out, 2, cores=(0,))
     sending = pack(qkv_vis, qkv_txt, vis_segments, txt_segments)
     received = lax.all_to_all(sending, "seq", split_axis=0, concat_axis=0, tiled=True)
-    chunks = [place(where, w_out, near, swap(near), part, swap(part, cores=(0,))).reshape(-1, 2 * half)]
-    chunks.append(shift_y(chunks[0]))
-    chunks.append(shift_y(chunks[1]))
-    far_chunks = [swap(chunks[1])]
-    received, far_chunks[0] = lax.optimization_barrier((received, far_chunks[0]))
+    halves = place(where, w_out, near, swap(near), part, swap(part, cores=(0,)))
+    chunks = [[half.reshape(-1, half.shape[2]) for half in halves]]
+    for _ in range(3):
+        chunks.append([shift_y(half) for half in chunks[-1]])
     own_kv = received[:, A_ROWS + HALF : SEND_ROWS]
     far_kv = swap(own_kv)
     whole, whole_lse = attend_whole(received)
-    whole, far_kv, chunks[2] = lax.optimization_barrier((whole, far_kv, chunks[2]))
-    chunks.append(shift_y(chunks[2]))
     returning = attend_shared(where, received, own_kv, far_kv, whole, whole_lse)
-    returning, chunks[2] = lax.optimization_barrier((returning, chunks[2]))
+    returning, chunks[1:] = lax.optimization_barrier((returning, chunks[1:]))
     returned = lax.all_to_all(returning, "seq", split_axis=0, concat_axis=0, tiled=True)
-    chunks.append(shift_y(lax.dynamic_slice_in_dim(chunks[3], core * half, half, 1)))
-    far_chunks += [swap(chunk) for chunk in chunks[2:]]
-    vis_out, txt_out, lse_slots = project(where, returned, chunks, far_chunks)
+    opposite = shift_y(jnp.where(core == 0, *chunks[3]))
+    far_chunks = [[swap(half) for half in chunk] for chunk in chunks[1:]]
+    weights = [half for chunk in chunks + far_chunks for half in chunk] + [opposite, swap(opposite)]
+    vis_out, txt_out, lse_slots = project(where, returned, weights)
     return vis_out, txt_out, lse_slots
 
 

time: 126 us -> 127 us (level)
  waiting for transfers between devices: 40 us -> 14.4 us
  starting transfers between devices: 60.4 us -> 80.4 us
  local copies, waits for them, and re-layouts: 2.37 us -> 5.2 us
  Pallas kernels: 21.5 us -> 23 us
    ppermute x13 -> x19, starting transfers between devices: 43.6 us -> 60.6 us  [permute(): return lax.ppermute(operand, AXES, pairs)]
    ppermute x13 -> x19, waiting for transfers between devices: 24.6 us -> 11.3 us  [permute(): return lax.ppermute(operand, AXES, pairs)]
    all_to_all x1, waiting for transfers between devices: 11.2 us -> 0.01 us  [on_device(): lax.all_to_all(sending, 'seq', split_axis=0, concat_axis=0, tiled=True)]
    unnamed x8 -> x34, local copies, waits for them, and re-layouts: 1.06 us -> 4.99 us
    all_to_all x1, starting transfers between devices: 4.79 us -> 7.76 us  [on_device(): lax.all_to_all(returning, 'seq', split_axis=0, concat_axis=0, tiled=True)]
    pallas_call x1, Pallas kernels: 5.34 us -> 6.75 us  [project(): pl.pallas_call(project_kernel, grid_spec=pltpu.PrefetchScalarGridSpec(num...]
  transfers between devices with their start and end apart: 15 -> 21, of which waited for: 7 -> 8; matrix products, arithmetic and copies ran while one was open for 1% -> 1% of each run, Pallas kernels for 11% -> 11%
where the time goes in v8:
time: 127 us; the launch traced here: 125 us
  starting transfers between devices  80.4 us (63%)
  Pallas kernels  23 us (18%)
  waiting for transfers between devices  14.4 us (11%)
  local copies, waits for them, and re-layouts  5.2 us (4%)
  other arithmetic  1.45 us (1%)
    ppermute x19, starting transfers between devices, permute(): return lax.ppermute(operand, AXES, pairs)  60.6 us
    all_to_all x1, starting transfers between devices, on_device(): lax.all_to_all(sending, 'seq', split_axis=0, concat_axis=0, tiled=True)  12 us
    ppermute x19, waiting for transfers between devices, permute(): return lax.ppermute(operand, AXES, pairs)  11.3 us
    all_to_all x1, starting transfers between devices, on_device(): lax.all_to_all(returning, 'seq', split_axis=0, concat_axis=0, tiled=True)  7.76 us
    pallas_call x1, Pallas kernels, attend_whole(): pl.pallas_call(whole_kernel, grid=(steps,), in_specs=[pl.BlockSpec((N_SEQ...  6.82 us
    pallas_call x1, Pallas kernels, project(): pl.pallas_call(project_kernel, grid_spec=pltpu.PrefetchScalarGridSpec(num...  6.75 us
    unnamed x34, local copies, waits for them, and re-layouts  4.99 us
    pallas_call x1, Pallas kernels, attend_shared(): pl.pallas_call(shared_kernel, grid_spec=pltpu.PrefetchScalarGridSpec(num_...  4.73 us
  transfers between devices with their start and end apart: 21, of which 8 were waited for; matrix products, arithmetic and copies ran while one was open for 1% of the time, Pallas kernels for 11%

profile of v8, /device:TPU:1, one launch (start us, length us, event | category | flops | bytes accessed | tf_op | source)
XLA Modules:
  0.0 125.5 jit_solution(2638992131129314742)
XLA Ops:
  0.6 2.9 %pack.1 = bf16[16,584,128]{2,1,0:T(8,128)(2,1)} custom-call(s32[1,112]{1,0:T(1,128)} %bitcast.13, s32[1,16]{1,0:T(1,128)} %bitcast.14, bf16[112,9216]{1,0:T(8,128)(2,1)} %vv.1, bf16[112,9216]{1,0:T(8,128)(2,1)} %vv.1, bf16[112,9216]{1,0:T(8,128)(2,1)} %vv.1, bf16[16,9216]{1,0:T(8,128)(2,1)} %tv.1, bf16[16,9216]{1,0:T(8,128)(2,1)} %tv.1, bf16[16,9216]{1,0:T(8,128)(2,1)} %tv.1), custom_call_target="tpu_custom_call" | custom-call | tf_op jit(solution)/shard_map/pack/pallas_call | solution.py:66
  3.6 12.0 %all-to-all-start = ((bf16[16,584,128]{2,1,0:T(8,128)(2,1)}), bf16[16,584,128]{2,1,0:T(8,128)(2,1)S(1)}, u32[]{:S(2)}, u32[]{:S(2)}) async-start(bf16[16,584,128]{2,1,0:T(8,128)(2,1)} %pack.1), calls=%async_computation | async-start | bytes 4784128 | tf_op jit(solution)/shard_map/all_to_all | solution.py:439
  15.5 4.4 %collective-permute-start.1 = (bf16[96,1536]{1,0:T(8,128)(2,1)S(1)}, bf16[96,1536]{1,0:T(8,128)(2,1)S(1)}, u32[]{:S(2)}, u32[]{:S(2)}) collective-permute-start(bf16[96,1536]{1,0:T(8,128)(2,1)S(1)} %copy-done.6), channel_id=1, source_target_pairs={{0,16},{1,49},{2,18},{3,51},{4,20},{5,53},{6,22},{7,55},{8,24},{9,... | collective-permute-start | bytes 884744 | tf_op jit(solution)/shard_map/ppermute | solution.py:406
  20.9 2.7 %collective-permute-done.1.near = bf16[96,1536]{1,0:T(8,128)(2,1)S(1)} collective-permute-done((bf16[96,1536]{1,0:T(8,128)(2,1)S(1)}, bf16[96,1536]{1,0:T(8,128)(2,1)S(1)}, u32[]{:S(2)}, u32[]{:S(2)}) %collective-permute-start.1) | collective-permute-done | bytes 294944 | tf_op jit(solution)/shard_map/ppermute | solution.py:406
  23.6 3.8 %collective-permute-start.2 = (bf16[96,1536]{1,0:T(8,128)(2,1)S(1)}, bf16[96,1536]{1,0:T(8,128)(2,1)}, u32[]{:S(2)}, u32[]{:S(2)}) collective-permute-start(bf16[96,1536]{1,0:T(8,128)(2,1)S(1)} %collective-permute-done.1.near), channel_id=1, source_target_pairs={{0,1},{1,0},{2,3},{3,2},{4,5},{5,4},{6,7},{7,6},{8,9},{9,8},{10,11... | collective-permute-start | bytes 884744 | tf_op jit(solution)/shard_map/ppermute | solution.py:406
  28.1 1.3 %collective-permute-start.4 = (bf16[96,1536]{1,0:T(8,128)(2,1)S(1)}, bf16[96,1536]{1,0:T(8,128)(2,1)}, u32[]{:S(2)}, u32[]{:S(2)}) collective-permute-start(bf16[96,1536]{1,0:T(8,128)(2,1)S(1)} %collective-permute-done.3.part), channel_id=1, source_target_pairs={{0,1},{2,3},{4,5},{6,7},{8,9},{10,11},{12,13},{14,15},{16,17},{18,... | collective-permute-start | bytes 884744 | tf_op jit(solution)/shard_map/ppermute | solution.py:406
  30.3 1.8 %collective-permute-done.4.part_far = bf16[96,1536]{1,0:T(8,128)(2,1)} collective-permute-done((bf16[96,1536]{1,0:T(8,128)(2,1)S(1)}, bf16[96,1536]{1,0:T(8,128)(2,1)}, u32[]{:S(2)}, u32[]{:S(2)}) %collective-permute-start.4) | collective-permute-done | bytes 294944 | tf_op jit(solution)/shard_map/ppermute | solution.py:406
  34.0 1.8 %place.1 = (bf16[2,96,1536]{2,1,0:T(8,128)(2,1)S(1)}, bf16[2,96,1536]{2,1,0:T(8,128)(2,1)S(1)}) custom-call(s32[7]{0:T(128)S(1)} %concatenate.3.where, bf16[96,1536]{1,0:T(8,128)(2,1)S(1)} %copy-done.6, bf16[96,1536]{1,0:T(8,128)(2,1)S(1)} %copy-done.8, bf16[96,1536]{1,0:T(8,128)(2,1)} %collective-permute-done.2.near_far, bf16[96,1536]{1,0:T(8,128)(2,1)S(1)} %copy-done.10, ...), custom_call_target="tpu_custom_call" | custom-call | tf_op jit(solution)/shard_map/place/pallas_call | solution.py:291
  35.8 5.1 %collective-permute-start.6 = (bf16[192,1536]{1,0:T(8,128)(2,1)S(1)}, bf16[192,1536]{1,0:T(8,128)(2,1)S(1)}, u32[]{:S(2)}, u32[]{:S(2)}) collective-permute-start(bf16[192,1536]{1,0:T(8,128)(2,1)S(1)} %bitcast.11), channel_id=1, source_target_pairs={{0,64},{1,449},{2,66},{3,451},{4,68},{5,453},{6,70},{7,455},{8,72}... | collective-permute-start | bytes 1769480 | tf_op jit(solution)/shard_map/ppermute | solution.py:406
  41.7 3.0 %collective-permute-start.5 = (bf16[192,1536]{1,0:T(8,128)(2,1)S(1)}, bf16[192,1536]{1,0:T(8,128)(2,1)S(1)}, u32[]{:S(2)}, u32[]{:S(2)}) collective-permute-start(bf16[192,1536]{1,0:T(8,128)(2,1)S(1)} %bitcast.9), channel_id=1, source_target_pairs={{0,64},{1,449},{2,66},{3,451},{4,68},{5,453},{6,70},{7,455},{8,72}... | collective-permute-start | bytes 1769480 | tf_op jit(solution)/shard_map/ppermute | solution.py:406
  44.7 3.0 %collective-permute-done.6.refs_3_ = bf16[192,1536]{1,0:T(8,128)(2,1)S(1)} collective-permute-done((bf16[192,1536]{1,0:T(8,128)(2,1)S(1)}, bf16[192,1536]{1,0:T(8,128)(2,1)S(1)}, u32[]{:S(2)}, u32[]{:S(2)}) %collective-permute-start.6) | collective-permute-done | bytes 589856 | tf_op jit(solution)/shard_map/ppermute | solution.py:406
  47.7 5.3 %collective-permute-start.8 = (bf16[192,1536]{1,0:T(8,128)(2,1)S(1)}, bf16[192,1536]{1,0:T(8,128)(2,1)}, u32[]{:S(2)}, u32[]{:S(2)}) collective-permute-start(bf16[192,1536]{1,0:T(8,128)(2,1)S(1)} %collective-permute-done.6.refs_3_), channel_id=1, source_target_pairs={{0,64},{1,449},{2,66},{3,451},{4,68},{5,453},{6,70},{7,455},{8,72}... | collective-permute-start | bytes 1769480 | tf_op jit(solution)/shard_map/ppermute | solution.py:406
  53.0 1.0 collective-permute-done.5.refs_2_
  54.0 5.3 %collective-permute-start.7 = (bf16[192,1536]{1,0:T(8,128)(2,1)S(1)}, bf16[192,1536]{1,0:T(8,128)(2,1)}, u32[]{:S(2)}, u32[]{:S(2)}) collective-permute-start(bf16[192,1536]{1,0:T(8,128)(2,1)S(1)} %collective-permute-done.5.refs_2_), channel_id=1, source_target_pairs={{0,64},{1,449},{2,66},{3,451},{4,68},{5,453},{6,70},{7,455},{8,72}... | collective-permute-start | bytes 1769480 | tf_op jit(solution)/shard_map/ppermute | solution.py:406
  60.3 5.3 %collective-permute-start.10 = (bf16[192,1536]{1,0:T(8,128)(2,1)}, bf16[192,1536]{1,0:T(8,128)(2,1)}, u32[]{:S(2)}, u32[]{:S(2)}) collective-permute-start(bf16[192,1536]{1,0:T(8,128)(2,1)} %collective-permute-done.8.refs_5_), channel_id=1, source_target_pairs={{0,64},{1,449},{2,66},{3,451},{4,68},{5,453},{6,70},{7,455},{8,72}... | collective-permute-start | bytes 1769480 | tf_op jit(solution)/shard_map/ppermute | solution.py:406
  65.7 1.0 collective-permute-done.7.refs_4_
  66.7 5.3 %collective-permute-start.9 = (bf16[192,1536]{1,0:T(8,128)(2,1)}, bf16[192,1536]{1,0:T(8,128)(2,1)}, u32[]{:S(2)}, u32[]{:S(2)}) collective-permute-start(bf16[192,1536]{1,0:T(8,128)(2,1)} %collective-permute-done.7.refs_4_), channel_id=1, source_target_pairs={{0,64},{1,449},{2,66},{3,451},{4,68},{5,453},{6,70},{7,455},{8,72}... | collective-permute-start | bytes 1769480 | tf_op jit(solution)/shard_map/ppermute | solution.py:406
  72.0 1.9 %collective-permute-start = (bf16[16,128,128]{2,1,0:T(8,128)(2,1)S(1)}, bf16[16,128,128]{2,1,0:T(8,128)(2,1)S(1)}, u32[]{:S(2)}, u32[]{:S(2)}) collective-permute-start(bf16[16,128,128]{2,1,0:T(8,128)(2,1)S(1)} %slice.4.own_kv), channel_id=1, source_target_pairs={{0,1},{1,0},{2,3},{3,2},{4,5},{5,4},{6,7},{7,6},{8,9},{9,8},{10,11... | collective-permute-start | bytes 1572872 | tf_op jit(solution)/shard_map/ppermute | solution.py:406
  74.0 6.8 %attend_whole.1 = (bf16[16,128,128]{2,1,0:T(8,128)(2,1)S(1)}, f32[16,128]{1,0:T(8,128)S(1)}) custom-call(bf16[16,584,128]{2,1,0:T(8,128)(2,1)S(1)} %all-to-all-done.cut.q.k.v, bf16[16,584,128]{2,1,0:T(8,128)(2,1)S(1)} %all-to-all-done.cut.q.k.v, bf16[16,584,128]{2,1,0:T(8,128)(2,1)S(1)} %all-to-all-done.cut.q.k.v, ...), custom_call_target="tpu_custom_call" | custom-call | flops 134217728 | bytes 2097152 | tf_op jit(solution)/shard_map/attend_whole/pallas_call | solution.py:214
  80.8 4.7 %attend_shared.1 = bf16[16,224,128]{2,1,0:T(8,128)(2,1)} custom-call(s32[7]{0:T(128)S(1)} %concatenate.3.where, bf16[16,584,128]{2,1,0:T(8,128)(2,1)S(1)} %all-to-all-done.cut.q.k.v, bf16[16,584,128]{2,1,0:T(8,128)(2,1)S(1)} %all-to-all-done.cut.q.k.v, bf16[16,128,128]{2,1,0:T(8,128)(2,1)S(1)} %slice.4.own_kv, ...), custom_call_target="tpu_custom_call" | custom-call | flops 67108864 | bytes 2097152 | tf_op jit(solution)/shard_map/attend_shared/pallas_call | solution.py:241
  85.6 7.8 %all-to-all-start.1 = ((bf16[16,224,128]{2,1,0:T(8,128)(2,1)}), bf16[16,224,128]{2,1,0:T(8,128)(2,1)}, u32[]{:S(2)}, u32[]{:S(2)}) async-start(bf16[16,224,128]{2,1,0:T(8,128)(2,1)} %attend_shared.1), calls=%async_computation.1 | async-start | bytes 1835008 | tf_op jit(solution)/shard_map/all_to_all | solution.py:449
  93.3 1.1 broadcast_select_fusion
  94.5 3.3 %collective-permute-start.17 = (bf16[192,1536]{1,0:T(8,128)(2,1)S(1)}, bf16[192,1536]{1,0:T(8,128)(2,1)S(1)}, u32[]{:S(2)}, u32[]{:S(2)}) collective-permute-start(bf16[192,1536]{1,0:T(8,128)(2,1)S(1)} %broadcast_select_fusion), channel_id=1, source_target_pairs={{0,64},{1,449},{2,66},{3,451},{4,68},{5,453},{6,70},{7,455},{8,72}... | collective-permute-start | bytes 1769480 | tf_op jit(solution)/shard_map/ppermute | solution.py:406
  97.8 1.9 %collective-permute-start.11 = (bf16[192,1536]{1,0:T(8,128)(2,1)S(1)}, bf16[192,1536]{1,0:T(8,128)(2,1)S(1)}, u32[]{:S(2)}, u32[]{:S(2)}) collective-permute-start(bf16[192,1536]{1,0:T(8,128)(2,1)S(1)} %copy-done.5), channel_id=1, source_target_pairs={{0,1},{1,0},{2,3},{3,2},{4,5},{5,4},{6,7},{7,6},{8,9},{9,8},{10,11... | collective-permute-start | bytes 1769480 | tf_op jit(solution)/shard_map/ppermute | solution.py:406
  99.7 2.4 %collective-permute-start.12 = (bf16[192,1536]{1,0:T(8,128)(2,1)S(1)}, bf16[192,1536]{1,0:T(8,128)(2,1)S(1)}, u32[]{:S(2)}, u32[]{:S(2)}) collective-permute-start(bf16[192,1536]{1,0:T(8,128)(2,1)S(1)} %copy-done.3), channel_id=1, source_target_pairs={{0,1},{1,0},{2,3},{3,2},{4,5},{5,4},{6,7},{7,6},{8,9},{9,8},{10,11... | collective-permute-start | bytes 1769480 | tf_op jit(solution)/shard_map/ppermute | solution.py:406
  102.1 1.9 %collective-permute-start.15 = (bf16[192,1536]{1,0:T(8,128)(2,1)}, bf16[192,1536]{1,0:T(8,128)(2,1)}, u32[]{:S(2)}, u32[]{:S(2)}) collective-permute-start(bf16[192,1536]{1,0:T(8,128)(2,1)} %collective-permute-done.9.refs_6_), channel_id=1, source_target_pairs={{0,1},{1,0},{2,3},{3,2},{4,5},{5,4},{6,7},{7,6},{8,9},{9,8},{10,11... | collective-permute-start | bytes 1769480 | tf_op jit(solution)/shard_map/ppermute | solution.py:406
  104.1 2.4 %collective-permute-start.13 = (bf16[192,1536]{1,0:T(8,128)(2,1)}, bf16[192,1536]{1,0:T(8,128)(2,1)S(1)}, u32[]{:S(2)}, u32[]{:S(2)}) collective-permute-start(bf16[192,1536]{1,0:T(8,128)(2,1)} %collective-permute-done.7.refs_4_), channel_id=1, source_target_pairs={{0,1},{1,0},{2,3},{3,2},{4,5},{5,4},{6,7},{7,6},{8,9},{9,8},{10,11... | collective-permute-start | bytes 1769480 | tf_op jit(solution)/shard_map/ppermute | solution.py:406
  106.5 3.0 %collective-permute-start.14 = (bf16[192,1536]{1,0:T(8,128)(2,1)}, bf16[192,1536]{1,0:T(8,128)(2,1)S(1)}, u32[]{:S(2)}, u32[]{:S(2)}) collective-permute-start(bf16[192,1536]{1,0:T(8,128)(2,1)} %collective-permute-done.8.refs_5_), channel_id=1, source_target_pairs={{0,1},{1,0},{2,3},{3,2},{4,5},{5,4},{6,7},{7,6},{8,9},{9,8},{10,11... | collective-permute-start | bytes 1769480 | tf_op jit(solution)/shard_map/ppermute | solution.py:406
  109.5 1.9 %collective-permute-start.16 = (bf16[192,1536]{1,0:T(8,128)(2,1)}, bf16[192,1536]{1,0:T(8,128)(2,1)}, u32[]{:S(2)}, u32[]{:S(2)}) collective-permute-start(bf16[192,1536]{1,0:T(8,128)(2,1)} %collective-permute-done.10.refs_7_), channel_id=1, source_target_pairs={{0,1},{1,0},{2,3},{3,2},{4,5},{5,4},{6,7},{7,6},{8,9},{9,8},{10,11... | collective-permute-start | bytes 1769480 | tf_op jit(solution)/shard_map/ppermute | solution.py:406
  111.5 2.4 %collective-permute-start.18 = (bf16[192,1536]{1,0:T(8,128)(2,1)S(1)}, bf16[192,1536]{1,0:T(8,128)(2,1)}, u32[]{:S(2)}, u32[]{:S(2)}) collective-permute-start(bf16[192,1536]{1,0:T(8,128)(2,1)S(1)} %collective-permute-done.17.refs_14_), channel_id=1, source_target_pairs={{0,1},{1,0},{2,3},{3,2},{4,5},{5,4},{6,7},{7,6},{8,9},{9,8},{10,11... | collective-permute-start | bytes 1769480 | tf_op jit(solution)/shard_map/ppermute | solution.py:406
  115.6 3.1 %all-to-all-done.1.ret = bf16[16,224,128]{2,1,0:T(8,128)(2,1)} async-done(((bf16[16,224,128]{2,1,0:T(8,128)(2,1)}), bf16[16,224,128]{2,1,0:T(8,128)(2,1)}, u32[]{:S(2)}, u32[]{:S(2)}) %all-to-all-start.1) | async-done | bytes 917536 | tf_op jit(solution)/shard_map/all_to_all | solution.py:449
  118.7 6.7 %project.1 = (bf16[112,1536]{1,0:T(8,128)(2,1)}, bf16[16,3072]{1,0:T(8,128)(2,1)}, f32[2,2048]{1,0:T(2,128)}) custom-call(s32[7]{0:T(128)S(1)} %concatenate.3.where, bf16[16,224,128]{2,1,0:T(8,128)(2,1)} %all-to-all-done.1.ret, bf16[192,1536]{1,0:T(8,128)(2,1)S(1)} %bitcast.10, bf16[192,1536]{1,0:T(8,128)(2,1)S(1)} %bitcast.12, ...), custom_call_target="tpu_custom_call" | custom-call | tf_op jit(solution)/shard_map/project/pallas_call | solution.py:370
  (58 shorter events, 8.1 us)
Async XLA Ops:
  3.6 12.0 %copy-start.6 = (bf16[96,1536]{1,0:T(8,128)(2,1)S(1)}, bf16[96,1536]{1,0:T(8,128)(2,1)}, u32[]{:S(2)}) copy-start(bf16[96,1536]{1,0:T(8,128)(2,1)} %mine.1) | copy-start | bytes 884740
  3.6 17.1 %copy-start.16 = (s32[24]{0:T(128)S(1)}, s32[24]{0:T(128)}, u32[]{:S(2)}) copy-start(s32[24]{0:T(128)} %param.10) | copy-start | bytes 292
  3.6 68.4 %all-to-all-start = ((bf16[16,584,128]{2,1,0:T(8,128)(2,1)}), bf16[16,584,128]{2,1,0:T(8,128)(2,1)S(1)}, u32[]{:S(2)}, u32[]{:S(2)}) async-start(bf16[16,584,128]{2,1,0:T(8,128)(2,1)} %pack.1), calls=%async_computation | async-start | bytes 4784128 | tf_op jit(solution)/shard_map/all_to_all | solution.py:439
  15.5 8.0 %collective-permute-start.1 = (bf16[96,1536]{1,0:T(8,128)(2,1)S(1)}, bf16[96,1536]{1,0:T(8,128)(2,1)S(1)}, u32[]{:S(2)}, u32[]{:S(2)}) collective-permute-start(bf16[96,1536]{1,0:T(8,128)(2,1)S(1)} %copy-done.6), channel_id=1, source_target_pairs={{0,16},{1,49},{2,18},{3,51},{4,20},{5,53},{6,22},{7,55},{8,24},{9,... | collective-permute-start | bytes 884744 | tf_op jit(solution)/shard_map/ppermute | solution.py:406
  19.9 8.2 %collective-permute-start.3 = (bf16[96,1536]{1,0:T(8,128)(2,1)S(1)}, bf16[96,1536]{1,0:T(8,128)(2,1)S(1)}, u32[]{:S(2)}, u32[]{:S(2)}) collective-permute-start(bf16[96,1536]{1,0:T(8,128)(2,1)S(1)} %copy-done.6), channel_id=1, source_target_pairs={{0,32},{2,34},{4,36},{6,38},{8,40},{10,42},{12,44},{14,46},{16,48}... | collective-permute-start | bytes 884744 | tf_op jit(solution)/shard_map/ppermute | solution.py:406
  23.6 6.7 %collective-permute-start.2 = (bf16[96,1536]{1,0:T(8,128)(2,1)S(1)}, bf16[96,1536]{1,0:T(8,128)(2,1)}, u32[]{:S(2)}, u32[]{:S(2)}) collective-permute-start(bf16[96,1536]{1,0:T(8,128)(2,1)S(1)} %collective-permute-done.1.near), channel_id=1, source_target_pairs={{0,1},{1,0},{2,3},{3,2},{4,5},{5,4},{6,7},{7,6},{8,9},{9,8},{10,11... | collective-permute-start | bytes 884744 | tf_op jit(solution)/shard_map/ppermute | solution.py:406
  28.1 4.0 %collective-permute-start.4 = (bf16[96,1536]{1,0:T(8,128)(2,1)S(1)}, bf16[96,1536]{1,0:T(8,128)(2,1)}, u32[]{:S(2)}, u32[]{:S(2)}) collective-permute-start(bf16[96,1536]{1,0:T(8,128)(2,1)S(1)} %collective-permute-done.3.part), channel_id=1, source_target_pairs={{0,1},{2,3},{4,5},{6,7},{8,9},{10,11},{12,13},{14,15},{16,17},{18,... | collective-permute-start | bytes 884744 | tf_op jit(solution)/shard_map/ppermute | solution.py:406
  32.1 1.0 copy-start.8
  35.8 11.9 %collective-permute-start.6 = (bf16[192,1536]{1,0:T(8,128)(2,1)S(1)}, bf16[192,1536]{1,0:T(8,128)(2,1)S(1)}, u32[]{:S(2)}, u32[]{:S(2)}) collective-permute-start(bf16[192,1536]{1,0:T(8,128)(2,1)S(1)} %bitcast.11), channel_id=1, source_target_pairs={{0,64},{1,449},{2,66},{3,451},{4,68},{5,453},{6,70},{7,455},{8,72}... | collective-permute-start | bytes 1769480 | tf_op jit(solution)/shard_map/ppermute | solution.py:406
  41.7 12.3 %collective-permute-start.5 = (bf16[192,1536]{1,0:T(8,128)(2,1)S(1)}, bf16[192,1536]{1,0:T(8,128)(2,1)S(1)}, u32[]{:S(2)}, u32[]{:S(2)}) collective-permute-start(bf16[192,1536]{1,0:T(8,128)(2,1)S(1)} %bitcast.9), channel_id=1, source_target_pairs={{0,64},{1,449},{2,66},{3,451},{4,68},{5,453},{6,70},{7,455},{8,72}... | collective-permute-start | bytes 1769480 | tf_op jit(solution)/shard_map/ppermute | solution.py:406
  47.7 19.0 %copy-start.2 = (bf16[192,1536]{1,0:T(8,128)(2,1)}, bf16[192,1536]{1,0:T(8,128)(2,1)S(1)}, u32[]{:S(2)}) copy-start(bf16[192,1536]{1,0:T(8,128)(2,1)S(1)} %collective-permute-done.6.refs_3_) | copy-start | bytes 1769476
  47.7 12.6 %collective-permute-start.8 = (bf16[192,1536]{1,0:T(8,128)(2,1)S(1)}, bf16[192,1536]{1,0:T(8,128)(2,1)}, u32[]{:S(2)}, u32[]{:S(2)}) collective-permute-start(bf16[192,1536]{1,0:T(8,128)(2,1)S(1)} %collective-permute-done.6.refs_3_), channel_id=1, source_target_pairs={{0,64},{1,449},{2,66},{3,451},{4,68},{5,453},{6,70},{7,455},{8,72}... | collective-permute-start | bytes 1769480 | tf_op jit(solution)/shard_map/ppermute | solution.py:406
  54.0 12.6 %copy-start.4 = (bf16[192,1536]{1,0:T(8,128)(2,1)}, bf16[192,1536]{1,0:T(8,128)(2,1)S(1)}, u32[]{:S(2)}) copy-start(bf16[192,1536]{1,0:T(8,128)(2,1)S(1)} %collective-permute-done.5.refs_2_) | copy-start | bytes 1769476
  54.0 12.6 %collective-permute-start.7 = (bf16[192,1536]{1,0:T(8,128)(2,1)S(1)}, bf16[192,1536]{1,0:T(8,128)(2,1)}, u32[]{:S(2)}, u32[]{:S(2)}) collective-permute-start(bf16[192,1536]{1,0:T(8,128)(2,1)S(1)} %collective-permute-done.5.refs_2_), channel_id=1, source_target_pairs={{0,64},{1,449},{2,66},{3,451},{4,68},{5,453},{6,70},{7,455},{8,72}... | collective-permute-start | bytes 1769480 | tf_op jit(solution)/shard_map/ppermute | solution.py:406
  60.3 25.2 %collective-permute-start.10 = (bf16[192,1536]{1,0:T(8,128)(2,1)}, bf16[192,1536]{1,0:T(8,128)(2,1)}, u32[]{:S(2)}, u32[]{:S(2)}) collective-permute-start(bf16[192,1536]{1,0:T(8,128)(2,1)} %collective-permute-done.8.refs_5_), channel_id=1, source_target_pairs={{0,64},{1,449},{2,66},{3,451},{4,68},{5,453},{6,70},{7,455},{8,72}... | collective-permute-start | bytes 1769480 | tf_op jit(solution)/shard_map/ppermute | solution.py:406
  66.7 18.9 %collective-permute-start.9 = (bf16[192,1536]{1,0:T(8,128)(2,1)}, bf16[192,1536]{1,0:T(8,128)(2,1)}, u32[]{:S(2)}, u32[]{:S(2)}) collective-permute-start(bf16[192,1536]{1,0:T(8,128)(2,1)} %collective-permute-done.7.refs_4_), channel_id=1, source_target_pairs={{0,64},{1,449},{2,66},{3,451},{4,68},{5,453},{6,70},{7,455},{8,72}... | collective-permute-start | bytes 1769480 | tf_op jit(solution)/shard_map/ppermute | solution.py:406
  72.0 8.8 %collective-permute-start = (bf16[16,128,128]{2,1,0:T(8,128)(2,1)S(1)}, bf16[16,128,128]{2,1,0:T(8,128)(2,1)S(1)}, u32[]{:S(2)}, u32[]{:S(2)}) collective-permute-start(bf16[16,128,128]{2,1,0:T(8,128)(2,1)S(1)} %slice.4.own_kv), channel_id=1, source_target_pairs={{0,1},{1,0},{2,3},{3,2},{4,5},{5,4},{6,7},{7,6},{8,9},{9,8},{10,11... | collective-permute-start | bytes 1572872 | tf_op jit(solution)/shard_map/ppermute | solution.py:406
  85.5 12.2 %copy-start.5 = (bf16[192,1536]{1,0:T(8,128)(2,1)S(1)}, bf16[192,1536]{1,0:T(8,128)(2,1)}, u32[]{:S(2)}) copy-start(bf16[192,1536]{1,0:T(8,128)(2,1)} %copy-done.4) | copy-start | bytes 1769476
  85.5 14.2 %copy-start.3 = (bf16[192,1536]{1,0:T(8,128)(2,1)S(1)}, bf16[192,1536]{1,0:T(8,128)(2,1)}, u32[]{:S(2)}) copy-start(bf16[192,1536]{1,0:T(8,128)(2,1)} %copy-done.2) | copy-start | bytes 1769476
  85.5 33.2 %copy-start.1 = (bf16[2,96,1536]{2,1,0:T(8,128)(2,1)S(1)}, bf16[2,96,1536]{2,1,0:T(8,128)(2,1)}, u32[]{:S(2)}) copy-start(bf16[2,96,1536]{2,1,0:T(8,128)(2,1)} %copy-done) | copy-start | bytes 1769476
  85.6 33.2 %all-to-all-start.1 = ((bf16[16,224,128]{2,1,0:T(8,128)(2,1)}), bf16[16,224,128]{2,1,0:T(8,128)(2,1)}, u32[]{:S(2)}, u32[]{:S(2)}) async-start(bf16[16,224,128]{2,1,0:T(8,128)(2,1)} %attend_shared.1), calls=%async_computation.1 | async-start | bytes 1835008 | tf_op jit(solution)/shard_map/all_to_all | solution.py:449
  94.5 12.0 %collective-permute-start.17 = (bf16[192,1536]{1,0:T(8,128)(2,1)S(1)}, bf16[192,1536]{1,0:T(8,128)(2,1)S(1)}, u32[]{:S(2)}, u32[]{:S(2)}) collective-permute-start(bf16[192,1536]{1,0:T(8,128)(2,1)S(1)} %broadcast_select_fusion), channel_id=1, source_target_pairs={{0,64},{1,449},{2,66},{3,451},{4,68},{5,453},{6,70},{7,455},{8,72}... | collective-permute-start | bytes 1769480 | tf_op jit(solution)/shard_map/ppermute | solution.py:406
  97.8 11.7 %collective-permute-start.11 = (bf16[192,1536]{1,0:T(8,128)(2,1)S(1)}, bf16[192,1536]{1,0:T(8,128)(2,1)S(1)}, u32[]{:S(2)}, u32[]{:S(2)}) collective-permute-start(bf16[192,1536]{1,0:T(8,128)(2,1)S(1)} %copy-done.5), channel_id=1, source_target_pairs={{0,1},{1,0},{2,3},{3,2},{4,5},{5,4},{6,7},{7,6},{8,9},{9,8},{10,11... | collective-permute-start | bytes 1769480 | tf_op jit(solution)/shard_map/ppermute | solution.py:406
  99.7 11.7 %collective-permute-start.12 = (bf16[192,1536]{1,0:T(8,128)(2,1)S(1)}, bf16[192,1536]{1,0:T(8,128)(2,1)S(1)}, u32[]{:S(2)}, u32[]{:S(2)}) collective-permute-start(bf16[192,1536]{1,0:T(8,128)(2,1)S(1)} %copy-done.3), channel_id=1, source_target_pairs={{0,1},{1,0},{2,3},{3,2},{4,5},{5,4},{6,7},{7,6},{8,9},{9,8},{10,11... | collective-permute-start | bytes 1769480 | tf_op jit(solution)/shard_map/ppermute | solution.py:406
  102.1 12.6 %collective-permute-start.15 = (bf16[192,1536]{1,0:T(8,128)(2,1)}, bf16[192,1536]{1,0:T(8,128)(2,1)}, u32[]{:S(2)}, u32[]{:S(2)}) collective-permute-start(bf16[192,1536]{1,0:T(8,128)(2,1)} %collective-permute-done.9.refs_6_), channel_id=1, source_target_pairs={{0,1},{1,0},{2,3},{3,2},{4,5},{5,4},{6,7},{7,6},{8,9},{9,8},{10,11... | collective-permute-start | bytes 1769480 | tf_op jit(solution)/shard_map/ppermute | solution.py:406
  104.1 9.9 %collective-permute-start.13 = (bf16[192,1536]{1,0:T(8,128)(2,1)}, bf16[192,1536]{1,0:T(8,128)(2,1)S(1)}, u32[]{:S(2)}, u32[]{:S(2)}) collective-permute-start(bf16[192,1536]{1,0:T(8,128)(2,1)} %collective-permute-done.7.refs_4_), channel_id=1, source_target_pairs={{0,1},{1,0},{2,3},{3,2},{4,5},{5,4},{6,7},{7,6},{8,9},{9,8},{10,11... | collective-permute-start | bytes 1769480 | tf_op jit(solution)/shard_map/ppermute | solution.py:406
  106.5 5.0 %copy-start.11 = (bf16[192,1536]{1,0:T(8,128)(2,1)}, bf16[192,1536]{1,0:T(8,128)(2,1)S(1)}, u32[]{:S(2)}) copy-start(bf16[192,1536]{1,0:T(8,128)(2,1)S(1)} %collective-permute-done.17.refs_14_) | copy-start | bytes 1769476
  106.5 7.4 %collective-permute-start.14 = (bf16[192,1536]{1,0:T(8,128)(2,1)}, bf16[192,1536]{1,0:T(8,128)(2,1)S(1)}, u32[]{:S(2)}, u32[]{:S(2)}) collective-permute-start(bf16[192,1536]{1,0:T(8,128)(2,1)} %collective-permute-done.8.refs_5_), channel_id=1, source_target_pairs={{0,1},{1,0},{2,3},{3,2},{4,5},{5,4},{6,7},{7,6},{8,9},{9,8},{10,11... | collective-permute-start | bytes 1769480 | tf_op jit(solution)/shard_map/ppermute | solution.py:406
  109.5 4.4 %copy-start.12 = (bf16[192,1536]{1,0:T(8,128)(2,1)}, bf16[192,1536]{1,0:T(8,128)(2,1)S(1)}, u32[]{:S(2)}) copy-start(bf16[192,1536]{1,0:T(8,128)(2,1)S(1)} %collective-permute-done.11.refs_8_) | copy-start | bytes 1769476
  109.5 5.2 %collective-permute-start.16 = (bf16[192,1536]{1,0:T(8,128)(2,1)}, bf16[192,1536]{1,0:T(8,128)(2,1)}, u32[]{:S(2)}, u32[]{:S(2)}) collective-permute-start(bf16[192,1536]{1,0:T(8,128)(2,1)} %collective-permute-done.10.refs_7_), channel_id=1, source_target_pairs={{0,1},{1,0},{2,3},{3,2},{4,5},{5,4},{6,7},{7,6},{8,9},{9,8},{10,11... | collective-permute-start | bytes 1769480 | tf_op jit(solution)/shard_map/ppermute | solution.py:406
  111.5 2.4 %copy-start.13 = (bf16[192,1536]{1,0:T(8,128)(2,1)}, bf16[192,1536]{1,0:T(8,128)(2,1)S(1)}, u32[]{:S(2)}) copy-start(bf16[192,1536]{1,0:T(8,128)(2,1)S(1)} %collective-permute-done.12.refs_9_) | copy-start | bytes 1769476
  111.5 4.2 %collective-permute-start.18 = (bf16[192,1536]{1,0:T(8,128)(2,1)S(1)}, bf16[192,1536]{1,0:T(8,128)(2,1)}, u32[]{:S(2)}, u32[]{:S(2)}) collective-permute-start(bf16[192,1536]{1,0:T(8,128)(2,1)S(1)} %collective-permute-done.17.refs_14_), channel_id=1, source_target_pairs={{0,1},{1,0},{2,3},{3,2},{4,5},{5,4},{6,7},{7,6},{8,9},{9,8},{10,11... | collective-permute-start | bytes 1769480 | tf_op jit(solution)/shard_map/ppermute | solution.py:406
  (6 other events, 4.9 us)

commit v9 on v8

--- a/solution.py
+++ b/solution.py
@@ -186,7 +186,8 @@
 Q_ROWS = 512
 STEP_ROWS = 1024
 VMEM = 32 * 2**20
-PLACE_VMEM = 8 * 2**20
+PLACE_VMEM = 60 * 2**20
+JOIN_VMEM = 60 * 2**20
 PROJECT_VMEM = 50 * 2**20
 
 
@@ -302,6 +303,42 @@
     )(where, mine, near, near_far, part, part_far)
 
 
+def join_kernel(*refs):
+    halves, wholes, (held, in_sems, out_sems) = refs[:6], refs[6:9], refs[9:]
+    rows = halves[0].shape[0]
+    loads = [
+        pltpu.make_async_copy(half, held.at[index // 2, pl.ds(index % 2 * rows, rows)], in_sems.at[index])
+        for index, half in enumerate(halves)
+    ]
+    for load in loads:
+        load.start()
+    stores = []
+    for index, whole in enumerate(wholes):
+        loads[2 * index].wait()
+        loads[2 * index + 1].wait()
+        stores.append(pltpu.make_async_copy(held.at[index], whole, out_sems.at[index]))
+        stores[-1].start()
+    for store in stores:
+        store.wait()
+
+
+def join(chunks):
+    rows, columns = chunks[0][0].shape
+    return pl.pallas_call(
+        join_kernel,
+        in_specs=[pl.BlockSpec(memory_space=pl.ANY)] * 6,
+        out_specs=[pl.BlockSpec(memory_space=pl.ANY)] * 3,
+        out_shape=[jax.ShapeDtypeStruct((2 * rows, columns), jnp.bfloat16)] * 3,
+        scratch_shapes=[
+            pltpu.VMEM((3, 2 * rows, columns), jnp.bfloat16),
+            pltpu.SemaphoreType.DMA((6,)),
+            pltpu.SemaphoreType.DMA((3,)),
+        ],
+        compiler_params=pltpu.CompilerParams(vmem_limit_bytes=JOIN_VMEM),
+        name="join",
+    )(*[half for chunk in chunks for half in chunk])
+
+
 def slot_of(ret, head):
     chip, member = head // 3, head % 3
     low, high = ret.at[2 * chip], ret.at[2 * chip + 1]
@@ -322,24 +359,22 @@
 
 
 HOPS = (0, 1, 2, 3, -1, -2, -3)
-PIECES = 2 * len(HOPS) + 2
+PIECES = 2 + 6 + 2
 
 
 def project_kernel(where, ret, *refs):
     weights, (vis_out, txt_out, slots, held, sems) = refs[:PIECES], refs[PIECES:]
     y, core = where[0], where[2]
     sign = 1 - 2 * core
-    half_rows = TRIO // 2
+    places = [(0, 0, 1), (0, 1, 1)] + [(chunk, 0, 2) for chunk in range(1, 7)] + [(7, core, 1), (7, 1 - core, 1)]
     copies = []
-    for index in range(PIECES):
-        chunk, half = index // 2, index % 2
-        if chunk == len(HOPS):
-            half = core if half == 0 else 1 - core
-        start = chunk % 2 * TRIO + half * half_rows
-        to = held.at[chunk // 2, pl.ds(pl.multiple_of(start, 64), half_rows)]
+    for index, (chunk, half, count) in enumerate(places):
+        start = chunk % 2 * TRIO + half * (TRIO // 2)
+        to = held.at[chunk // 2, pl.ds(pl.multiple_of(start, 64), count * (TRIO // 2))]
         copies.append(pltpu.make_async_copy(weights[index], to, sems.at[index]))
     for copy in copies:
         copy.start()
+    arrivals = [copies[:2]] + [[copy] for copy in copies[2:8]] + [copies[8:]]
     for slot in range(SLOTS):
         valid = where[5 + slot] > 0
         for source, row in enumerate(slot_of(ret, where[3 + slot])):
@@ -357,8 +392,8 @@
         attention = jnp.concatenate([low[:ROWS], shared, high[:ROWS]], axis=1)
         txt_out[:, pl.ds(pl.multiple_of(chip * TRIO, TRIO), TRIO)] = attention[VIS_ROWS:]
         pieces.append(attention)
-        copies[2 * index].wait()
-        copies[2 * index + 1].wait()
+        for copy in arrivals[index]:
+            copy.wait()
         if index % 2 == 1:
             both = jnp.concatenate(pieces[-2:], axis=1)
             total += jnp.dot(both, held[index // 2], preferred_element_type=jnp.float32)
@@ -448,8 +483,8 @@
     returning, chunks[1:] = lax.optimization_barrier((returning, chunks[1:]))
     returned = lax.all_to_all(returning, "seq", split_axis=0, concat_axis=0, tiled=True)
     opposite = shift_y(jnp.where(core == 0, *chunks[3]))
-    far_chunks = [[swap(half) for half in chunk] for chunk in chunks[1:]]
-    weights = [half for chunk in chunks + far_chunks for half in chunk] + [opposite, swap(opposite)]
+    hops = join(chunks[1:])
+    weights = [*chunks[0], *hops, *map(swap, hops), opposite, swap(opposite)]
     vis_out, txt_out, lse_slots = project(where, returned, weights)
     return vis_out, txt_out, lse_slots
 

time: 127 us -> 125 us (0.984)
  starting transfers between devices: 80.4 us -> 74 us
  waiting for transfers between devices: 14.4 us -> 18.3 us
  Pallas kernels: 23 us -> 26.1 us
  local copies, waits for them, and re-layouts: 5.2 us -> 3.57 us
    ppermute x19 -> x16, starting transfers between devices: 60.6 us -> 54.4 us  [permute(): return lax.ppermute(operand, AXES, pairs)]
    pallas_call x0 -> x1, Pallas kernels: none -> 3.07 us  [join(): pl.pallas_call(join_kernel, in_specs=[pl.BlockSpec(memory_space=pl.ANY)]...]
    ppermute x19 -> x16, waiting for transfers between devices: 11.3 us -> 14 us  [permute(): return lax.ppermute(operand, AXES, pairs)]
    unnamed x34 -> x26, local copies, waits for them, and re-layouts: 4.99 us -> 2.82 us
    pallas_call x1, Pallas kernels: 1.75 us -> 3.24 us  [place(): pl.pallas_call(place_kernel, grid_spec=pltpu.PrefetchScalarGridSpec(num_s...]
    pallas_call x1, Pallas kernels: 6.75 us -> 5.34 us  [project(): pl.pallas_call(project_kernel, grid_spec=pltpu.PrefetchScalarGridSpec(num...]
  transfers between devices with their start and end apart: 21 -> 18, of which waited for: 8 -> 8; matrix products, arithmetic and copies ran while one was open for 1% -> 2% of each run, Pallas kernels for 11% -> 14%
where the time goes in v9:
time: 125 us; the launch traced here: 124 us
  starting transfers between devices  74 us (59%)
  Pallas kernels  26.1 us (21%)
  waiting for transfers between devices  18.3 us (15%)
  local copies, waits for them, and re-layouts  3.57 us (3%)
    ppermute x16, starting transfers between devices, permute(): return lax.ppermute(operand, AXES, pairs)  54.4 us
    ppermute x16, waiting for transfers between devices, permute(): return lax.ppermute(operand, AXES, pairs)  14 us
    all_to_all x1, starting transfers between devices, on_device(): lax.all_to_all(sending, 'seq', split_axis=0, concat_axis=0, tiled=True)  12 us
    all_to_all x1, starting transfers between devices, on_device(): lax.all_to_all(returning, 'seq', split_axis=0, concat_axis=0, tiled=True)  7.64 us
    pallas_call x1, Pallas kernels, attend_whole(): pl.pallas_call(whole_kernel, grid=(steps,), in_specs=[pl.BlockSpec((N_SEQ...  6.82 us
    pallas_call x1, Pallas kernels, project(): pl.pallas_call(project_kernel, grid_spec=pltpu.PrefetchScalarGridSpec(num...  5.34 us
    pallas_call x1, Pallas kernels, attend_shared(): pl.pallas_call(shared_kernel, grid_spec=pltpu.PrefetchScalarGridSpec(num_...  4.73 us
    all_to_all x1, waiting for transfers between devices, on_device(): lax.all_to_all(returning, 'seq', split_axis=0, concat_axis=0, tiled=True)  4.31 us
  transfers between devices with their start and end apart: 18, of which 8 were waited for; matrix products, arithmetic and copies ran while one was open for 2% of the time, Pallas kernels for 14%

profile of v9, /device:TPU:1, one launch (start us, length us, event | category | flops | bytes accessed | tf_op | source)
XLA Modules:
  0.0 124.2 jit_solution(13521880420293269956)
XLA Ops:
  0.6 2.9 %pack.1 = bf16[16,584,128]{2,1,0:T(8,128)(2,1)} custom-call(s32[1,112]{1,0:T(1,128)} %bitcast.13, s32[1,16]{1,0:T(1,128)} %bitcast.14, bf16[112,9216]{1,0:T(8,128)(2,1)} %vv.1, bf16[112,9216]{1,0:T(8,128)(2,1)} %vv.1, bf16[112,9216]{1,0:T(8,128)(2,1)} %vv.1, bf16[16,9216]{1,0:T(8,128)(2,1)} %tv.1, bf16[16,9216]{1,0:T(8,128)(2,1)} %tv.1, bf16[16,9216]{1,0:T(8,128)(2,1)} %tv.1), custom_call_target="tpu_custom_call" | custom-call | tf_op jit(solution)/shard_map/pack/pallas_call | solution.py:66
  3.6 12.0 %all-to-all-start = ((bf16[16,584,128]{2,1,0:T(8,128)(2,1)}), bf16[16,584,128]{2,1,0:T(8,128)(2,1)S(1)}, u32[]{:S(2)}, u32[]{:S(2)}) async-start(bf16[16,584,128]{2,1,0:T(8,128)(2,1)} %pack.1), calls=%async_computation | async-start | bytes 4784128 | tf_op jit(solution)/shard_map/all_to_all | solution.py:474
  15.6 4.4 %collective-permute-start.1 = (bf16[96,1536]{1,0:T(8,128)(2,1)S(1)}, bf16[96,1536]{1,0:T(8,128)(2,1)S(1)}, u32[]{:S(2)}, u32[]{:S(2)}) collective-permute-start(bf16[96,1536]{1,0:T(8,128)(2,1)S(1)} %copy-done.8), channel_id=1, source_target_pairs={{0,16},{1,49},{2,18},{3,51},{4,20},{5,53},{6,22},{7,55},{8,24},{9,... | collective-permute-start | bytes 884744 | tf_op jit(solution)/shard_map/ppermute | solution.py:441
  20.9 2.7 %collective-permute-done.1.near = bf16[96,1536]{1,0:T(8,128)(2,1)S(1)} collective-permute-done((bf16[96,1536]{1,0:T(8,128)(2,1)S(1)}, bf16[96,1536]{1,0:T(8,128)(2,1)S(1)}, u32[]{:S(2)}, u32[]{:S(2)}) %collective-permute-start.1) | collective-permute-done | bytes 294944 | tf_op jit(solution)/shard_map/ppermute | solution.py:441
  23.6 3.8 %collective-permute-start.2 = (bf16[96,1536]{1,0:T(8,128)(2,1)S(1)}, bf16[96,1536]{1,0:T(8,128)(2,1)}, u32[]{:S(2)}, u32[]{:S(2)}) collective-permute-start(bf16[96,1536]{1,0:T(8,128)(2,1)S(1)} %collective-permute-done.1.near), channel_id=1, source_target_pairs={{0,1},{1,0},{2,3},{3,2},{4,5},{5,4},{6,7},{7,6},{8,9},{9,8},{10,11... | collective-permute-start | bytes 884744 | tf_op jit(solution)/shard_map/ppermute | solution.py:441
  27.4 1.3 %collective-permute-start.4 = (bf16[96,1536]{1,0:T(8,128)(2,1)S(1)}, bf16[96,1536]{1,0:T(8,128)(2,1)S(1)}, u32[]{:S(2)}, u32[]{:S(2)}) collective-permute-start(bf16[96,1536]{1,0:T(8,128)(2,1)S(1)} %collective-permute-done.3.part), channel_id=1, source_target_pairs={{0,1},{2,3},{4,5},{6,7},{8,9},{10,11},{12,13},{14,15},{16,17},{18,... | collective-permute-start | bytes 884744 | tf_op jit(solution)/shard_map/ppermute | solution.py:441
  29.5 2.5 %collective-permute-done.4.part_far = bf16[96,1536]{1,0:T(8,128)(2,1)S(1)} collective-permute-done((bf16[96,1536]{1,0:T(8,128)(2,1)S(1)}, bf16[96,1536]{1,0:T(8,128)(2,1)S(1)}, u32[]{:S(2)}, u32[]{:S(2)}) %collective-permute-start.4) | collective-permute-done | bytes 294944 | tf_op jit(solution)/shard_map/ppermute | solution.py:441
  32.7 3.2 %place.1 = (bf16[2,96,1536]{2,1,0:T(8,128)(2,1)}, bf16[2,96,1536]{2,1,0:T(8,128)(2,1)}) custom-call(s32[7]{0:T(128)} %concatenate.3.where, bf16[96,1536]{1,0:T(8,128)(2,1)} %mine.1, bf16[96,1536]{1,0:T(8,128)(2,1)} %copy-done.9, bf16[96,1536]{1,0:T(8,128)(2,1)} %collective-permute-done.2.near_far, bf16[96,1536]{1,0:T(8,128)(2,1)} %copy-done.10, ...), custom_call_target="tpu_custom_call" | custom-call | tf_op jit(solution)/shard_map/place/pallas_call | solution.py:292
  35.9 5.1 %collective-permute-start.6 = (bf16[192,1536]{1,0:T(8,128)(2,1)}, bf16[192,1536]{1,0:T(8,128)(2,1)S(1)}, u32[]{:S(2)}, u32[]{:S(2)}) collective-permute-start(bf16[192,1536]{1,0:T(8,128)(2,1)} %bitcast.11), channel_id=1, source_target_pairs={{0,64},{1,449},{2,66},{3,451},{4,68},{5,453},{6,70},{7,455},{8,72}... | collective-permute-start | bytes 1769480 | tf_op jit(solution)/shard_map/ppermute | solution.py:441
  41.0 3.0 %collective-permute-start.5 = (bf16[192,1536]{1,0:T(8,128)(2,1)}, bf16[192,1536]{1,0:T(8,128)(2,1)S(1)}, u32[]{:S(2)}, u32[]{:S(2)}) collective-permute-start(bf16[192,1536]{1,0:T(8,128)(2,1)} %bitcast.9), channel_id=1, source_target_pairs={{0,64},{1,449},{2,66},{3,451},{4,68},{5,453},{6,70},{7,455},{8,72}... | collective-permute-start | bytes 1769480 | tf_op jit(solution)/shard_map/ppermute | solution.py:441
  44.0 4.1 %collective-permute-done.6.refs_1_ = bf16[192,1536]{1,0:T(8,128)(2,1)S(1)} collective-permute-done((bf16[192,1536]{1,0:T(8,128)(2,1)}, bf16[192,1536]{1,0:T(8,128)(2,1)S(1)}, u32[]{:S(2)}, u32[]{:S(2)}) %collective-permute-start.6) | collective-permute-done | bytes 589856 | tf_op jit(solution)/shard_map/ppermute | solution.py:441
  48.1 5.2 %collective-permute-start.8 = (bf16[192,1536]{1,0:T(8,128)(2,1)S(1)}, bf16[192,1536]{1,0:T(8,128)(2,1)}, u32[]{:S(2)}, u32[]{:S(2)}) collective-permute-start(bf16[192,1536]{1,0:T(8,128)(2,1)S(1)} %collective-permute-done.6.refs_1_), channel_id=1, source_target_pairs={{0,64},{1,449},{2,66},{3,451},{4,68},{5,453},{6,70},{7,455},{8,72}... | collective-permute-start | bytes 1769480 | tf_op jit(solution)/shard_map/ppermute | solution.py:441
  53.4 1.1 collective-permute-done.5.refs_0_
  54.5 5.2 %collective-permute-start.7 = (bf16[192,1536]{1,0:T(8,128)(2,1)S(1)}, bf16[192,1536]{1,0:T(8,128)(2,1)}, u32[]{:S(2)}, u32[]{:S(2)}) collective-permute-start(bf16[192,1536]{1,0:T(8,128)(2,1)S(1)} %collective-permute-done.5.refs_0_), channel_id=1, source_target_pairs={{0,64},{1,449},{2,66},{3,451},{4,68},{5,453},{6,70},{7,455},{8,72}... | collective-permute-start | bytes 1769480 | tf_op jit(solution)/shard_map/ppermute | solution.py:441
  60.7 5.3 %collective-permute-start.10 = (bf16[192,1536]{1,0:T(8,128)(2,1)}, bf16[192,1536]{1,0:T(8,128)(2,1)S(1)}, u32[]{:S(2)}, u32[]{:S(2)}) collective-permute-start(bf16[192,1536]{1,0:T(8,128)(2,1)} %collective-permute-done.8.refs_3_), channel_id=1, source_target_pairs={{0,64},{1,449},{2,66},{3,451},{4,68},{5,453},{6,70},{7,455},{8,72}... | collective-permute-start | bytes 1769480 | tf_op jit(solution)/shard_map/ppermute | solution.py:441
  66.0 1.0 collective-permute-done.7.refs_2_
  67.0 5.3 %collective-permute-start.9 = (bf16[192,1536]{1,0:T(8,128)(2,1)}, bf16[192,1536]{1,0:T(8,128)(2,1)}, u32[]{:S(2)}, u32[]{:S(2)}) collective-permute-start(bf16[192,1536]{1,0:T(8,128)(2,1)} %collective-permute-done.7.refs_2_), channel_id=1, source_target_pairs={{0,64},{1,449},{2,66},{3,451},{4,68},{5,453},{6,70},{7,455},{8,72}... | collective-permute-start | bytes 1769480 | tf_op jit(solution)/shard_map/ppermute | solution.py:441
  72.4 1.9 %collective-permute-start = (bf16[16,128,128]{2,1,0:T(8,128)(2,1)S(1)}, bf16[16,128,128]{2,1,0:T(8,128)(2,1)S(1)}, u32[]{:S(2)}, u32[]{:S(2)}) collective-permute-start(bf16[16,128,128]{2,1,0:T(8,128)(2,1)S(1)} %slice.4.own_kv), channel_id=1, source_target_pairs={{0,1},{1,0},{2,3},{3,2},{4,5},{5,4},{6,7},{7,6},{8,9},{9,8},{10,11... | collective-permute-start | bytes 1572872 | tf_op jit(solution)/shard_map/ppermute | solution.py:441
  74.3 6.8 %attend_whole.1 = (bf16[16,128,128]{2,1,0:T(8,128)(2,1)S(1)}, f32[16,128]{1,0:T(8,128)S(1)}) custom-call(bf16[16,584,128]{2,1,0:T(8,128)(2,1)S(1)} %all-to-all-done.cut.q.k.v, bf16[16,584,128]{2,1,0:T(8,128)(2,1)S(1)} %all-to-all-done.cut.q.k.v, bf16[16,584,128]{2,1,0:T(8,128)(2,1)S(1)} %all-to-all-done.cut.q.k.v, ...), custom_call_target="tpu_custom_call" | custom-call | flops 134217728 | bytes 2097152 | tf_op jit(solution)/shard_map/attend_whole/pallas_call | solution.py:215
  81.2 4.7 %attend_shared.1 = bf16[16,224,128]{2,1,0:T(8,128)(2,1)} custom-call(s32[7]{0:T(128)S(1)} %copy-done.2, bf16[16,584,128]{2,1,0:T(8,128)(2,1)S(1)} %all-to-all-done.cut.q.k.v, bf16[16,584,128]{2,1,0:T(8,128)(2,1)S(1)} %all-to-all-done.cut.q.k.v, bf16[16,128,128]{2,1,0:T(8,128)(2,1)S(1)} %slice.4.own_kv, ...), custom_call_target="tpu_custom_call" | custom-call | flops 67108864 | bytes 2097152 | tf_op jit(solution)/shard_map/attend_shared/pallas_call | solution.py:242
  85.9 7.6 %all-to-all-start.1 = ((bf16[16,224,128]{2,1,0:T(8,128)(2,1)}), bf16[16,224,128]{2,1,0:T(8,128)(2,1)S(1)}, u32[]{:S(2)}, u32[]{:S(2)}) async-start(bf16[16,224,128]{2,1,0:T(8,128)(2,1)} %attend_shared.1), calls=%async_computation.1 | async-start | bytes 1835008 | tf_op jit(solution)/shard_map/all_to_all | solution.py:484
  94.4 3.1 %collective-permute-start.14 = (bf16[192,1536]{1,0:T(8,128)(2,1)}, bf16[192,1536]{1,0:T(8,128)(2,1)S(1)}, u32[]{:S(2)}, u32[]{:S(2)}) collective-permute-start(bf16[192,1536]{1,0:T(8,128)(2,1)} %broadcast_select_fusion), channel_id=1, source_target_pairs={{0,64},{1,449},{2,66},{3,451},{4,68},{5,453},{6,70},{7,455},{8,72}... | collective-permute-start | bytes 1769480 | tf_op jit(solution)/shard_map/ppermute | solution.py:441
  97.5 3.1 %join.1 = (bf16[384,1536]{1,0:T(8,128)(2,1)}, bf16[384,1536]{1,0:T(8,128)(2,1)}, bf16[384,1536]{1,0:T(8,128)(2,1)}) custom-call(bf16[192,1536]{1,0:T(8,128)(2,1)} %copy-done.7, bf16[192,1536]{1,0:T(8,128)(2,1)} %copy-done.6, bf16[192,1536]{1,0:T(8,128)(2,1)} %collective-permute-done.7.refs_2_, bf16[192,1536]{1,0:T(8,128)(2,1)} %collective-permute-done.8.refs_3_, ...), custom_call_target="tpu_custom_call" | custom-call | tf_op jit(solution)/shard_map/join/pallas_call | solution.py:327
  100.6 2.0 %collective-permute-start.11 = (bf16[384,1536]{1,0:T(8,128)(2,1)}, bf16[384,1536]{1,0:T(8,128)(2,1)S(1)}, u32[]{:S(2)}, u32[]{:S(2)}) collective-permute-start(bf16[384,1536]{1,0:T(8,128)(2,1)} %get-tuple-element.28.refs_2_), channel_id=1, source_target_pairs={{0,1},{1,0},{2,3},{3,2},{4,5},{5,4},{6,7},{7,6},{8,9},{9,8},{10,11... | collective-permute-start | bytes 3538952 | tf_op jit(solution)/shard_map/ppermute | solution.py:441
  102.7 2.3 %collective-permute-start.12 = (bf16[384,1536]{1,0:T(8,128)(2,1)}, bf16[384,1536]{1,0:T(8,128)(2,1)S(1)}, u32[]{:S(2)}, u32[]{:S(2)}) collective-permute-start(bf16[384,1536]{1,0:T(8,128)(2,1)} %get-tuple-element.29.refs_3_), channel_id=1, source_target_pairs={{0,1},{1,0},{2,3},{3,2},{4,5},{5,4},{6,7},{7,6},{8,9},{9,8},{10,11... | collective-permute-start | bytes 3538952 | tf_op jit(solution)/shard_map/ppermute | solution.py:441
  105.0 2.0 %collective-permute-start.13 = (bf16[384,1536]{1,0:T(8,128)(2,1)}, bf16[384,1536]{1,0:T(8,128)(2,1)}, u32[]{:S(2)}, u32[]{:S(2)}) collective-permute-start(bf16[384,1536]{1,0:T(8,128)(2,1)} %get-tuple-element.30.refs_4_), channel_id=1, source_target_pairs={{0,1},{1,0},{2,3},{3,2},{4,5},{5,4},{6,7},{7,6},{8,9},{9,8},{10,11... | collective-permute-start | bytes 3538952 | tf_op jit(solution)/shard_map/ppermute | solution.py:441
  107.0 3.8 %collective-permute-start.15 = (bf16[192,1536]{1,0:T(8,128)(2,1)S(1)}, bf16[192,1536]{1,0:T(8,128)(2,1)S(1)}, u32[]{:S(2)}, u32[]{:S(2)}) collective-permute-start(bf16[192,1536]{1,0:T(8,128)(2,1)S(1)} %collective-permute-done.14.refs_8_), channel_id=1, source_target_pairs={{0,1},{1,0},{2,3},{3,2},{4,5},{5,4},{6,7},{7,6},{8,9},{9,8},{10,11... | collective-permute-start | bytes 1769480 | tf_op jit(solution)/shard_map/ppermute | solution.py:441
  110.8 1.6 %collective-permute-done.15.refs_9_ = bf16[192,1536]{1,0:T(8,128)(2,1)S(1)} collective-permute-done((bf16[192,1536]{1,0:T(8,128)(2,1)S(1)}, bf16[192,1536]{1,0:T(8,128)(2,1)S(1)}, u32[]{:S(2)}, u32[]{:S(2)}) %collective-permute-start.15) | collective-permute-done | bytes 589856 | tf_op jit(solution)/shard_map/ppermute | solution.py:441
  112.5 1.0 copy-done.4
  113.5 1.0 copy-done.5
  114.5 4.3 %all-to-all-done.1.ret = bf16[16,224,128]{2,1,0:T(8,128)(2,1)S(1)} async-done(((bf16[16,224,128]{2,1,0:T(8,128)(2,1)}), bf16[16,224,128]{2,1,0:T(8,128)(2,1)S(1)}, u32[]{:S(2)}, u32[]{:S(2)}) %all-to-all-start.1) | async-done | bytes 917536 | tf_op jit(solution)/shard_map/all_to_all | solution.py:484
  118.8 5.3 %project.1 = (bf16[112,1536]{1,0:T(8,128)(2,1)}, bf16[16,3072]{1,0:T(8,128)(2,1)}, f32[2,2048]{1,0:T(2,128)}) custom-call(s32[7]{0:T(128)S(1)} %copy-done.2, bf16[16,224,128]{2,1,0:T(8,128)(2,1)S(1)} %all-to-all-done.1.ret, bf16[192,1536]{1,0:T(8,128)(2,1)S(1)} %bitcast.10, bf16[192,1536]{1,0:T(8,128)(2,1)S(1)} %bitcast.12, ...), custom_call_target="tpu_custom_call" | custom-call | tf_op jit(solution)/shard_map/project/pallas_call | solution.py:405
  (45 shorter events, 4.4 us)
Async XLA Ops:
  3.6 12.0 %copy-start.8 = (bf16[96,1536]{1,0:T(8,128)(2,1)S(1)}, bf16[96,1536]{1,0:T(8,128)(2,1)}, u32[]{:S(2)}) copy-start(bf16[96,1536]{1,0:T(8,128)(2,1)} %mine.1) | copy-start | bytes 884740
  3.6 17.1 %copy-start.12 = (s32[24]{0:T(128)S(1)}, s32[24]{0:T(128)}, u32[]{:S(2)}) copy-start(s32[24]{0:T(128)} %param.10) | copy-start | bytes 292
  3.6 68.8 %all-to-all-start = ((bf16[16,584,128]{2,1,0:T(8,128)(2,1)}), bf16[16,584,128]{2,1,0:T(8,128)(2,1)S(1)}, u32[]{:S(2)}, u32[]{:S(2)}) async-start(bf16[16,584,128]{2,1,0:T(8,128)(2,1)} %pack.1), calls=%async_computation | async-start | bytes 4784128 | tf_op jit(solution)/shard_map/all_to_all | solution.py:474
  15.6 8.0 %collective-permute-start.1 = (bf16[96,1536]{1,0:T(8,128)(2,1)S(1)}, bf16[96,1536]{1,0:T(8,128)(2,1)S(1)}, u32[]{:S(2)}, u32[]{:S(2)}) collective-permute-start(bf16[96,1536]{1,0:T(8,128)(2,1)S(1)} %copy-done.8), channel_id=1, source_target_pairs={{0,16},{1,49},{2,18},{3,51},{4,20},{5,53},{6,22},{7,55},{8,24},{9,... | collective-permute-start | bytes 884744 | tf_op jit(solution)/shard_map/ppermute | solution.py:441
  19.9 7.4 %collective-permute-start.3 = (bf16[96,1536]{1,0:T(8,128)(2,1)S(1)}, bf16[96,1536]{1,0:T(8,128)(2,1)S(1)}, u32[]{:S(2)}, u32[]{:S(2)}) collective-permute-start(bf16[96,1536]{1,0:T(8,128)(2,1)S(1)} %copy-done.8), channel_id=1, source_target_pairs={{0,32},{2,34},{4,36},{6,38},{8,40},{10,42},{12,44},{14,46},{16,48}... | collective-permute-start | bytes 884744 | tf_op jit(solution)/shard_map/ppermute | solution.py:441
  23.6 8.4 %copy-start.9 = (bf16[96,1536]{1,0:T(8,128)(2,1)}, bf16[96,1536]{1,0:T(8,128)(2,1)S(1)}, u32[]{:S(2)}) copy-start(bf16[96,1536]{1,0:T(8,128)(2,1)S(1)} %collective-permute-done.1.near) | copy-start | bytes 884740
  23.6 5.9 %collective-permute-start.2 = (bf16[96,1536]{1,0:T(8,128)(2,1)S(1)}, bf16[96,1536]{1,0:T(8,128)(2,1)}, u32[]{:S(2)}, u32[]{:S(2)}) collective-permute-start(bf16[96,1536]{1,0:T(8,128)(2,1)S(1)} %collective-permute-done.1.near), channel_id=1, source_target_pairs={{0,1},{1,0},{2,3},{3,2},{4,5},{5,4},{6,7},{7,6},{8,9},{9,8},{10,11... | collective-permute-start | bytes 884744 | tf_op jit(solution)/shard_map/ppermute | solution.py:441
  27.4 4.6 %copy-start.10 = (bf16[96,1536]{1,0:T(8,128)(2,1)}, bf16[96,1536]{1,0:T(8,128)(2,1)S(1)}, u32[]{:S(2)}) copy-start(bf16[96,1536]{1,0:T(8,128)(2,1)S(1)} %collective-permute-done.3.part) | copy-start | bytes 884740
  27.4 4.6 %collective-permute-start.4 = (bf16[96,1536]{1,0:T(8,128)(2,1)S(1)}, bf16[96,1536]{1,0:T(8,128)(2,1)S(1)}, u32[]{:S(2)}, u32[]{:S(2)}) collective-permute-start(bf16[96,1536]{1,0:T(8,128)(2,1)S(1)} %collective-permute-done.3.part), channel_id=1, source_target_pairs={{0,1},{2,3},{4,5},{6,7},{8,9},{10,11},{12,13},{14,15},{16,17},{18,... | collective-permute-start | bytes 884744 | tf_op jit(solution)/shard_map/ppermute | solution.py:441
  32.0 0.7 copy-start.11
  35.9 12.2 %collective-permute-start.6 = (bf16[192,1536]{1,0:T(8,128)(2,1)}, bf16[192,1536]{1,0:T(8,128)(2,1)S(1)}, u32[]{:S(2)}, u32[]{:S(2)}) collective-permute-start(bf16[192,1536]{1,0:T(8,128)(2,1)} %bitcast.11), channel_id=1, source_target_pairs={{0,64},{1,449},{2,66},{3,451},{4,68},{5,453},{6,70},{7,455},{8,72}... | collective-permute-start | bytes 1769480 | tf_op jit(solution)/shard_map/ppermute | solution.py:441
  41.0 13.4 %collective-permute-start.5 = (bf16[192,1536]{1,0:T(8,128)(2,1)}, bf16[192,1536]{1,0:T(8,128)(2,1)S(1)}, u32[]{:S(2)}, u32[]{:S(2)}) collective-permute-start(bf16[192,1536]{1,0:T(8,128)(2,1)} %bitcast.9), channel_id=1, source_target_pairs={{0,64},{1,449},{2,66},{3,451},{4,68},{5,453},{6,70},{7,455},{8,72}... | collective-permute-start | bytes 1769480 | tf_op jit(solution)/shard_map/ppermute | solution.py:441
  48.1 18.9 %copy-start.6 = (bf16[192,1536]{1,0:T(8,128)(2,1)}, bf16[192,1536]{1,0:T(8,128)(2,1)S(1)}, u32[]{:S(2)}) copy-start(bf16[192,1536]{1,0:T(8,128)(2,1)S(1)} %collective-permute-done.6.refs_1_) | copy-start | bytes 1769476
  48.1 12.5 %collective-permute-start.8 = (bf16[192,1536]{1,0:T(8,128)(2,1)S(1)}, bf16[192,1536]{1,0:T(8,128)(2,1)}, u32[]{:S(2)}, u32[]{:S(2)}) collective-permute-start(bf16[192,1536]{1,0:T(8,128)(2,1)S(1)} %collective-permute-done.6.refs_1_), channel_id=1, source_target_pairs={{0,64},{1,449},{2,66},{3,451},{4,68},{5,453},{6,70},{7,455},{8,72}... | collective-permute-start | bytes 1769480 | tf_op jit(solution)/shard_map/ppermute | solution.py:441
  54.5 12.5 %copy-start.7 = (bf16[192,1536]{1,0:T(8,128)(2,1)}, bf16[192,1536]{1,0:T(8,128)(2,1)S(1)}, u32[]{:S(2)}) copy-start(bf16[192,1536]{1,0:T(8,128)(2,1)S(1)} %collective-permute-done.5.refs_0_) | copy-start | bytes 1769476
  54.5 12.5 %collective-permute-start.7 = (bf16[192,1536]{1,0:T(8,128)(2,1)S(1)}, bf16[192,1536]{1,0:T(8,128)(2,1)}, u32[]{:S(2)}, u32[]{:S(2)}) collective-permute-start(bf16[192,1536]{1,0:T(8,128)(2,1)S(1)} %collective-permute-done.5.refs_0_), channel_id=1, source_target_pairs={{0,64},{1,449},{2,66},{3,451},{4,68},{5,453},{6,70},{7,455},{8,72}... | collective-permute-start | bytes 1769480 | tf_op jit(solution)/shard_map/ppermute | solution.py:441
  60.7 25.2 %collective-permute-start.10 = (bf16[192,1536]{1,0:T(8,128)(2,1)}, bf16[192,1536]{1,0:T(8,128)(2,1)S(1)}, u32[]{:S(2)}, u32[]{:S(2)}) collective-permute-start(bf16[192,1536]{1,0:T(8,128)(2,1)} %collective-permute-done.8.refs_3_), channel_id=1, source_target_pairs={{0,64},{1,449},{2,66},{3,451},{4,68},{5,453},{6,70},{7,455},{8,72}... | collective-permute-start | bytes 1769480 | tf_op jit(solution)/shard_map/ppermute | solution.py:441
  67.0 18.9 %collective-permute-start.9 = (bf16[192,1536]{1,0:T(8,128)(2,1)}, bf16[192,1536]{1,0:T(8,128)(2,1)}, u32[]{:S(2)}, u32[]{:S(2)}) collective-permute-start(bf16[192,1536]{1,0:T(8,128)(2,1)} %collective-permute-done.7.refs_2_), channel_id=1, source_target_pairs={{0,64},{1,449},{2,66},{3,451},{4,68},{5,453},{6,70},{7,455},{8,72}... | collective-permute-start | bytes 1769480 | tf_op jit(solution)/shard_map/ppermute | solution.py:441
  72.4 8.8 %copy-start.2 = (s32[7]{0:T(128)S(1)}, s32[7]{0:T(128)}, u32[]{:S(2)}) copy-start(s32[7]{0:T(128)} %concatenate.3.where) | copy-start | bytes 88
  72.4 8.8 %collective-permute-start = (bf16[16,128,128]{2,1,0:T(8,128)(2,1)S(1)}, bf16[16,128,128]{2,1,0:T(8,128)(2,1)S(1)}, u32[]{:S(2)}, u32[]{:S(2)}) collective-permute-start(bf16[16,128,128]{2,1,0:T(8,128)(2,1)S(1)} %slice.4.own_kv), channel_id=1, source_target_pairs={{0,1},{1,0},{2,3},{3,2},{4,5},{5,4},{6,7},{7,6},{8,9},{9,8},{10,11... | collective-permute-start | bytes 1572872 | tf_op jit(solution)/shard_map/ppermute | solution.py:441
  85.9 8.5 %copy-start.3 = (bf16[192,1536]{1,0:T(8,128)(2,1)}, bf16[192,1536]{1,0:T(8,128)(2,1)S(1)}, u32[]{:S(2)}) copy-start(bf16[192,1536]{1,0:T(8,128)(2,1)S(1)} %collective-permute-done.10.refs_5_) | copy-start | bytes 1769476
  85.9 32.9 %all-to-all-start.1 = ((bf16[16,224,128]{2,1,0:T(8,128)(2,1)}), bf16[16,224,128]{2,1,0:T(8,128)(2,1)S(1)}, u32[]{:S(2)}, u32[]{:S(2)}) async-start(bf16[16,224,128]{2,1,0:T(8,128)(2,1)} %attend_shared.1), calls=%async_computation.1 | async-start | bytes 1835008 | tf_op jit(solution)/shard_map/all_to_all | solution.py:484
  94.4 24.4 %copy-start = (bf16[2,96,1536]{2,1,0:T(8,128)(2,1)S(1)}, bf16[2,96,1536]{2,1,0:T(8,128)(2,1)}, u32[]{:S(2)}) copy-start(bf16[2,96,1536]{2,1,0:T(8,128)(2,1)} %get-tuple-element.19) | copy-start | bytes 1769476
  94.4 24.4 %copy-start.1 = (bf16[2,96,1536]{2,1,0:T(8,128)(2,1)S(1)}, bf16[2,96,1536]{2,1,0:T(8,128)(2,1)}, u32[]{:S(2)}) copy-start(bf16[2,96,1536]{2,1,0:T(8,128)(2,1)} %get-tuple-element.20) | copy-start | bytes 1769476
  94.4 12.6 %collective-permute-start.14 = (bf16[192,1536]{1,0:T(8,128)(2,1)}, bf16[192,1536]{1,0:T(8,128)(2,1)S(1)}, u32[]{:S(2)}, u32[]{:S(2)}) collective-permute-start(bf16[192,1536]{1,0:T(8,128)(2,1)} %broadcast_select_fusion), channel_id=1, source_target_pairs={{0,64},{1,449},{2,66},{3,451},{4,68},{5,453},{6,70},{7,455},{8,72}... | collective-permute-start | bytes 1769480 | tf_op jit(solution)/shard_map/ppermute | solution.py:441
  100.6 11.8 %collective-permute-start.11 = (bf16[384,1536]{1,0:T(8,128)(2,1)}, bf16[384,1536]{1,0:T(8,128)(2,1)S(1)}, u32[]{:S(2)}, u32[]{:S(2)}) collective-permute-start(bf16[384,1536]{1,0:T(8,128)(2,1)} %get-tuple-element.28.refs_2_), channel_id=1, source_target_pairs={{0,1},{1,0},{2,3},{3,2},{4,5},{5,4},{6,7},{7,6},{8,9},{9,8},{10,11... | collective-permute-start | bytes 3538952 | tf_op jit(solution)/shard_map/ppermute | solution.py:441
  102.7 9.8 %collective-permute-start.12 = (bf16[384,1536]{1,0:T(8,128)(2,1)}, bf16[384,1536]{1,0:T(8,128)(2,1)S(1)}, u32[]{:S(2)}, u32[]{:S(2)}) collective-permute-start(bf16[384,1536]{1,0:T(8,128)(2,1)} %get-tuple-element.29.refs_3_), channel_id=1, source_target_pairs={{0,1},{1,0},{2,3},{3,2},{4,5},{5,4},{6,7},{7,6},{8,9},{9,8},{10,11... | collective-permute-start | bytes 3538952 | tf_op jit(solution)/shard_map/ppermute | solution.py:441
  105.0 9.6 %collective-permute-start.13 = (bf16[384,1536]{1,0:T(8,128)(2,1)}, bf16[384,1536]{1,0:T(8,128)(2,1)}, u32[]{:S(2)}, u32[]{:S(2)}) collective-permute-start(bf16[384,1536]{1,0:T(8,128)(2,1)} %get-tuple-element.30.refs_4_), channel_id=1, source_target_pairs={{0,1},{1,0},{2,3},{3,2},{4,5},{5,4},{6,7},{7,6},{8,9},{9,8},{10,11... | collective-permute-start | bytes 3538952 | tf_op jit(solution)/shard_map/ppermute | solution.py:441
  107.0 5.4 %collective-permute-start.15 = (bf16[192,1536]{1,0:T(8,128)(2,1)S(1)}, bf16[192,1536]{1,0:T(8,128)(2,1)S(1)}, u32[]{:S(2)}, u32[]{:S(2)}) collective-permute-start(bf16[192,1536]{1,0:T(8,128)(2,1)S(1)} %collective-permute-done.14.refs_8_), channel_id=1, source_target_pairs={{0,1},{1,0},{2,3},{3,2},{4,5},{5,4},{6,7},{7,6},{8,9},{9,8},{10,11... | collective-permute-start | bytes 1769480 | tf_op jit(solution)/shard_map/ppermute | solution.py:441
  112.5 1.0 copy-start.4
  113.5 1.0 copy-start.5

commit v10 on v9

--- a/solution.py
+++ b/solution.py
@@ -23,7 +23,7 @@
 RET_ROWS = ROWS + HALF
 WHOLE_LSE = RET_ROWS
 SHARED_LSE = WHOLE_LSE + N_SEQ
-RETURN = SHARED_LSE + N_SEQ
+RETURN = SHARED_LSE + N_SEQ // 2
 PACK_CHIPS = 4
 VIS_SEQ = VIS_ROWS * N_SEQ
 TXT_SEQ = TXT_ROWS * N_SEQ
@@ -177,7 +177,6 @@
 
     attend(lambda block: q_wide[block * Q_ROWS : (block + 1) * Q_ROWS, :], k_wide, v_turned, write)
     out[:, :ROWS, :] = whole[...]
-    log_totals.append(jnp.zeros((RETURN - SHARED_LSE - len(log_totals), HEAD_DIM), jnp.float32))
     rows = jnp.concatenate([whole_lse[...], *log_totals], axis=0).astype(jnp.bfloat16)
     for device in range(N_SEQ):
         out[device, WHOLE_LSE:, :] = rows
@@ -346,7 +345,7 @@
     rows = []
     for source in range(N_SEQ):
         whole = [ref[WHOLE_LSE : WHOLE_LSE + N_SEQ, :].astype(jnp.float32) for ref in (low, high)]
-        shared = [ref[SHARED_LSE : SHARED_LSE + N_SEQ, :].astype(jnp.float32) for ref in (low, high)]
+        shared = [ref[SHARED_LSE:RETURN, :].astype(jnp.float32) for ref in (low, high)]
         left, right = (item[source // 2 : source // 2 + 1] for item in shared)
         if source % 2 == 0:
             right = pltpu.roll(right, HALF, 1)

time: 125 us -> 124 us (level)
  starting transfers between devices: 74 us -> 72.7 us
    ppermute x16, starting transfers between devices: 54.4 us -> 53.1 us  [permute(): return lax.ppermute(operand, AXES, pairs)]
    unnamed x26 -> x24, local copies, waits for them, and re-layouts: 2.82 us -> 2.83 us
where the time goes in v10:
time: 124 us
  starting transfers between devices  72.7 us (59%)
  Pallas kernels  26.1 us (21%)
  waiting for transfers between devices  18.6 us (15%)
  local copies, waits for them, and re-layouts  3.64 us (3%)
  other arithmetic  1.45 us (1%)
    ppermute x16, starting transfers between devices, permute(): return lax.ppermute(operand, AXES, pairs)  53.1 us
    ppermute x16, waiting for transfers between devices, permute(): return lax.ppermute(operand, AXES, pairs)  14 us
    all_to_all x1, starting transfers between devices, on_device(): lax.all_to_all(sending, 'seq', split_axis=0, concat_axis=0, tiled=True)  12 us
    all_to_all x1, starting transfers between devices, on_device(): lax.all_to_all(returning, 'seq', split_axis=0, concat_axis=0, tiled=True)  7.63 us
    pallas_call x1, Pallas kernels, attend_whole(): pl.pallas_call(whole_kernel, grid=(steps,), in_specs=[pl.BlockSpec((N_SEQ...  6.82 us
    pallas_call x1, Pallas kernels, project(): pl.pallas_call(project_kernel, grid_spec=pltpu.PrefetchScalarGridSpec(num...  5.34 us
    pallas_call x1, Pallas kernels, attend_shared(): pl.pallas_call(shared_kernel, grid_spec=pltpu.PrefetchScalarGridSpec(num_...  4.7 us
    all_to_all x1, waiting for transfers between devices, on_device(): lax.all_to_all(returning, 'seq', split_axis=0, concat_axis=0, tiled=True)  4.66 us
  transfers between devices with their start and end apart: 18, of which 8 were waited for; matrix products, arithmetic and copies ran while one was open for 2% of the time, Pallas kernels for 14%

profile of v10, /device:TPU:1, one launch (start us, length us, event | category | flops | bytes accessed | tf_op | source)
XLA Modules:
  0.0 123.5 jit_solution(14942092997777016531)
XLA Ops:
  0.6 2.9 %pack.1 = bf16[16,584,128]{2,1,0:T(8,128)(2,1)} custom-call(s32[1,112]{1,0:T(1,128)} %bitcast.13, s32[1,16]{1,0:T(1,128)} %bitcast.14, bf16[112,9216]{1,0:T(8,128)(2,1)} %vv.1, bf16[112,9216]{1,0:T(8,128)(2,1)} %vv.1, bf16[112,9216]{1,0:T(8,128)(2,1)} %vv.1, bf16[16,9216]{1,0:T(8,128)(2,1)} %tv.1, bf16[16,9216]{1,0:T(8,128)(2,1)} %tv.1, bf16[16,9216]{1,0:T(8,128)(2,1)} %tv.1), custom_call_target="tpu_custom_call" | custom-call | tf_op jit(solution)/shard_map/pack/pallas_call | solution.py:66
  3.6 12.0 %all-to-all-start = ((bf16[16,584,128]{2,1,0:T(8,128)(2,1)}), bf16[16,584,128]{2,1,0:T(8,128)(2,1)S(1)}, u32[]{:S(2)}, u32[]{:S(2)}) async-start(bf16[16,584,128]{2,1,0:T(8,128)(2,1)} %pack.1), calls=%async_computation | async-start | bytes 4784128 | tf_op jit(solution)/shard_map/all_to_all | solution.py:473
  15.6 4.4 %collective-permute-start.1 = (bf16[96,1536]{1,0:T(8,128)(2,1)S(1)}, bf16[96,1536]{1,0:T(8,128)(2,1)S(1)}, u32[]{:S(2)}, u32[]{:S(2)}) collective-permute-start(bf16[96,1536]{1,0:T(8,128)(2,1)S(1)} %copy-done.7), channel_id=1, source_target_pairs={{0,16},{1,49},{2,18},{3,51},{4,20},{5,53},{6,22},{7,55},{8,24},{9,... | collective-permute-start | bytes 884744 | tf_op jit(solution)/shard_map/ppermute | solution.py:440
  20.9 2.7 %collective-permute-done.1.near = bf16[96,1536]{1,0:T(8,128)(2,1)S(1)} collective-permute-done((bf16[96,1536]{1,0:T(8,128)(2,1)S(1)}, bf16[96,1536]{1,0:T(8,128)(2,1)S(1)}, u32[]{:S(2)}, u32[]{:S(2)}) %collective-permute-start.1) | collective-permute-done | bytes 294944 | tf_op jit(solution)/shard_map/ppermute | solution.py:440
  23.6 3.8 %collective-permute-start.2 = (bf16[96,1536]{1,0:T(8,128)(2,1)S(1)}, bf16[96,1536]{1,0:T(8,128)(2,1)}, u32[]{:S(2)}, u32[]{:S(2)}) collective-permute-start(bf16[96,1536]{1,0:T(8,128)(2,1)S(1)} %collective-permute-done.1.near), channel_id=1, source_target_pairs={{0,1},{1,0},{2,3},{3,2},{4,5},{5,4},{6,7},{7,6},{8,9},{9,8},{10,11... | collective-permute-start | bytes 884744 | tf_op jit(solution)/shard_map/ppermute | solution.py:440
  27.4 1.3 %collective-permute-start.4 = (bf16[96,1536]{1,0:T(8,128)(2,1)S(1)}, bf16[96,1536]{1,0:T(8,128)(2,1)S(1)}, u32[]{:S(2)}, u32[]{:S(2)}) collective-permute-start(bf16[96,1536]{1,0:T(8,128)(2,1)S(1)} %collective-permute-done.3.part), channel_id=1, source_target_pairs={{0,1},{2,3},{4,5},{6,7},{8,9},{10,11},{12,13},{14,15},{16,17},{18,... | collective-permute-start | bytes 884744 | tf_op jit(solution)/shard_map/ppermute | solution.py:440
  29.6 2.4 %collective-permute-done.4.part_far = bf16[96,1536]{1,0:T(8,128)(2,1)S(1)} collective-permute-done((bf16[96,1536]{1,0:T(8,128)(2,1)S(1)}, bf16[96,1536]{1,0:T(8,128)(2,1)S(1)}, u32[]{:S(2)}, u32[]{:S(2)}) %collective-permute-start.4) | collective-permute-done | bytes 294944 | tf_op jit(solution)/shard_map/ppermute | solution.py:440
  32.7 3.3 %place.1 = (bf16[2,96,1536]{2,1,0:T(8,128)(2,1)}, bf16[2,96,1536]{2,1,0:T(8,128)(2,1)}) custom-call(s32[7]{0:T(128)} %concatenate.3.where, bf16[96,1536]{1,0:T(8,128)(2,1)} %mine.1, bf16[96,1536]{1,0:T(8,128)(2,1)} %copy-done.8, bf16[96,1536]{1,0:T(8,128)(2,1)} %collective-permute-done.2.near_far, bf16[96,1536]{1,0:T(8,128)(2,1)} %copy-done.9, ...), custom_call_target="tpu_custom_call" | custom-call | tf_op jit(solution)/shard_map/place/pallas_call | solution.py:291
  36.0 5.1 %collective-permute-start.6 = (bf16[192,1536]{1,0:T(8,128)(2,1)}, bf16[192,1536]{1,0:T(8,128)(2,1)S(1)}, u32[]{:S(2)}, u32[]{:S(2)}) collective-permute-start(bf16[192,1536]{1,0:T(8,128)(2,1)} %bitcast.11), channel_id=1, source_target_pairs={{0,64},{1,449},{2,66},{3,451},{4,68},{5,453},{6,70},{7,455},{8,72}... | collective-permute-start | bytes 1769480 | tf_op jit(solution)/shard_map/ppermute | solution.py:440
  41.0 3.0 %collective-permute-start.5 = (bf16[192,1536]{1,0:T(8,128)(2,1)}, bf16[192,1536]{1,0:T(8,128)(2,1)S(1)}, u32[]{:S(2)}, u32[]{:S(2)}) collective-permute-start(bf16[192,1536]{1,0:T(8,128)(2,1)} %bitcast.9), channel_id=1, source_target_pairs={{0,64},{1,449},{2,66},{3,451},{4,68},{5,453},{6,70},{7,455},{8,72}... | collective-permute-start | bytes 1769480 | tf_op jit(solution)/shard_map/ppermute | solution.py:440
  44.0 4.1 %collective-permute-done.6.refs_1_ = bf16[192,1536]{1,0:T(8,128)(2,1)S(1)} collective-permute-done((bf16[192,1536]{1,0:T(8,128)(2,1)}, bf16[192,1536]{1,0:T(8,128)(2,1)S(1)}, u32[]{:S(2)}, u32[]{:S(2)}) %collective-permute-start.6) | collective-permute-done | bytes 589856 | tf_op jit(solution)/shard_map/ppermute | solution.py:440
  48.2 5.2 %collective-permute-start.8 = (bf16[192,1536]{1,0:T(8,128)(2,1)S(1)}, bf16[192,1536]{1,0:T(8,128)(2,1)}, u32[]{:S(2)}, u32[]{:S(2)}) collective-permute-start(bf16[192,1536]{1,0:T(8,128)(2,1)S(1)} %collective-permute-done.6.refs_1_), channel_id=1, source_target_pairs={{0,64},{1,449},{2,66},{3,451},{4,68},{5,453},{6,70},{7,455},{8,72}... | collective-permute-start | bytes 1769480 | tf_op jit(solution)/shard_map/ppermute | solution.py:440
  53.4 1.1 collective-permute-done.5.refs_0_
  54.5 5.2 %collective-permute-start.7 = (bf16[192,1536]{1,0:T(8,128)(2,1)S(1)}, bf16[192,1536]{1,0:T(8,128)(2,1)}, u32[]{:S(2)}, u32[]{:S(2)}) collective-permute-start(bf16[192,1536]{1,0:T(8,128)(2,1)S(1)} %collective-permute-done.5.refs_0_), channel_id=1, source_target_pairs={{0,64},{1,449},{2,66},{3,451},{4,68},{5,453},{6,70},{7,455},{8,72}... | collective-permute-start | bytes 1769480 | tf_op jit(solution)/shard_map/ppermute | solution.py:440
  60.7 5.3 %collective-permute-start.10 = (bf16[192,1536]{1,0:T(8,128)(2,1)}, bf16[192,1536]{1,0:T(8,128)(2,1)}, u32[]{:S(2)}, u32[]{:S(2)}) collective-permute-start(bf16[192,1536]{1,0:T(8,128)(2,1)} %collective-permute-done.8.refs_3_), channel_id=1, source_target_pairs={{0,64},{1,449},{2,66},{3,451},{4,68},{5,453},{6,70},{7,455},{8,72}... | collective-permute-start | bytes 1769480 | tf_op jit(solution)/shard_map/ppermute | solution.py:440
  67.0 5.3 %collective-permute-start.9 = (bf16[192,1536]{1,0:T(8,128)(2,1)}, bf16[192,1536]{1,0:T(8,128)(2,1)}, u32[]{:S(2)}, u32[]{:S(2)}) collective-permute-start(bf16[192,1536]{1,0:T(8,128)(2,1)} %collective-permute-done.7.refs_2_), channel_id=1, source_target_pairs={{0,64},{1,449},{2,66},{3,451},{4,68},{5,453},{6,70},{7,455},{8,72}... | collective-permute-start | bytes 1769480 | tf_op jit(solution)/shard_map/ppermute | solution.py:440
  72.4 1.9 %collective-permute-start = (bf16[16,128,128]{2,1,0:T(8,128)(2,1)S(1)}, bf16[16,128,128]{2,1,0:T(8,128)(2,1)S(1)}, u32[]{:S(2)}, u32[]{:S(2)}) collective-permute-start(bf16[16,128,128]{2,1,0:T(8,128)(2,1)S(1)} %slice.4.own_kv), channel_id=1, source_target_pairs={{0,1},{1,0},{2,3},{3,2},{4,5},{5,4},{6,7},{7,6},{8,9},{9,8},{10,11... | collective-permute-start | bytes 1572872 | tf_op jit(solution)/shard_map/ppermute | solution.py:440
  74.4 6.8 %attend_whole.1 = (bf16[16,128,128]{2,1,0:T(8,128)(2,1)S(1)}, f32[16,128]{1,0:T(8,128)S(1)}) custom-call(bf16[16,584,128]{2,1,0:T(8,128)(2,1)S(1)} %all-to-all-done.cut.q.k.v, bf16[16,584,128]{2,1,0:T(8,128)(2,1)S(1)} %all-to-all-done.cut.q.k.v, bf16[16,584,128]{2,1,0:T(8,128)(2,1)S(1)} %all-to-all-done.cut.q.k.v, ...), custom_call_target="tpu_custom_call" | custom-call | flops 134217728 | bytes 2097152 | tf_op jit(solution)/shard_map/attend_whole/pallas_call | solution.py:214
  81.2 4.7 %attend_shared.1 = bf16[16,216,128]{2,1,0:T(8,128)(2,1)} custom-call(s32[7]{0:T(128)S(1)} %copy-done.2, bf16[16,584,128]{2,1,0:T(8,128)(2,1)S(1)} %all-to-all-done.cut.q.k.v, bf16[16,584,128]{2,1,0:T(8,128)(2,1)S(1)} %all-to-all-done.cut.q.k.v, bf16[16,128,128]{2,1,0:T(8,128)(2,1)S(1)} %slice.4.own_kv, ...), custom_call_target="tpu_custom_call" | custom-call | flops 67108864 | bytes 2097152 | tf_op jit(solution)/shard_map/attend_shared/pallas_call | solution.py:241
  85.9 7.6 %all-to-all-start.1 = ((bf16[16,216,128]{2,1,0:T(8,128)(2,1)}), bf16[16,216,128]{2,1,0:T(8,128)(2,1)S(1)}, u32[]{:S(2)}, u32[]{:S(2)}) async-start(bf16[16,216,128]{2,1,0:T(8,128)(2,1)} %attend_shared.1), calls=%async_computation.1 | async-start | bytes 1769472 | tf_op jit(solution)/shard_map/all_to_all | solution.py:483
  93.5 1.1 broadcast_select_fusion
  94.7 3.1 %collective-permute-start.14 = (bf16[192,1536]{1,0:T(8,128)(2,1)S(1)}, bf16[192,1536]{1,0:T(8,128)(2,1)S(1)}, u32[]{:S(2)}, u32[]{:S(2)}) collective-permute-start(bf16[192,1536]{1,0:T(8,128)(2,1)S(1)} %broadcast_select_fusion), channel_id=1, source_target_pairs={{0,64},{1,449},{2,66},{3,451},{4,68},{5,453},{6,70},{7,455},{8,72}... | collective-permute-start | bytes 1769480 | tf_op jit(solution)/shard_map/ppermute | solution.py:440
  97.8 3.1 %join.1 = (bf16[384,1536]{1,0:T(8,128)(2,1)}, bf16[384,1536]{1,0:T(8,128)(2,1)}, bf16[384,1536]{1,0:T(8,128)(2,1)}) custom-call(bf16[192,1536]{1,0:T(8,128)(2,1)} %copy-done.6, bf16[192,1536]{1,0:T(8,128)(2,1)} %copy-done.5, bf16[192,1536]{1,0:T(8,128)(2,1)} %collective-permute-done.7.refs_2_, bf16[192,1536]{1,0:T(8,128)(2,1)} %collective-permute-done.8.refs_3_, ...), custom_call_target="tpu_custom_call" | custom-call | tf_op jit(solution)/shard_map/join/pallas_call | solution.py:326
  100.9 1.9 %collective-permute-start.11 = (bf16[384,1536]{1,0:T(8,128)(2,1)}, bf16[384,1536]{1,0:T(8,128)(2,1)S(1)}, u32[]{:S(2)}, u32[]{:S(2)}) collective-permute-start(bf16[384,1536]{1,0:T(8,128)(2,1)} %get-tuple-element.28.refs_2_), channel_id=1, source_target_pairs={{0,1},{1,0},{2,3},{3,2},{4,5},{5,4},{6,7},{7,6},{8,9},{9,8},{10,11... | collective-permute-start | bytes 3538952 | tf_op jit(solution)/shard_map/ppermute | solution.py:440
  102.8 2.4 %collective-permute-start.12 = (bf16[384,1536]{1,0:T(8,128)(2,1)}, bf16[384,1536]{1,0:T(8,128)(2,1)S(1)}, u32[]{:S(2)}, u32[]{:S(2)}) collective-permute-start(bf16[384,1536]{1,0:T(8,128)(2,1)} %get-tuple-element.29.refs_3_), channel_id=1, source_target_pairs={{0,1},{1,0},{2,3},{3,2},{4,5},{5,4},{6,7},{7,6},{8,9},{9,8},{10,11... | collective-permute-start | bytes 3538952 | tf_op jit(solution)/shard_map/ppermute | solution.py:440
  105.2 1.9 %collective-permute-start.13 = (bf16[384,1536]{1,0:T(8,128)(2,1)}, bf16[384,1536]{1,0:T(8,128)(2,1)}, u32[]{:S(2)}, u32[]{:S(2)}) collective-permute-start(bf16[384,1536]{1,0:T(8,128)(2,1)} %get-tuple-element.30.refs_4_), channel_id=1, source_target_pairs={{0,1},{1,0},{2,3},{3,2},{4,5},{5,4},{6,7},{7,6},{8,9},{9,8},{10,11... | collective-permute-start | bytes 3538952 | tf_op jit(solution)/shard_map/ppermute | solution.py:440
  107.2 2.7 %collective-permute-start.15 = (bf16[192,1536]{1,0:T(8,128)(2,1)S(1)}, bf16[192,1536]{1,0:T(8,128)(2,1)S(1)}, u32[]{:S(2)}, u32[]{:S(2)}) collective-permute-start(bf16[192,1536]{1,0:T(8,128)(2,1)S(1)} %collective-permute-done.14.refs_8_), channel_id=1, source_target_pairs={{0,1},{1,0},{2,3},{3,2},{4,5},{5,4},{6,7},{7,6},{8,9},{9,8},{10,11... | collective-permute-start | bytes 1769480 | tf_op jit(solution)/shard_map/ppermute | solution.py:440
  109.8 1.6 %collective-permute-done.15.refs_9_ = bf16[192,1536]{1,0:T(8,128)(2,1)S(1)} collective-permute-done((bf16[192,1536]{1,0:T(8,128)(2,1)S(1)}, bf16[192,1536]{1,0:T(8,128)(2,1)S(1)}, u32[]{:S(2)}, u32[]{:S(2)}) %collective-permute-start.15) | collective-permute-done | bytes 589856 | tf_op jit(solution)/shard_map/ppermute | solution.py:440
  111.4 1.0 copy-done.3
  112.5 1.0 copy-done.4
  113.5 4.7 %all-to-all-done.1.ret = bf16[16,216,128]{2,1,0:T(8,128)(2,1)S(1)} async-done(((bf16[16,216,128]{2,1,0:T(8,128)(2,1)}), bf16[16,216,128]{2,1,0:T(8,128)(2,1)S(1)}, u32[]{:S(2)}, u32[]{:S(2)}) %all-to-all-start.1) | async-done | bytes 884768 | tf_op jit(solution)/shard_map/all_to_all | solution.py:483
  118.2 5.3 %project.1 = (bf16[112,1536]{1,0:T(8,128)(2,1)}, bf16[16,3072]{1,0:T(8,128)(2,1)}, f32[2,2048]{1,0:T(2,128)}) custom-call(s32[7]{0:T(128)S(1)} %copy-done.2, bf16[16,216,128]{2,1,0:T(8,128)(2,1)S(1)} %all-to-all-done.1.ret, bf16[192,1536]{1,0:T(8,128)(2,1)S(1)} %bitcast.10, bf16[192,1536]{1,0:T(8,128)(2,1)S(1)} %bitcast.12, ...), custom_call_target="tpu_custom_call" | custom-call | tf_op jit(solution)/shard_map/project/pallas_call | solution.py:404
  (43 shorter events, 4.6 us)
Async XLA Ops:
  3.6 12.0 %copy-start.7 = (bf16[96,1536]{1,0:T(8,128)(2,1)S(1)}, bf16[96,1536]{1,0:T(8,128)(2,1)}, u32[]{:S(2)}) copy-start(bf16[96,1536]{1,0:T(8,128)(2,1)} %mine.1) | copy-start | bytes 884740
  3.6 17.1 %copy-start.11 = (s32[24]{0:T(128)S(1)}, s32[24]{0:T(128)}, u32[]{:S(2)}) copy-start(s32[24]{0:T(128)} %param.10) | copy-start | bytes 292
  3.6 68.8 %all-to-all-start = ((bf16[16,584,128]{2,1,0:T(8,128)(2,1)}), bf16[16,584,128]{2,1,0:T(8,128)(2,1)S(1)}, u32[]{:S(2)}, u32[]{:S(2)}) async-start(bf16[16,584,128]{2,1,0:T(8,128)(2,1)} %pack.1), calls=%async_computation | async-start | bytes 4784128 | tf_op jit(solution)/shard_map/all_to_all | solution.py:473
  15.6 8.0 %collective-permute-start.1 = (bf16[96,1536]{1,0:T(8,128)(2,1)S(1)}, bf16[96,1536]{1,0:T(8,128)(2,1)S(1)}, u32[]{:S(2)}, u32[]{:S(2)}) collective-permute-start(bf16[96,1536]{1,0:T(8,128)(2,1)S(1)} %copy-done.7), channel_id=1, source_target_pairs={{0,16},{1,49},{2,18},{3,51},{4,20},{5,53},{6,22},{7,55},{8,24},{9,... | collective-permute-start | bytes 884744 | tf_op jit(solution)/shard_map/ppermute | solution.py:440
  19.9 7.4 %collective-permute-start.3 = (bf16[96,1536]{1,0:T(8,128)(2,1)S(1)}, bf16[96,1536]{1,0:T(8,128)(2,1)S(1)}, u32[]{:S(2)}, u32[]{:S(2)}) collective-permute-start(bf16[96,1536]{1,0:T(8,128)(2,1)S(1)} %copy-done.7), channel_id=1, source_target_pairs={{0,32},{2,34},{4,36},{6,38},{8,40},{10,42},{12,44},{14,46},{16,48}... | collective-permute-start | bytes 884744 | tf_op jit(solution)/shard_map/ppermute | solution.py:440
  23.6 8.4 %copy-start.8 = (bf16[96,1536]{1,0:T(8,128)(2,1)}, bf16[96,1536]{1,0:T(8,128)(2,1)S(1)}, u32[]{:S(2)}) copy-start(bf16[96,1536]{1,0:T(8,128)(2,1)S(1)} %collective-permute-done.1.near) | copy-start | bytes 884740
  23.6 6.0 %collective-permute-start.2 = (bf16[96,1536]{1,0:T(8,128)(2,1)S(1)}, bf16[96,1536]{1,0:T(8,128)(2,1)}, u32[]{:S(2)}, u32[]{:S(2)}) collective-permute-start(bf16[96,1536]{1,0:T(8,128)(2,1)S(1)} %collective-permute-done.1.near), channel_id=1, source_target_pairs={{0,1},{1,0},{2,3},{3,2},{4,5},{5,4},{6,7},{7,6},{8,9},{9,8},{10,11... | collective-permute-start | bytes 884744 | tf_op jit(solution)/shard_map/ppermute | solution.py:440
  27.4 4.6 %copy-start.9 = (bf16[96,1536]{1,0:T(8,128)(2,1)}, bf16[96,1536]{1,0:T(8,128)(2,1)S(1)}, u32[]{:S(2)}) copy-start(bf16[96,1536]{1,0:T(8,128)(2,1)S(1)} %collective-permute-done.3.part) | copy-start | bytes 884740
  27.4 4.6 %collective-permute-start.4 = (bf16[96,1536]{1,0:T(8,128)(2,1)S(1)}, bf16[96,1536]{1,0:T(8,128)(2,1)S(1)}, u32[]{:S(2)}, u32[]{:S(2)}) collective-permute-start(bf16[96,1536]{1,0:T(8,128)(2,1)S(1)} %collective-permute-done.3.part), channel_id=1, source_target_pairs={{0,1},{2,3},{4,5},{6,7},{8,9},{10,11},{12,13},{14,15},{16,17},{18,... | collective-permute-start | bytes 884744 | tf_op jit(solution)/shard_map/ppermute | solution.py:440
  32.0 0.7 copy-start.10
  36.0 12.2 %collective-permute-start.6 = (bf16[192,1536]{1,0:T(8,128)(2,1)}, bf16[192,1536]{1,0:T(8,128)(2,1)S(1)}, u32[]{:S(2)}, u32[]{:S(2)}) collective-permute-start(bf16[192,1536]{1,0:T(8,128)(2,1)} %bitcast.11), channel_id=1, source_target_pairs={{0,64},{1,449},{2,66},{3,451},{4,68},{5,453},{6,70},{7,455},{8,72}... | collective-permute-start | bytes 1769480 | tf_op jit(solution)/shard_map/ppermute | solution.py:440
  41.0 13.4 %collective-permute-start.5 = (bf16[192,1536]{1,0:T(8,128)(2,1)}, bf16[192,1536]{1,0:T(8,128)(2,1)S(1)}, u32[]{:S(2)}, u32[]{:S(2)}) collective-permute-start(bf16[192,1536]{1,0:T(8,128)(2,1)} %bitcast.9), channel_id=1, source_target_pairs={{0,64},{1,449},{2,66},{3,451},{4,68},{5,453},{6,70},{7,455},{8,72}... | collective-permute-start | bytes 1769480 | tf_op jit(solution)/shard_map/ppermute | solution.py:440
  48.2 18.9 %copy-start.5 = (bf16[192,1536]{1,0:T(8,128)(2,1)}, bf16[192,1536]{1,0:T(8,128)(2,1)S(1)}, u32[]{:S(2)}) copy-start(bf16[192,1536]{1,0:T(8,128)(2,1)S(1)} %collective-permute-done.6.refs_1_) | copy-start | bytes 1769476
  48.2 12.5 %collective-permute-start.8 = (bf16[192,1536]{1,0:T(8,128)(2,1)S(1)}, bf16[192,1536]{1,0:T(8,128)(2,1)}, u32[]{:S(2)}, u32[]{:S(2)}) collective-permute-start(bf16[192,1536]{1,0:T(8,128)(2,1)S(1)} %collective-permute-done.6.refs_1_), channel_id=1, source_target_pairs={{0,64},{1,449},{2,66},{3,451},{4,68},{5,453},{6,70},{7,455},{8,72}... | collective-permute-start | bytes 1769480 | tf_op jit(solution)/shard_map/ppermute | solution.py:440
  54.5 12.5 %copy-start.6 = (bf16[192,1536]{1,0:T(8,128)(2,1)}, bf16[192,1536]{1,0:T(8,128)(2,1)S(1)}, u32[]{:S(2)}) copy-start(bf16[192,1536]{1,0:T(8,128)(2,1)S(1)} %collective-permute-done.5.refs_0_) | copy-start | bytes 1769476
  54.5 12.5 %collective-permute-start.7 = (bf16[192,1536]{1,0:T(8,128)(2,1)S(1)}, bf16[192,1536]{1,0:T(8,128)(2,1)}, u32[]{:S(2)}, u32[]{:S(2)}) collective-permute-start(bf16[192,1536]{1,0:T(8,128)(2,1)S(1)} %collective-permute-done.5.refs_0_), channel_id=1, source_target_pairs={{0,64},{1,449},{2,66},{3,451},{4,68},{5,453},{6,70},{7,455},{8,72}... | collective-permute-start | bytes 1769480 | tf_op jit(solution)/shard_map/ppermute | solution.py:440
  60.7 25.2 %collective-permute-start.10 = (bf16[192,1536]{1,0:T(8,128)(2,1)}, bf16[192,1536]{1,0:T(8,128)(2,1)}, u32[]{:S(2)}, u32[]{:S(2)}) collective-permute-start(bf16[192,1536]{1,0:T(8,128)(2,1)} %collective-permute-done.8.refs_3_), channel_id=1, source_target_pairs={{0,64},{1,449},{2,66},{3,451},{4,68},{5,453},{6,70},{7,455},{8,72}... | collective-permute-start | bytes 1769480 | tf_op jit(solution)/shard_map/ppermute | solution.py:440
  67.0 18.9 %collective-permute-start.9 = (bf16[192,1536]{1,0:T(8,128)(2,1)}, bf16[192,1536]{1,0:T(8,128)(2,1)}, u32[]{:S(2)}, u32[]{:S(2)}) collective-permute-start(bf16[192,1536]{1,0:T(8,128)(2,1)} %collective-permute-done.7.refs_2_), channel_id=1, source_target_pairs={{0,64},{1,449},{2,66},{3,451},{4,68},{5,453},{6,70},{7,455},{8,72}... | collective-permute-start | bytes 1769480 | tf_op jit(solution)/shard_map/ppermute | solution.py:440
  72.4 8.8 %collective-permute-start = (bf16[16,128,128]{2,1,0:T(8,128)(2,1)S(1)}, bf16[16,128,128]{2,1,0:T(8,128)(2,1)S(1)}, u32[]{:S(2)}, u32[]{:S(2)}) collective-permute-start(bf16[16,128,128]{2,1,0:T(8,128)(2,1)S(1)} %slice.4.own_kv), channel_id=1, source_target_pairs={{0,1},{1,0},{2,3},{3,2},{4,5},{5,4},{6,7},{7,6},{8,9},{9,8},{10,11... | collective-permute-start | bytes 1572872 | tf_op jit(solution)/shard_map/ppermute | solution.py:440
  74.3 6.8 %copy-start.2 = (s32[7]{0:T(128)S(1)}, s32[7]{0:T(128)}, u32[]{:S(2)}) copy-start(s32[7]{0:T(128)} %concatenate.3.where) | copy-start | bytes 88
  85.9 32.3 %all-to-all-start.1 = ((bf16[16,216,128]{2,1,0:T(8,128)(2,1)}), bf16[16,216,128]{2,1,0:T(8,128)(2,1)S(1)}, u32[]{:S(2)}, u32[]{:S(2)}) async-start(bf16[16,216,128]{2,1,0:T(8,128)(2,1)} %attend_shared.1), calls=%async_computation.1 | async-start | bytes 1769472 | tf_op jit(solution)/shard_map/all_to_all | solution.py:483
  94.7 23.5 %copy-start = (bf16[2,96,1536]{2,1,0:T(8,128)(2,1)S(1)}, bf16[2,96,1536]{2,1,0:T(8,128)(2,1)}, u32[]{:S(2)}) copy-start(bf16[2,96,1536]{2,1,0:T(8,128)(2,1)} %get-tuple-element.19) | copy-start | bytes 1769476
  94.7 23.5 %copy-start.1 = (bf16[2,96,1536]{2,1,0:T(8,128)(2,1)S(1)}, bf16[2,96,1536]{2,1,0:T(8,128)(2,1)}, u32[]{:S(2)}) copy-start(bf16[2,96,1536]{2,1,0:T(8,128)(2,1)} %get-tuple-element.20) | copy-start | bytes 1769476
  94.7 12.5 %collective-permute-start.14 = (bf16[192,1536]{1,0:T(8,128)(2,1)S(1)}, bf16[192,1536]{1,0:T(8,128)(2,1)S(1)}, u32[]{:S(2)}, u32[]{:S(2)}) collective-permute-start(bf16[192,1536]{1,0:T(8,128)(2,1)S(1)} %broadcast_select_fusion), channel_id=1, source_target_pairs={{0,64},{1,449},{2,66},{3,451},{4,68},{5,453},{6,70},{7,455},{8,72}... | collective-permute-start | bytes 1769480 | tf_op jit(solution)/shard_map/ppermute | solution.py:440
  100.9 10.6 %collective-permute-start.11 = (bf16[384,1536]{1,0:T(8,128)(2,1)}, bf16[384,1536]{1,0:T(8,128)(2,1)S(1)}, u32[]{:S(2)}, u32[]{:S(2)}) collective-permute-start(bf16[384,1536]{1,0:T(8,128)(2,1)} %get-tuple-element.28.refs_2_), channel_id=1, source_target_pairs={{0,1},{1,0},{2,3},{3,2},{4,5},{5,4},{6,7},{7,6},{8,9},{9,8},{10,11... | collective-permute-start | bytes 3538952 | tf_op jit(solution)/shard_map/ppermute | solution.py:440
  102.8 8.6 %collective-permute-start.12 = (bf16[384,1536]{1,0:T(8,128)(2,1)}, bf16[384,1536]{1,0:T(8,128)(2,1)S(1)}, u32[]{:S(2)}, u32[]{:S(2)}) collective-permute-start(bf16[384,1536]{1,0:T(8,128)(2,1)} %get-tuple-element.29.refs_3_), channel_id=1, source_target_pairs={{0,1},{1,0},{2,3},{3,2},{4,5},{5,4},{6,7},{7,6},{8,9},{9,8},{10,11... | collective-permute-start | bytes 3538952 | tf_op jit(solution)/shard_map/ppermute | solution.py:440
  105.2 8.3 %collective-permute-start.13 = (bf16[384,1536]{1,0:T(8,128)(2,1)}, bf16[384,1536]{1,0:T(8,128)(2,1)}, u32[]{:S(2)}, u32[]{:S(2)}) collective-permute-start(bf16[384,1536]{1,0:T(8,128)(2,1)} %get-tuple-element.30.refs_4_), channel_id=1, source_target_pairs={{0,1},{1,0},{2,3},{3,2},{4,5},{5,4},{6,7},{7,6},{8,9},{9,8},{10,11... | collective-permute-start | bytes 3538952 | tf_op jit(solution)/shard_map/ppermute | solution.py:440
  107.2 4.3 %collective-permute-start.15 = (bf16[192,1536]{1,0:T(8,128)(2,1)S(1)}, bf16[192,1536]{1,0:T(8,128)(2,1)S(1)}, u32[]{:S(2)}, u32[]{:S(2)}) collective-permute-start(bf16[192,1536]{1,0:T(8,128)(2,1)S(1)} %collective-permute-done.14.refs_8_), channel_id=1, source_target_pairs={{0,1},{1,0},{2,3},{3,2},{4,5},{5,4},{6,7},{7,6},{8,9},{9,8},{10,11... | collective-permute-start | bytes 1769480 | tf_op jit(solution)/shard_map/ppermute | solution.py:440
  111.4 1.0 copy-start.3
  112.5 1.1 copy-start.4

commit v11 on v10

--- a/solution.py
+++ b/solution.py
@@ -187,7 +187,7 @@
 VMEM = 32 * 2**20
 PLACE_VMEM = 60 * 2**20
 JOIN_VMEM = 60 * 2**20
-PROJECT_VMEM = 50 * 2**20
+PROJECT_VMEM = 51 * 2**20
 
 
 def attention_scratch():
@@ -261,29 +261,35 @@
     )(where, received, received, own_kv, far_kv, whole, whole_lse)
 
 
-def place_kernel(where, mine, near, near_far, part, part_far, *halves):
+def place_kernel(where, mine, near, near_far, part, part_far, low, high, held, sems):
     x, core = where[1], where[2]
     sign = 1 - 2 * core
 
-    def put(to, shard):
-        to = (to + X_SIZE) % X_SIZE
-        for half, out in enumerate(halves):
-
-            @pl.when(to // 2 == half)
-            def _():
-                out[to % 2] = shard[...]
-
-    put(x, mine)
-    put(x - sign, near)
-    put(x + sign, near_far)
+    def load(shard, to, index):
+        return pltpu.make_async_copy(shard, held.at[(to + X_SIZE) % X_SIZE], sems.at[index])
+
+    loads = [load(mine, x, 0), load(near, x - sign, 1), load(near_far, x + sign, 2)]
+    for copy in loads:
+        copy.start()
 
     @pl.when(core == 0)
     def _():
-        put(x + 2, part)
+        load(part, x + 2, 3).start()
 
     @pl.when(core == 1)
     def _():
-        put(x + 2, part_far)
+        load(part_far, x + 2, 3).start()
+
+    for copy in loads + [load(part, x + 2, 3)]:
+        copy.wait()
+    stores = [
+        pltpu.make_async_copy(held.at[pl.ds(2 * half, 2)], out, sems.at[4 + half])
+        for half, out in enumerate((low, high))
+    ]
+    for store in stores:
+        store.start()
+    for store in stores:
+        store.wait()
 
 
 def place(where, mine, near, near_far, part, part_far):
@@ -293,8 +299,12 @@
         grid_spec=pltpu.PrefetchScalarGridSpec(
             num_scalar_prefetch=1,
             grid=(),
-            in_specs=[pl.BlockSpec(memory_space=pltpu.VMEM)] * 5,
-            out_specs=[pl.BlockSpec(memory_space=pltpu.VMEM)] * 2,
+            in_specs=[pl.BlockSpec(memory_space=pl.ANY)] * 5,
+            out_specs=[pl.BlockSpec(memory_space=pl.ANY)] * 2,
+            scratch_shapes=[
+                pltpu.VMEM((X_SIZE, rows, columns), jnp.bfloat16),
+                pltpu.SemaphoreType.DMA((6,)),
+            ],
         ),
         out_shape=[jax.ShapeDtypeStruct((2, rows, columns), jnp.bfloat16)] * 2,
         compiler_params=pltpu.CompilerParams(vmem_limit_bytes=PLACE_VMEM),
@@ -303,7 +313,7 @@
 
 
 def join_kernel(*refs):
-    halves, wholes, (held, in_sems, out_sems) = refs[:6], refs[6:9], refs[9:]
+    halves, wholes, (held, in_sems, out_sems) = refs[:8], refs[8:12], refs[12:]
     rows = halves[0].shape[0]
     loads = [
         pltpu.make_async_copy(half, held.at[index // 2, pl.ds(index % 2 * rows, rows)], in_sems.at[index])
@@ -325,13 +335,13 @@
     rows, columns = chunks[0][0].shape
     return pl.pallas_call(
         join_kernel,
-        in_specs=[pl.BlockSpec(memory_space=pl.ANY)] * 6,
-        out_specs=[pl.BlockSpec(memory_space=pl.ANY)] * 3,
-        out_shape=[jax.ShapeDtypeStruct((2 * rows, columns), jnp.bfloat16)] * 3,
+        in_specs=[pl.BlockSpec(memory_space=pl.ANY)] * 8,
+        out_specs=[pl.BlockSpec(memory_space=pl.ANY)] * 4,
+        out_shape=[jax.ShapeDtypeStruct((2 * rows, columns), jnp.bfloat16)] * 4,
         scratch_shapes=[
-            pltpu.VMEM((3, 2 * rows, columns), jnp.bfloat16),
-            pltpu.SemaphoreType.DMA((6,)),
-            pltpu.SemaphoreType.DMA((3,)),
+            pltpu.VMEM((4, 2 * rows, columns), jnp.bfloat16),
+            pltpu.SemaphoreType.DMA((8,)),
+            pltpu.SemaphoreType.DMA((4,)),
         ],
         compiler_params=pltpu.CompilerParams(vmem_limit_bytes=JOIN_VMEM),
         name="join",
@@ -358,14 +368,14 @@
 
 
 HOPS = (0, 1, 2, 3, -1, -2, -3)
-PIECES = 2 + 6 + 2
+PIECES = 7 + 2
 
 
 def project_kernel(where, ret, *refs):
     weights, (vis_out, txt_out, slots, held, sems) = refs[:PIECES], refs[PIECES:]
     y, core = where[0], where[2]
     sign = 1 - 2 * core
-    places = [(0, 0, 1), (0, 1, 1)] + [(chunk, 0, 2) for chunk in range(1, 7)] + [(7, core, 1), (7, 1 - core, 1)]
+    places = [(chunk, 0, 2) for chunk in range(7)] + [(7, core, 1), (7, 1 - core, 1)]
     copies = []
     for index, (chunk, half, count) in enumerate(places):
         start = chunk % 2 * TRIO + half * (TRIO // 2)
@@ -373,7 +383,7 @@
         copies.append(pltpu.make_async_copy(weights[index], to, sems.at[index]))
     for copy in copies:
         copy.start()
-    arrivals = [copies[:2]] + [[copy] for copy in copies[2:8]] + [copies[8:]]
+    arrivals = [[copy] for copy in copies[:7]] + [copies[7:]]
     for slot in range(SLOTS):
         valid = where[5 + slot] > 0
         for source, row in enumerate(slot_of(ret, where[3 + slot])):
@@ -482,8 +492,8 @@
     returning, chunks[1:] = lax.optimization_barrier((returning, chunks[1:]))
     returned = lax.all_to_all(returning, "seq", split_axis=0, concat_axis=0, tiled=True)
     opposite = shift_y(jnp.where(core == 0, *chunks[3]))
-    hops = join(chunks[1:])
-    weights = [*chunks[0], *hops, *map(swap, hops), opposite, swap(opposite)]
+    hops = join(chunks)
+    weights = [*hops, *map(swap, hops[1:]), opposite, swap(opposite)]
     vis_out, txt_out, lse_slots = project(where, returned, weights)
     return vis_out, txt_out, lse_slots
 

time: 124 us -> 124 us (level)
    unnamed x24 -> x20, local copies, waits for them, and re-layouts: 2.83 us -> 2.82 us
  transfers between devices with their start and end apart: 18 -> 18, of which waited for: 8 -> 8; matrix products, arithmetic and copies ran while one was open for 2% -> 2% of each run, Pallas kernels for 14% -> 15%
where the time goes in v11:
time: 124 us; the launch traced here: 123 us
  starting transfers between devices  72.4 us (58%)
  Pallas kernels  26.8 us (22%)
  waiting for transfers between devices  18.3 us (15%)
  local copies, waits for them, and re-layouts  3.58 us (3%)
  other arithmetic  1.45 us (1%)
    ppermute x16, starting transfers between devices, permute(): return lax.ppermute(operand, AXES, pairs)  52.8 us
    ppermute x16, waiting for transfers between devices, permute(): return lax.ppermute(operand, AXES, pairs)  14 us
    all_to_all x1, starting transfers between devices, on_device(): lax.all_to_all(sending, 'seq', split_axis=0, concat_axis=0, tiled=True)  12 us
    all_to_all x1, starting transfers between devices, on_device(): lax.all_to_all(returning, 'seq', split_axis=0, concat_axis=0, tiled=True)  7.63 us
    pallas_call x1, Pallas kernels, attend_whole(): pl.pallas_call(whole_kernel, grid=(steps,), in_specs=[pl.BlockSpec((N_SEQ...  6.82 us
    pallas_call x1, Pallas kernels, project(): pl.pallas_call(project_kernel, grid_spec=pltpu.PrefetchScalarGridSpec(num...  5.45 us
    pallas_call x1, Pallas kernels, attend_shared(): pl.pallas_call(shared_kernel, grid_spec=pltpu.PrefetchScalarGridSpec(num_...  4.78 us
    all_to_all x1, waiting for transfers between devices, on_device(): lax.all_to_all(returning, 'seq', split_axis=0, concat_axis=0, tiled=True)  4.29 us
  transfers between devices with their start and end apart: 18, of which 8 were waited for; matrix products, arithmetic and copies ran while one was open for 2% of the time, Pallas kernels for 15%

profile of v11, /device:TPU:1, one launch (start us, length us, event | category | flops | bytes accessed | tf_op | source)
XLA Modules:
  0.0 123.4 jit_solution(5311124721394683664)
XLA Ops:
  0.6 2.9 %pack.1 = bf16[16,584,128]{2,1,0:T(8,128)(2,1)} custom-call(s32[1,112]{1,0:T(1,128)} %bitcast.13, s32[1,16]{1,0:T(1,128)} %bitcast.14, bf16[112,9216]{1,0:T(8,128)(2,1)} %vv.1, bf16[112,9216]{1,0:T(8,128)(2,1)} %vv.1, bf16[112,9216]{1,0:T(8,128)(2,1)} %vv.1, bf16[16,9216]{1,0:T(8,128)(2,1)} %tv.1, bf16[16,9216]{1,0:T(8,128)(2,1)} %tv.1, bf16[16,9216]{1,0:T(8,128)(2,1)} %tv.1), custom_call_target="tpu_custom_call" | custom-call | tf_op jit(solution)/shard_map/pack/pallas_call | solution.py:66
  3.6 12.0 %all-to-all-start = ((bf16[16,584,128]{2,1,0:T(8,128)(2,1)}), bf16[16,584,128]{2,1,0:T(8,128)(2,1)S(1)}, u32[]{:S(2)}, u32[]{:S(2)}) async-start(bf16[16,584,128]{2,1,0:T(8,128)(2,1)} %pack.1), calls=%async_computation | async-start | bytes 4784128 | tf_op jit(solution)/shard_map/all_to_all | solution.py:483
  15.5 4.4 %collective-permute-start.1 = (bf16[96,1536]{1,0:T(8,128)(2,1)S(1)}, bf16[96,1536]{1,0:T(8,128)(2,1)S(1)}, u32[]{:S(2)}, u32[]{:S(2)}) collective-permute-start(bf16[96,1536]{1,0:T(8,128)(2,1)S(1)} %copy-done.5), channel_id=1, source_target_pairs={{0,16},{1,49},{2,18},{3,51},{4,20},{5,53},{6,22},{7,55},{8,24},{9,... | collective-permute-start | bytes 884744 | tf_op jit(solution)/shard_map/ppermute | solution.py:450
  20.9 2.7 %collective-permute-done.1.near = bf16[96,1536]{1,0:T(8,128)(2,1)S(1)} collective-permute-done((bf16[96,1536]{1,0:T(8,128)(2,1)S(1)}, bf16[96,1536]{1,0:T(8,128)(2,1)S(1)}, u32[]{:S(2)}, u32[]{:S(2)}) %collective-permute-start.1) | collective-permute-done | bytes 294944 | tf_op jit(solution)/shard_map/ppermute | solution.py:450
  23.6 3.8 %collective-permute-start.2 = (bf16[96,1536]{1,0:T(8,128)(2,1)S(1)}, bf16[96,1536]{1,0:T(8,128)(2,1)}, u32[]{:S(2)}, u32[]{:S(2)}) collective-permute-start(bf16[96,1536]{1,0:T(8,128)(2,1)S(1)} %collective-permute-done.1.near), channel_id=1, source_target_pairs={{0,1},{1,0},{2,3},{3,2},{4,5},{5,4},{6,7},{7,6},{8,9},{9,8},{10,11... | collective-permute-start | bytes 884744 | tf_op jit(solution)/shard_map/ppermute | solution.py:450
  27.4 1.3 %collective-permute-start.4 = (bf16[96,1536]{1,0:T(8,128)(2,1)S(1)}, bf16[96,1536]{1,0:T(8,128)(2,1)S(1)}, u32[]{:S(2)}, u32[]{:S(2)}) collective-permute-start(bf16[96,1536]{1,0:T(8,128)(2,1)S(1)} %collective-permute-done.3.part), channel_id=1, source_target_pairs={{0,1},{2,3},{4,5},{6,7},{8,9},{10,11},{12,13},{14,15},{16,17},{18,... | collective-permute-start | bytes 884744 | tf_op jit(solution)/shard_map/ppermute | solution.py:450
  29.5 2.5 %collective-permute-done.4.part_far = bf16[96,1536]{1,0:T(8,128)(2,1)S(1)} collective-permute-done((bf16[96,1536]{1,0:T(8,128)(2,1)S(1)}, bf16[96,1536]{1,0:T(8,128)(2,1)S(1)}, u32[]{:S(2)}, u32[]{:S(2)}) %collective-permute-start.4) | collective-permute-done | bytes 294944 | tf_op jit(solution)/shard_map/ppermute | solution.py:450
  32.7 3.0 %place.1 = (bf16[2,96,1536]{2,1,0:T(8,128)(2,1)}, bf16[2,96,1536]{2,1,0:T(8,128)(2,1)}) custom-call(s32[7]{0:T(128)} %concatenate.3.where, bf16[96,1536]{1,0:T(8,128)(2,1)} %mine.1, bf16[96,1536]{1,0:T(8,128)(2,1)} %copy-done.6, bf16[96,1536]{1,0:T(8,128)(2,1)} %collective-permute-done.2.near_far, bf16[96,1536]{1,0:T(8,128)(2,1)} %copy-done.7, ...), custom_call_target="tpu_custom_call" | custom-call | tf_op jit(solution)/shard_map/place/pallas_call | solution.py:297
  35.7 5.1 %collective-permute-start.6 = (bf16[192,1536]{1,0:T(8,128)(2,1)}, bf16[192,1536]{1,0:T(8,128)(2,1)S(1)}, u32[]{:S(2)}, u32[]{:S(2)}) collective-permute-start(bf16[192,1536]{1,0:T(8,128)(2,1)} %bitcast.11), channel_id=1, source_target_pairs={{0,64},{1,449},{2,66},{3,451},{4,68},{5,453},{6,70},{7,455},{8,72}... | collective-permute-start | bytes 1769480 | tf_op jit(solution)/shard_map/ppermute | solution.py:450
  40.8 3.0 %collective-permute-start.5 = (bf16[192,1536]{1,0:T(8,128)(2,1)}, bf16[192,1536]{1,0:T(8,128)(2,1)S(1)}, u32[]{:S(2)}, u32[]{:S(2)}) collective-permute-start(bf16[192,1536]{1,0:T(8,128)(2,1)} %bitcast.9), channel_id=1, source_target_pairs={{0,64},{1,449},{2,66},{3,451},{4,68},{5,453},{6,70},{7,455},{8,72}... | collective-permute-start | bytes 1769480 | tf_op jit(solution)/shard_map/ppermute | solution.py:450
  43.8 4.1 %collective-permute-done.6.refs_3_ = bf16[192,1536]{1,0:T(8,128)(2,1)S(1)} collective-permute-done((bf16[192,1536]{1,0:T(8,128)(2,1)}, bf16[192,1536]{1,0:T(8,128)(2,1)S(1)}, u32[]{:S(2)}, u32[]{:S(2)}) %collective-permute-start.6) | collective-permute-done | bytes 589856 | tf_op jit(solution)/shard_map/ppermute | solution.py:450
  47.9 5.2 %collective-permute-start.8 = (bf16[192,1536]{1,0:T(8,128)(2,1)S(1)}, bf16[192,1536]{1,0:T(8,128)(2,1)}, u32[]{:S(2)}, u32[]{:S(2)}) collective-permute-start(bf16[192,1536]{1,0:T(8,128)(2,1)S(1)} %collective-permute-done.6.refs_3_), channel_id=1, source_target_pairs={{0,64},{1,449},{2,66},{3,451},{4,68},{5,453},{6,70},{7,455},{8,72}... | collective-permute-start | bytes 1769480 | tf_op jit(solution)/shard_map/ppermute | solution.py:450
  53.1 1.1 collective-permute-done.5.refs_2_
  54.2 5.2 %collective-permute-start.7 = (bf16[192,1536]{1,0:T(8,128)(2,1)S(1)}, bf16[192,1536]{1,0:T(8,128)(2,1)}, u32[]{:S(2)}, u32[]{:S(2)}) collective-permute-start(bf16[192,1536]{1,0:T(8,128)(2,1)S(1)} %collective-permute-done.5.refs_2_), channel_id=1, source_target_pairs={{0,64},{1,449},{2,66},{3,451},{4,68},{5,453},{6,70},{7,455},{8,72}... | collective-permute-start | bytes 1769480 | tf_op jit(solution)/shard_map/ppermute | solution.py:450
  60.4 5.3 %collective-permute-start.10 = (bf16[192,1536]{1,0:T(8,128)(2,1)}, bf16[192,1536]{1,0:T(8,128)(2,1)}, u32[]{:S(2)}, u32[]{:S(2)}) collective-permute-start(bf16[192,1536]{1,0:T(8,128)(2,1)} %collective-permute-done.8.refs_5_), channel_id=1, source_target_pairs={{0,64},{1,449},{2,66},{3,451},{4,68},{5,453},{6,70},{7,455},{8,72}... | collective-permute-start | bytes 1769480 | tf_op jit(solution)/shard_map/ppermute | solution.py:450
  66.8 5.3 %collective-permute-start.9 = (bf16[192,1536]{1,0:T(8,128)(2,1)}, bf16[192,1536]{1,0:T(8,128)(2,1)}, u32[]{:S(2)}, u32[]{:S(2)}) collective-permute-start(bf16[192,1536]{1,0:T(8,128)(2,1)} %collective-permute-done.7.refs_4_), channel_id=1, source_target_pairs={{0,64},{1,449},{2,66},{3,451},{4,68},{5,453},{6,70},{7,455},{8,72}... | collective-permute-start | bytes 1769480 | tf_op jit(solution)/shard_map/ppermute | solution.py:450
  72.2 1.9 %collective-permute-start = (bf16[16,128,128]{2,1,0:T(8,128)(2,1)S(1)}, bf16[16,128,128]{2,1,0:T(8,128)(2,1)S(1)}, u32[]{:S(2)}, u32[]{:S(2)}) collective-permute-start(bf16[16,128,128]{2,1,0:T(8,128)(2,1)S(1)} %slice.4.own_kv), channel_id=1, source_target_pairs={{0,1},{1,0},{2,3},{3,2},{4,5},{5,4},{6,7},{7,6},{8,9},{9,8},{10,11... | collective-permute-start | bytes 1572872 | tf_op jit(solution)/shard_map/ppermute | solution.py:450
  74.1 6.8 %attend_whole.1 = (bf16[16,128,128]{2,1,0:T(8,128)(2,1)S(1)}, f32[16,128]{1,0:T(8,128)S(1)}) custom-call(bf16[16,584,128]{2,1,0:T(8,128)(2,1)S(1)} %all-to-all-done.cut.q.k.v, bf16[16,584,128]{2,1,0:T(8,128)(2,1)S(1)} %all-to-all-done.cut.q.k.v, bf16[16,584,128]{2,1,0:T(8,128)(2,1)S(1)} %all-to-all-done.cut.q.k.v, ...), custom_call_target="tpu_custom_call" | custom-call | flops 134217728 | bytes 2097152 | tf_op jit(solution)/shard_map/attend_whole/pallas_call | solution.py:214
  80.9 4.8 %attend_shared.1 = bf16[16,216,128]{2,1,0:T(8,128)(2,1)} custom-call(s32[7]{0:T(128)S(1)} %copy-done, bf16[16,584,128]{2,1,0:T(8,128)(2,1)S(1)} %all-to-all-done.cut.q.k.v, bf16[16,584,128]{2,1,0:T(8,128)(2,1)S(1)} %all-to-all-done.cut.q.k.v, bf16[16,128,128]{2,1,0:T(8,128)(2,1)S(1)} %slice.4.own_kv, bf16[16,128,128]{2,1,0:T(8,128)(2,1)S(1)} %collective-permute-done.far_kv, ...), custom_call_target="tpu_custom_call" | custom-call | flops 67108864 | bytes 2097152 | tf_op jit(solution)/shard_map/attend_shared/pallas_call | solution.py:241
  85.7 7.6 %all-to-all-start.1 = ((bf16[16,216,128]{2,1,0:T(8,128)(2,1)}), bf16[16,216,128]{2,1,0:T(8,128)(2,1)S(1)}, u32[]{:S(2)}, u32[]{:S(2)}) async-start(bf16[16,216,128]{2,1,0:T(8,128)(2,1)} %attend_shared.1), calls=%async_computation.1 | async-start | bytes 1769472 | tf_op jit(solution)/shard_map/all_to_all | solution.py:493
  93.4 1.1 broadcast_select_fusion
  94.5 3.0 %collective-permute-start.14 = (bf16[192,1536]{1,0:T(8,128)(2,1)S(1)}, bf16[192,1536]{1,0:T(8,128)(2,1)S(1)}, u32[]{:S(2)}, u32[]{:S(2)}) collective-permute-start(bf16[192,1536]{1,0:T(8,128)(2,1)S(1)} %broadcast_select_fusion), channel_id=1, source_target_pairs={{0,64},{1,449},{2,66},{3,451},{4,68},{5,453},{6,70},{7,455},{8,72}... | collective-permute-start | bytes 1769480 | tf_op jit(solution)/shard_map/ppermute | solution.py:450
  97.5 3.8 %join.1 = (bf16[384,1536]{1,0:T(8,128)(2,1)}, bf16[384,1536]{1,0:T(8,128)(2,1)}, bf16[384,1536]{1,0:T(8,128)(2,1)}, bf16[384,1536]{1,0:T(8,128)(2,1)}) custom-call(bf16[192,1536]{1,0:T(8,128)(2,1)} %bitcast.10, bf16[192,1536]{1,0:T(8,128)(2,1)} %bitcast.12, bf16[192,1536]{1,0:T(8,128)(2,1)} %copy-done.4, bf16[192,1536]{1,0:T(8,128)(2,1)} %copy-done.3, ...), custom_call_target="tpu_custom_call" | custom-call | tf_op jit(solution)/shard_map/join/pallas_call | solution.py:336
  101.3 1.9 %collective-permute-start.11 = (bf16[384,1536]{1,0:T(8,128)(2,1)}, bf16[384,1536]{1,0:T(8,128)(2,1)S(1)}, u32[]{:S(2)}, u32[]{:S(2)}) collective-permute-start(bf16[384,1536]{1,0:T(8,128)(2,1)} %get-tuple-element.30.refs_1_), channel_id=1, source_target_pairs={{0,1},{1,0},{2,3},{3,2},{4,5},{5,4},{6,7},{7,6},{8,9},{9,8},{10,11... | collective-permute-start | bytes 3538952 | tf_op jit(solution)/shard_map/ppermute | solution.py:450
  103.2 2.4 %collective-permute-start.12 = (bf16[384,1536]{1,0:T(8,128)(2,1)}, bf16[384,1536]{1,0:T(8,128)(2,1)S(1)}, u32[]{:S(2)}, u32[]{:S(2)}) collective-permute-start(bf16[384,1536]{1,0:T(8,128)(2,1)} %get-tuple-element.31.refs_2_), channel_id=1, source_target_pairs={{0,1},{1,0},{2,3},{3,2},{4,5},{5,4},{6,7},{7,6},{8,9},{9,8},{10,11... | collective-permute-start | bytes 3538952 | tf_op jit(solution)/shard_map/ppermute | solution.py:450
  105.7 1.9 %collective-permute-start.13 = (bf16[384,1536]{1,0:T(8,128)(2,1)}, bf16[384,1536]{1,0:T(8,128)(2,1)}, u32[]{:S(2)}, u32[]{:S(2)}) collective-permute-start(bf16[384,1536]{1,0:T(8,128)(2,1)} %get-tuple-element.32.refs_3_), channel_id=1, source_target_pairs={{0,1},{1,0},{2,3},{3,2},{4,5},{5,4},{6,7},{7,6},{8,9},{9,8},{10,11... | collective-permute-start | bytes 3538952 | tf_op jit(solution)/shard_map/ppermute | solution.py:450
  107.6 2.4 %collective-permute-start.15 = (bf16[192,1536]{1,0:T(8,128)(2,1)S(1)}, bf16[192,1536]{1,0:T(8,128)(2,1)S(1)}, u32[]{:S(2)}, u32[]{:S(2)}) collective-permute-start(bf16[192,1536]{1,0:T(8,128)(2,1)S(1)} %collective-permute-done.14.refs_7_), channel_id=1, source_target_pairs={{0,1},{1,0},{2,3},{3,2},{4,5},{5,4},{6,7},{7,6},{8,9},{9,8},{10,11... | collective-permute-start | bytes 1769480 | tf_op jit(solution)/shard_map/ppermute | solution.py:450
  110.0 1.6 %collective-permute-done.15.refs_8_ = bf16[192,1536]{1,0:T(8,128)(2,1)S(1)} collective-permute-done((bf16[192,1536]{1,0:T(8,128)(2,1)S(1)}, bf16[192,1536]{1,0:T(8,128)(2,1)S(1)}, u32[]{:S(2)}, u32[]{:S(2)}) %collective-permute-start.15) | collective-permute-done | bytes 589856 | tf_op jit(solution)/shard_map/ppermute | solution.py:450
  111.6 1.0 copy-done.1
  112.7 1.0 copy-done.2
  113.7 4.3 %all-to-all-done.1.ret = bf16[16,216,128]{2,1,0:T(8,128)(2,1)S(1)} async-done(((bf16[16,216,128]{2,1,0:T(8,128)(2,1)}), bf16[16,216,128]{2,1,0:T(8,128)(2,1)S(1)}, u32[]{:S(2)}, u32[]{:S(2)}) %all-to-all-start.1) | async-done | bytes 884768 | tf_op jit(solution)/shard_map/all_to_all | solution.py:493
  118.0 5.4 %project.1 = (bf16[112,1536]{1,0:T(8,128)(2,1)}, bf16[16,3072]{1,0:T(8,128)(2,1)}, f32[2,2048]{1,0:T(2,128)}) custom-call(s32[7]{0:T(128)S(1)} %copy-done, bf16[16,216,128]{2,1,0:T(8,128)(2,1)S(1)} %all-to-all-done.1.ret, bf16[384,1536]{1,0:T(8,128)(2,1)} %get-tuple-element.29.refs_0_, bf16[384,1536]{1,0:T(8,128)(2,1)} %get-tuple-element.30.refs_1_, ...), custom_call_target="tpu_custom_call" | custom-call | tf_op jit(solution)/shard_map/project/pallas_call | solution.py:414
  (39 shorter events, 4.5 us)
Async XLA Ops:
  3.6 12.0 %copy-start.5 = (bf16[96,1536]{1,0:T(8,128)(2,1)S(1)}, bf16[96,1536]{1,0:T(8,128)(2,1)}, u32[]{:S(2)}) copy-start(bf16[96,1536]{1,0:T(8,128)(2,1)} %mine.1) | copy-start | bytes 884740
  3.6 17.1 %copy-start.9 = (s32[24]{0:T(128)S(1)}, s32[24]{0:T(128)}, u32[]{:S(2)}) copy-start(s32[24]{0:T(128)} %param.10) | copy-start | bytes 292
  3.6 68.5 %all-to-all-start = ((bf16[16,584,128]{2,1,0:T(8,128)(2,1)}), bf16[16,584,128]{2,1,0:T(8,128)(2,1)S(1)}, u32[]{:S(2)}, u32[]{:S(2)}) async-start(bf16[16,584,128]{2,1,0:T(8,128)(2,1)} %pack.1), calls=%async_computation | async-start | bytes 4784128 | tf_op jit(solution)/shard_map/all_to_all | solution.py:483
  15.5 8.0 %collective-permute-start.1 = (bf16[96,1536]{1,0:T(8,128)(2,1)S(1)}, bf16[96,1536]{1,0:T(8,128)(2,1)S(1)}, u32[]{:S(2)}, u32[]{:S(2)}) collective-permute-start(bf16[96,1536]{1,0:T(8,128)(2,1)S(1)} %copy-done.5), channel_id=1, source_target_pairs={{0,16},{1,49},{2,18},{3,51},{4,20},{5,53},{6,22},{7,55},{8,24},{9,... | collective-permute-start | bytes 884744 | tf_op jit(solution)/shard_map/ppermute | solution.py:450
  19.9 7.4 %collective-permute-start.3 = (bf16[96,1536]{1,0:T(8,128)(2,1)S(1)}, bf16[96,1536]{1,0:T(8,128)(2,1)S(1)}, u32[]{:S(2)}, u32[]{:S(2)}) collective-permute-start(bf16[96,1536]{1,0:T(8,128)(2,1)S(1)} %copy-done.5), channel_id=1, source_target_pairs={{0,32},{2,34},{4,36},{6,38},{8,40},{10,42},{12,44},{14,46},{16,48}... | collective-permute-start | bytes 884744 | tf_op jit(solution)/shard_map/ppermute | solution.py:450
  23.6 8.4 %copy-start.6 = (bf16[96,1536]{1,0:T(8,128)(2,1)}, bf16[96,1536]{1,0:T(8,128)(2,1)S(1)}, u32[]{:S(2)}) copy-start(bf16[96,1536]{1,0:T(8,128)(2,1)S(1)} %collective-permute-done.1.near) | copy-start | bytes 884740
  23.6 5.9 %collective-permute-start.2 = (bf16[96,1536]{1,0:T(8,128)(2,1)S(1)}, bf16[96,1536]{1,0:T(8,128)(2,1)}, u32[]{:S(2)}, u32[]{:S(2)}) collective-permute-start(bf16[96,1536]{1,0:T(8,128)(2,1)S(1)} %collective-permute-done.1.near), channel_id=1, source_target_pairs={{0,1},{1,0},{2,3},{3,2},{4,5},{5,4},{6,7},{7,6},{8,9},{9,8},{10,11... | collective-permute-start | bytes 884744 | tf_op jit(solution)/shard_map/ppermute | solution.py:450
  27.4 4.6 %copy-start.7 = (bf16[96,1536]{1,0:T(8,128)(2,1)}, bf16[96,1536]{1,0:T(8,128)(2,1)S(1)}, u32[]{:S(2)}) copy-start(bf16[96,1536]{1,0:T(8,128)(2,1)S(1)} %collective-permute-done.3.part) | copy-start | bytes 884740
  27.4 4.6 %collective-permute-start.4 = (bf16[96,1536]{1,0:T(8,128)(2,1)S(1)}, bf16[96,1536]{1,0:T(8,128)(2,1)S(1)}, u32[]{:S(2)}, u32[]{:S(2)}) collective-permute-start(bf16[96,1536]{1,0:T(8,128)(2,1)S(1)} %collective-permute-done.3.part), channel_id=1, source_target_pairs={{0,1},{2,3},{4,5},{6,7},{8,9},{10,11},{12,13},{14,15},{16,17},{18,... | collective-permute-start | bytes 884744 | tf_op jit(solution)/shard_map/ppermute | solution.py:450
  32.0 0.7 copy-start.8
  35.7 12.2 %collective-permute-start.6 = (bf16[192,1536]{1,0:T(8,128)(2,1)}, bf16[192,1536]{1,0:T(8,128)(2,1)S(1)}, u32[]{:S(2)}, u32[]{:S(2)}) collective-permute-start(bf16[192,1536]{1,0:T(8,128)(2,1)} %bitcast.11), channel_id=1, source_target_pairs={{0,64},{1,449},{2,66},{3,451},{4,68},{5,453},{6,70},{7,455},{8,72}... | collective-permute-start | bytes 1769480 | tf_op jit(solution)/shard_map/ppermute | solution.py:450
  40.8 13.4 %collective-permute-start.5 = (bf16[192,1536]{1,0:T(8,128)(2,1)}, bf16[192,1536]{1,0:T(8,128)(2,1)S(1)}, u32[]{:S(2)}, u32[]{:S(2)}) collective-permute-start(bf16[192,1536]{1,0:T(8,128)(2,1)} %bitcast.9), channel_id=1, source_target_pairs={{0,64},{1,449},{2,66},{3,451},{4,68},{5,453},{6,70},{7,455},{8,72}... | collective-permute-start | bytes 1769480 | tf_op jit(solution)/shard_map/ppermute | solution.py:450
  47.9 18.9 %copy-start.3 = (bf16[192,1536]{1,0:T(8,128)(2,1)}, bf16[192,1536]{1,0:T(8,128)(2,1)S(1)}, u32[]{:S(2)}) copy-start(bf16[192,1536]{1,0:T(8,128)(2,1)S(1)} %collective-permute-done.6.refs_3_) | copy-start | bytes 1769476
  47.9 12.5 %collective-permute-start.8 = (bf16[192,1536]{1,0:T(8,128)(2,1)S(1)}, bf16[192,1536]{1,0:T(8,128)(2,1)}, u32[]{:S(2)}, u32[]{:S(2)}) collective-permute-start(bf16[192,1536]{1,0:T(8,128)(2,1)S(1)} %collective-permute-done.6.refs_3_), channel_id=1, source_target_pairs={{0,64},{1,449},{2,66},{3,451},{4,68},{5,453},{6,70},{7,455},{8,72}... | collective-permute-start | bytes 1769480 | tf_op jit(solution)/shard_map/ppermute | solution.py:450
  54.2 12.5 %copy-start.4 = (bf16[192,1536]{1,0:T(8,128)(2,1)}, bf16[192,1536]{1,0:T(8,128)(2,1)S(1)}, u32[]{:S(2)}) copy-start(bf16[192,1536]{1,0:T(8,128)(2,1)S(1)} %collective-permute-done.5.refs_2_) | copy-start | bytes 1769476
  54.2 12.5 %collective-permute-start.7 = (bf16[192,1536]{1,0:T(8,128)(2,1)S(1)}, bf16[192,1536]{1,0:T(8,128)(2,1)}, u32[]{:S(2)}, u32[]{:S(2)}) collective-permute-start(bf16[192,1536]{1,0:T(8,128)(2,1)S(1)} %collective-permute-done.5.refs_2_), channel_id=1, source_target_pairs={{0,64},{1,449},{2,66},{3,451},{4,68},{5,453},{6,70},{7,455},{8,72}... | collective-permute-start | bytes 1769480 | tf_op jit(solution)/shard_map/ppermute | solution.py:450
  60.4 25.3 %collective-permute-start.10 = (bf16[192,1536]{1,0:T(8,128)(2,1)}, bf16[192,1536]{1,0:T(8,128)(2,1)}, u32[]{:S(2)}, u32[]{:S(2)}) collective-permute-start(bf16[192,1536]{1,0:T(8,128)(2,1)} %collective-permute-done.8.refs_5_), channel_id=1, source_target_pairs={{0,64},{1,449},{2,66},{3,451},{4,68},{5,453},{6,70},{7,455},{8,72}... | collective-permute-start | bytes 1769480 | tf_op jit(solution)/shard_map/ppermute | solution.py:450
  66.8 19.0 %collective-permute-start.9 = (bf16[192,1536]{1,0:T(8,128)(2,1)}, bf16[192,1536]{1,0:T(8,128)(2,1)}, u32[]{:S(2)}, u32[]{:S(2)}) collective-permute-start(bf16[192,1536]{1,0:T(8,128)(2,1)} %collective-permute-done.7.refs_4_), channel_id=1, source_target_pairs={{0,64},{1,449},{2,66},{3,451},{4,68},{5,453},{6,70},{7,455},{8,72}... | collective-permute-start | bytes 1769480 | tf_op jit(solution)/shard_map/ppermute | solution.py:450
  72.2 8.8 %collective-permute-start = (bf16[16,128,128]{2,1,0:T(8,128)(2,1)S(1)}, bf16[16,128,128]{2,1,0:T(8,128)(2,1)S(1)}, u32[]{:S(2)}, u32[]{:S(2)}) collective-permute-start(bf16[16,128,128]{2,1,0:T(8,128)(2,1)S(1)} %slice.4.own_kv), channel_id=1, source_target_pairs={{0,1},{1,0},{2,3},{3,2},{4,5},{5,4},{6,7},{7,6},{8,9},{9,8},{10,11... | collective-permute-start | bytes 1572872 | tf_op jit(solution)/shard_map/ppermute | solution.py:450
  74.1 6.8 %copy-start = (s32[7]{0:T(128)S(1)}, s32[7]{0:T(128)}, u32[]{:S(2)}) copy-start(s32[7]{0:T(128)} %concatenate.3.where) | copy-start | bytes 88
  85.7 32.3 %all-to-all-start.1 = ((bf16[16,216,128]{2,1,0:T(8,128)(2,1)}), bf16[16,216,128]{2,1,0:T(8,128)(2,1)S(1)}, u32[]{:S(2)}, u32[]{:S(2)}) async-start(bf16[16,216,128]{2,1,0:T(8,128)(2,1)} %attend_shared.1), calls=%async_computation.1 | async-start | bytes 1769472 | tf_op jit(solution)/shard_map/all_to_all | solution.py:493
  94.5 13.1 %collective-permute-start.14 = (bf16[192,1536]{1,0:T(8,128)(2,1)S(1)}, bf16[192,1536]{1,0:T(8,128)(2,1)S(1)}, u32[]{:S(2)}, u32[]{:S(2)}) collective-permute-start(bf16[192,1536]{1,0:T(8,128)(2,1)S(1)} %broadcast_select_fusion), channel_id=1, source_target_pairs={{0,64},{1,449},{2,66},{3,451},{4,68},{5,453},{6,70},{7,455},{8,72}... | collective-permute-start | bytes 1769480 | tf_op jit(solution)/shard_map/ppermute | solution.py:450
  101.3 10.3 %collective-permute-start.11 = (bf16[384,1536]{1,0:T(8,128)(2,1)}, bf16[384,1536]{1,0:T(8,128)(2,1)S(1)}, u32[]{:S(2)}, u32[]{:S(2)}) collective-permute-start(bf16[384,1536]{1,0:T(8,128)(2,1)} %get-tuple-element.30.refs_1_), channel_id=1, source_target_pairs={{0,1},{1,0},{2,3},{3,2},{4,5},{5,4},{6,7},{7,6},{8,9},{9,8},{10,11... | collective-permute-start | bytes 3538952 | tf_op jit(solution)/shard_map/ppermute | solution.py:450
  103.2 8.4 %collective-permute-start.12 = (bf16[384,1536]{1,0:T(8,128)(2,1)}, bf16[384,1536]{1,0:T(8,128)(2,1)S(1)}, u32[]{:S(2)}, u32[]{:S(2)}) collective-permute-start(bf16[384,1536]{1,0:T(8,128)(2,1)} %get-tuple-element.31.refs_2_), channel_id=1, source_target_pairs={{0,1},{1,0},{2,3},{3,2},{4,5},{5,4},{6,7},{7,6},{8,9},{9,8},{10,11... | collective-permute-start | bytes 3538952 | tf_op jit(solution)/shard_map/ppermute | solution.py:450
  105.7 8.1 %collective-permute-start.13 = (bf16[384,1536]{1,0:T(8,128)(2,1)}, bf16[384,1536]{1,0:T(8,128)(2,1)}, u32[]{:S(2)}, u32[]{:S(2)}) collective-permute-start(bf16[384,1536]{1,0:T(8,128)(2,1)} %get-tuple-element.32.refs_3_), channel_id=1, source_target_pairs={{0,1},{1,0},{2,3},{3,2},{4,5},{5,4},{6,7},{7,6},{8,9},{9,8},{10,11... | collective-permute-start | bytes 3538952 | tf_op jit(solution)/shard_map/ppermute | solution.py:450
  107.6 4.0 %collective-permute-start.15 = (bf16[192,1536]{1,0:T(8,128)(2,1)S(1)}, bf16[192,1536]{1,0:T(8,128)(2,1)S(1)}, u32[]{:S(2)}, u32[]{:S(2)}) collective-permute-start(bf16[192,1536]{1,0:T(8,128)(2,1)S(1)} %collective-permute-done.14.refs_7_), channel_id=1, source_target_pairs={{0,1},{1,0},{2,3},{3,2},{4,5},{5,4},{6,7},{7,6},{8,9},{9,8},{10,11... | collective-permute-start | bytes 1769480 | tf_op jit(solution)/shard_map/ppermute | solution.py:450
  111.6 1.0 copy-start.1
  112.7 1.0 copy-start.2
